TPU v7x, 32 devices: a whole 2x2x4 slice. The times are simulated.
32 devices in a mesh: rep: 8 (over z, core), shard: 4 (over y, x).
Axes of the slice: x: 2, y: 2, z: 4, core: 2. Of those that a mesh axis runs over, the one named last changes fastest.
Arguments:
- tokens: bfloat16 [8, 1024, 2048], P('rep', 'shard'), may hold values from -8 to 8
- piece_start: int32 [8], P('rep'), may hold values from 0 to 768
- positions: int32 [8, 1024], P('rep', 'shard'), may hold values from 0 to 2046, as said below
- w_query: float32 [2048, 2048], P('shard', 'rep'), may hold values from -0.125 to 0.125
- w_key: float32 [2048, 2048], P('shard', 'rep'), may hold values from -0.125 to 0.125
- w_value: float32 [2048, 2048], P('shard', 'rep'), may hold values from -0.125 to 0.125
- w_out: float32 [2048, 2048], P('shard', 'rep'), may hold values from -0.125 to 0.125
- query_gain: float32 [2048], P('shard'), may hold values from 0.9 to 1.6
- key_gain: float32 [2048], P('shard'), may hold values from 0.9 to 1.6
- attn_gain: float32 [2048], P('shard'), may hold values from 0.5 to 1.5
- w_gate: float32 [2048, 8192], P('shard', 'rep'), may hold values from -0.125 to 0.125
- w_up: float32 [2048, 8192], P('shard', 'rep'), may hold values from -0.125 to 0.125
- w_down: float32 [8192, 2048], P('shard', 'rep'), may hold values from -0.0625 to 0.0625
- mlp_gain: float32 [2048], P('shard'), may hold values from 0.5 to 1.5
- cotangent: bfloat16 [8, 1024, 2048], P('rep', 'shard'), may hold values from -6 to 6
Outputs:
- output: bfloat16 [8, 1024, 2048], P('rep', 'shard')
- grad_tokens: float32 [8, 1024, 2048], P('rep', 'shard')
- grad_w_query: float32 [2048, 2048], P('shard', 'rep')
- grad_w_key: float32 [2048, 2048], P('shard', 'rep')
- grad_w_value: float32 [2048, 2048], P('shard', 'rep')
- grad_w_out: float32 [2048, 2048], P('shard', 'rep')
- grad_query_gain: float32 [2048], P('shard')
- grad_key_gain: float32 [2048], P('shard')
- grad_attn_gain: float32 [2048], P('shard')
- grad_w_gate: float32 [2048, 8192], P('shard', 'rep')
- grad_w_up: float32 [2048, 8192], P('shard', 'rep')
- grad_w_down: float32 [8192, 2048], P('shard', 'rep')
- grad_mlp_gain: float32 [2048], P('shard')
Inputs may be any that keep to these rules, and one draw needn't show every extreme that they name: `positions`: along each sequence the position ids rise by 1 or 2 from one token to the next, and the last token's id is 2046.
All inputs are finite; a program needn't handle non-finite values.
Results may differ from a plain program's by a relative error of at most 0.025.
Values may be sent and summed in bfloat16 or wider, within the bound.
No kernel may reach another device: no remote copies, remote signals or barrier semaphores. Data moves between devices by JAX's collectives and lax.ppermute only.
A program may use at most 512 MiB of HBM per device.

v0:
```python
import jax
import jax.numpy as jnp
from jax import lax
from jax.sharding import PartitionSpec as P

HEADS = 16
HEAD_DIM = 128
PIECE = 256


epsilon = 1e-06
rope_base = 500000.0


def to_low(tensor):
    return tensor.astype(jnp.bfloat16)


def mat_mul(left, right):
    return jnp.dot(left, right, preferred_element_type=jnp.float32)


def dot_first(left, right):
    return lax.dot_general(
        left, right, (((0,), (0,)), ((), ())), preferred_element_type=jnp.float32
    )


def dot_last(left, right):
    return lax.dot_general(
        left, right, (((1,), (1,)), ((), ())), preferred_element_type=jnp.float32
    )


def rms_norm(tensor):
    inv_rms = lax.rsqrt(jnp.mean(tensor * tensor, axis=-1, keepdims=True) + epsilon)
    return (tensor * inv_rms, inv_rms)


def norm_back(upstream, normed, inv_rms, gain_vec):
    gain_grad = jnp.sum(upstream * normed, axis=0)
    scaled = upstream * gain_vec
    result = inv_rms * (scaled - normed * jnp.mean(scaled * normed, axis=-1, keepdims=True))
    return (result, gain_grad)


def frequencies():
    return jnp.power(
        jnp.float32(rope_base), -2.0 * jnp.arange(HEAD_DIM // 2, dtype=jnp.float32) / HEAD_DIM
    )


def rotate(tensor, cosines, sines, direction):
    row_count = tensor.shape[0]
    split_heads = tensor.reshape(row_count, HEADS, 2, HEAD_DIM // 2)
    first_half = split_heads[:, :, 0]
    second_half = split_heads[:, :, 1]
    new_first = first_half * cosines - direction * second_half * sines
    new_second = second_half * cosines + direction * first_half * sines
    return jnp.stack([new_first, new_second], axis=2).reshape(row_count, HEADS * HEAD_DIM)


def piece_mask(piece_first, row_first, row_count, col_count):
    row_pos = row_first + lax.iota(jnp.int32, row_count)[:, None]
    col_pos = lax.iota(jnp.int32, col_count)[None, :]
    row_inside = (row_pos >= piece_first) & (row_pos < piece_first + PIECE)
    col_inside = (col_pos >= piece_first) & (col_pos < piece_first + PIECE)
    return (col_pos <= row_pos) | row_inside & col_inside


def masked_scores(query_block, key_block, piece_first, row_first):
    query_count = query_block.shape[0]
    key_count = key_block.shape[0]
    query_heads = query_block.reshape(query_count, HEADS, HEAD_DIM)
    key_heads = key_block.reshape(key_count, HEADS, HEAD_DIM)
    scores = jnp.einsum(
        "qhd,khd->hqk", query_heads, key_heads, preferred_element_type=jnp.float32
    ) * HEAD_DIM ** (-0.5)
    allowed = piece_mask(piece_first, row_first, query_count, key_count)
    return jnp.where(allowed[None], scores, -1e30)


def body(
    tokens,
    piece_start,
    positions,
    w_query,
    w_key,
    w_value,
    w_out,
    query_gain,
    key_gain,
    attn_gain,
    w_gate,
    w_up,
    w_down,
    mlp_gain,
    cotangent,
):
    seq_count, span_len, model_width = tokens.shape
    row_count = seq_count * span_len
    shard_count = lax.axis_size("shard")
    score_scale = HEAD_DIM ** (-0.5)
    row_first = lax.axis_index("shard") * span_len
    tok_low = tokens.reshape(row_count, model_width)
    tok_full = tok_low.astype(jnp.float32)
    angles = positions.reshape(row_count).astype(jnp.float32)[:, None] * frequencies()
    cosines = jnp.cos(angles)[:, None, :]
    sines = jnp.sin(angles)[:, None, :]
    query_rows, key_rows_m, value_rows_m, out_rows_m, gate_rows, up_rows, down_rows = (
        lax.all_gather(to_low(w_query), "rep", axis=1, tiled=True),
        lax.all_gather(to_low(w_key), "rep", axis=1, tiled=True),
        lax.all_gather(to_low(w_value), "rep", axis=1, tiled=True),
        lax.all_gather(to_low(w_out), "rep", axis=1, tiled=True),
        lax.all_gather(to_low(w_gate), "rep", axis=1, tiled=True),
        lax.all_gather(to_low(w_up), "rep", axis=1, tiled=True),
        lax.all_gather(to_low(w_down), "rep", axis=1, tiled=True),
    )
    query_low, key_low, value_low, out_low, qgain_low, kgain_low, again_low = (
        lax.all_gather(query_rows, "shard", axis=0, tiled=True),
        lax.all_gather(key_rows_m, "shard", axis=0, tiled=True),
        lax.all_gather(value_rows_m, "shard", axis=0, tiled=True),
        lax.all_gather(out_rows_m, "shard", axis=0, tiled=True),
        lax.all_gather(to_low(query_gain), "shard", axis=0, tiled=True),
        lax.all_gather(to_low(key_gain), "shard", axis=0, tiled=True),
        lax.all_gather(to_low(attn_gain), "shard", axis=0, tiled=True),
    )
    qgain_full = qgain_low.astype(jnp.float32)
    kgain_full = kgain_low.astype(jnp.float32)
    again_full = again_low.astype(jnp.float32)
    query_raw = mat_mul(tok_low, query_low)
    key_raw = mat_mul(tok_low, key_low)
    query_hat, query_inv = rms_norm(query_raw)
    key_hat, key_inv = rms_norm(key_raw)
    queries = to_low(rotate(query_hat * qgain_full, cosines, sines, 1.0))
    key_rows = to_low(rotate(key_hat * kgain_full, cosines, sines, 1.0))
    value_rows = to_low(mat_mul(tok_low, value_low))
    key_all, value_all = (
        lax.all_gather(
            key_rows.reshape(seq_count, span_len, model_width), "shard", axis=1, tiled=True
        ),
        lax.all_gather(
            value_rows.reshape(seq_count, span_len, model_width), "shard", axis=1, tiled=True
        ),
    )
    query_seq = queries.reshape(seq_count, span_len, model_width)

    def attend(packed):
        query_block, key_block, value_block, piece_first = packed
        scores = masked_scores(query_block, key_block, piece_first, row_first)
        row_max = jnp.max(scores, axis=-1, keepdims=True)
        row_total = jnp.sum(jnp.exp(scores - row_max), axis=-1, keepdims=True)
        log_block = row_max + jnp.log(row_total)
        weights_low = to_low(jnp.exp(scores - log_block))
        value_heads = value_block.reshape(key_block.shape[0], HEADS, HEAD_DIM)
        mixed_heads = jnp.einsum(
            "hqk,khd->qhd", weights_low, value_heads, preferred_element_type=jnp.float32
        )
        return (
            to_low(mixed_heads.reshape(query_block.shape[0], HEADS * HEAD_DIM)),
            log_block[:, :, 0],
        )

    mixed_low, log_total = lax.map(attend, (query_seq, key_all, value_all, piece_start))
    mixed_rows = mixed_low.reshape(row_count, model_width)
    branch = mat_mul(mixed_rows, out_low)
    branch_hat, branch_inv = rms_norm(branch)
    hidden = tok_full + branch_hat * again_full
    hidden_low = to_low(hidden)
    gate_low, up_low, down_low, mgain_low = (
        lax.all_gather(gate_rows, "shard", axis=0, tiled=True),
        lax.all_gather(up_rows, "shard", axis=0, tiled=True),
        lax.all_gather(down_rows, "shard", axis=0, tiled=True),
        lax.all_gather(to_low(mlp_gain), "shard", axis=0, tiled=True),
    )
    mgain_full = mgain_low.astype(jnp.float32)
    gate_val = mat_mul(hidden_low, gate_low)
    up_val = mat_mul(hidden_low, up_low)
    gate_sig = jax.nn.sigmoid(gate_val)
    gate_act = gate_val * gate_sig
    inner_low = to_low(gate_act * up_val)
    second = mat_mul(inner_low, down_low)
    second_hat, second_inv = rms_norm(second)
    output_rows = hidden + second_hat * mgain_full
    output = to_low(output_rows).reshape(seq_count, span_len, model_width)
    gate_back, up_back, down_back = (
        lax.all_gather(gate_rows, "shard", axis=0, tiled=True),
        lax.all_gather(up_rows, "shard", axis=0, tiled=True),
        lax.all_gather(down_rows, "shard", axis=0, tiled=True),
    )
    grad_out = cotangent.reshape(row_count, model_width).astype(jnp.float32)
    grad_second, grad_mgain = norm_back(grad_out, second_hat, second_inv, mgain_full)
    grad_second_low = to_low(grad_second)
    grad_inner = dot_last(grad_second_low, down_back)
    grad_gate_low = to_low(grad_inner * up_val * gate_sig * (1.0 + gate_val * (1.0 - gate_sig)))
    grad_up_low = to_low(grad_inner * gate_act)
    ff_width = grad_inner.shape[1]
    down_share = lax.psum_scatter(
        dot_first(inner_low, grad_second_low).astype(jnp.bfloat16),
        "shard",
        scatter_dimension=0,
        tiled=True,
    )
    gate_up_low = jnp.concatenate([grad_gate_low, grad_up_low], axis=1)
    gate_share = lax.psum_scatter(
        dot_first(hidden_low, gate_up_low).astype(jnp.bfloat16),
        "shard",
        scatter_dimension=0,
        tiled=True,
    ).astype(jnp.float32)
    grad_hidden = grad_out + dot_last(grad_gate_low, gate_back) + dot_last(grad_up_low, up_back)
    query_back, key_back, value_back, out_back = (
        lax.all_gather(query_rows, "shard", axis=0, tiled=True),
        lax.all_gather(key_rows_m, "shard", axis=0, tiled=True),
        lax.all_gather(value_rows_m, "shard", axis=0, tiled=True),
        lax.all_gather(out_rows_m, "shard", axis=0, tiled=True),
    )
    grad_branch, grad_again = norm_back(grad_hidden, branch_hat, branch_inv, again_full)
    grad_branch_low = to_low(grad_branch)
    grad_mixed = to_low(dot_last(grad_branch_low, out_back)).reshape(
        seq_count, span_len, model_width
    )

    def attend_back(packed):
        query_block, key_block, value_block, grad_block, log_block, piece_first = packed
        query_count = query_block.shape[0]
        key_count = key_block.shape[0]
        scores = masked_scores(query_block, key_block, piece_first, row_first)
        softmax_out = jnp.exp(scores - log_block[:, :, None])
        weights_low = to_low(softmax_out)
        query_heads = query_block.reshape(query_count, HEADS, HEAD_DIM)
        key_heads = key_block.reshape(key_count, HEADS, HEAD_DIM)
        value_heads = value_block.reshape(key_count, HEADS, HEAD_DIM)
        grad_heads = grad_block.reshape(query_count, HEADS, HEAD_DIM)
        grad_probs = jnp.einsum(
            "qhd,khd->hqk", grad_heads, value_heads, preferred_element_type=jnp.float32
        )
        row_delta = jnp.sum(softmax_out * grad_probs, axis=-1, keepdims=True)
        grad_scores = to_low(softmax_out * (grad_probs - row_delta))
        grad_query_heads = (
            jnp.einsum("hqk,khd->qhd", grad_scores, key_heads, preferred_element_type=jnp.float32)
            * score_scale
        )
        grad_key_heads = (
            jnp.einsum("hqk,qhd->khd", grad_scores, query_heads, preferred_element_type=jnp.float32)
            * score_scale
        )
        grad_value_heads = jnp.einsum(
            "hqk,qhd->khd", weights_low, grad_heads, preferred_element_type=jnp.float32
        )
        return (
            grad_query_heads.reshape(query_count, HEADS * HEAD_DIM),
            grad_key_heads.reshape(key_count, HEADS * HEAD_DIM),
            grad_value_heads.reshape(key_count, HEADS * HEAD_DIM),
        )

    grad_query_seq, grad_key_part, grad_value_part = lax.map(
        attend_back, (query_seq, key_all, value_all, grad_mixed, log_total, piece_start)
    )
    grad_key_seq, grad_value_seq = (
        lax.psum_scatter(
            grad_key_part.astype(jnp.bfloat16), "shard", scatter_dimension=1, tiled=True
        ).astype(jnp.float32),
        lax.psum_scatter(
            grad_value_part.astype(jnp.bfloat16), "shard", scatter_dimension=1, tiled=True
        ).astype(jnp.float32),
    )
    grad_query_rot = rotate(grad_query_seq.reshape(row_count, model_width), cosines, sines, -1.0)
    grad_key_rot = rotate(grad_key_seq.reshape(row_count, model_width), cosines, sines, -1.0)
    grad_query_raw, grad_qgain = norm_back(grad_query_rot, query_hat, query_inv, qgain_full)
    grad_key_raw, grad_kgain = norm_back(grad_key_rot, key_hat, key_inv, kgain_full)
    grad_query_low = to_low(grad_query_raw)
    grad_key_low = to_low(grad_key_raw)
    grad_value_low = to_low(grad_value_seq.reshape(row_count, model_width))
    projections_low = jnp.concatenate([grad_query_low, grad_key_low, grad_value_low], axis=1)
    attn_share = lax.psum_scatter(
        jnp.concatenate(
            [dot_first(tok_low, projections_low), dot_first(mixed_rows, grad_branch_low)], axis=1
        ).astype(jnp.bfloat16),
        "shard",
        scatter_dimension=0,
        tiled=True,
    ).astype(jnp.float32)
    grad_input = (
        grad_hidden
        + dot_last(grad_query_low, query_back)
        + dot_last(grad_key_low, key_back)
        + dot_last(grad_value_low, value_back)
    )
    totals = (
        lax.psum_scatter(
            attn_share[:, :model_width].astype(jnp.bfloat16), "rep", scatter_dimension=1, tiled=True
        ).astype(jnp.float32),
        lax.psum_scatter(
            attn_share[:, model_width : 2 * model_width].astype(jnp.bfloat16),
            "rep",
            scatter_dimension=1,
            tiled=True,
        ).astype(jnp.float32),
        lax.psum_scatter(
            attn_share[:, 2 * model_width : 3 * model_width].astype(jnp.bfloat16),
            "rep",
            scatter_dimension=1,
            tiled=True,
        ).astype(jnp.float32),
        lax.psum_scatter(
            attn_share[:, 3 * model_width :].astype(jnp.bfloat16),
            "rep",
            scatter_dimension=1,
            tiled=True,
        ).astype(jnp.float32),
        lax.psum_scatter(
            gate_share[:, :ff_width].astype(jnp.bfloat16), "rep", scatter_dimension=1, tiled=True
        ).astype(jnp.float32),
        lax.psum_scatter(
            gate_share[:, ff_width:].astype(jnp.bfloat16), "rep", scatter_dimension=1, tiled=True
        ).astype(jnp.float32),
        lax.psum_scatter(down_share, "rep", scatter_dimension=1, tiled=True).astype(jnp.float32),
    )
    gain_total = lax.psum(
        jnp.stack([grad_qgain, grad_kgain, grad_again, grad_mgain]), ("rep", "shard")
    )
    own_rows = model_width // shard_count
    gain_own = lax.dynamic_slice_in_dim(gain_total, lax.axis_index("shard") * own_rows, own_rows, 1)
    return (
        output,
        grad_input.reshape(seq_count, span_len, model_width),
        totals[0],
        totals[1],
        totals[2],
        totals[3],
        gain_own[0],
        gain_own[1],
        gain_own[2],
        totals[4],
        totals[5],
        totals[6],
        gain_own[3],
    )


def solution(mesh):
    in_specs = (
        P("rep", "shard", None),
        P("rep"),
        P("rep", "shard"),
        P("shard", "rep"),
        P("shard", "rep"),
        P("shard", "rep"),
        P("shard", "rep"),
        P("shard"),
        P("shard"),
        P("shard"),
        P("shard", "rep"),
        P("shard", "rep"),
        P("shard", "rep"),
        P("shard"),
        P("rep", "shard", None),
    )
    out_specs = (
        P("rep", "shard", None),
        P("rep", "shard", None),
        P("shard", "rep"),
        P("shard", "rep"),
        P("shard", "rep"),
        P("shard", "rep"),
        P("shard"),
        P("shard"),
        P("shard"),
        P("shard", "rep"),
        P("shard", "rep"),
        P("shard", "rep"),
        P("shard"),
    )
    return jax.shard_map(body, mesh=mesh, in_specs=in_specs, out_specs=out_specs, check_vma=False)
```

profile of v0, /device:TPU:4, one launch (start us, length us, event | category | flops | bytes accessed | tf_op | source)
XLA Modules:
  0.0 4149.7 jit_solution(68243543071563641)
XLA Ops:
  13.0 29.0 all-gather.30.cloned.1.call-done
  42.1 32.0 all-gather.26.cloned.1.call-done
  74.2 32.0 all-gather.22.cloned.1.call-done
  112.5 8.0 all-gather.2
  120.6 7.1 all-gather.1
  128.8 66.2 %all-gather.32.cloned.1.call-done = bf16[2048,2048]{1,0:T(8,128)(2,1)} async-done(((bf16[512,2048]{1,0:T(8,128)(2,1)}), bf16[2048,2048]{1,0:T(8,128)(2,1)}) %all-gather.32.cloned.1.call-update) | async-done | bytes 8388624 | tf_op jit(solution)/shard_map/all_gather | solution.py:121
  194.9 5.8 multiply_reduce_fusion.9
  205.9 78.4 %all-gather.28.cloned.1.call-done = bf16[2048,2048]{1,0:T(8,128)(2,1)} async-done(((bf16[512,2048]{1,0:T(8,128)(2,1)}), bf16[2048,2048]{1,0:T(8,128)(2,1)}) %all-gather.28.cloned.1.call-update) | async-done | bytes 8388624 | tf_op jit(solution)/shard_map/all_gather | solution.py:120
  284.3 5.8 multiply_reduce_fusion.10
  300.8 72.8 %all-gather.24.cloned.1.call-done = bf16[2048,2048]{1,0:T(8,128)(2,1)} async-done(((bf16[512,2048]{1,0:T(8,128)(2,1)}), bf16[2048,2048]{1,0:T(8,128)(2,1)}) %all-gather.24.cloned.1.call-update) | async-done | bytes 8388624 | tf_op jit(solution)/shard_map/all_gather | solution.py:122
  373.6 6.7 convolution_convert_fusion.5
  380.4 26.0 all-gather.36.cloned.1.call-done
  406.5 83.5 %all-gather.40.cloned.1.call-done = bf16[512,8192]{1,0:T(8,128)(2,1)} async-done(((bf16[512,1024]{1,0:T(8,128)(2,1)}), bf16[512,8192]{1,0:T(8,128)(2,1)}) %all-gather.40.cloned.1.call-update) | async-done | bytes 8388624 | tf_op jit(solution)/shard_map/all_gather | solution.py:115
  490.1 82.2 %all-gather.44.cloned.1.call-done = bf16[512,8192]{1,0:T(8,128)(2,1)} async-done(((bf16[512,1024]{1,0:T(8,128)(2,1)}), bf16[512,8192]{1,0:T(8,128)(2,1)}) %all-gather.44.cloned.1.call-update) | async-done | bytes 8388624 | tf_op jit(solution)/shard_map/all_gather | solution.py:116
  572.3 82.4 %all-gather.48.cloned.1.call-done = bf16[2048,2048]{1,0:T(8,128)(2,1)} async-done(((bf16[2048,256]{1,0:T(8,128)(2,1)}), bf16[2048,2048]{1,0:T(8,128)(2,1)}) %all-gather.48.cloned.1.call-update) | async-done | bytes 8388624 | tf_op jit(solution)/shard_map/all_gather | solution.py:117
  655.6 8.0 all-gather.3
  663.6 7.1 all-gather.4
  671.3 36.7 all-gather.34.cloned.1.call-done
  707.9 5.5 fusion
  713.4 4.4 exponential_reduce_fusion
  720.0 42.9 %all-gather.52.cloned.1.call-done = bf16[1024,2048]{1,0:T(8,128)(2,1)} async-done(((bf16[256,2048]{1,0:T(8,128)(2,1)}), bf16[1024,2048]{1,0:T(8,128)(2,1)}) %all-gather.52.cloned.1.call-update) | async-done | bytes 4194320 | tf_op jit(solution)/shard_map/all_gather | solution.py:142
  762.9 10.3 fusion.24
  773.2 79.3 %all-gather.38.cloned.1.call-done = bf16[2048,2048]{1,0:T(8,128)(2,1)} async-done(((bf16[512,2048]{1,0:T(8,128)(2,1)}), bf16[2048,2048]{1,0:T(8,128)(2,1)}) %all-gather.38.cloned.1.call-update) | async-done | bytes 8388624 | tf_op jit(solution)/shard_map/all_gather | solution.py:123
  852.5 5.8 multiply_reduce_fusion.8
  860.0 291.4 %all-gather.42.cloned.1.call-done = bf16[2048,8192]{1,0:T(8,128)(2,1)} async-done(((bf16[512,8192]{1,0:T(8,128)(2,1)}), bf16[2048,8192]{1,0:T(8,128)(2,1)}) %all-gather.42.cloned.1.call-update) | async-done | bytes 33554448 | tf_op jit(solution)/shard_map/all_gather | solution.py:171
  1151.4 20.6 fusion.51
  1172.1 278.3 %all-gather.46.cloned.1.call-done = bf16[2048,8192]{1,0:T(8,128)(2,1)} async-done(((bf16[512,8192]{1,0:T(8,128)(2,1)}), bf16[2048,8192]{1,0:T(8,128)(2,1)}) %all-gather.46.cloned.1.call-update) | async-done | bytes 33554448 | tf_op jit(solution)/shard_map/all_gather | solution.py:172
  1450.3 27.1 multiply_convert_fusion.4
  1477.4 271.8 %all-gather.50.cloned.1.call-done = bf16[8192,2048]{1,0:T(8,128)(2,1)} async-done(((bf16[2048,2048]{1,0:T(8,128)(2,1)}), bf16[8192,2048]{1,0:T(8,128)(2,1)}) %all-gather.50.cloned.1.call-update) | async-done | bytes 33554448 | tf_op jit(solution)/shard_map/all_gather | solution.py:173
  1749.3 16.4 multiply_reduce_fusion.7
  1767.1 22.4 multiply_convert_fusion.2
  1789.5 17.8 convert_add_fusion
  1807.3 19.3 multiply_reduce_fusion.1
  1826.6 4.1 multiply_convert_fusion.7
  1831.7 5.7 convolution_convert_fusion.4
  1838.0 14.3 multiply_reduce_fusion
  1852.3 12.2 multiply_convert_fusion
  1864.6 4.0 multiply_convert_fusion.1
  1869.2 9.6 convolution_convert_fusion.3
  1878.8 6.5 copy.79
  1886.8 5.7 convolution_convert_fusion.2
  1892.5 6.4 convolution_multiply_fusion
  1898.9 22.9 reduce-scatter.14.cloned.1.call-done
  1931.0 3.6 multiply_reduce_fusion.3
  1938.7 39.0 reduce-scatter.16.cloned.1.call-done
  1977.7 13.7 convert_bitcast_fusion
  1991.4 23.9 pad_maximum_fusion
  2016.6 28.8 convolution_convert_fusion
  2047.3 16.9 convolution_convert_fusion.1
  2064.2 240.0 %reduce-scatter.18.cloned.1.call-done = bf16[512,8192]{0,1:T(8,128)(2,1)} async-done(((bf16[2048,8192]{0,1:T(8,128)(2,1)}), bf16[512,8192]{0,1:T(8,128)(2,1)}) %reduce-scatter.18.cloned.1.call-update) | async-done | bytes 8388624 | tf_op jit(solution)/shard_map/reduce_scatter | solution.py:276
  2304.2 6.0 fusion.47
  2313.5 1111.8 %all-reduce.4.cloned.1.call-done = bf16[2048,16384]{1,0:T(8,128)(2,1)} async-done(((bf16[2048,16384]{1,0:T(8,128)(2,1)}), bf16[2048,16384]{1,0:T(8,128)(2,1)}) %all-reduce.4.cloned.1.call-update) | async-done | bytes 67108880
  3425.4 13.1 fusion.46
  3439.1 279.0 %reduce-scatter.34.cloned.1.call-done = bf16[2048,2048]{1,0:T(8,128)(2,1)} async-done(((bf16[8192,2048]{1,0:T(8,128)(2,1)}), bf16[2048,2048]{1,0:T(8,128)(2,1)}) %reduce-scatter.34.cloned.1.call-update) | async-done | bytes 8388624
  3718.9 41.5 psum.7
  3761.1 6.0 convolution_add_fusion.3
  3767.2 5.9 convolution_add_fusion.2
  3773.2 3.7 fusion.17
  3778.8 15.0 reduce-scatter.22.cloned.1.call-done
  3795.6 35.4 reduce-scatter.24.cloned.1.call-done
  3832.9 35.6 reduce-scatter.26.cloned.1.call-done
  3870.4 88.6 %reduce-scatter.28.cloned.1.call-done = bf16[512,1024]{1,0:T(8,128)(2,1)} async-done(((bf16[512,8192]{1,0:T(8,128)(2,1)}), bf16[512,1024]{1,0:T(8,128)(2,1)}) %reduce-scatter.28.cloned.1.call-update) | async-done | bytes 1048592 | tf_op jit(solution)/shard_map/reduce_scatter | solution.py:312
  3961.8 87.4 %reduce-scatter.30.cloned.1.call-done = bf16[512,1024]{1,0:T(8,128)(2,1)} async-done(((bf16[512,8192]{1,0:T(8,128)(2,1)}), bf16[512,1024]{1,0:T(8,128)(2,1)}) %reduce-scatter.30.cloned.1.call-update) | async-done | bytes 1048592 | tf_op jit(solution)/shard_map/reduce_scatter | solution.py:315
  4052.1 87.6 %reduce-scatter.32.cloned.1.call-done = bf16[2048,256]{1,0:T(8,128)(2,1)} async-done(((bf16[2048,2048]{1,0:T(8,128)(2,1)}), bf16[2048,256]{1,0:T(8,128)(2,1)}) %reduce-scatter.32.cloned.1.call-update) | async-done | bytes 1048592 | tf_op jit(solution)/shard_map/reduce_scatter | solution.py:318
  (231 shorter events, 75.4 us)
Async XLA Ops:
  7.2 34.8 all-gather.30.cloned.1.call-start
  9.0 97.2 %copy-start.33 = (f32[512,256]{1,0:T(8,128)S(1)}, f32[512,256]{1,0:T(8,128)}, u32[]{:S(2)}) copy-start(f32[512,256]{1,0:T(8,128)} %param.21) | copy-start | bytes 1572868
  9.0 65.1 %all-gather.26.cloned.1.call-start = ((), (), s32[]{:S(2)}) async-start(), calls=%async_computation.13 | async-start | bytes 2359296 | tf_op jit(solution)/shard_map/all_gather | solution.py:111
  10.9 96.2 %copy-start.25 = (f32[512,1024]{1,0:T(8,128)S(1)}, f32[512,1024]{1,0:T(8,128)}, u32[]{:S(2)}) copy-start(f32[512,1024]{1,0:T(8,128)} %param.25) | copy-start | bytes 6291460
  10.9 95.3 %all-gather.22.cloned.1.call-start = ((), (), s32[]{:S(2)}) async-start(), calls=%async_computation.11 | async-start | bytes 2359296 | tf_op jit(solution)/shard_map/all_gather | solution.py:113
  12.9 182.0 %all-gather.32.cloned.1.call-start = ((), (), s32[]{:S(2)}) async-start(), calls=%async_computation.16 | async-start | bytes 10485760 | tf_op jit(solution)/shard_map/all_gather | solution.py:121
  42.0 242.3 %all-gather.28.cloned.1.call-start = ((), (), s32[]{:S(2)}) async-start(), calls=%async_computation.14 | async-start | bytes 10485760 | tf_op jit(solution)/shard_map/all_gather | solution.py:120
  74.1 299.5 %all-gather.24.cloned.1.call-start = ((), (), s32[]{:S(2)}) async-start(), calls=%async_computation.12 | async-start | bytes 10485760 | tf_op jit(solution)/shard_map/all_gather | solution.py:122
  106.2 300.2 %all-gather.36.cloned.1.call-start = ((), (), s32[]{:S(2)}) async-start(), calls=%async_computation.18 | async-start | bytes 2359296 | tf_op jit(solution)/shard_map/all_gather | solution.py:114
  107.0 383.0 %all-gather.40.cloned.1.call-start = ((), (), s32[]{:S(2)}) async-start(), calls=%async_computation.20 | async-start | bytes 9437184 | tf_op jit(solution)/shard_map/all_gather | solution.py:115
  108.3 12.3 copy-start.51
  108.3 12.3 copy-start.48
  108.3 86.6 %copy-start.14 = (bf16[1,256,2048]{2,1,0:T(8,128)(2,1)S(1)}, bf16[1,256,2048]{2,1,0:T(8,128)(2,1)}, u32[]{:S(2)}) copy-start(bf16[1,256,2048]{2,1,0:T(8,128)(2,1)} %param.15) | copy-start | bytes 3145732
  108.3 463.9 %all-gather.44.cloned.1.call-start = ((), (), s32[]{:S(2)}) async-start(), calls=%async_computation.22 | async-start | bytes 9437184 | tf_op jit(solution)/shard_map/all_gather | solution.py:116
  111.3 543.5 %all-gather.48.cloned.1.call-start = ((), (), s32[]{:S(2)}) async-start(), calls=%async_computation.24 | async-start | bytes 9437184 | tf_op jit(solution)/shard_map/all_gather | solution.py:117
  112.4 595.5 %all-gather.34.cloned.1.call-start = ((), (), s32[]{:S(2)}) async-start(), calls=%async_computation.17 | async-start | bytes 5242880 | tf_op jit(solution)/shard_map/all_gather | solution.py:139
  120.6 80.2 %copy-start.35 = (f32[4,1,512]{2,1,0:T(1,128)}, f32[4,1,512]{2,1,0:T(1,128)S(1)}, u32[]{:S(2)}) copy-start(f32[4,1,512]{2,1,0:T(1,128)S(1)} %convert_element_type.265) | copy-start | bytes 24580
  127.8 162.3 %copy-start.37 = (f32[4,1,512]{2,1,0:T(1,128)}, f32[4,1,512]{2,1,0:T(1,128)S(1)}, u32[]{:S(2)}) copy-start(f32[4,1,512]{2,1,0:T(1,128)S(1)} %convert_element_type.264) | copy-start | bytes 24580
  128.7 167.5 %copy-start.31 = (f32[256,64]{0,1:T(8,128)}, f32[256,64]{0,1:T(8,128)S(1)}, u32[]{:S(2)}) copy-start(f32[256,64]{0,1:T(8,128)S(1)} %get-tuple-element.145) | copy-start | bytes 196612
  300.8 462.2 %all-gather.52.cloned.1.call-start = ((), (), s32[]{:S(2)}) async-start(), calls=%async_computation.36 | async-start | bytes 5242880 | tf_op jit(solution)/shard_map/all_gather | solution.py:142
  380.3 472.2 %all-gather.38.cloned.1.call-start = ((), (), s32[]{:S(2)}) async-start(), calls=%async_computation.19 | async-start | bytes 10485760 | tf_op jit(solution)/shard_map/all_gather | solution.py:123
  406.4 745.0 %all-gather.42.cloned.1.call-start = ((), (), s32[]{:S(2)}) async-start(), calls=%async_computation.21 | async-start | bytes 41943040 | tf_op jit(solution)/shard_map/all_gather | solution.py:171
  490.0 960.3 %all-gather.46.cloned.1.call-start = ((), (), s32[]{:S(2)}) async-start(), calls=%async_computation.23 | async-start | bytes 41943040 | tf_op jit(solution)/shard_map/all_gather | solution.py:172
  572.2 1177.0 %all-gather.50.cloned.1.call-start = ((), (), s32[]{:S(2)}) async-start(), calls=%async_computation.25 | async-start | bytes 41943040 | tf_op jit(solution)/shard_map/all_gather | solution.py:173
  654.7 8.9 copy-start.50
  654.7 16.4 copy-start.27
  654.7 16.4 copy-start.28
  654.8 1267.1 %reduce-scatter.14.cloned.1.call-start = ((), (), s32[]{:S(2)}) async-start(), calls=%async_computation.26 | async-start | bytes 5242880 | tf_op jit(solution)/shard_map/reduce_scatter | solution.py:261
  671.3 42.1 %copy-start.12 = (bf16[256,16,2,64]{0,3,2,1:T(8,128)(2,1)}, bf16[256,16,2,64]{0,3,2,1:T(8,128)(2,1)S(1)}, u32[]{:S(2)}) copy-start(bf16[256,16,2,64]{0,3,2,1:T(8,128)(2,1)S(1)} %pad_maximum_fusion.3) | copy-start | bytes 3145732
  713.4 6.6 copy-start
  773.2 85.1 %copy-start.15 = (bf16[16,128,256]{2,1,0:T(8,128)(2,1)}, bf16[16,128,256]{2,1,0:T(8,128)(2,1)S(1)}, u32[]{:S(2)}) copy-start(bf16[16,128,256]{2,1,0:T(8,128)(2,1)S(1)} %fusion.24) | copy-start | bytes 3145732
  860.0 590.3 %copy-start.17 = (bf16[256,2048]{1,0:T(8,128)(2,1)}, bf16[256,2048]{1,0:T(8,128)(2,1)S(1)}, u32[]{:S(2)}) copy-start(bf16[256,2048]{1,0:T(8,128)(2,1)S(1)} %fusion.27) | copy-start | bytes 3145732
  1749.3 16.4 copy-start.21
  1765.7 60.9 %copy-start.6 = (f32[256,2048]{1,0:T(8,128)}, f32[256,2048]{1,0:T(8,128)S(1)}, u32[]{:S(2)}) copy-start(f32[256,2048]{1,0:T(8,128)S(1)} %get-tuple-element.157) | copy-start | bytes 6291460
  1767.1 22.4 copy-start.45
  1852.3 12.3 copy-start.13
  1864.6 4.6 copy-start.1
  1869.2 108.6 %reduce-scatter.16.cloned.1.call-start = ((), (), s32[]{:S(2)}) async-start(), calls=%async_computation.27 | async-start | bytes 5242880 | tf_op jit(solution)/shard_map/reduce_scatter | solution.py:264
  1885.3 418.9 %reduce-scatter.18.cloned.1.call-start = ((), (), s32[]{:S(2)}) async-start(), calls=%async_computation.28 | async-start | bytes 41943040 | tf_op jit(solution)/shard_map/reduce_scatter | solution.py:276
  1886.8 5.7 copy-start.11
  1892.5 30.9 copy-start.32
  1892.5 30.9 copy-start.34
  1925.9 5.1 copy-start.38
  1926.0 5.1 copy-start.43
  1928.0 6.7 copy-start.3
  1928.0 6.7 copy-start.36
  1928.0 6.7 copy-start.41
  1931.0 4.4 copy-start.5
  1931.0 4.8 copy-start.9
  2015.4 1410.0 %all-reduce.4.cloned.1.call-start = ((), (), s32[]{:S(2)}) async-start(), calls=%async_computation.37 | async-start | bytes 134217728
  2045.4 1672.8 %reduce-scatter.34.cloned.1.call-start = ((), (), s32[]{:S(2)}) async-start(), calls=%async_computation.38 | async-start | bytes 41943040
  2064.1 1712.7 %reduce-scatter.20.cloned.1.call-start = ((), (), s32[]{:S(2)}) async-start(), calls=%async_computation.29 | async-start | bytes 2359296 | tf_op jit(solution)/shard_map/reduce_scatter | solution.py:291
  2310.1 1483.6 %reduce-scatter.22.cloned.1.call-start = ((), (), s32[]{:S(2)}) async-start(), calls=%async_computation.30 | async-start | bytes 2359296 | tf_op jit(solution)/shard_map/reduce_scatter | solution.py:294
  2310.9 1520.1 %reduce-scatter.24.cloned.1.call-start = ((), (), s32[]{:S(2)}) async-start(), calls=%async_computation.31 | async-start | bytes 2359296 | tf_op jit(solution)/shard_map/reduce_scatter | solution.py:300
  2311.5 1557.1 %reduce-scatter.26.cloned.1.call-start = ((), (), s32[]{:S(2)}) async-start(), calls=%async_computation.32 | async-start | bytes 2359296 | tf_op jit(solution)/shard_map/reduce_scatter | solution.py:306
  2312.2 1646.8 %reduce-scatter.28.cloned.1.call-start = ((), (), s32[]{:S(2)}) async-start(), calls=%async_computation.33 | async-start | bytes 9437184 | tf_op jit(solution)/shard_map/reduce_scatter | solution.py:312
  3438.5 610.8 %reduce-scatter.30.cloned.1.call-start = ((), (), s32[]{:S(2)}) async-start(), calls=%async_computation.34 | async-start | bytes 9437184 | tf_op jit(solution)/shard_map/reduce_scatter | solution.py:315
  3439.1 700.6 %reduce-scatter.32.cloned.1.call-start = ((), (), s32[]{:S(2)}) async-start(), calls=%async_computation.35 | async-start | bytes 9437184 | tf_op jit(solution)/shard_map/reduce_scatter | solution.py:318
  3718.2 42.9 %copy-start.19 = (bf16[256,2048]{1,0:T(8,128)(2,1)S(1)}, bf16[256,2048]{1,0:T(8,128)(2,1)}, u32[]{:S(2)}) copy-start(bf16[256,2048]{1,0:T(8,128)(2,1)} %multiply_convert_fusion.6) | copy-start | bytes 3145732
  3718.2 42.9 %copy-start.29 = (f32[256,2048]{1,0:T(8,128)S(1)}, f32[256,2048]{1,0:T(8,128)}, u32[]{:S(2)}) copy-start(f32[256,2048]{1,0:T(8,128)} %get-tuple-element.158) | copy-start | bytes 6291460
  3761.1 6.1 copy-start.20
  3761.1 12.0 slice-start
  3767.2 6.0 copy-start.30
  3767.2 6.0 slice-start.1
  (19 other events, 32.3 us)
Sparse Core Ops, SparseCore 0:
  10.2 31.7 all-gather.29
  44.1 29.8 all-gather.25
  76.3 29.8 all-gather.21
  107.9 86.9 all-gather.31
  196.6 87.5 all-gather.27
  286.0 87.5 all-gather.23
  375.8 30.5 all-gather.35
  408.6 81.3 all-gather.39
  491.6 80.5 all-gather.43
  573.7 81.0 all-gather.47
  657.1 50.7 all-gather.33
  710.2 52.6 all-gather.51
  764.8 87.6 all-gather.37
  854.2 297.2 all-gather.41
  1153.1 297.2 all-gather.45
  1452.0 297.2 all-gather.49
  1869.3 52.5 reduce-scatter.13
  1925.0 52.6 reduce-scatter.15
  2015.5 288.5 reduce-scatter.17
  2307.9 1117.3 all-reduce.3
  3428.4 289.7 reduce-scatter.33
  3720.6 35.9 reduce-scatter.19
  3759.0 34.7 reduce-scatter.21
  3796.6 34.4 reduce-scatter.23
  3834.0 34.4 reduce-scatter.25
  3870.8 88.2 reduce-scatter.27
  3961.3 87.9 reduce-scatter.29
  4051.7 87.9 reduce-scatter.31
where the time goes:
time: 4160 us; the launch traced here: 4150 us
  waiting for transfers between devices  3630 us (87%)
  matrix products  284 us (7%)
  other arithmetic  86.4 us (2%)
  blocking collectives  71.8 us (2%)
  local copies, waits for them, and re-layouts  58.8 us (1%)
    unnamed x30, waiting for transfers between devices  1390 us
    all_gather x1, waiting for transfers between devices, body(): lax.all_gather(gate_rows, 'shard', axis=0, tiled=True)  291 us
    all_gather x1, waiting for transfers between devices, body(): lax.all_gather(up_rows, 'shard', axis=0, tiled=True)  278 us
    all_gather x1, waiting for transfers between devices, body(): lax.all_gather(down_rows, 'shard', axis=0, tiled=True)  272 us
    reduce_scatter x1, waiting for transfers between devices, body(): lax.psum_scatter(jnp.concatenate([dot_first(tok_low, projections_low), do...  240 us
    reduce_scatter x1, waiting for transfers between devices, body(): lax.psum_scatter(gate_share[:, :ff_width].astype(jnp.bfloat16), 'rep', sc...  88.6 us
    dot_general x7, matrix products, mat_mul(): return jnp.dot(left, right, preferred_element_type=jnp.float32)  88.2 us
    reduce_scatter x1, waiting for transfers between devices, body(): lax.psum_scatter(down_share, 'rep', scatter_dimension=1, tiled=True)  87.6 us
  transfers between devices with their start and end apart: 28, of which 27 were waited for; matrix products, arithmetic and copies ran while one was open for 6% of the time, Pallas kernels for 0%

commit v1 on v0

v1 whole, which is shorter than its diff:
```python
import jax
import jax.numpy as jnp
from jax import lax
from jax.sharding import PartitionSpec as P

HEADS = 16
HEAD_DIM = 128
PIECE = 256
SCALE = HEAD_DIM ** (-0.5)

epsilon = 1e-06
rope_base = 500000.0

F32 = jnp.float32
BF16 = jnp.bfloat16

SQUARE = ((0, 0), (0, 2), (1, 0), (1, 1), (0, 1), (0, 3), (1, 2), (1, 3))


def token_order(count):
    return SQUARE if count == 4 else tuple((0, j) for j in range(count))


def to_low(tensor):
    return tensor.astype(BF16)


def dot(left, right, contract):
    return lax.dot_general(left, right, ((contract[0], contract[1]), ((), ())), preferred_element_type=F32)


def mm(left, right):
    return dot(left, right, ((1,), (0,)))


def mm_first(left, right):
    return dot(left, right, ((0,), (0,)))


def mm_last(left, right):
    return dot(left, right, ((1,), (1,)))


def send_shard(value, k):
    count = lax.axis_size("shard")
    return lax.ppermute(value, "shard", [(s, s ^ k) for s in range(count)])


def gather_tokens(own):
    count = lax.axis_size("shard")
    if count != 4:
        return jnp.concatenate([own] + [send_shard(own, k) for k in range(1, count)])
    half = own.shape[0] // 2
    a0, b0 = own[:half], own[half:]
    a2 = send_shard(a0, 2)
    b1 = send_shard(b0, 1)
    a02 = jnp.concatenate([a0, a2])
    b01 = jnp.concatenate([b0, b1])
    a13 = send_shard(a02, 1)
    b23 = send_shard(b01, 2)
    return jnp.concatenate([a02, b01, a13, b23])


def scatter_tokens(keep, send):
    count = lax.axis_size("shard")
    if count != 4:
        parts = jnp.split(jnp.concatenate([keep, send]), count)
        return parts[0] + sum(send_shard(to_low(parts[k]), k).astype(F32) for k in range(1, count))
    q = keep.shape[0] // 2
    send_low = to_low(send)
    a_in = send_shard(send_low[:q], 1)
    b_in = send_shard(send_low[q:], 2)
    a02 = keep[:q] + a_in.astype(F32)
    b01 = keep[q:] + b_in.astype(F32)
    h = q // 2
    a_last = send_shard(to_low(a02[h:]), 2)
    b_last = send_shard(to_low(b01[h:]), 1)
    return jnp.concatenate([a02[:h] + a_last.astype(F32), b01[:h] + b_last.astype(F32)])


def swap_blocks(rows, k):
    order = token_order(lax.axis_size("shard"))
    step = rows.shape[-1] // len(order)
    index = [order.index((h, j ^ k)) for h, j in order]
    return jnp.concatenate([rows[..., i * step : (i + 1) * step] for i in index], axis=-1)


def sum_rows(rows):
    return rows + sum(swap_blocks(send_shard(rows, k), k) for k in range(1, lax.axis_size("shard")))


def unrelative(blocks, s):
    shape = blocks.shape
    bits = shape[0].bit_length() - 1
    cube = blocks.reshape((2,) * bits + shape[1:])
    for bit in range(bits):
        cube = jnp.where((s >> bit) % 2 == 1, jnp.flip(cube, bits - 1 - bit), cube)
    return cube.reshape(shape)


def exchange_shard(blocks, s):
    relative = unrelative(blocks, s)
    got = jnp.stack([relative[0]] + [send_shard(relative[k], k) for k in range(1, blocks.shape[0])])
    return unrelative(got, s)


def rows_perm(count, heads, k):
    c = count // heads
    return [(s, heads * (s % c) + (s // c + k) % heads) for s in range(count)]


def spread_heads(blocks, s):
    heads, count = blocks.shape[0], lax.axis_size("shard")
    q = s // (count // heads)
    got = [lax.ppermute(pick(blocks, (q + k) % heads), "shard", rows_perm(count, heads, k)) for k in range(heads)]
    return reverse_pick(jnp.stack(got), s % heads)


def collect_heads(blocks, s):
    heads, count = blocks.shape[0], lax.axis_size("shard")
    q = s // (count // heads)
    got = [
        lax.ppermute(pick(blocks, (s - k) % heads), "shard", flip(rows_perm(count, heads, k))) for k in range(heads)
    ]
    return roll_pick(jnp.stack(got), -q)


def ring(value, count):
    return lax.ppermute(value, "rep", [(r, (r + 2) % count) for r in range(count)])


def sibling(value, count):
    return lax.ppermute(value, "rep", [(r, r ^ 1) for r in range(count)])


def gather_pairs(own, count):
    pairs = []
    current = own
    for step in range(count // 2):
        if step:
            current = ring(current, count)
        pairs.append(jnp.concatenate([current, sibling(current, count)]))
    return pairs


def scatter_pairs(parts, count):
    half = parts[0].shape[0] // 2
    total = None
    for step in list(range(1, count // 2)) + [0]:
        part = parts[step]
        mine = part[:half] + sibling(to_low(part[half:]), count).astype(F32)
        total = mine if total is None else ring(to_low(total), count).astype(F32) + mine
    return total


def heads_perm(shard_count, rep_count, per, k):
    group = shard_count // per
    pairs = []
    for r in range(rep_count):
        for s in range(shard_count):
            j = (s % per + k) % per
            target = (r // group * group + s // per, per * (r % group) + j)
            pairs.append((r * shard_count + s, target[0] * shard_count + target[1]))
    return pairs


def down_perm(shard_count, rep_count, k):
    m = rep_count // shard_count
    pairs = []
    for r in range(rep_count):
        for s in range(shard_count):
            target = (m * s + (r % m + k) % m, r // m)
            pairs.append((r * shard_count + s, target[0] * shard_count + target[1]))
    return pairs


def flip(pairs):
    return [(b, a) for a, b in pairs]


def permute(value, pairs):
    return lax.ppermute(value, ("rep", "shard"), pairs)


def pick(values, index):
    return lax.dynamic_index_in_dim(values, index, 0, keepdims=False)


def roll_pick(values, shift):
    n = values.shape[0]
    if n == 1:
        return values
    return lax.dynamic_slice_in_dim(jnp.concatenate([values, values]), shift % n, n, 0)


def reverse_pick(values, base):
    n = values.shape[0]
    if n == 1:
        return values
    return roll_pick(values[::-1], n - 1 - base)


def frequencies():
    return jnp.power(jnp.float32(rope_base), -2.0 * jnp.arange(HEAD_DIM // 2, dtype=F32) / HEAD_DIM)


def rotate(tensor, cosines, sines, direction):
    half = HEAD_DIM // 2
    first, second = tensor[..., :half], tensor[..., half:]
    return jnp.concatenate(
        [first * cosines - direction * second * sines, second * cosines + direction * first * sines], axis=-1
    )


def allowed_pairs(piece_first, place):
    inside = (place >= piece_first) & (place < piece_first + PIECE)
    return (place[None, :] <= place[:, None]) | (inside[:, None] & inside[None, :])


def attend(q, k, v, allowed):
    scores = jnp.einsum("hqd,hkd->hqk", q, k, preferred_element_type=F32) * SCALE
    scores = jnp.where(allowed[None], scores, -1e30)
    row_max = jnp.max(scores, axis=-1, keepdims=True)
    log_total = row_max + jnp.log(jnp.sum(jnp.exp(scores - row_max), axis=-1, keepdims=True))
    weights = to_low(jnp.exp(scores - log_total))
    return to_low(jnp.einsum("hqk,hkd->hqd", weights, v, preferred_element_type=F32)), log_total


def attend_back(q, k, v, grad, log_total, allowed):
    scores = jnp.einsum("hqd,hkd->hqk", q, k, preferred_element_type=F32) * SCALE
    scores = jnp.where(allowed[None], scores, -1e30)
    probs = jnp.exp(scores - log_total)
    grad_probs = jnp.einsum("hqd,hkd->hqk", grad, v, preferred_element_type=F32)
    delta = jnp.sum(probs * grad_probs, axis=-1, keepdims=True)
    grad_scores = to_low(probs * (grad_probs - delta))
    dq = jnp.einsum("hqk,hkd->hqd", grad_scores, k, preferred_element_type=F32) * SCALE
    dk = jnp.einsum("hqk,hqd->hkd", grad_scores, q, preferred_element_type=F32) * SCALE
    dv = jnp.einsum("hqk,hqd->hkd", to_low(probs), grad, preferred_element_type=F32)
    return dq, dk, dv


def heads_first(tensor, heads):
    rows, width = tensor.shape
    return tensor.reshape(rows, heads, width // heads).transpose(1, 0, 2)


def heads_last(tensor):
    heads, rows, width = tensor.shape
    return tensor.transpose(1, 0, 2).reshape(rows, heads * width)


def body(
    tokens,
    piece_start,
    positions,
    w_query,
    w_key,
    w_value,
    w_out,
    query_gain,
    key_gain,
    attn_gain,
    w_gate,
    w_up,
    w_down,
    mlp_gain,
    cotangent,
):
    S = lax.axis_size("shard")
    R = lax.axis_size("rep")
    s = lax.axis_index("shard")
    r = lax.axis_index("rep")
    _, span, width = tokens.shape
    heads = HEADS // S
    per = HEADS // R
    m = R // S
    own_width = width // S
    x_own = tokens.reshape(span, width)

    own_qkv = jnp.concatenate(
        [
            to_low(w).reshape(own_width, per, HEAD_DIM).transpose(1, 0, 2)
            for w in (w_query, w_key, w_value)
        ],
        axis=2,
    )
    got = jnp.stack(
        [permute(pick(own_qkv, (s + k) % per), heads_perm(S, R, per, k)) for k in range(per)]
    )
    got = reverse_pick(got, s % per).reshape(per * own_width, 3 * HEAD_DIM)
    qkv_w = lax.all_gather(got, "rep", axis=0, tiled=True).reshape(heads, width, 3 * HEAD_DIM)
    own_out = spread_heads(to_low(w_out).reshape(heads, HEAD_DIM, -1), s).reshape(own_width, -1)
    out_w = lax.all_gather(own_out, "rep", axis=1, tiled=True)

    gains_own = jnp.stack([to_low(g).astype(F32) for g in (query_gain, key_gain, attn_gain, mlp_gain)])
    small = jnp.concatenate([positions.reshape(span).astype(F32), gains_own.reshape(-1)])
    small_all = [small] + [send_shard(small, k) for k in range(1, S)]
    gains = unrelative(jnp.stack([v[span:].reshape(4, own_width) for v in small_all]), s)
    gains = gains.transpose(1, 0, 2).reshape(4, width)
    head_gains = gains[:2].reshape(2, heads, S, HEAD_DIM)
    head_gains = lax.dynamic_index_in_dim(head_gains, s, 2, keepdims=False)
    qgain, kgain = head_gains[0][:, None, :], head_gains[1][:, None, :]
    again, mgain = gains[2], gains[3]
    order = token_order(S)
    step = S * span // len(order)
    place_pos = jnp.concatenate([small_all[j][h * step : (h + 1) * step] for h, j in order])
    place = jnp.concatenate([(s ^ j) * span + h * step + lax.iota(jnp.int32, step) for h, j in order])
    angles = place_pos[:, None] * frequencies()
    cosines, sines = jnp.cos(angles), jnp.sin(angles)
    allowed = allowed_pairs(piece_start[0], place)

    x_all = gather_tokens(x_own)
    raw = jnp.einsum("tk,qkn->qtn", x_all, qkv_w, preferred_element_type=F32)
    qraw, kraw, vraw = raw[..., :HEAD_DIM], raw[..., HEAD_DIM : 2 * HEAD_DIM], raw[..., 2 * HEAD_DIM :]
    squares = jnp.stack([jnp.sum(qraw * qraw, axis=(0, 2)), jnp.sum(kraw * kraw, axis=(0, 2))])
    inv = lax.rsqrt(sum_rows(squares) / width + epsilon)
    qinv, kinv = inv[0][None, :, None], inv[1][None, :, None]
    qhat, khat = qraw * qinv, kraw * kinv
    q = to_low(rotate(qhat * qgain, cosines, sines, 1.0))
    k = to_low(rotate(khat * kgain, cosines, sines, 1.0))
    v = to_low(vraw)
    o_heads, log_total = attend(q, k, v, allowed)
    o = heads_last(o_heads)
    rows = S * span // 2
    a_send = mm(o[rows:], out_w)
    a_keep = mm(o[:rows], out_w)
    a = scatter_tokens(a_keep, a_send)
    ainv = lax.rsqrt(jnp.mean(a * a, axis=-1, keepdims=True) + epsilon)
    ahat = a * ainv
    h = x_own.astype(F32) + ahat * again
    hb = to_low(h)

    gate_w = lax.all_gather(to_low(w_gate), "shard", axis=0, tiled=True)
    up_w = lax.all_gather(to_low(w_up), "shard", axis=0, tiled=True)
    unit = to_low(w_down).reshape(m, w_down.shape[0] // m, w_down.shape[1])
    got = jnp.stack([permute(pick(unit, (r + k) % m), down_perm(S, R, k)) for k in range(m)])
    got = reverse_pick(got, r % m)
    own_down = jnp.concatenate([got[i] for i in range(m)], axis=1)
    down_w = lax.all_gather(own_down, "shard", axis=1, tiled=True)

    hb_pairs = gather_pairs(hb, R)
    kept = []
    z_parts = []
    for pair in hb_pairs:
        g = mm(pair, gate_w)
        u = mm(pair, up_w)
        sig = jax.nn.sigmoid(g)
        inner = to_low(g * sig * u)
        kept.append((g, u, inner))
        z_parts.append(mm(inner, down_w))
    z = scatter_pairs(z_parts, R)
    zinv = lax.rsqrt(jnp.mean(z * z, axis=-1, keepdims=True) + epsilon)
    zhat = z * zinv
    output = to_low(h + zhat * mgain).reshape(tokens.shape)

    dy = cotangent.reshape(span, width).astype(F32)
    grad_mgain = jnp.sum(dy * zhat, axis=0)
    scaled = dy * mgain
    dz = to_low(zinv * (scaled - zhat * jnp.mean(scaled * zhat, axis=-1, keepdims=True)))
    dz_pairs = gather_pairs(dz, R)
    dh_parts, dgs, dus = [], [], []
    for pair, (g, u, inner) in zip(dz_pairs, kept):
        dm = mm_last(pair, down_w)
        sig = jax.nn.sigmoid(g)
        dg = to_low(dm * u * sig * (1.0 + g * (1.0 - sig)))
        du = to_low(dm * g * sig)
        dgs.append(dg)
        dus.append(du)
        dh_parts.append(mm_last(dg, gate_w) + mm_last(du, up_w))
    dh = dy + scatter_pairs(dh_parts, R)
    hb_all = jnp.concatenate(hb_pairs)
    down_grad = to_low(mm_first(jnp.concatenate([t[2] for t in kept]), jnp.concatenate(dz_pairs)))
    gate_grad = to_low(mm_first(hb_all, jnp.concatenate(dgs)))
    up_grad = to_low(mm_first(hb_all, jnp.concatenate(dus)))
    grad_gate = lax.psum_scatter(gate_grad, "shard", scatter_dimension=0, tiled=True).astype(F32)
    grad_up = lax.psum_scatter(up_grad, "shard", scatter_dimension=0, tiled=True).astype(F32)
    down_share = lax.psum_scatter(down_grad, "shard", scatter_dimension=1, tiled=True)
    slots = down_share.reshape(down_share.shape[0], m, -1).transpose(1, 0, 2)
    back = jnp.stack([permute(pick(slots, (r - k) % m), flip(down_perm(S, R, k))) for k in range(m)])
    grad_down = roll_pick(back, -(r % m)).reshape(w_down.shape).astype(F32)

    grad_again = jnp.sum(dh * ahat, axis=0)
    scaled = dh * again
    da = to_low(ainv * (scaled - ahat * jnp.mean(scaled * ahat, axis=-1, keepdims=True)))
    da_all = gather_tokens(da)
    do = heads_first(to_low(mm_last(da_all, out_w)), heads)
    out_grad = to_low(mm_first(o, da_all))
    dq, dk, dv = attend_back(q, k, v, do, log_total, allowed)
    dq_rot = rotate(dq, cosines, sines, -1.0)
    dk_rot = rotate(dk, cosines, sines, -1.0)
    grad_qgain = jnp.sum(dq_rot * qhat, axis=1)
    grad_kgain = jnp.sum(dk_rot * khat, axis=1)
    qs, ks = dq_rot * qgain, dk_rot * kgain
    means = jnp.stack([jnp.sum(qs * qhat, axis=(0, 2)), jnp.sum(ks * khat, axis=(0, 2))])
    means = sum_rows(means) / width
    dqraw = to_low(qinv * (qs - qhat * means[0][None, :, None]))
    dkraw = to_low(kinv * (ks - khat * means[1][None, :, None]))
    dqkv = jnp.concatenate([dqraw, dkraw, to_low(dv)], axis=2)
    dx_send = jnp.einsum("qtn,qkn->tk", dqkv[:, rows:], qkv_w, preferred_element_type=F32)
    dx_keep = jnp.einsum("qtn,qkn->tk", dqkv[:, :rows], qkv_w, preferred_element_type=F32)
    dx = dh + scatter_tokens(dx_keep, dx_send)
    qkv_grad = to_low(jnp.einsum("tk,qtn->qkn", x_all, dqkv, preferred_element_type=F32))
    qkv_grad = qkv_grad.reshape(heads * width, 3 * HEAD_DIM)

    out_share = lax.psum_scatter(out_grad, "rep", scatter_dimension=1, tiled=True)
    grad_out = collect_heads(out_share.reshape(heads, HEAD_DIM, -1), s).reshape(w_out.shape).astype(F32)
    qkv_share = lax.psum_scatter(qkv_grad, "rep", scatter_dimension=0, tiled=True)
    slots = qkv_share.reshape(per, own_width, 3 * HEAD_DIM)
    back = jnp.stack([permute(pick(slots, (s - k) % per), flip(heads_perm(S, R, per, k))) for k in range(per)])
    back = roll_pick(back, -(s % per)).reshape(per, own_width, 3, HEAD_DIM)
    back = back.transpose(2, 1, 0, 3).reshape(3, own_width, per * HEAD_DIM).astype(F32)

    head_grads = collect_heads(jnp.stack([grad_qgain, grad_kgain], axis=1), s)
    head_grads = head_grads.transpose(1, 0, 2).reshape(2, own_width)
    wide = jnp.stack([grad_again, grad_mgain]).reshape(2, S, own_width).transpose(1, 0, 2)
    wide = jnp.sum(exchange_shard(wide, s), axis=0)
    gain_grads = jnp.concatenate([head_grads, wide])
    step = 1
    while step < R:
        gain_grads = gain_grads + lax.ppermute(gain_grads, "rep", [(i, i ^ step) for i in range(R)])
        step *= 2

    return (
        output,
        dx.reshape(tokens.shape),
        back[0],
        back[1],
        back[2],
        grad_out,
        gain_grads[0],
        gain_grads[1],
        gain_grads[2],
        grad_gate,
        grad_up,
        grad_down,
        gain_grads[3],
    )


def solution(mesh):
    grid = P("shard", "rep")
    rows = P("rep", "shard", None)
    gain = P("shard")
    in_specs = (rows, P("rep"), P("rep", "shard"), grid, grid, grid, grid, gain, gain, gain, grid, grid, grid, gain, rows)
    out_specs = (rows, rows, grid, grid, grid, grid, gain, gain, gain, grid, grid, grid, gain)
    return jax.shard_map(body, mesh=mesh, in_specs=in_specs, out_specs=out_specs, check_vma=False)
```

time: 4160 us -> 1100 us (0.26)
  waiting for transfers between devices: 3630 us -> 537 us
  starting transfers between devices: 1.13 us -> 148 us
  blocking collectives: 71.8 us -> 0 us
  matrix products: 284 us -> 237 us
    all_gather x16 -> x5, waiting for transfers between devices: 1580 us -> 70 us  [the longest x1 46.7 us: body(): down_w = lax.all_gather(own_down, 'shard', axis=1, tiled=True)]
    unnamed x30 -> x10, waiting for transfers between devices: 1390 us -> 0.16 us
    reduce_scatter x10 -> x5, waiting for transfers between devices: 652 us -> 17.4 us  [the longest x1 17.4 us: body(): lax.psum_scatter(qkv_grad, 'rep', scatter_dimension=0, tiled=True)]
    ppermute x0 -> x79, waiting for transfers between devices: none -> 449 us  [the longest x12 188 us: ring(): lax.ppermute(value, 'rep', [(r, (r + 2) % count) for r in range(count)])]
    ppermute x0 -> x79, starting transfers between devices: none -> 147 us  [the longest x28 75.7 us: send_shard(): return lax.ppermute(value, 'shard', [(s, s ^ k) for s in range(count)])]
    dot_general x24 -> x41, matrix products: 284 us -> 237 us  [the longest x31 158 us: dot(): lax.dot_general(left, right, ((contract[0], contract[1]), ((), ())), pref...]
  transfers between devices with their start and end apart: 28 -> 89, of which waited for: 27 -> 42; matrix products, arithmetic and copies ran while one was open for 6% -> 32% of each run, Pallas kernels for 0% -> 0%
where the time goes in v1:
time: 1100 us; the launch traced here: 1090 us
  waiting for transfers between devices  537 us (49%)
  matrix products  237 us (22%)
  starting transfers between devices  148 us (13%)
  local copies, waits for them, and re-layouts  77.3 us (7%)
  other arithmetic  75.5 us (7%)
  between operations  18 us (2%)
    ppermute x12, waiting for transfers between devices, ring(): lax.ppermute(value, 'rep', [(r, (r + 2) % count) for r in range(count)])  188 us
    ppermute x28, waiting for transfers between devices, send_shard(): return lax.ppermute(value, 'shard', [(s, s ^ k) for s in range(count)])  167 us
    dot_general x31, matrix products, dot(): lax.dot_general(left, right, ((contract[0], contract[1]), ((), ())), pref...  158 us
    ppermute x8, waiting for transfers between devices, permute(): return lax.ppermute(value, ('rep', 'shard'), pairs)  77.9 us
    ppermute x28, starting transfers between devices, send_shard(): return lax.ppermute(value, 'shard', [(s, s ^ k) for s in range(count)])  75.7 us
    ppermute x8, starting transfers between devices, permute(): return lax.ppermute(value, ('rep', 'shard'), pairs)  48.4 us
    all_gather x1, waiting for transfers between devices, body(): down_w = lax.all_gather(own_down, 'shard', axis=1, tiled=True)  46.7 us
    unnamed x287, local copies, waits for them, and re-layouts  45.3 us
  transfers between devices with their start and end apart: 89, of which 42 were waited for; matrix products, arithmetic and copies ran while one was open for 32% of the time, Pallas kernels for 0%

profile of v1, /device:TPU:4, one launch (start us, length us, event | category | flops | bytes accessed | tf_op | source)
XLA Modules:
  0.0 1091.7 jit_solution(4074348532004729017)
XLA Ops:
  16.1 6.7 collective-permute-done.1
  43.4 4.4 collective-permute-start.22
  64.3 9.2 collective-permute-done.2
  74.6 9.8 collective-permute-start.4
  89.7 18.0 %collective-permute-done.4 = bf16[256,2048]{1,0:T(8,128)(2,1)S(1)} collective-permute-done((bf16[256,2048]{1,0:T(8,128)(2,1)S(1)}, bf16[256,2048]{1,0:T(8,128)(2,1)S(1)}, u32[]{:S(2)}, u32[]{:S(2)}) %collective-permute-start.4) | collective-permute-done | bytes 1048608 | tf_op jit(solution)/shard_map/ppermute | solution.py:46
  108.8 10.0 collective-permute-done.5
  119.8 10.1 fusion.38
  130.4 16.4 %collective-permute-start.8 = (f32[2,1024]{1,0:T(2,128)S(1)}, f32[2,1024]{1,0:T(2,128)S(1)}, u32[]{:S(2)}, u32[]{:S(2)}) collective-permute-start(f32[2,1024]{1,0:T(2,128)S(1)} %pad_maximum_fusion.26), channel_id=1, source_target_pairs={{0,3},{1,2},{2,1},{3,0},{4,7},{5,6},{6,5},{7,4},{8,11},{9,10},{10,... | collective-permute-start | bytes 24584 | tf_op jit(solution)/shard_map/ppermute | solution.py:46
  146.9 18.9 %collective-permute-start.7 = (f32[2,1024]{1,0:T(2,128)S(1)}, f32[2,1024]{1,0:T(2,128)S(1)}, u32[]{:S(2)}, u32[]{:S(2)}) collective-permute-start(f32[2,1024]{1,0:T(2,128)S(1)} %pad_maximum_fusion.26), channel_id=1, source_target_pairs={{0,2},{1,3},{2,0},{3,1},{4,6},{5,7},{6,4},{7,5},{8,10},{9,11},{10,... | collective-permute-start | bytes 24584 | tf_op jit(solution)/shard_map/ppermute | solution.py:46
  174.6 3.9 exponential_reduce_fusion
  180.4 7.5 convolution_convert_fusion.2
  202.3 27.1 %collective-permute-done.16 = bf16[256,2048]{1,0:T(8,128)(2,1)} collective-permute-done((bf16[256,2048]{1,0:T(8,128)(2,1)}, bf16[256,2048]{1,0:T(8,128)(2,1)}, u32[]{:S(2)}, u32[]{:S(2)}) %collective-permute-start.16) | collective-permute-done | bytes 1048608 | tf_op jit(solution)/shard_map/ppermute | solution.py:46
  237.7 22.3 %collective-permute-done.19 = bf16[128,2048]{1,0:T(8,128)(2,1)S(1)} collective-permute-done((bf16[128,2048]{1,0:T(8,128)(2,1)S(1)}, bf16[128,2048]{1,0:T(8,128)(2,1)S(1)}, u32[]{:S(2)}, u32[]{:S(2)}) %collective-permute-start.19) | collective-permute-done | bytes 524320 | tf_op jit(solution)/shard_map/ppermute | solution.py:46
  263.7 22.1 %collective-permute-done.20 = bf16[256,2048]{1,0:T(8,128)(2,1)S(1)} collective-permute-done((bf16[256,2048]{1,0:T(8,128)(2,1)S(1)}, bf16[256,2048]{1,0:T(8,128)(2,1)S(1)}, u32[]{:S(2)}, u32[]{:S(2)}) %collective-permute-start.20) | collective-permute-done | bytes 1048608 | tf_op jit(solution)/shard_map/ppermute | solution.py:129
  291.4 6.5 fusion.135
  297.8 23.2 %all-gather.12.cloned.1.call-done = bf16[2048,1024]{1,0:T(8,128)(2,1)} async-done(((bf16[512,1024]{1,0:T(8,128)(2,1)}), bf16[2048,1024]{1,0:T(8,128)(2,1)}) %all-gather.12.cloned.1.call-update) | async-done | bytes 4194320 | tf_op jit(solution)/shard_map/all_gather | solution.py:334
  321.1 7.5 multiply_convert_fusion.15
  328.6 46.7 %all-gather.14.cloned.1.call-done = bf16[1024,2048]{1,0:T(8,128)(2,1)} async-done(((bf16[1024,512]{1,0:T(8,128)(2,1)}), bf16[1024,2048]{1,0:T(8,128)(2,1)}) %all-gather.14.cloned.1.call-update) | async-done | bytes 4194320 | tf_op jit(solution)/shard_map/all_gather | solution.py:339
  375.4 4.8 fusion.136
  389.1 3.8 multiply_convert_fusion.14
  396.5 12.2 %collective-permute-done.30 = bf16[256,2048]{1,0:T(8,128)(2,1)S(1)} collective-permute-done((bf16[256,2048]{1,0:T(8,128)(2,1)S(1)}, bf16[256,2048]{1,0:T(8,128)(2,1)S(1)}, u32[]{:S(2)}, u32[]{:S(2)}) %collective-permute-start.30) | collective-permute-done | bytes 1048608 | tf_op jit(solution)/shard_map/ppermute | solution.py:129
  412.3 18.1 %collective-permute-done.25 = bf16[256,2048]{1,0:T(8,128)(2,1)S(1)} collective-permute-done((bf16[256,2048]{1,0:T(8,128)(2,1)S(1)}, bf16[256,2048]{1,0:T(8,128)(2,1)S(1)}, u32[]{:S(2)}, u32[]{:S(2)}) %collective-permute-start.25) | collective-permute-done | bytes 1048608 | tf_op jit(solution)/shard_map/ppermute | solution.py:129
  434.6 3.8 multiply_convert_fusion.13
  441.0 3.8 multiply_convert_fusion.12
  447.9 9.3 collective-permute-done.29
  458.2 25.1 %collective-permute-done.33 = bf16[256,2048]{1,0:T(8,128)(2,1)S(1)} collective-permute-done((bf16[256,2048]{1,0:T(8,128)(2,1)S(1)}, bf16[256,2048]{1,0:T(8,128)(2,1)S(1)}, u32[]{:S(2)}, u32[]{:S(2)}) %collective-permute-start.33) | collective-permute-done | bytes 1048608 | tf_op jit(solution)/shard_map/ppermute | solution.py:129
  486.8 24.3 %collective-permute-done.36 = bf16[256,2048]{1,0:T(8,128)(2,1)S(1)} collective-permute-done((bf16[256,2048]{1,0:T(8,128)(2,1)S(1)}, bf16[256,2048]{1,0:T(8,128)(2,1)S(1)}, u32[]{:S(2)}, u32[]{:S(2)}) %collective-permute-start.36) | collective-permute-done | bytes 1048608 | tf_op jit(solution)/shard_map/ppermute | solution.py:129
  513.7 4.9 multiply_convert_fusion.10
  523.9 14.6 %collective-permute-done.40 = bf16[256,2048]{1,0:T(8,128)(2,1)S(1)} collective-permute-done((bf16[256,2048]{1,0:T(8,128)(2,1)S(1)}, bf16[256,2048]{1,0:T(8,128)(2,1)S(1)}, u32[]{:S(2)}, u32[]{:S(2)}) %collective-permute-start.40) | collective-permute-done | bytes 1048608 | tf_op jit(solution)/shard_map/ppermute | solution.py:129
  538.5 7.3 multiply_convert_fusion.4
  546.3 20.0 %collective-permute-done.44 = bf16[256,2048]{1,0:T(8,128)(2,1)S(1)} collective-permute-done((bf16[256,2048]{1,0:T(8,128)(2,1)S(1)}, bf16[256,2048]{1,0:T(8,128)(2,1)S(1)}, u32[]{:S(2)}, u32[]{:S(2)}) %collective-permute-start.44) | collective-permute-done | bytes 1048608 | tf_op jit(solution)/shard_map/ppermute | solution.py:129
  566.4 7.2 multiply_convert_fusion.8
  573.7 4.4 fusion.143
  578.0 4.6 convolution_add_fusion.2
  584.6 7.5 multiply_convert_fusion.6
  592.1 4.3 fusion.144
  596.4 4.6 convolution_add_fusion.1
  601.9 4.3 fusion.145
  606.2 4.6 convolution_add_fusion
  611.5 16.9 %collective-permute-done.43 = bf16[256,2048]{1,0:T(8,128)(2,1)S(1)} collective-permute-done((bf16[256,2048]{1,0:T(8,128)(2,1)S(1)}, bf16[256,2048]{1,0:T(8,128)(2,1)S(1)}, u32[]{:S(2)}, u32[]{:S(2)}) %collective-permute-start.43) | collective-permute-done | bytes 1048608 | tf_op jit(solution)/shard_map/ppermute | solution.py:129
  629.3 25.8 %collective-permute-done.47 = bf16[256,2048]{1,0:T(8,128)(2,1)S(1)} collective-permute-done((bf16[256,2048]{1,0:T(8,128)(2,1)S(1)}, bf16[256,2048]{1,0:T(8,128)(2,1)S(1)}, u32[]{:S(2)}, u32[]{:S(2)}) %collective-permute-start.47) | collective-permute-done | bytes 1048608 | tf_op jit(solution)/shard_map/ppermute | solution.py:129
  660.5 9.8 collective-permute-done.50
  673.8 19.2 %collective-permute-done.52 = bf16[256,2048]{1,0:T(8,128)(2,1)S(1)} collective-permute-done((bf16[256,2048]{1,0:T(8,128)(2,1)S(1)}, bf16[256,2048]{1,0:T(8,128)(2,1)S(1)}, u32[]{:S(2)}, u32[]{:S(2)}) %collective-permute-start.52) | collective-permute-done | bytes 1048608 | tf_op jit(solution)/shard_map/ppermute | solution.py:46
  708.7 12.8 %fusion.35 = bf16[1024,2048]{1,0:T(8,128)(2,1)} fusion(bf16[2048,2048]{1,0:T(8,128)(2,1)} %constant_dynamic-update-slice_fusion.76, bf16[512,1024]{1,0:T(8,128)(2,1)S(1)} %copy-done.87, bf16[512,1024]{1,0:T(8,128)(2,1)S(1)} %copy-done.85, bf16[512,1024]{1,0:T(8,128)(2,1)S(1)} %copy-done.83, bf16[512,1024]{1,0:T(8,128)(2,1)S(1)} %copy-done.89), kind=kOutput, calls=%fused_computation.39 | convolution fusion | flops 8608808960 | bytes 16777216 | tf_op jit(solution)/shard_map/dot_general | solution.py:29
  722.7 14.5 %fusion.29 = bf16[2048,1024]{1,0:T(8,128)(2,1)} fusion(bf16[2048,2048]{1,0:T(8,128)(2,1)} %get-tuple-element.106, bf16[512,1024]{1,0:T(8,128)(2,1)} %get-tuple-element.81, bf16[512,1024]{1,0:T(8,128)(2,1)} %copy-done.93, bf16[512,1024]{1,0:T(8,128)(2,1)S(1)} %copy-done.91, bf16[512,1024]{1,0:T(8,128)(2,1)} %copy-done.92), kind=kOutput, calls=%fused_computation.37 | convolution fusion | flops 8608808960 | bytes 16777216 | tf_op jit(solution)/shard_map/dot_general | solution.py:29
  738.5 15.1 %fusion.32 = bf16[2048,1024]{1,0:T(8,128)(2,1)} fusion(bf16[2048,2048]{1,0:T(8,128)(2,1)} %get-tuple-element.106, bf16[512,1024]{1,0:T(8,128)(2,1)} %copy-done.82, bf16[512,1024]{1,0:T(8,128)(2,1)} %copy-done.81, bf16[512,1024]{1,0:T(8,128)(2,1)S(1)} %copy-done.79, bf16[512,1024]{1,0:T(8,128)(2,1)} %copy-done.80), kind=kOutput, calls=%fused_computation.38 | convolution fusion | flops 8608808960 | bytes 16777216 | tf_op jit(solution)/shard_map/dot_general | solution.py:29
  753.8 5.5 convolution_convert_fusion.4
  759.4 12.9 %multiply_reduce_fusion = (f32[4,1024]{1,0:T(4,128)S(1)}, f32[4,1024,1024]{1,2,0:T(8,128)}) fusion(f32[4,1024,1024]{1,2,0:T(8,128)} %copy-done, f32[4,1024]{1,0:T(4,128)S(1)} %copy-done.53, pred[1024,1024]{0,1:T(8,128)(4,1)S(1)} %copy-done.7, bf16[4,1024,128]{1,2,0:T(8,128)(2,1)S(1)} %bitcast.285, f32[4,1024,384]{1,2,0:T(8,128)} %copy-done.1), kind=kOutput, calls=%fused_computation.1 | convolution fusion | flops 1094709248 | bytes 36732928 | tf_op jit(solution)/shard_map/hqd,hkd->hqk/dot_general | solution.py:233
  772.4 13.1 %multiply_convert_fusion = bf16[4,1024,1024]{1,2,0:T(8,128)(2,1)S(1)} fusion(f32[4,1024,1024]{1,2,0:T(8,128)} %get-tuple-element.181, f32[4,1024,1024]{1,2,0:T(8,128)} %copy-done, f32[4,1024]{1,0:T(4,128)S(1)} %get-tuple-element.180, f32[4,1024]{1,0:T(4,128)S(1)} %copy-done.53, pred[1024,1024]{0,1:T(8,128)(4,1)S(1)} %copy-done.7), kind=kLoop, calls=%fused_computation | loop fusion | flops 25165824 | bytes 43024384 | tf_op jit(solution)/shard_map/convert_element_type | solution.py:25
  785.5 4.2 convolution_multiply_fusion.1
  795.8 12.3 %convolution_convert_fusion.3 = bf16[4,1024,128]{1,2,0:T(8,128)(2,1)} fusion(bf16[4,1024,128]{1,2,0:T(8,128)(2,1)} %bitcast.286, f32[4,1024,1024]{1,2,0:T(8,128)} %copy-done, f32[4,1024]{1,0:T(4,128)S(1)} %copy-done.53, pred[1024,1024]{0,1:T(8,128)(4,1)S(1)} %copy-done.7), kind=kOutput, calls=%fused_computation.165 | convolution fusion | flops 1091043328 | bytes 19939328 | tf_op jit(solution)/shard_map/hqk,hqd->hkd/dot_general | solution.py:238
  813.1 4.0 multiply_convert_fusion.2
  818.1 12.2 %convert_bitcast_fusion = bf16[4,2048,384]{1,2,0:T(8,128)(2,1)} fusion(bf16[1024,2048]{1,0:T(8,128)(2,1)} %constant_dynamic-update-slice_fusion, bf16[4,1024,128]{1,2,0:T(8,128)(2,1)S(1)} %copy-done.44, bf16[4,1024,128]{1,2,0:T(8,128)(2,1)S(1)} %get-tuple-element.72, bf16[4,1024,128]{1,2,0:T(8,128)(2,1)S(1)} %get-tuple-element.71), kind=kOutput, calls=%fused_computation.7 | convolution fusion | flops 6455033856 | bytes 13631488 | tf_op jit(solution)/shard_map/tk,qtn->qkn/dot_general | solution.py:402
  830.3 8.8 copy.99
  852.2 7.8 bitcast_convert_fusion
  863.0 6.4 convolution_bitcast_fusion
  869.4 30.7 %collective-permute-done.57 = bf16[256,2048]{1,0:T(8,128)(2,1)S(1)} collective-permute-done((bf16[256,2048]{1,0:T(8,128)(2,1)}, bf16[256,2048]{1,0:T(8,128)(2,1)S(1)}, u32[]{:S(2)}, u32[]{:S(2)}) %collective-permute-start.57) | collective-permute-done | bytes 1048608 | tf_op jit(solution)/shard_map/ppermute | solution.py:46
  918.4 9.4 collective-permute-done.60
  944.1 4.3 collective-permute-start.77
  955.0 47.9 %collective-permute-done.77 = bf16[1024,256]{1,0:T(8,128)(2,1)S(1)} collective-permute-done((bf16[1024,256]{1,0:T(8,128)(2,1)S(1)}, bf16[1024,256]{1,0:T(8,128)(2,1)S(1)}, u32[]{:S(2)}, u32[]{:S(2)}) %collective-permute-start.77) | collective-permute-done | bytes 524320 | tf_op jit(solution)/shard_map/ppermute | solution.py:182
  1002.9 15.1 %collective-permute-done.78 = bf16[1024,256]{1,0:T(8,128)(2,1)S(1)} collective-permute-done((bf16[1024,256]{1,0:T(8,128)(2,1)S(1)}, bf16[1024,256]{1,0:T(8,128)(2,1)S(1)}, u32[]{:S(2)}, u32[]{:S(2)}) %collective-permute-start.78) | collective-permute-done | bytes 524320 | tf_op jit(solution)/shard_map/ppermute | solution.py:182
  1018.7 17.4 %reduce-scatter.6.cloned.1.call-done = bf16[1024,384]{1,0:T(8,128)(2,1)} async-done(((bf16[8192,384]{1,0:T(8,128)(2,1)}), bf16[1024,384]{1,0:T(8,128)(2,1)}) %reduce-scatter.6.cloned.1.call-update) | async-done | bytes 786448 | tf_op jit(solution)/shard_map/reduce_scatter | solution.py:407
  1037.7 33.1 %collective-permute-start.61 = (bf16[512,384]{0,1:T(8,128)(2,1)S(1)}, bf16[512,384]{0,1:T(8,128)(2,1)S(1)}, u32[]{:S(2)}, u32[]{:S(2)}) collective-permute-start(bf16[512,384]{0,1:T(8,128)(2,1)S(1)} %bitcast.303), channel_id=1, source_target_pairs={{0,0},{1,1},{4,2},{5,3},{2,4},{3,5},{6,6},{7,7},{8,8},{9,9},{12,10... | collective-permute-start | bytes 1179656 | tf_op jit(solution)/shard_map/ppermute | solution.py:182
  1074.2 6.3 collective-permute-done.61
  (615 shorter events, 244.5 us)
Async XLA Ops:
  7.2 112.7 %all-gather.6.cloned.1.call-start = ((), (), s32[]{:S(2)}) async-start(), calls=%async_computation.5 | async-start | bytes 7077888 | tf_op jit(solution)/shard_map/all_gather | solution.py:291
  12.3 12.3 %collective-permute-start = (bf16[512,384]{1,0:T(8,128)(2,1)S(1)}, bf16[512,384]{1,0:T(8,128)(2,1)S(1)}, u32[]{:S(2)}, u32[]{:S(2)}) collective-permute-start(bf16[512,384]{1,0:T(8,128)(2,1)S(1)} %bitcast.301), channel_id=1, source_target_pairs={{0,0},{1,1},{2,4},{3,5},{4,2},{5,3},{6,6},{7,7},{8,8},{9,9},{10,12... | collective-permute-start | bytes 1179656 | tf_op jit(solution)/shard_map/ppermute | solution.py:182
  26.0 163.3 %all-gather.8.cloned.1.call-start = ((), (), s32[]{:S(2)}) async-start(), calls=%async_computation.6 | async-start | bytes 2359296 | tf_op jit(solution)/shard_map/all_gather | solution.py:293
  34.9 256.4 %all-gather.10.cloned.1.call-start = ((), (), s32[]{:S(2)}) async-start(), calls=%async_computation.7 | async-start | bytes 5242880 | tf_op jit(solution)/shard_map/all_gather | solution.py:333
  36.1 284.9 %all-gather.12.cloned.1.call-start = ((), (), s32[]{:S(2)}) async-start(), calls=%async_computation.8 | async-start | bytes 5242880 | tf_op jit(solution)/shard_map/all_gather | solution.py:334
  37.0 20.3 %collective-permute-start.11 = (f32[2304]{0:T(1024)}, f32[2304]{0:T(1024)}, u32[]{:S(2)}, u32[]{:S(2)}) collective-permute-start(f32[2304]{0:T(1024)} %pad_maximum_fusion.25), channel_id=1, source_target_pairs={{0,3},{1,2},{2,1},{3,0},{4,7},{5,6},{6,5},{7,4},{8,11},{9,10},{10,... | collective-permute-start | bytes 27656 | tf_op jit(solution)/shard_map/ppermute | solution.py:46
  37.1 16.2 %collective-permute-start.10 = (f32[2304]{0:T(1024)}, f32[2304]{0:T(1024)}, u32[]{:S(2)}, u32[]{:S(2)}) collective-permute-start(f32[2304]{0:T(1024)} %pad_maximum_fusion.25), channel_id=1, source_target_pairs={{0,2},{1,3},{2,0},{3,1},{4,6},{5,7},{6,4},{7,5},{8,10},{9,11},{10,... | collective-permute-start | bytes 27656 | tf_op jit(solution)/shard_map/ppermute | solution.py:46
  37.7 20.2 %collective-permute-start.9 = (f32[2304]{0:T(1024)}, f32[2304]{0:T(1024)}, u32[]{:S(2)}, u32[]{:S(2)}) collective-permute-start(f32[2304]{0:T(1024)} %pad_maximum_fusion.25), channel_id=1, source_target_pairs={{0,1},{1,0},{2,3},{3,2},{4,5},{5,4},{6,7},{7,6},{8,9},{9,8},{10,11... | collective-permute-start | bytes 27656 | tf_op jit(solution)/shard_map/ppermute | solution.py:46
  43.4 153.7 %collective-permute-start.22 = (bf16[1024,256]{1,0:T(8,128)(2,1)}, bf16[1024,256]{1,0:T(8,128)(2,1)}, u32[]{:S(2)}, u32[]{:S(2)}) collective-permute-start(bf16[1024,256]{1,0:T(8,128)(2,1)} %get-tuple-element.123), channel_id=1, source_target_pairs={{0,0},{1,8},{2,16},{3,24},{4,4},{5,12},{6,20},{7,28},{8,1},{9,9},{... | collective-permute-start | bytes 1572872 | tf_op jit(solution)/shard_map/ppermute | solution.py:182
  47.8 149.3 %collective-permute-start.23 = (bf16[1024,256]{1,0:T(8,128)(2,1)}, bf16[1024,256]{1,0:T(8,128)(2,1)}, u32[]{:S(2)}, u32[]{:S(2)}) collective-permute-start(bf16[1024,256]{1,0:T(8,128)(2,1)} %get-tuple-element.124), channel_id=1, source_target_pairs={{0,4},{1,12},{2,20},{3,28},{4,0},{5,8},{6,16},{7,24},{8,5},{9,13},... | collective-permute-start | bytes 1572872 | tf_op jit(solution)/shard_map/ppermute | solution.py:182
  49.1 326.3 %all-gather.14.cloned.1.call-start = ((), (), s32[]{:S(2)}) async-start(), calls=%async_computation.9 | async-start | bytes 5242880 | tf_op jit(solution)/shard_map/all_gather | solution.py:339
  53.3 31.2 %collective-permute-start.3 = (bf16[128,2048]{1,0:T(8,128)(2,1)}, bf16[128,2048]{1,0:T(8,128)(2,1)S(1)}, u32[]{:S(2)}, u32[]{:S(2)}) collective-permute-start(bf16[128,2048]{1,0:T(8,128)(2,1)} %get-tuple-element.127), channel_id=1, source_target_pairs={{0,1},{1,0},{2,3},{3,2},{4,5},{5,4},{6,7},{7,6},{8,9},{9,8},{10,11... | collective-permute-start | bytes 1572872 | tf_op jit(solution)/shard_map/ppermute | solution.py:46
  57.2 16.2 %collective-permute-start.2 = (bf16[128,2048]{1,0:T(8,128)(2,1)}, bf16[128,2048]{1,0:T(8,128)(2,1)S(1)}, u32[]{:S(2)}, u32[]{:S(2)}) collective-permute-start(bf16[128,2048]{1,0:T(8,128)(2,1)} %get-tuple-element.128), channel_id=1, source_target_pairs={{0,2},{1,3},{2,0},{3,1},{4,6},{5,7},{6,4},{7,5},{8,10},{9,11},{10,... | collective-permute-start | bytes 1572872 | tf_op jit(solution)/shard_map/ppermute | solution.py:46
  74.6 33.1 %collective-permute-start.4 = (bf16[256,2048]{1,0:T(8,128)(2,1)S(1)}, bf16[256,2048]{1,0:T(8,128)(2,1)S(1)}, u32[]{:S(2)}, u32[]{:S(2)}) collective-permute-start(bf16[256,2048]{1,0:T(8,128)(2,1)S(1)} %pad_maximum_fusion.7), channel_id=1, source_target_pairs={{0,1},{1,0},{2,3},{3,2},{4,5},{5,4},{6,7},{7,6},{8,9},{9,8},{10,11... | collective-permute-start | bytes 3145736 | tf_op jit(solution)/shard_map/ppermute | solution.py:46
  85.6 33.2 %collective-permute-start.5 = (bf16[256,2048]{1,0:T(8,128)(2,1)S(1)}, bf16[256,2048]{1,0:T(8,128)(2,1)S(1)}, u32[]{:S(2)}, u32[]{:S(2)}) collective-permute-start(bf16[256,2048]{1,0:T(8,128)(2,1)S(1)} %pad_maximum_fusion.8), channel_id=1, source_target_pairs={{0,2},{1,3},{2,0},{3,1},{4,6},{5,7},{6,4},{7,5},{8,10},{9,11},{10,... | collective-permute-start | bytes 3145736 | tf_op jit(solution)/shard_map/ppermute | solution.py:46
  130.4 36.9 %collective-permute-start.8 = (f32[2,1024]{1,0:T(2,128)S(1)}, f32[2,1024]{1,0:T(2,128)S(1)}, u32[]{:S(2)}, u32[]{:S(2)}) collective-permute-start(f32[2,1024]{1,0:T(2,128)S(1)} %pad_maximum_fusion.26), channel_id=1, source_target_pairs={{0,3},{1,2},{2,1},{3,0},{4,7},{5,6},{6,5},{7,4},{8,11},{9,10},{10,... | collective-permute-start | bytes 24584 | tf_op jit(solution)/shard_map/ppermute | solution.py:46
  146.9 20.5 %collective-permute-start.7 = (f32[2,1024]{1,0:T(2,128)S(1)}, f32[2,1024]{1,0:T(2,128)S(1)}, u32[]{:S(2)}, u32[]{:S(2)}) collective-permute-start(f32[2,1024]{1,0:T(2,128)S(1)} %pad_maximum_fusion.26), channel_id=1, source_target_pairs={{0,2},{1,3},{2,0},{3,1},{4,6},{5,7},{6,4},{7,5},{8,10},{9,11},{10,... | collective-permute-start | bytes 24584 | tf_op jit(solution)/shard_map/ppermute | solution.py:46
  193.6 35.8 %collective-permute-start.16 = (bf16[256,2048]{1,0:T(8,128)(2,1)}, bf16[256,2048]{1,0:T(8,128)(2,1)}, u32[]{:S(2)}, u32[]{:S(2)}) collective-permute-start(bf16[256,2048]{1,0:T(8,128)(2,1)} %get-tuple-element.99), channel_id=1, source_target_pairs={{0,1},{1,0},{2,3},{3,2},{4,5},{5,4},{6,7},{7,6},{8,9},{9,8},{10,11... | collective-permute-start | bytes 3145736 | tf_op jit(solution)/shard_map/ppermute | solution.py:46
  195.2 37.9 %collective-permute-start.18 = (bf16[256,2048]{1,0:T(8,128)(2,1)}, bf16[256,2048]{1,0:T(8,128)(2,1)}, u32[]{:S(2)}, u32[]{:S(2)}) collective-permute-start(bf16[256,2048]{1,0:T(8,128)(2,1)} %get-tuple-element.100), channel_id=1, source_target_pairs={{0,2},{1,3},{2,0},{3,1},{4,6},{5,7},{6,4},{7,5},{8,10},{9,11},{10,... | collective-permute-start | bytes 3145736 | tf_op jit(solution)/shard_map/ppermute | solution.py:46
  200.2 730.3 %reduce-scatter.8.cloned.1.call-start = ((), (), s32[]{:S(2)}) async-start(), calls=%async_computation.11 | async-start | bytes 2359296 | tf_op jit(solution)/shard_map/reduce_scatter | solution.py:405
  235.6 24.4 %collective-permute-start.19 = (bf16[128,2048]{1,0:T(8,128)(2,1)S(1)}, bf16[128,2048]{1,0:T(8,128)(2,1)S(1)}, u32[]{:S(2)}, u32[]{:S(2)}) collective-permute-start(bf16[128,2048]{1,0:T(8,128)(2,1)S(1)} %slice.851), channel_id=1, source_target_pairs={{0,1},{1,0},{2,3},{3,2},{4,5},{5,4},{6,7},{7,6},{8,9},{9,8},{10,11... | collective-permute-start | bytes 1572872 | tf_op jit(solution)/shard_map/ppermute | solution.py:46
  235.7 24.5 %collective-permute-start.17 = (bf16[128,2048]{1,0:T(8,128)(2,1)S(1)}, bf16[128,2048]{1,0:T(8,128)(2,1)S(1)}, u32[]{:S(2)}, u32[]{:S(2)}) collective-permute-start(bf16[128,2048]{1,0:T(8,128)(2,1)S(1)} %slice.852), channel_id=1, source_target_pairs={{0,2},{1,3},{2,0},{3,1},{4,6},{5,7},{6,4},{7,5},{8,10},{9,11},{10,... | collective-permute-start | bytes 1572872 | tf_op jit(solution)/shard_map/ppermute | solution.py:46
  263.6 22.2 %collective-permute-start.20 = (bf16[256,2048]{1,0:T(8,128)(2,1)S(1)}, bf16[256,2048]{1,0:T(8,128)(2,1)S(1)}, u32[]{:S(2)}, u32[]{:S(2)}) collective-permute-start(bf16[256,2048]{1,0:T(8,128)(2,1)S(1)} %get-tuple-element.67), channel_id=1, source_target_pairs={{0,8},{4,12},{8,16},{12,20},{16,24},{20,28},{24,0},{28,4},{1,9},{5... | collective-permute-start | bytes 3145736 | tf_op jit(solution)/shard_map/ppermute | solution.py:129
  263.6 23.5 %collective-permute-start.34 = (bf16[256,2048]{1,0:T(8,128)(2,1)S(1)}, bf16[256,2048]{1,0:T(8,128)(2,1)S(1)}, u32[]{:S(2)}, u32[]{:S(2)}) collective-permute-start(bf16[256,2048]{1,0:T(8,128)(2,1)S(1)} %get-tuple-element.67), channel_id=1, source_target_pairs={{0,4},{4,0},{8,12},{12,8},{16,20},{20,16},{24,28},{28,24},{1,5},{5... | collective-permute-start | bytes 3145736 | tf_op jit(solution)/shard_map/ppermute | solution.py:133
  285.8 94.7 %collective-permute-start.26 = (bf16[256,2048]{1,0:T(8,128)(2,1)S(1)}, bf16[256,2048]{1,0:T(8,128)(2,1)S(1)}, u32[]{:S(2)}, u32[]{:S(2)}) collective-permute-start(bf16[256,2048]{1,0:T(8,128)(2,1)S(1)} %collective-permute-done.20), channel_id=1, source_target_pairs={{0,8},{4,12},{8,16},{12,20},{16,24},{20,28},{24,0},{28,4},{1,9},{5... | collective-permute-start | bytes 3145736 | tf_op jit(solution)/shard_map/ppermute | solution.py:129
  380.9 27.8 %collective-permute-start.30 = (bf16[256,2048]{1,0:T(8,128)(2,1)S(1)}, bf16[256,2048]{1,0:T(8,128)(2,1)S(1)}, u32[]{:S(2)}, u32[]{:S(2)}) collective-permute-start(bf16[256,2048]{1,0:T(8,128)(2,1)S(1)} %collective-permute-done.26), channel_id=1, source_target_pairs={{0,8},{4,12},{8,16},{12,20},{16,24},{20,28},{24,0},{28,4},{1,9},{5... | collective-permute-start | bytes 3145736 | tf_op jit(solution)/shard_map/ppermute | solution.py:129
  383.8 46.5 %collective-permute-start.25 = (bf16[256,2048]{1,0:T(8,128)(2,1)S(1)}, bf16[256,2048]{1,0:T(8,128)(2,1)S(1)}, u32[]{:S(2)}, u32[]{:S(2)}) collective-permute-start(bf16[256,2048]{1,0:T(8,128)(2,1)S(1)} %fusion.58), channel_id=1, source_target_pairs={{0,8},{4,12},{8,16},{12,20},{16,24},{20,28},{24,0},{28,4},{1,9},{5... | collective-permute-start | bytes 3145736 | tf_op jit(solution)/shard_map/ppermute | solution.py:129
  396.4 33.9 %collective-permute-start.28 = (bf16[256,2048]{1,0:T(8,128)(2,1)S(1)}, bf16[256,2048]{1,0:T(8,128)(2,1)S(1)}, u32[]{:S(2)}, u32[]{:S(2)}) collective-permute-start(bf16[256,2048]{1,0:T(8,128)(2,1)S(1)} %slice.847), channel_id=1, source_target_pairs={{0,4},{4,0},{8,12},{12,8},{16,20},{20,16},{24,28},{28,24},{1,5},{5... | collective-permute-start | bytes 3145736 | tf_op jit(solution)/shard_map/ppermute | solution.py:133
  408.7 22.4 %collective-permute-start.31 = (bf16[256,2048]{1,0:T(8,128)(2,1)S(1)}, bf16[256,2048]{1,0:T(8,128)(2,1)S(1)}, u32[]{:S(2)}, u32[]{:S(2)}) collective-permute-start(bf16[256,2048]{1,0:T(8,128)(2,1)S(1)} %collective-permute-done.30), channel_id=1, source_target_pairs={{0,4},{4,0},{8,12},{12,8},{16,20},{20,16},{24,28},{28,24},{1,5},{5... | collective-permute-start | bytes 3145736 | tf_op jit(solution)/shard_map/ppermute | solution.py:133
  430.8 26.4 %collective-permute-start.29 = (bf16[256,2048]{1,0:T(8,128)(2,1)S(1)}, bf16[256,2048]{1,0:T(8,128)(2,1)S(1)}, u32[]{:S(2)}, u32[]{:S(2)}) collective-permute-start(bf16[256,2048]{1,0:T(8,128)(2,1)S(1)} %fusion.57), channel_id=1, source_target_pairs={{0,8},{4,12},{8,16},{12,20},{16,24},{20,28},{24,0},{28,4},{1,9},{5... | collective-permute-start | bytes 3145736 | tf_op jit(solution)/shard_map/ppermute | solution.py:129
  440.9 16.3 %collective-permute-start.32 = (bf16[256,2048]{1,0:T(8,128)(2,1)S(1)}, bf16[256,2048]{1,0:T(8,128)(2,1)S(1)}, u32[]{:S(2)}, u32[]{:S(2)}) collective-permute-start(bf16[256,2048]{1,0:T(8,128)(2,1)S(1)} %slice.846), channel_id=1, source_target_pairs={{0,4},{4,0},{8,12},{12,8},{16,20},{20,16},{24,28},{28,24},{1,5},{5... | collective-permute-start | bytes 3145736 | tf_op jit(solution)/shard_map/ppermute | solution.py:133
  457.7 25.6 %collective-permute-start.33 = (bf16[256,2048]{1,0:T(8,128)(2,1)S(1)}, bf16[256,2048]{1,0:T(8,128)(2,1)S(1)}, u32[]{:S(2)}, u32[]{:S(2)}) collective-permute-start(bf16[256,2048]{1,0:T(8,128)(2,1)S(1)} %fusion.55), channel_id=1, source_target_pairs={{0,8},{4,12},{8,16},{12,20},{16,24},{20,28},{24,0},{28,4},{1,9},{5... | collective-permute-start | bytes 3145736 | tf_op jit(solution)/shard_map/ppermute | solution.py:129
  486.8 24.3 %collective-permute-start.36 = (bf16[256,2048]{1,0:T(8,128)(2,1)S(1)}, bf16[256,2048]{1,0:T(8,128)(2,1)S(1)}, u32[]{:S(2)}, u32[]{:S(2)}) collective-permute-start(bf16[256,2048]{1,0:T(8,128)(2,1)S(1)} %get-tuple-element.65), channel_id=1, source_target_pairs={{0,8},{4,12},{8,16},{12,20},{16,24},{20,28},{24,0},{28,4},{1,9},{5... | collective-permute-start | bytes 3145736 | tf_op jit(solution)/shard_map/ppermute | solution.py:129
  511.1 27.4 %collective-permute-start.48 = (bf16[256,2048]{1,0:T(8,128)(2,1)S(1)}, bf16[256,2048]{1,0:T(8,128)(2,1)S(1)}, u32[]{:S(2)}, u32[]{:S(2)}) collective-permute-start(bf16[256,2048]{1,0:T(8,128)(2,1)S(1)} %get-tuple-element.65), channel_id=1, source_target_pairs={{0,4},{4,0},{8,12},{12,8},{16,20},{20,16},{24,28},{28,24},{1,5},{5... | collective-permute-start | bytes 3145736 | tf_op jit(solution)/shard_map/ppermute | solution.py:133
  511.6 26.9 %collective-permute-start.40 = (bf16[256,2048]{1,0:T(8,128)(2,1)S(1)}, bf16[256,2048]{1,0:T(8,128)(2,1)S(1)}, u32[]{:S(2)}, u32[]{:S(2)}) collective-permute-start(bf16[256,2048]{1,0:T(8,128)(2,1)S(1)} %collective-permute-done.36), channel_id=1, source_target_pairs={{0,8},{4,12},{8,16},{12,20},{16,24},{20,28},{24,0},{28,4},{1,9},{5... | collective-permute-start | bytes 3145736 | tf_op jit(solution)/shard_map/ppermute | solution.py:129
  523.7 22.1 %collective-permute-start.38 = (bf16[256,2048]{1,0:T(8,128)(2,1)S(1)}, bf16[256,2048]{1,0:T(8,128)(2,1)S(1)}, u32[]{:S(2)}, u32[]{:S(2)}) collective-permute-start(bf16[256,2048]{1,0:T(8,128)(2,1)S(1)} %slice.844), channel_id=1, source_target_pairs={{0,4},{4,0},{8,12},{12,8},{16,20},{20,16},{24,28},{28,24},{1,5},{5... | collective-permute-start | bytes 3145736 | tf_op jit(solution)/shard_map/ppermute | solution.py:133
  538.4 27.9 %collective-permute-start.44 = (bf16[256,2048]{1,0:T(8,128)(2,1)S(1)}, bf16[256,2048]{1,0:T(8,128)(2,1)S(1)}, u32[]{:S(2)}, u32[]{:S(2)}) collective-permute-start(bf16[256,2048]{1,0:T(8,128)(2,1)S(1)} %collective-permute-done.40), channel_id=1, source_target_pairs={{0,8},{4,12},{8,16},{12,20},{16,24},{20,28},{24,0},{28,4},{1,9},{5... | collective-permute-start | bytes 3145736 | tf_op jit(solution)/shard_map/ppermute | solution.py:129
  538.4 27.9 %collective-permute-start.41 = (bf16[256,2048]{1,0:T(8,128)(2,1)S(1)}, bf16[256,2048]{1,0:T(8,128)(2,1)S(1)}, u32[]{:S(2)}, u32[]{:S(2)}) collective-permute-start(bf16[256,2048]{1,0:T(8,128)(2,1)S(1)} %collective-permute-done.40), channel_id=1, source_target_pairs={{0,4},{4,0},{8,12},{12,8},{16,20},{20,16},{24,28},{28,24},{1,5},{5... | collective-permute-start | bytes 3145736 | tf_op jit(solution)/shard_map/ppermute | solution.py:133
  546.1 55.1 %collective-permute-start.39 = (bf16[256,2048]{1,0:T(8,128)(2,1)S(1)}, bf16[256,2048]{1,0:T(8,128)(2,1)S(1)}, u32[]{:S(2)}, u32[]{:S(2)}) collective-permute-start(bf16[256,2048]{1,0:T(8,128)(2,1)S(1)} %fusion.52), channel_id=1, source_target_pairs={{0,8},{4,12},{8,16},{12,20},{16,24},{20,28},{24,0},{28,4},{1,9},{5... | collective-permute-start | bytes 3145736 | tf_op jit(solution)/shard_map/ppermute | solution.py:129
  566.3 16.6 %collective-permute-start.45 = (bf16[256,2048]{1,0:T(8,128)(2,1)S(1)}, bf16[256,2048]{1,0:T(8,128)(2,1)S(1)}, u32[]{:S(2)}, u32[]{:S(2)}) collective-permute-start(bf16[256,2048]{1,0:T(8,128)(2,1)S(1)} %collective-permute-done.44), channel_id=1, source_target_pairs={{0,4},{4,0},{8,12},{12,8},{16,20},{20,16},{24,28},{28,24},{1,5},{5... | collective-permute-start | bytes 3145736 | tf_op jit(solution)/shard_map/ppermute | solution.py:133
  582.8 18.4 %collective-permute-start.42 = (bf16[256,2048]{1,0:T(8,128)(2,1)S(1)}, bf16[256,2048]{1,0:T(8,128)(2,1)S(1)}, u32[]{:S(2)}, u32[]{:S(2)}) collective-permute-start(bf16[256,2048]{1,0:T(8,128)(2,1)S(1)} %slice.843), channel_id=1, source_target_pairs={{0,4},{4,0},{8,12},{12,8},{16,20},{20,16},{24,28},{28,24},{1,5},{5... | collective-permute-start | bytes 3145736 | tf_op jit(solution)/shard_map/ppermute | solution.py:133
  601.7 26.7 %collective-permute-start.43 = (bf16[256,2048]{1,0:T(8,128)(2,1)S(1)}, bf16[256,2048]{1,0:T(8,128)(2,1)S(1)}, u32[]{:S(2)}, u32[]{:S(2)}) collective-permute-start(bf16[256,2048]{1,0:T(8,128)(2,1)S(1)} %fusion.51), channel_id=1, source_target_pairs={{0,8},{4,12},{8,16},{12,20},{16,24},{20,28},{24,0},{28,4},{1,9},{5... | collective-permute-start | bytes 3145736 | tf_op jit(solution)/shard_map/ppermute | solution.py:129
  601.8 26.7 %collective-permute-start.46 = (bf16[256,2048]{1,0:T(8,128)(2,1)S(1)}, bf16[256,2048]{1,0:T(8,128)(2,1)S(1)}, u32[]{:S(2)}, u32[]{:S(2)}) collective-permute-start(bf16[256,2048]{1,0:T(8,128)(2,1)S(1)} %slice.842), channel_id=1, source_target_pairs={{0,4},{4,0},{8,12},{12,8},{16,20},{20,16},{24,28},{28,24},{1,5},{5... | collective-permute-start | bytes 3145736 | tf_op jit(solution)/shard_map/ppermute | solution.py:133
  610.9 18.3 %collective-permute-start.49 = (bf16[256,2048]{1,0:T(8,128)(2,1)S(1)}, bf16[256,2048]{1,0:T(8,128)(2,1)S(1)}, u32[]{:S(2)}, u32[]{:S(2)}) collective-permute-start(bf16[256,2048]{1,0:T(8,128)(2,1)S(1)} %slice.841), channel_id=1, source_target_pairs={{0,4},{4,0},{8,12},{12,8},{16,20},{20,16},{24,28},{28,24},{1,5},{5... | collective-permute-start | bytes 3145736 | tf_op jit(solution)/shard_map/ppermute | solution.py:133
  629.0 26.1 %collective-permute-start.47 = (bf16[256,2048]{1,0:T(8,128)(2,1)S(1)}, bf16[256,2048]{1,0:T(8,128)(2,1)S(1)}, u32[]{:S(2)}, u32[]{:S(2)}) collective-permute-start(bf16[256,2048]{1,0:T(8,128)(2,1)S(1)} %fusion.49), channel_id=1, source_target_pairs={{0,8},{4,12},{8,16},{12,20},{16,24},{20,28},{24,0},{28,4},{1,9},{5... | collective-permute-start | bytes 3145736 | tf_op jit(solution)/shard_map/ppermute | solution.py:129
  659.0 12.1 %collective-permute-start.51 = (bf16[128,2048]{1,0:T(8,128)(2,1)S(1)}, bf16[128,2048]{1,0:T(8,128)(2,1)S(1)}, u32[]{:S(2)}, u32[]{:S(2)}) collective-permute-start(bf16[128,2048]{1,0:T(8,128)(2,1)S(1)} %get-tuple-element.118), channel_id=1, source_target_pairs={{0,1},{1,0},{2,3},{3,2},{4,5},{5,4},{6,7},{7,6},{8,9},{9,8},{10,11... | collective-permute-start | bytes 1572872 | tf_op jit(solution)/shard_map/ppermute | solution.py:46
  670.5 22.5 %collective-permute-start.52 = (bf16[256,2048]{1,0:T(8,128)(2,1)S(1)}, bf16[256,2048]{1,0:T(8,128)(2,1)S(1)}, u32[]{:S(2)}, u32[]{:S(2)}) collective-permute-start(bf16[256,2048]{1,0:T(8,128)(2,1)S(1)} %pad_maximum_fusion.13), channel_id=1, source_target_pairs={{0,1},{1,0},{2,3},{3,2},{4,5},{5,4},{6,7},{7,6},{8,9},{9,8},{10,11... | collective-permute-start | bytes 3145736 | tf_op jit(solution)/shard_map/ppermute | solution.py:46
  671.2 21.9 %collective-permute-start.53 = (bf16[256,2048]{1,0:T(8,128)(2,1)S(1)}, bf16[256,2048]{1,0:T(8,128)(2,1)S(1)}, u32[]{:S(2)}, u32[]{:S(2)}) collective-permute-start(bf16[256,2048]{1,0:T(8,128)(2,1)S(1)} %pad_maximum_fusion.14), channel_id=1, source_target_pairs={{0,2},{1,3},{2,0},{3,1},{4,6},{5,7},{6,4},{7,5},{8,10},{9,11},{10,... | collective-permute-start | bytes 3145736 | tf_op jit(solution)/shard_map/ppermute | solution.py:46
  698.9 241.5 %reduce-scatter.14.cloned.1.call-start = ((), (), s32[]{:S(2)}) async-start(), calls=%async_computation.14 | async-start | bytes 5242880 | tf_op jit(solution)/shard_map/reduce_scatter | solution.py:377
  721.5 227.9 %reduce-scatter.12.cloned.1.call-start = ((), (), s32[]{:S(2)}) async-start(), calls=%async_computation.13 | async-start | bytes 5242880 | tf_op jit(solution)/shard_map/reduce_scatter | solution.py:376
  737.3 215.0 %reduce-scatter.10.cloned.1.call-start = ((), (), s32[]{:S(2)}) async-start(), calls=%async_computation.12 | async-start | bytes 5242880 | tf_op jit(solution)/shard_map/reduce_scatter | solution.py:375
  753.6 282.5 %reduce-scatter.6.cloned.1.call-start = ((), (), s32[]{:S(2)}) async-start(), calls=%async_computation.10 | async-start | bytes 7077888 | tf_op jit(solution)/shard_map/reduce_scatter | solution.py:407
  794.3 15.8 %collective-permute-start.56 = (f32[2,1024]{1,0:T(2,128)S(1)}, f32[2,1024]{1,0:T(2,128)S(1)}, u32[]{:S(2)}, u32[]{:S(2)}) collective-permute-start(f32[2,1024]{1,0:T(2,128)S(1)} %pad_maximum_fusion.27), channel_id=1, source_target_pairs={{0,3},{1,2},{2,1},{3,0},{4,7},{5,6},{6,5},{7,4},{8,11},{9,10},{10,... | collective-permute-start | bytes 24584 | tf_op jit(solution)/shard_map/ppermute | solution.py:46
  846.0 15.8 %collective-permute-start.70 = (f32[2,128]{1,0:T(2,128)S(1)}, f32[2,128]{1,0:T(2,128)S(1)}, u32[]{:S(2)}, u32[]{:S(2)}) collective-permute-start(f32[2,128]{1,0:T(2,128)S(1)} %get-tuple-element.166), channel_id=1, source_target_pairs={{3,0},{0,1},{1,2},{2,3},{7,4},{4,5},{5,6},{6,7},{11,8},{8,9},{9,10... | collective-permute-start | bytes 3080 | tf_op jit(solution)/shard_map/ppermute | solution.py:123
  847.1 15.8 %collective-permute-start.67 = (f32[2,128]{1,0:T(2,128)S(1)}, f32[2,128]{1,0:T(2,128)S(1)}, u32[]{:S(2)}, u32[]{:S(2)}) collective-permute-start(f32[2,128]{1,0:T(2,128)S(1)} %get-tuple-element.167), channel_id=1, source_target_pairs={{0,0},{1,1},{2,2},{3,3},{4,4},{5,5},{6,6},{7,7},{8,8},{9,9},{10,10... | collective-permute-start | bytes 3080 | tf_op jit(solution)/shard_map/ppermute | solution.py:123
  847.1 15.8 %collective-permute-start.68 = (f32[2,128]{1,0:T(2,128)S(1)}, f32[2,128]{1,0:T(2,128)S(1)}, u32[]{:S(2)}, u32[]{:S(2)}) collective-permute-start(f32[2,128]{1,0:T(2,128)S(1)} %get-tuple-element.168), channel_id=1, source_target_pairs={{1,0},{2,1},{3,2},{0,3},{5,4},{6,5},{7,6},{4,7},{9,8},{10,9},{11,1... | collective-permute-start | bytes 3080 | tf_op jit(solution)/shard_map/ppermute | solution.py:123
  849.0 13.9 %collective-permute-start.69 = (f32[2,128]{1,0:T(2,128)S(1)}, f32[2,128]{1,0:T(2,128)S(1)}, u32[]{:S(2)}, u32[]{:S(2)}) collective-permute-start(f32[2,128]{1,0:T(2,128)S(1)} %get-tuple-element.169), channel_id=1, source_target_pairs={{2,0},{3,1},{0,2},{1,3},{6,4},{7,5},{4,6},{5,7},{10,8},{11,9},{8,1... | collective-permute-start | bytes 3080 | tf_op jit(solution)/shard_map/ppermute | solution.py:123
  861.5 38.7 %collective-permute-start.57 = (bf16[256,2048]{1,0:T(8,128)(2,1)}, bf16[256,2048]{1,0:T(8,128)(2,1)S(1)}, u32[]{:S(2)}, u32[]{:S(2)}) collective-permute-start(bf16[256,2048]{1,0:T(8,128)(2,1)} %get-tuple-element.97), channel_id=1, source_target_pairs={{0,1},{1,0},{2,3},{3,2},{4,5},{5,4},{6,7},{7,6},{8,9},{9,8},{10,11... | collective-permute-start | bytes 3145736 | tf_op jit(solution)/shard_map/ppermute | solution.py:46
  861.9 38.3 %collective-permute-start.59 = (bf16[256,2048]{1,0:T(8,128)(2,1)}, bf16[256,2048]{1,0:T(8,128)(2,1)}, u32[]{:S(2)}, u32[]{:S(2)}) collective-permute-start(bf16[256,2048]{1,0:T(8,128)(2,1)} %get-tuple-element.98), channel_id=1, source_target_pairs={{0,2},{1,3},{2,0},{3,1},{4,6},{5,7},{6,4},{7,5},{8,10},{9,11},{10,... | collective-permute-start | bytes 3145736 | tf_op jit(solution)/shard_map/ppermute | solution.py:46
  904.7 23.1 %collective-permute-start.60 = (bf16[128,2048]{1,0:T(8,128)(2,1)S(1)}, bf16[128,2048]{1,0:T(8,128)(2,1)}, u32[]{:S(2)}, u32[]{:S(2)}) collective-permute-start(bf16[128,2048]{1,0:T(8,128)(2,1)S(1)} %slice.849), channel_id=1, source_target_pairs={{0,1},{1,0},{2,3},{3,2},{4,5},{5,4},{6,7},{7,6},{8,9},{9,8},{10,11... | collective-permute-start | bytes 1572872 | tf_op jit(solution)/shard_map/ppermute | solution.py:46
  916.3 13.1 %collective-permute-start.58 = (bf16[128,2048]{1,0:T(8,128)(2,1)S(1)}, bf16[128,2048]{1,0:T(8,128)(2,1)S(1)}, u32[]{:S(2)}, u32[]{:S(2)}) collective-permute-start(bf16[128,2048]{1,0:T(8,128)(2,1)S(1)} %slice.850), channel_id=1, source_target_pairs={{0,2},{1,3},{2,0},{3,1},{4,6},{5,7},{6,4},{7,5},{8,10},{9,11},{10,... | collective-permute-start | bytes 1572872 | tf_op jit(solution)/shard_map/ppermute | solution.py:46
  944.1 58.8 %collective-permute-start.77 = (bf16[1024,256]{1,0:T(8,128)(2,1)S(1)}, bf16[1024,256]{1,0:T(8,128)(2,1)S(1)}, u32[]{:S(2)}, u32[]{:S(2)}) collective-permute-start(bf16[1024,256]{1,0:T(8,128)(2,1)S(1)} %bitcast.298), channel_id=1, source_target_pairs={{0,0},{8,1},{16,2},{24,3},{4,4},{12,5},{20,6},{28,7},{1,8},{9,9},{... | collective-permute-start | bytes 1572872 | tf_op jit(solution)/shard_map/ppermute | solution.py:182
  948.4 69.6 %collective-permute-start.78 = (bf16[1024,256]{1,0:T(8,128)(2,1)S(1)}, bf16[1024,256]{1,0:T(8,128)(2,1)S(1)}, u32[]{:S(2)}, u32[]{:S(2)}) collective-permute-start(bf16[1024,256]{1,0:T(8,128)(2,1)S(1)} %bitcast.295), channel_id=1, source_target_pairs={{4,0},{12,1},{20,2},{28,3},{0,4},{8,5},{16,6},{24,7},{5,8},{13,9},... | collective-permute-start | bytes 1572872 | tf_op jit(solution)/shard_map/ppermute | solution.py:182
  1037.7 42.7 %collective-permute-start.61 = (bf16[512,384]{0,1:T(8,128)(2,1)S(1)}, bf16[512,384]{0,1:T(8,128)(2,1)S(1)}, u32[]{:S(2)}, u32[]{:S(2)}) collective-permute-start(bf16[512,384]{0,1:T(8,128)(2,1)S(1)} %bitcast.303), channel_id=1, source_target_pairs={{0,0},{1,1},{4,2},{5,3},{2,4},{3,5},{6,6},{7,7},{8,8},{9,9},{12,10... | collective-permute-start | bytes 1179656 | tf_op jit(solution)/shard_map/ppermute | solution.py:182
  (127 other events, 1280.5 us)
Sparse Core Ops, SparseCore 0:
  26.2 82.8 all-gather.5
  111.2 76.2 all-gather.7
  189.9 74.6 all-gather.9
  266.9 54.1 all-gather.11
  322.7 52.5 all-gather.13
  699.0 33.9 reduce-scatter.7
  736.0 51.2 reduce-scatter.13
  790.5 52.9 reduce-scatter.11
  846.4 82.1 reduce-scatter.9
  930.9 105.1 reduce-scatter.5

commit v2 on v1

v2 whole, which is shorter than its diff:
```python
import jax
import jax.numpy as jnp
from jax import lax
from jax.experimental import pallas as pl
from jax.experimental.pallas import tpu as pltpu
from jax.sharding import PartitionSpec as P

HEADS = 16
HEAD_DIM = 128
PIECE = 256
SCALE = HEAD_DIM ** (-0.5)

LOG2_E = 1.4426950408889634
VMEM = 24 << 20
WIDE_VMEM = 56 << 20

epsilon = 1e-06
rope_base = 500000.0

F32 = jnp.float32
BF16 = jnp.bfloat16

SQUARE = ((0, 0), (0, 2), (1, 0), (1, 1), (0, 1), (0, 3), (1, 2), (1, 3))


def token_order(count):
    return SQUARE if count == 4 else tuple((0, j) for j in range(count))


def to_low(tensor):
    return tensor.astype(BF16)


def dot(left, right, contract):
    return lax.dot_general(left, right, ((contract[0], contract[1]), ((), ())), preferred_element_type=F32)


def mm(left, right):
    return dot(left, right, ((1,), (0,)))


def mm_first(left, right):
    return dot(left, right, ((0,), (0,)))


def mm_last(left, right):
    return dot(left, right, ((1,), (1,)))


def after(value, *others):
    return lax.optimization_barrier((value,) + others)[0]


def send_shard(value, k):
    count = lax.axis_size("shard")
    return lax.ppermute(value, "shard", [(s, s ^ k) for s in range(count)])


def gather_tokens(own, first_hold=(), last_hold=()):
    count = lax.axis_size("shard")
    if count != 4:
        others = [send_shard(own, k) for k in range(1, count)]
        return jnp.concatenate([own] + others), others[0]
    half = own.shape[0] // 2
    a0, b0 = own[:half], own[half:]
    a2 = send_shard(a0, 2)
    b1 = send_shard(b0, 1)
    if first_hold:
        a2, b1 = after(a2, *first_hold), after(b1, *first_hold)
    a02 = jnp.concatenate([a0, a2])
    b01 = jnp.concatenate([b0, b1])
    a13 = send_shard(a02, 1)
    b23 = send_shard(b01, 2)
    if last_hold:
        a13, b23 = after(a13, *last_hold), after(b23, *last_hold)
    return jnp.concatenate([a02, b01, a13, b23]), a2


def scatter_tokens(keep, send, first_hold=(), last_hold=()):
    count = lax.axis_size("shard")
    if count != 4:
        parts = jnp.split(jnp.concatenate([keep, send]), count)
        return parts[0] + sum(send_shard(to_low(parts[k]), k).astype(F32) for k in range(1, count))
    q = keep.shape[0] // 2
    send_low = to_low(send)
    a_in = send_shard(send_low[:q], 1)
    b_in = send_shard(send_low[q:], 2)
    if first_hold:
        a_in, b_in = after(a_in, *first_hold), after(b_in, *first_hold)
    a02 = keep[:q] + a_in.astype(F32)
    b01 = keep[q:] + b_in.astype(F32)
    h = q // 2
    a_last = send_shard(to_low(a02[h:]), 2)
    b_last = send_shard(to_low(b01[h:]), 1)
    if last_hold:
        a_last, b_last = after(a_last, *last_hold), after(b_last, *last_hold)
    return jnp.concatenate([a02[:h] + a_last.astype(F32), b01[:h] + b_last.astype(F32)])


def swap_blocks(rows, k):
    order = token_order(lax.axis_size("shard"))
    step = rows.shape[-1] // len(order)
    index = [order.index((h, j ^ k)) for h, j in order]
    return jnp.concatenate([rows[..., i * step : (i + 1) * step] for i in index], axis=-1)


def sum_rows(rows):
    return rows + sum(swap_blocks(send_shard(rows, k), k) for k in range(1, lax.axis_size("shard")))


def unrelative(blocks, s):
    shape = blocks.shape
    bits = shape[0].bit_length() - 1
    cube = blocks.reshape((2,) * bits + shape[1:])
    for bit in range(bits):
        cube = jnp.where((s >> bit) % 2 == 1, jnp.flip(cube, bits - 1 - bit), cube)
    return cube.reshape(shape)


def exchange_shard(blocks, s):
    relative = unrelative(blocks, s)
    got = jnp.stack([relative[0]] + [send_shard(relative[k], k) for k in range(1, blocks.shape[0])])
    return unrelative(got, s)


def rows_perm(count, heads, k):
    c = count // heads
    return [(s, heads * (s % c) + (s // c + k) % heads) for s in range(count)]


def spread_heads(blocks, s):
    heads, count = blocks.shape[0], lax.axis_size("shard")
    q = s // (count // heads)
    got = [lax.ppermute(pick(blocks, (q + k) % heads), "shard", rows_perm(count, heads, k)) for k in range(heads)]
    return reverse_pick(jnp.stack(got), s % heads)


def collect_heads(blocks, s):
    heads, count = blocks.shape[0], lax.axis_size("shard")
    q = s // (count // heads)
    got = [
        lax.ppermute(pick(blocks, (s - k) % heads), "shard", flip(rows_perm(count, heads, k))) for k in range(heads)
    ]
    return roll_pick(jnp.stack(got), -q)


def ring(value, count):
    return lax.ppermute(value, "rep", [(r, (r + 2) % count) for r in range(count)])


def sibling(value, count):
    return lax.ppermute(value, "rep", [(r, r ^ 1) for r in range(count)])


def gather_pairs(own, count):
    blocks = [own]
    for _ in range(count // 2 - 1):
        blocks.append(ring(blocks[-1], count))
    pairs = []
    for i, block in enumerate(blocks):
        other = sibling(block, count)
        pairs.append((block, after(other, blocks[i + 1]) if i + 1 < len(blocks) else other))
    return pairs


def scatter_pairs(part_of, count, beside=lambda i, low: ()):
    total = low = None
    for i, step in enumerate(list(range(1, count // 2)) + [0]):
        part = part_of(step, low)
        half = part.shape[0] // 2
        mine = part[:half] + sibling(to_low(part[half:]), count).astype(F32)
        if total is None:
            total = mine
        else:
            got = ring(low, count)
            hold = beside(i - 1, low)
            if hold:
                got = after(got, *hold)
            total = got.astype(F32) + mine
        low = to_low(total)
    return total


def heads_perm(shard_count, rep_count, per, k):
    group = shard_count // per
    pairs = []
    for r in range(rep_count):
        for s in range(shard_count):
            j = (s % per + k) % per
            target = (r // group * group + s // per, per * (r % group) + j)
            pairs.append((r * shard_count + s, target[0] * shard_count + target[1]))
    return pairs


def flip_rep(value, d):
    count = lax.axis_size("rep")
    return lax.ppermute(value, "rep", [(i, i ^ d) for i in range(count)])


def sum_rep(value):
    return value + sum(flip_rep(value, d) for d in range(1, lax.axis_size("rep")))


def spread_down(rows, s):
    S, R = lax.axis_size("shard"), lax.axis_size("rep")
    columns = rows.shape[1]
    share = rows.shape[0] // R
    units = rows.reshape(R // S, S, share, columns)
    pieces = [lax.dynamic_index_in_dim(units, s ^ k, 1, keepdims=False) for k in range(S)]
    return [pieces[0]] + [send_shard(pieces[k], k) for k in range(1, S)]


def cross_down(pieces, s, r):
    R = lax.axis_size("rep")
    m = pieces[0].shape[0]
    pieces = jnp.concatenate(pieces)
    blocks = [pick(pieces, (((r ^ d) // m) ^ s) * m + (r ^ d) % m) for d in range(R)]
    return [blocks[0]] + [flip_rep(blocks[d], d) for d in range(1, R)]


def join_down(blocks, r):
    share, columns = blocks[0].shape
    out = jnp.zeros((share, len(blocks) * columns), blocks[0].dtype)
    for d, block in enumerate(blocks):
        out = lax.dynamic_update_slice_in_dim(out, block, (r ^ d) * columns, 1)
    return out


def return_cross(rows, r):
    R = lax.axis_size("rep")
    columns = rows.shape[1] // R
    blocks = [lax.dynamic_slice_in_dim(rows, (r ^ d) * columns, columns, 1) for d in range(R)]
    return [blocks[0]] + [flip_rep(blocks[d], d) for d in range(1, R)]


def return_spread(blocks, s, r):
    S, R = lax.axis_size("shard"), lax.axis_size("rep")
    m = R // S
    share, columns = blocks[0].shape
    pieces = jnp.zeros((R, share, columns), blocks[0].dtype)
    for d, block in enumerate(blocks):
        other = r ^ d
        pieces = lax.dynamic_update_slice_in_dim(pieces, block[None], ((other // m) ^ s) * m + other % m, 0)
    pieces = pieces.reshape(S, m, share, columns)
    return [pieces[0]] + [send_shard(pieces[k], k) for k in range(1, S)]


def place_units(pieces, s):
    m, share, columns = pieces[0].shape
    S = len(pieces)
    units = jnp.zeros((m, S, share, columns), pieces[0].dtype)
    for k, piece in enumerate(pieces):
        units = lax.dynamic_update_slice_in_dim(units, piece[:, None], s ^ k, 1)
    return units.reshape(m * S * share, columns)


def flip(pairs):
    return [(b, a) for a, b in pairs]


def permute(value, pairs):
    return lax.ppermute(value, ("rep", "shard"), pairs)


def pick(values, index):
    return lax.dynamic_index_in_dim(values, index, 0, keepdims=False)


def roll_pick(values, shift):
    n = values.shape[0]
    if n == 1:
        return values
    return lax.dynamic_slice_in_dim(jnp.concatenate([values, values]), shift % n, n, 0)


def reverse_pick(values, base):
    n = values.shape[0]
    if n == 1:
        return values
    return roll_pick(values[::-1], n - 1 - base)


def frequencies():
    return jnp.power(jnp.float32(rope_base), -2.0 * jnp.arange(HEAD_DIM // 2, dtype=F32) / HEAD_DIM)


def bias_of(piece_first, row, col):
    row_in = (row >= piece_first) & (row < piece_first + PIECE)
    col_in = (col >= piece_first) & (col < piece_first + PIECE)
    return jnp.where((col <= row) | (row_in & col_in), 0.0, -1e30).astype(F32)


def attend_kernel(where_ref, q_ref, k_ref, v_ref, row_ref, col_ref, o_ref, bias_ref):
    @pl.when(pl.program_id(1) == 0)
    def _():
        bias_ref[...] = bias_of(where_ref[where_ref.shape[0] - 1], row_ref[...], col_ref[...])

    scores = mm_last(q_ref[0], k_ref[0]) * (SCALE * LOG2_E) + bias_ref[...]
    powers = jnp.exp2(scores - jnp.max(scores, axis=-1, keepdims=True))
    weights = powers * (1.0 / jnp.sum(powers, axis=-1, keepdims=True))
    o_ref[...] = to_low(mm(to_low(weights), v_ref[0]))


def attend(q, k, v, place, where, block=256):
    heads, n, hd = q.shape
    whole = pl.BlockSpec((1, n, hd), lambda b, t, w: (t, 0, 0))
    return pl.pallas_call(
        attend_kernel,
        out_shape=jax.ShapeDtypeStruct((n, heads * hd), BF16),
        grid_spec=pltpu.PrefetchScalarGridSpec(
            num_scalar_prefetch=1,
            grid=(n // block, heads),
            in_specs=[
                pl.BlockSpec((1, block, hd), lambda b, t, w: (t, b, 0)),
                whole,
                whole,
                pl.BlockSpec((block, 1), lambda b, t, w: (b, 0)),
                pl.BlockSpec((1, n), lambda b, t, w: (0, 0)),
            ],
            out_specs=pl.BlockSpec((block, hd), lambda b, t, w: (b, w[t])),
            scratch_shapes=[pltpu.VMEM((block, n), F32)],
        ),
        compiler_params=pltpu.CompilerParams(vmem_limit_bytes=VMEM),
        cost_estimate=pl.CostEstimate(
            flops=4 * heads * n * n * hd, bytes_accessed=8 * heads * n * hd, transcendentals=heads * n * n
        ),
        name="attend",
    )(where, q, k, v, place[:, None], place[None, :])


def attend_back_kernel(where_ref, q_ref, k_ref, v_ref, do_ref, row_ref, col_ref, dq_ref, dk_ref, dv_ref, bias_ref):
    b = pl.program_id(1)

    @pl.when(pl.program_id(0) == 0)
    def _():
        bias_ref[b] = bias_of(where_ref[where_ref.shape[0] - 1], row_ref[...], col_ref[...])

    q, k, v, do = q_ref[0], k_ref[0], v_ref[0], do_ref[...]
    scores = mm_last(k, q) * (SCALE * LOG2_E) + bias_ref[b]
    powers = jnp.exp2(scores - jnp.max(scores, axis=0, keepdims=True))
    probs = powers * (1.0 / jnp.sum(powers, axis=0, keepdims=True))
    grad_probs = mm_last(v, do)
    delta = jnp.sum(probs * grad_probs, axis=0, keepdims=True)
    grad_scores = to_low(probs * (grad_probs - delta))
    dq_ref[0] = mm_first(grad_scores, k) * SCALE
    dk = mm(grad_scores, q) * SCALE
    dv = mm(to_low(probs), do)

    @pl.when(b == 0)
    def _():
        dk_ref[0] = dk
        dv_ref[0] = dv

    @pl.when(b > 0)
    def _():
        dk_ref[0] += dk
        dv_ref[0] += dv


def attend_back(q, k, v, do, place, where, block=512):
    heads, n, hd = q.shape
    one = pl.BlockSpec((1, block, hd), lambda t, b, w: (t, b, 0))
    whole = pl.BlockSpec((1, n, hd), lambda t, b, w: (t, 0, 0))
    return pl.pallas_call(
        attend_back_kernel,
        out_shape=[jax.ShapeDtypeStruct((heads, n, hd), F32)] * 3,
        grid_spec=pltpu.PrefetchScalarGridSpec(
            num_scalar_prefetch=1,
            grid=(heads, n // block),
            in_specs=[
                one,
                whole,
                whole,
                pl.BlockSpec((block, hd), lambda t, b, w: (b, w[t])),
                pl.BlockSpec((1, block), lambda t, b, w: (0, b)),
                pl.BlockSpec((n, 1), lambda t, b, w: (0, 0)),
            ],
            out_specs=[one, whole, whole],
            scratch_shapes=[pltpu.VMEM((n // block, n, block), F32)],
        ),
        compiler_params=pltpu.CompilerParams(vmem_limit_bytes=32 << 20),
        cost_estimate=pl.CostEstimate(
            flops=10 * heads * n * n * hd, bytes_accessed=20 * heads * n * hd, transcendentals=heads * n * n
        ),
        name="attend_back",
    )(where, q, k, v, do, place[None, :], place[:, None])


def squares_kernel(heads, *refs):
    for i in (0, 1):
        part = slice(i * HEAD_DIM, (i + 1) * HEAD_DIM)
        total = sum(jnp.square(raw[:, part]) for raw in refs[:heads])
        refs[heads][i : i + 1, :] = jnp.sum(total.T, axis=0, keepdims=True)


def squares(raws, block=256):
    heads = len(raws)
    n = raws[0].shape[0]
    return pl.pallas_call(
        lambda *refs: squares_kernel(heads, *refs),
        out_shape=jax.ShapeDtypeStruct((2, n), F32),
        grid=(n // block,),
        in_specs=[pl.BlockSpec((block, 3 * HEAD_DIM), lambda b: (b, 0))] * heads,
        out_specs=pl.BlockSpec((2, block), lambda b: (0, b)),
        compiler_params=pltpu.CompilerParams(vmem_limit_bytes=VMEM),
        cost_estimate=pl.CostEstimate(flops=heads * n * 512, bytes_accessed=heads * n * 1536, transcendentals=0),
        name="squares",
    )(*raws)


def inner_products_kernel(dq_ref, q_ref, dk_ref, k_ref, out_ref):
    for i, (d_ref, v_ref) in enumerate(((dq_ref, q_ref), (dk_ref, k_ref))):
        total = sum(d_ref[t] * v_ref[t].astype(F32) for t in range(d_ref.shape[0]))
        out_ref[i : i + 1, :] = jnp.sum(total.T, axis=0, keepdims=True)


def inner_products(dq, q, dk, k, block=256):
    heads, n, hd = q.shape
    part = pl.BlockSpec((heads, block, hd), lambda b: (0, b, 0))
    return pl.pallas_call(
        inner_products_kernel,
        out_shape=jax.ShapeDtypeStruct((2, n), F32),
        grid=(n // block,),
        in_specs=[part] * 4,
        out_specs=pl.BlockSpec((2, block), lambda b: (0, b)),
        compiler_params=pltpu.CompilerParams(vmem_limit_bytes=WIDE_VMEM),
        cost_estimate=pl.CostEstimate(flops=heads * n * 512, bytes_accessed=heads * n * 1536, transcendentals=0),
        name="inner_products",
    )(dq, q, dk, k)


def turn_half(tensor):
    return pltpu.roll(tensor, HEAD_DIM // 2, 1)


def rope_kernel(heads, *refs):
    raws, (inv_ref, gain_ref, turn_ref, q_ref, k_ref, v_ref) = refs[:heads], refs[heads:]
    cosines, sines = turn_ref[:, :HEAD_DIM], turn_ref[:, HEAD_DIM:]
    for t in range(heads):
        for i, out in enumerate((q_ref, k_ref)):
            raw = raws[t][:, i * HEAD_DIM : (i + 1) * HEAD_DIM]
            value = raw * inv_ref[:, i : i + 1] * gain_ref[t, i : i + 1, :]
            out[t] = to_low(value * cosines + turn_half(value) * sines)
        v_ref[t] = to_low(raws[t][:, 2 * HEAD_DIM :])


def rope(raws, inv, gain, turn, block=256):
    heads = len(raws)
    n = raws[0].shape[0]
    rows = lambda width: pl.BlockSpec((block, width), lambda b: (b, 0))
    out = pl.BlockSpec((heads, block, HEAD_DIM), lambda b: (0, b, 0))
    return pl.pallas_call(
        lambda *refs: rope_kernel(heads, *refs),
        out_shape=[jax.ShapeDtypeStruct((heads, n, HEAD_DIM), BF16)] * 3,
        grid=(n // block,),
        in_specs=[rows(3 * HEAD_DIM)] * heads
        + [rows(2), pl.BlockSpec((heads, 2, HEAD_DIM), lambda b: (0, 0, 0)), rows(2 * HEAD_DIM)],
        out_specs=[out] * 3,
        compiler_params=pltpu.CompilerParams(vmem_limit_bytes=VMEM),
        cost_estimate=pl.CostEstimate(flops=heads * n * 2000, bytes_accessed=heads * n * 2304, transcendentals=0),
        name="rope",
    )(*raws, inv, gain, turn)


def rope_back_kernel(heads, *refs):
    raws, (dq_ref, dk_ref, dv_ref, inv_ref, mean_ref, gain_ref, turn_ref) = refs[:heads], refs[heads : heads + 7]
    outs, grad_ref = refs[heads + 7 : -1], refs[-1]

    @pl.when(pl.program_id(0) == 0)
    def _():
        grad_ref[...] = jnp.zeros_like(grad_ref)

    cosines, sines = turn_ref[:, :HEAD_DIM], turn_ref[:, HEAD_DIM:]
    for t in range(heads):
        for i, grad in enumerate((dq_ref, dk_ref)):
            part = slice(i * HEAD_DIM, (i + 1) * HEAD_DIM)
            inv = inv_ref[:, i : i + 1]
            hat = raws[t][:, part] * inv
            back = grad[t] * cosines - turn_half(grad[t]) * sines
            grad_ref[t, i : i + 1, :] += jnp.sum(back * hat, axis=0, keepdims=True)
            outs[t][:, part] = to_low(inv * (back * gain_ref[t, i : i + 1, :] - hat * mean_ref[:, i : i + 1]))
        outs[t][:, 2 * HEAD_DIM :] = to_low(dv_ref[t])


def rope_back(raws, dq, dk, dv, inv, mean, gain, turn, block=256):
    heads = len(raws)
    n = raws[0].shape[0]
    rows = lambda width: pl.BlockSpec((block, width), lambda b: (b, 0))
    grad = pl.BlockSpec((heads, block, HEAD_DIM), lambda b: (0, b, 0))
    gains = pl.BlockSpec((heads, 2, HEAD_DIM), lambda b: (0, 0, 0))
    out = pl.pallas_call(
        lambda *refs: rope_back_kernel(heads, *refs),
        out_shape=[jax.ShapeDtypeStruct((n, 3 * HEAD_DIM), BF16)] * heads
        + [jax.ShapeDtypeStruct((heads, 2, HEAD_DIM), F32)],
        grid=(n // block,),
        in_specs=[rows(3 * HEAD_DIM)] * heads + [grad] * 3 + [rows(2), rows(2), gains, rows(2 * HEAD_DIM)],
        out_specs=[rows(3 * HEAD_DIM)] * heads + [gains],
        compiler_params=pltpu.CompilerParams(vmem_limit_bytes=WIDE_VMEM),
        cost_estimate=pl.CostEstimate(flops=heads * n * 4000, bytes_accessed=heads * n * 3840, transcendentals=0),
        name="rope_back",
    )(*raws, dq, dk, dv, inv, mean, gain, turn)
    return out[:heads], out[heads]


def body(
    tokens,
    piece_start,
    positions,
    w_query,
    w_key,
    w_value,
    w_out,
    query_gain,
    key_gain,
    attn_gain,
    w_gate,
    w_up,
    w_down,
    mlp_gain,
    cotangent,
):
    S = lax.axis_size("shard")
    R = lax.axis_size("rep")
    s = lax.axis_index("shard")
    r = lax.axis_index("rep")
    _, span, width = tokens.shape
    heads = HEADS // S
    per = HEADS // R
    own_width = width // S
    x_own = tokens.reshape(span, width)

    by_ring = per * 2 == S
    chip, core = r // 2, r % 2

    def head_columns(j):
        start = j * HEAD_DIM
        return jnp.concatenate(
            [to_low(lax.dynamic_slice_in_dim(w, start, HEAD_DIM, 1)) for w in (w_query, w_key, w_value)], axis=1
        )

    def by_core(value):
        if not by_ring:
            return value
        middle = value.shape[1] // 2
        return jnp.where(core == 1, jnp.concatenate([value[:, middle:], value[:, :middle]], axis=1), value)

    own_columns = [head_columns((s + k) % per) for k in range(per)]
    got = [permute(value, heads_perm(S, R, per, k)) for k, value in enumerate(own_columns)]
    gains_own = jnp.stack([to_low(g).astype(F32) for g in (query_gain, key_gain, attn_gain, mlp_gain)])
    small = jnp.concatenate([positions.reshape(span).astype(F32), gains_own.reshape(-1)])
    small_all = [small] + [send_shard(small, k) for k in range(1, S)]
    own_out = spread_heads(after(to_low(w_out), *own_columns).reshape(heads, HEAD_DIM, -1), s)
    got, small_all, own_out = lax.optimization_barrier((got, small_all, own_out))

    got = reverse_pick(jnp.stack(got), s % per).reshape(per * own_width, 3 * HEAD_DIM)
    if by_ring:
        qkv_pairs = gather_pairs(got, R)
        qkv_w = [jnp.concatenate(pair) for pair in qkv_pairs]
        head_order = (chip - jnp.arange(heads)) % heads
        ring_start, ring_late, ring_end = qkv_pairs[1][0], qkv_pairs[-2][0], qkv_pairs[-1][0]
    else:
        qkv_w = list(lax.all_gather(got, "rep", axis=0, tiled=True).reshape(heads, width, 3 * HEAD_DIM))
        head_order = jnp.arange(heads)
        ring_start = ring_late = ring_end = qkv_w[-1]
    where = jnp.concatenate([head_order, piece_start]).astype(jnp.int32)
    x_all, x_first = gather_tokens(by_core(after(x_own, got)), (ring_start,), (ring_late,))
    gate_up = after(jnp.concatenate([to_low(w_gate), to_low(w_up)], axis=1), x_all)
    gate_up_w = lax.all_gather(gate_up, "shard", axis=0, tiled=True)
    pieces = spread_down(after(to_low(w_down), x_first), s)

    own_out = own_out.reshape(own_width, -1)
    columns = own_out.shape[1]
    out_w = jnp.zeros((own_width, width), BF16)
    for t, pair in enumerate(gather_pairs(after(own_out, ring_end), R)):
        for i, block in enumerate(pair):
            start = ((chip - t) % (R // 2) * 2 + (core ^ i)) * columns
            out_w = lax.dynamic_update_slice_in_dim(out_w, block, start, 1)
    down_blocks = cross_down([after(piece, out_w) for piece in pieces], s, r)

    gains = unrelative(jnp.stack([v[span:].reshape(4, own_width) for v in small_all]), s)
    gains = gains.transpose(1, 0, 2).reshape(4, width)
    head_gains = gains[:2].reshape(2, heads, S, HEAD_DIM)
    head_gains = lax.dynamic_index_in_dim(head_gains, s, 2, keepdims=False)
    head_gains = head_gains.transpose(1, 0, 2)
    if by_ring:
        head_gains = reverse_pick(head_gains, chip)
    again, mgain = gains[2], gains[3]
    order = token_order(S)
    step = S * span // len(order)
    place_pos = jnp.concatenate([small_all[j][h * step : (h + 1) * step] for h, j in order])
    place = jnp.concatenate([(s ^ j) * span + h * step + lax.iota(jnp.int32, step) for h, j in order])
    angles = place_pos[:, None] * frequencies()
    cosines, sines = jnp.cos(angles), jnp.sin(angles)
    turn = jnp.concatenate([cosines, cosines, -sines, sines], axis=1)

    raws = [mm(x_all, w) for w in qkv_w]
    inv = lax.rsqrt(sum_rows(squares(raws)) / width + epsilon).T
    q, k, v = rope(raws, inv, head_gains, turn)
    o = attend(q, k, v, place, where)
    rows = S * span // 2
    a_send = mm(o[rows:], out_w)
    a_keep = mm(o[:rows], out_w)
    down_blocks = [after(b, o) for b in down_blocks]
    a = scatter_tokens(a_keep, a_send, down_blocks)
    ainv = lax.rsqrt(jnp.mean(a * a, axis=-1, keepdims=True) + epsilon)
    ahat = a * ainv
    h = x_own.astype(F32) + ahat * again
    hb = to_low(h)

    down_w = lax.all_gather(join_down([after(b, hb) for b in down_blocks], r), "shard", axis=0, tiled=True)
    hb_pairs = [jnp.concatenate(pair) for pair in gather_pairs(hb, R)]
    kept = {}
    ff = w_gate.shape[1]

    def forward(t, hold):
        if t not in kept:
            pair = hb_pairs[t] if hold is None else after(hb_pairs[t], hold)
            gu = mm(pair, gate_up_w)
            g, u = gu[:, :ff], gu[:, ff:]
            inner = to_low(g * jax.nn.sigmoid(g) * u)
            kept[t] = (g, u, inner, mm(inner, down_w))
        return kept[t][3]

    forward(0, None)
    z = scatter_pairs(forward, R)
    zinv = lax.rsqrt(jnp.mean(z * z, axis=-1, keepdims=True) + epsilon)
    zhat = z * zinv
    output = to_low(h + zhat * mgain).reshape(tokens.shape)

    dy = cotangent.reshape(span, width).astype(F32)
    grad_mgain = jnp.sum(dy * zhat, axis=0)
    scaled = dy * mgain
    dz = to_low(zinv * (scaled - zhat * jnp.mean(scaled * zhat, axis=-1, keepdims=True)))
    dz_pairs = [jnp.concatenate(pair) for pair in gather_pairs(dz, R)]
    grads = {}

    def backward(t, hold):
        if t not in grads:
            pair = dz_pairs[t] if hold is None else after(dz_pairs[t], hold)
            g, u = kept[t][:2]
            dm = mm_last(pair, down_w)
            sig = jax.nn.sigmoid(g)
            dg = to_low(dm * u * sig * (1.0 + g * (1.0 - sig)))
            du = to_low(dm * g * sig)
            dgu = jnp.concatenate([dg, du], axis=1)
            grads[t] = (dgu, mm_last(dgu, gate_up_w))
        return grads[t][1]

    weight_grads = {}

    def weight_grad(i, _):
        steps = range(len(kept))
        if i == 0:
            all_inner = jnp.concatenate([kept[t][2] for t in steps])
            down_grad = to_low(mm_first(all_inner, jnp.concatenate(dz_pairs)))
            share = lax.psum_scatter(down_grad, "shard", scatter_dimension=0, tiled=True)
            weight_grads.update(down=down_grad, down_share=share)
            return (down_grad,)
        if i == len(kept) - 2:
            hb_all = jnp.concatenate(hb_pairs)
            weight_grads["gate_up"] = to_low(mm_first(hb_all, jnp.concatenate([grads[t][0] for t in steps])))
            return (weight_grads["gate_up"], weight_grads["down_share"])
        return ()

    backward(0, None)
    dh = dy + scatter_pairs(backward, R, weight_grad)
    grad_again = jnp.sum(dh * ahat, axis=0)
    scaled = dh * again
    da = to_low(ainv * (scaled - ahat * jnp.mean(scaled * ahat, axis=-1, keepdims=True)))
    down_back = return_cross(weight_grads["down_share"], r)
    da_all, _ = gather_tokens(da, down_back[: R // 2], down_back[R // 2 :])
    do = to_low(mm_last(da_all, out_w))
    gate_up_grad = after(weight_grads["gate_up"], da_all)
    gate_up_share = lax.psum_scatter(gate_up_grad, "shard", scatter_dimension=0, tiled=True).astype(F32)
    dq, dk, dv = attend_back(q, k, v, do, place, where)
    means = (sum_rows(inner_products(dq, q, dk, k)) / width).T
    dqkv, head_grads = rope_back(raws, dq, dk, dv, inv, means, head_gains, turn)
    if by_ring:
        head_grads = reverse_pick(head_grads, chip)
    down_back = return_spread(down_back, s, r)
    wide = jnp.stack([grad_again, grad_mgain]).reshape(2, S, own_width).transpose(1, 0, 2)
    wide = jnp.sum(exchange_shard(after(wide, dqkv[0]), s), axis=0)
    gain_sums = sum_rep(jnp.concatenate([head_grads.reshape(2, -1), wide], axis=1))
    out_grad = to_low(mm_first(o, after(da_all, *dqkv)))
    out_grad = after(out_grad, gate_up_share)

    late = {}

    def qkv_part(t, hold):
        return mm_first(x_all, dqkv[t] if hold is None else after(dqkv[t], hold))

    def input_grad(i, hold=None):
        if i < 2:
            part = slice(rows, None) if i == 0 else slice(rows)
            held = [d if hold is None else after(d, hold) for d in dqkv]
            late[i] = sum(mm_last(d[part], w) for d, w in zip(held, qkv_w))
            return (late[i], gain_sums) if i else (late[i], *down_back)
        return ()

    if by_ring:
        qkv_share = to_low(scatter_pairs(qkv_part, R, input_grad))
    else:
        parts = jnp.concatenate([qkv_part(t, None) for t in range(heads)])
        qkv_share = lax.psum_scatter(to_low(parts), "rep", scatter_dimension=0, tiled=True)
        input_grad(0), input_grad(1)
    dx = dh + by_core(scatter_tokens(late[1], late[0], (), (qkv_share,)))

    out_share = lax.psum_scatter(out_grad, "rep", scatter_dimension=1, tiled=True)
    grad_out = collect_heads(out_share.reshape(heads, HEAD_DIM, -1), s).reshape(w_out.shape).astype(F32)
    slots = qkv_share.reshape(per, own_width, 3 * HEAD_DIM)
    back = jnp.stack([permute(pick(slots, (s - k) % per), flip(heads_perm(S, R, per, k))) for k in range(per)])
    back = roll_pick(back, -(s % per)).reshape(per, own_width, 3, HEAD_DIM)
    back = back.transpose(2, 1, 0, 3).reshape(3, own_width, per * HEAD_DIM).astype(F32)

    grad_down = place_units(down_back, s).astype(F32)
    gain_sums = after(gain_sums, qkv_share)
    head_grads = collect_heads(gain_sums[:, : heads * HEAD_DIM].reshape(heads, 2, HEAD_DIM), s)
    head_grads = head_grads.transpose(1, 0, 2).reshape(2, own_width)
    gain_grads = jnp.concatenate([head_grads, gain_sums[:, heads * HEAD_DIM :]])

    return (
        output,
        dx.reshape(tokens.shape),
        back[0],
        back[1],
        back[2],
        grad_out,
        gain_grads[0],
        gain_grads[1],
        gain_grads[2],
        gate_up_share[:, :ff],
        gate_up_share[:, ff:],
        grad_down,
        gain_grads[3],
    )


def solution(mesh):
    grid = P("shard", "rep")
    rows = P("rep", "shard", None)
    gain = P("shard")
    in_specs = (rows, P("rep"), P("rep", "shard"), grid, grid, grid, grid, gain, gain, gain, grid, grid, grid, gain, rows)
    out_specs = (rows, rows, grid, grid, grid, grid, gain, gain, gain, grid, grid, grid, gain)
    return jax.shard_map(body, mesh=mesh, in_specs=in_specs, out_specs=out_specs, check_vma=False)
```

time: 1100 us -> 880 us (0.80)
  waiting for transfers between devices: 537 us -> 341 us
  starting transfers between devices: 148 us -> 89.1 us
  Pallas kernels: 0 us -> 57.5 us
  matrix products: 237 us -> 195 us
  local copies, waits for them, and re-layouts: 77.3 us -> 113 us
  other arithmetic: 75.5 us -> 53.8 us
    ppermute x28 -> x34, waiting for transfers between devices: 167 us -> 67.4 us  [send_shard(): return lax.ppermute(value, 'shard', [(s, s ^ k) for s in range(count)])]
    dot_general x10 -> x0, matrix products: 78.1 us -> none  [the longest x1 12.9 us: attend_back(): grad_probs = jnp.einsum('hqd,hkd->hqk', grad, v, preferred_element_type=F32)]
    all_gather x5 -> x2, waiting for transfers between devices: 70 us -> 0.02 us  [the longest x1 0.02 us: body(): gate_up_w = lax.all_gather(gate_up, 'shard', axis=0, tiled=True)]
    ppermute x8 -> x4, waiting for transfers between devices: 77.9 us -> 9.21 us  [permute(): return lax.ppermute(value, ('rep', 'shard'), pairs)]
    pallas_call x0 -> x6, Pallas kernels: none -> 57.5 us  [the longest x1 24.9 us: attend_back(): pl.pallas_call(attend_back_kernel, out_shape=[jax.ShapeDtypeStruct((heads...]
    ppermute x28 -> x34, starting transfers between devices: 75.7 us -> 33 us  [send_shard(): return lax.ppermute(value, 'shard', [(s, s ^ k) for s in range(count)])]
    ppermute x8 -> x4, starting transfers between devices: 48.4 us -> 8.3 us  [permute(): return lax.ppermute(value, ('rep', 'shard'), pairs)]
    dot_general x31 -> x38, matrix products: 158 us -> 195 us  [dot(): lax.dot_general(left, right, ((contract[0], contract[1]), ((), ())), pref...]
  transfers between devices with their start and end apart: 89 -> 125, of which waited for: 42 -> 48; matrix products, arithmetic and copies ran while one was open for 32% -> 34% of each run, Pallas kernels for 0% -> 7%
where the time goes in v2:
time: 880 us; the launch traced here: 868 us
  waiting for transfers between devices  341 us (39%)
  matrix products  195 us (22%)
  local copies, waits for them, and re-layouts  113 us (13%)
  starting transfers between devices  89.1 us (10%)
  Pallas kernels  57.5 us (7%)
  other arithmetic  53.8 us (6%)
  between operations  18 us (2%)
    ppermute x21, waiting for transfers between devices, ring(): lax.ppermute(value, 'rep', [(r, (r + 2) % count) for r in range(count)])  214 us
    dot_general x38, matrix products, dot(): lax.dot_general(left, right, ((contract[0], contract[1]), ((), ())), pref...  195 us
    unnamed x356, local copies, waits for them, and re-layouts  74 us
    ppermute x34, waiting for transfers between devices, send_shard(): return lax.ppermute(value, 'shard', [(s, s ^ k) for s in range(count)])  67.4 us
    ppermute x21, waiting for transfers between devices, flip_rep(): return lax.ppermute(value, 'rep', [(i, i ^ d) for i in range(count)])  34.8 us
    ppermute x34, starting transfers between devices, send_shard(): return lax.ppermute(value, 'shard', [(s, s ^ k) for s in range(count)])  33 us
    ppermute x21, starting transfers between devices, flip_rep(): return lax.ppermute(value, 'rep', [(i, i ^ d) for i in range(count)])  26.7 us
    pallas_call x1, Pallas kernels, attend_back(): pl.pallas_call(attend_back_kernel, out_shape=[jax.ShapeDtypeStruct((heads...  24.9 us
  transfers between devices with their start and end apart: 125, of which 48 were waited for; matrix products, arithmetic and copies ran while one was open for 34% of the time, Pallas kernels for 7%

profile of v2, /device:TPU:4, one launch (start us, length us, event | category | flops | bytes accessed | tf_op | source)
XLA Modules:
  0.0 867.7 jit_solution(1633363182634584814)
XLA Ops:
  43.3 12.7 %collective-permute-done.10 = bf16[1024,384]{1,0:T(8,128)(2,1)} collective-permute-done((bf16[1024,384]{1,0:T(8,128)(2,1)S(1)}, bf16[1024,384]{1,0:T(8,128)(2,1)}, u32[]{:S(2)}, u32[]{:S(2)}) %collective-permute-start.10) | collective-permute-done | bytes 786464 | tf_op jit(solution)/shard_map/ppermute | solution.py:148
  70.1 17.2 %collective-permute-done.13 = bf16[1024,384]{1,0:T(8,128)(2,1)} collective-permute-done((bf16[1024,384]{1,0:T(8,128)(2,1)}, bf16[1024,384]{1,0:T(8,128)(2,1)}, u32[]{:S(2)}, u32[]{:S(2)}) %collective-permute-start.13) | collective-permute-done | bytes 786464 | tf_op jit(solution)/shard_map/ppermute | solution.py:148
  95.4 4.7 fusion.104.refs_0_
  100.2 6.5 fusion.156.refs_1_
  110.7 4.5 fusion.157.refs_2_
  118.5 9.3 %collective-permute-done.26 = bf16[512,256]{1,0:T(8,128)(2,1)S(1)} collective-permute-done((bf16[512,256]{1,0:T(8,128)(2,1)S(1)}, bf16[512,256]{1,0:T(8,128)(2,1)S(1)}, u32[]{:S(2)}, u32[]{:S(2)}) %collective-permute-start.26) | collective-permute-done | bytes 262176 | tf_op jit(solution)/shard_map/ppermute | solution.py:148
  129.3 4.5 fusion.158.refs_3_
  152.0 3.8 rope.1
  155.8 15.2 %attend.1 = bf16[1024,512]{1,0:T(8,128)(2,1)S(1)} custom-call(s32[5]{0:T(128)S(1)} %pad_add_fusion.where_ref, bf16[4,1024,128]{2,1,0:T(8,128)(2,1)S(1)} %get-tuple-element.117.q_ref, bf16[4,1024,128]{2,1,0:T(8,128)(2,1)S(1)} %get-tuple-element.118.k_ref, bf16[4,1024,128]{2,1,0:T(8,128)(2,1)S(1)} %get-tuple-element.119.v_ref, s32[1024,1]{1,0:T(8,128)S(1)} %copy-done.15, ...), custom_call_target="tpu_custom_call" | custom-call | flops 2147483648 | bytes 4194304 | tf_op jit(solution)/shard_map/attend/pallas_call | solution.py:307
  180.9 5.3 collective-permute-done.40
  186.2 8.1 collective-permute-start.37
  195.1 3.9 collective-permute-done.38
  199.0 3.4 collective-permute-done.37
  203.8 3.2 collective-permute-done.35
  215.6 10.3 %collective-permute-done.43 = bf16[128,2048]{1,0:T(8,128)(2,1)S(1)} collective-permute-done((bf16[128,2048]{1,0:T(8,128)(2,1)S(1)}, bf16[128,2048]{1,0:T(8,128)(2,1)S(1)}, u32[]{:S(2)}, u32[]{:S(2)}) %collective-permute-start.43) | collective-permute-done | bytes 524320 | tf_op jit(solution)/shard_map/ppermute | solution.py:56
  234.5 23.9 %collective-permute-done.44 = bf16[256,2048]{1,0:T(8,128)(2,1)S(1)} collective-permute-done((bf16[256,2048]{1,0:T(8,128)(2,1)S(1)}, bf16[256,2048]{1,0:T(8,128)(2,1)S(1)}, u32[]{:S(2)}, u32[]{:S(2)}) %collective-permute-start.44) | collective-permute-done | bytes 1048608 | tf_op jit(solution)/shard_map/ppermute | solution.py:148
  258.7 24.3 %collective-permute-done.46 = bf16[256,2048]{1,0:T(8,128)(2,1)S(1)} collective-permute-done((bf16[256,2048]{1,0:T(8,128)(2,1)S(1)}, bf16[256,2048]{1,0:T(8,128)(2,1)S(1)}, u32[]{:S(2)}, u32[]{:S(2)}) %collective-permute-start.46) | collective-permute-done | bytes 1048608 | tf_op jit(solution)/shard_map/ppermute | solution.py:148
  283.2 7.5 fusion.51
  294.2 4.8 fusion.159
  300.7 5.8 collective-permute-done.50
  308.0 7.1 fusion.160
  321.0 13.7 %collective-permute-done.48 = bf16[256,2048]{1,0:T(8,128)(2,1)S(1)} collective-permute-done((bf16[256,2048]{1,0:T(8,128)(2,1)S(1)}, bf16[256,2048]{1,0:T(8,128)(2,1)S(1)}, u32[]{:S(2)}, u32[]{:S(2)}) %collective-permute-start.48) | collective-permute-done | bytes 1048608 | tf_op jit(solution)/shard_map/ppermute | solution.py:148
  335.6 4.6 fusion.162
  344.9 4.6 fusion.55
  354.5 6.8 collective-permute-done.52
  362.2 24.8 %collective-permute-done.55 = bf16[256,2048]{1,0:T(8,128)(2,1)S(1)} collective-permute-done((bf16[256,2048]{1,0:T(8,128)(2,1)S(1)}, bf16[256,2048]{1,0:T(8,128)(2,1)S(1)}, u32[]{:S(2)}, u32[]{:S(2)}) %collective-permute-start.55) | collective-permute-done | bytes 1048608 | tf_op jit(solution)/shard_map/ppermute | solution.py:148
  393.7 20.8 %collective-permute-done.58 = bf16[256,2048]{1,0:T(8,128)(2,1)} collective-permute-done((bf16[256,2048]{1,0:T(8,128)(2,1)}, bf16[256,2048]{1,0:T(8,128)(2,1)}, u32[]{:S(2)}, u32[]{:S(2)}) %collective-permute-start.58) | collective-permute-done | bytes 1048608 | tf_op jit(solution)/shard_map/ppermute | solution.py:148
  421.3 16.5 %collective-permute-done.60 = bf16[256,2048]{1,0:T(8,128)(2,1)S(1)} collective-permute-done((bf16[256,2048]{1,0:T(8,128)(2,1)}, bf16[256,2048]{1,0:T(8,128)(2,1)S(1)}, u32[]{:S(2)}, u32[]{:S(2)}) %collective-permute-start.60) | collective-permute-done | bytes 1048608 | tf_op jit(solution)/shard_map/ppermute | solution.py:148
  437.8 4.2 multiply_convert_fusion.8
  442.0 7.9 fusion.63
  450.6 5.4 multiply_convert_fusion.2
  461.6 15.9 %collective-permute-done.65 = bf16[256,2048]{1,0:T(8,128)(2,1)S(1)} collective-permute-done((bf16[256,2048]{1,0:T(8,128)(2,1)S(1)}, bf16[256,2048]{1,0:T(8,128)(2,1)S(1)}, u32[]{:S(2)}, u32[]{:S(2)}) %collective-permute-start.65) | collective-permute-done | bytes 1048608 | tf_op jit(solution)/shard_map/ppermute | solution.py:148
  481.0 3.0 multiply_convert_fusion.6
  484.0 10.2 %fusion.67 = f32[512,2048]{1,0:T(8,128)} fusion(bf16[2048,2048]{1,0:T(8,128)(2,1)} %all-gather.3.cloned.1.call-done, bf16[512,1024]{1,0:T(8,128)(2,1)S(1)} %get-tuple-element.259, bf16[512,1024]{1,0:T(8,128)(2,1)S(1)} %get-tuple-element.258), kind=kOutput, calls=%fused_computation.100 | convolution fusion | flops 4299161600 | bytes 14680064 | tf_op jit(solution)/shard_map/dot_general | solution.py:35
  499.6 10.7 %fusion.27 = bf16[1024,2048]{1,0:T(8,128)(2,1)} fusion(bf16[2048,2048]{1,0:T(8,128)(2,1)S(1)} %constant_dynamic-update-slice_fusion.38, bf16[512,1024]{1,0:T(8,128)(2,1)S(1)} %copy-done.76, bf16[512,1024]{1,0:T(8,128)(2,1)S(1)} %copy-done.74, bf16[512,1024]{1,0:T(8,128)(2,1)S(1)} %copy-done.72, bf16[512,1024]{1,0:T(8,128)(2,1)S(1)} %copy-done.78), kind=kOutput, calls=%fused_computation.27 | convolution fusion | flops 8608808960 | bytes 16777216 | tf_op jit(solution)/shard_map/dot_general | solution.py:35
  515.6 3.0 multiply_convert_fusion.4
  518.6 7.4 fusion.71
  527.7 7.2 fusion.79
  536.5 4.6 collective-permute-done.68
  542.7 34.5 %fusion.16 = bf16[2048,2048]{1,0:T(8,128)(2,1)} fusion(bf16[2048,2048]{1,0:T(8,128)(2,1)} %constant_dynamic-update-slice_fusion.46, bf16[512,1024]{1,0:T(8,128)(2,1)} %copy-done.129, bf16[512,1024]{1,0:T(8,128)(2,1)S(1)} %get-tuple-element.256, bf16[512,1024]{1,0:T(8,128)(2,1)S(1)} %copy-done.128, bf16[512,1024]{1,0:T(8,128)(2,1)S(1)} %copy-done.126, ...), kind=kOutput, calls=%fused_computation.16 | convolution fusion | flops 17251172352 | bytes 25165824 | tf_op jit(solution)/shard_map/dot_general | solution.py:35
  578.6 2.9 collective-permute-start.81
  585.3 4.0 multiply_reduce_fusion
  593.8 10.2 %collective-permute-done.74 = bf16[256,256]{1,0:T(8,128)(2,1)S(1)} collective-permute-done((bf16[256,256]{1,0:T(8,128)(2,1)S(1)}, bf16[256,256]{1,0:T(8,128)(2,1)S(1)}, u32[]{:S(2)}, u32[]{:S(2)}) %collective-permute-start.74) | collective-permute-done | bytes 131104 | tf_op jit(solution)/shard_map/ppermute | solution.py:197
  604.0 5.5 collective-permute-done.75
  615.0 15.1 %collective-permute-done.72 = bf16[128,2048]{1,0:T(8,128)(2,1)S(1)} collective-permute-done((bf16[128,2048]{1,0:T(8,128)(2,1)S(1)}, bf16[128,2048]{1,0:T(8,128)(2,1)S(1)}, u32[]{:S(2)}, u32[]{:S(2)}) %collective-permute-start.72) | collective-permute-done | bytes 524320 | tf_op jit(solution)/shard_map/ppermute | solution.py:56
  632.5 3.1 collective-permute-done.88
  635.8 21.2 %collective-permute-done.77 = bf16[256,2048]{1,0:T(8,128)(2,1)S(1)} collective-permute-done((bf16[256,2048]{1,0:T(8,128)(2,1)S(1)}, bf16[256,2048]{1,0:T(8,128)(2,1)S(1)}, u32[]{:S(2)}, u32[]{:S(2)}) %collective-permute-start.77) | collective-permute-done | bytes 1048608 | tf_op jit(solution)/shard_map/ppermute | solution.py:56
  659.1 3.3 convolution_convert_fusion.2.do_ref
  666.6 24.9 %attend_back.1 = (f32[4,1024,128]{2,1,0:T(8,128)S(1)}, f32[4,1024,128]{2,1,0:T(8,128)S(1)}, f32[4,1024,128]{2,1,0:T(8,128)S(1)}) custom-call(s32[5]{0:T(128)S(1)} %pad_add_fusion.where_ref, bf16[4,1024,128]{2,1,0:T(8,128)(2,1)S(1)} %copy-done.12, bf16[4,1024,128]{2,1,0:T(8,128)(2,1)S(1)} %copy-done.14, bf16[4,1024,128]{2,1,0:T(8,128)(2,1)S(1)} %copy-done.21, ...), custom_call_target="tpu_custom_call" | custom-call | flops 5368709120 | bytes 10485760 | tf_op jit(solution)/shard_map/attend_back/pallas_call | solution.py:364
  695.5 4.5 inner_products.1
  709.3 8.4 rope_back.1
  722.0 6.4 fusion.165
  730.2 3.9 collective-permute-start.104
  744.0 4.7 fusion.166
  753.6 2.8 fusion.114
  758.9 4.7 collective-permute-done.87
  764.4 4.6 fusion.167
  777.0 5.9 collective-permute-done.94
  784.6 4.6 fusion.168
  796.5 3.8 convolution_convert_fusion
  802.5 3.0 fusion.85
  805.5 3.4 collective-permute-done.109
  823.9 7.9 collective-permute-done.110
  839.0 11.2 %reduce-scatter.8.cloned.1.call-done = bf16[512,256]{1,0:T(8,128)(2,1)} async-done(((bf16[512,2048]{1,0:T(8,128)(2,1)}), bf16[512,256]{1,0:T(8,128)(2,1)}) %reduce-scatter.8.cloned.1.call-update) | async-done | bytes 262160 | tf_op jit(solution)/shard_map/reduce_scatter | solution.py:708
  (801 shorter events, 287.6 us)
Async XLA Ops:
  7.2 276.0 %all-gather.3.cloned.1.call-start = ((), (), s32[]{:S(2)}) async-start(), calls=%async_computation.3 | async-start | bytes 10485760 | tf_op jit(solution)/shard_map/all_gather | solution.py:568
  9.9 22.5 %collective-permute-start = (bf16[512,384]{1,0:T(8,128)(2,1)S(1)}, bf16[512,384]{1,0:T(8,128)(2,1)}, u32[]{:S(2)}, u32[]{:S(2)}) collective-permute-start(bf16[512,384]{1,0:T(8,128)(2,1)S(1)} %pad_maximum_fusion.17), channel_id=1, source_target_pairs={{0,0},{1,1},{2,4},{3,5},{4,2},{5,3},{6,6},{7,7},{8,8},{9,9},{10,12... | collective-permute-start | bytes 1179656 | tf_op jit(solution)/shard_map/ppermute | solution.py:262
  12.7 19.8 %collective-permute-start.1 = (bf16[512,384]{1,0:T(8,128)(2,1)}, bf16[512,384]{1,0:T(8,128)(2,1)}, u32[]{:S(2)}, u32[]{:S(2)}) collective-permute-start(bf16[512,384]{1,0:T(8,128)(2,1)} %pad_maximum_fusion.18), channel_id=1, source_target_pairs={{0,1},{1,0},{2,5},{3,4},{4,3},{5,2},{6,7},{7,6},{8,9},{9,8},{10,13... | collective-permute-start | bytes 1179656 | tf_op jit(solution)/shard_map/ppermute | solution.py:262
  34.2 21.9 %collective-permute-start.10 = (bf16[1024,384]{1,0:T(8,128)(2,1)S(1)}, bf16[1024,384]{1,0:T(8,128)(2,1)}, u32[]{:S(2)}, u32[]{:S(2)}) collective-permute-start(bf16[1024,384]{1,0:T(8,128)(2,1)S(1)} %bitcast.254), channel_id=1, source_target_pairs={{0,8},{4,12},{8,16},{12,20},{16,24},{20,28},{24,0},{28,4},{1,9},{5... | collective-permute-start | bytes 2359304 | tf_op jit(solution)/shard_map/ppermute | solution.py:148
  38.7 17.4 %collective-permute-start.11 = (bf16[128,2048]{1,0:T(8,128)(2,1)}, bf16[128,2048]{1,0:T(8,128)(2,1)}, u32[]{:S(2)}, u32[]{:S(2)}) collective-permute-start(bf16[128,2048]{1,0:T(8,128)(2,1)} %get-tuple-element.306), channel_id=1, source_target_pairs={{0,1},{1,0},{2,3},{3,2},{4,5},{5,4},{6,7},{7,6},{8,9},{9,8},{10,11... | collective-permute-start | bytes 1572872 | tf_op jit(solution)/shard_map/ppermute | solution.py:56
  38.7 18.7 %collective-permute-start.9 = (bf16[128,2048]{1,0:T(8,128)(2,1)}, bf16[128,2048]{1,0:T(8,128)(2,1)}, u32[]{:S(2)}, u32[]{:S(2)}) collective-permute-start(bf16[128,2048]{1,0:T(8,128)(2,1)} %get-tuple-element.308), channel_id=1, source_target_pairs={{0,2},{1,3},{2,0},{3,1},{4,6},{5,7},{6,4},{7,5},{8,10},{9,11},{10,... | collective-permute-start | bytes 1572872 | tf_op jit(solution)/shard_map/ppermute | solution.py:56
  61.7 115.3 %collective-permute-start.33 = (bf16[2,256,256]{2,1,0:T(8,128)(2,1)}, bf16[2,256,256]{2,1,0:T(8,128)(2,1)}, u32[]{:S(2)}, u32[]{:S(2)}) collective-permute-start(bf16[2,256,256]{2,1,0:T(8,128)(2,1)} %get-tuple-element.302), channel_id=1, source_target_pairs={{0,3},{1,2},{2,1},{3,0},{4,7},{5,6},{6,5},{7,4},{8,11},{9,10},{10,... | collective-permute-start | bytes 786440 | tf_op jit(solution)/shard_map/ppermute | solution.py:56
  62.3 29.9 %collective-permute-start.12 = (bf16[256,2048]{1,0:T(8,128)(2,1)S(1)}, bf16[256,2048]{1,0:T(8,128)(2,1)S(1)}, u32[]{:S(2)}, u32[]{:S(2)}) collective-permute-start(bf16[256,2048]{1,0:T(8,128)(2,1)S(1)} %pad_maximum_fusion.8), channel_id=1, source_target_pairs={{0,1},{1,0},{2,3},{3,2},{4,5},{5,4},{6,7},{7,6},{8,9},{9,8},{10,11... | collective-permute-start | bytes 3145736 | tf_op jit(solution)/shard_map/ppermute | solution.py:56
  63.6 29.6 %collective-permute-start.14 = (bf16[256,2048]{1,0:T(8,128)(2,1)S(1)}, bf16[256,2048]{1,0:T(8,128)(2,1)S(1)}, u32[]{:S(2)}, u32[]{:S(2)}) collective-permute-start(bf16[256,2048]{1,0:T(8,128)(2,1)S(1)} %pad_maximum_fusion.9), channel_id=1, source_target_pairs={{0,2},{1,3},{2,0},{3,1},{4,6},{5,7},{6,4},{7,5},{8,10},{9,11},{10,... | collective-permute-start | bytes 3145736 | tf_op jit(solution)/shard_map/ppermute | solution.py:56
  65.2 22.1 %collective-permute-start.13 = (bf16[1024,384]{1,0:T(8,128)(2,1)}, bf16[1024,384]{1,0:T(8,128)(2,1)}, u32[]{:S(2)}, u32[]{:S(2)}) collective-permute-start(bf16[1024,384]{1,0:T(8,128)(2,1)} %collective-permute-done.10), channel_id=1, source_target_pairs={{0,8},{4,12},{8,16},{12,20},{16,24},{20,28},{24,0},{28,4},{1,9},{5... | collective-permute-start | bytes 2359304 | tf_op jit(solution)/shard_map/ppermute | solution.py:148
  87.2 21.3 %collective-permute-start.18 = (bf16[1024,384]{1,0:T(8,128)(2,1)}, bf16[1024,384]{1,0:T(8,128)(2,1)}, u32[]{:S(2)}, u32[]{:S(2)}) collective-permute-start(bf16[1024,384]{1,0:T(8,128)(2,1)} %collective-permute-done.13), channel_id=1, source_target_pairs={{0,8},{4,12},{8,16},{12,20},{16,24},{20,28},{24,0},{28,4},{1,9},{5... | collective-permute-start | bytes 2359304 | tf_op jit(solution)/shard_map/ppermute | solution.py:148
  87.2 21.5 %collective-permute-start.17 = (bf16[1024,384]{1,0:T(8,128)(2,1)}, bf16[1024,384]{1,0:T(8,128)(2,1)}, u32[]{:S(2)}, u32[]{:S(2)}) collective-permute-start(bf16[1024,384]{1,0:T(8,128)(2,1)} %collective-permute-done.13), channel_id=1, source_target_pairs={{0,4},{4,0},{8,12},{12,8},{16,20},{20,16},{24,28},{28,24},{1,5},{5... | collective-permute-start | bytes 2359304 | tf_op jit(solution)/shard_map/ppermute | solution.py:152
  95.4 198.8 %all-gather.5.cloned.1.call-start = ((), (), s32[]{:S(2)}) async-start(), calls=%async_computation.4 | async-start | bytes 5242880 | tf_op jit(solution)/shard_map/all_gather | solution.py:610
  110.1 17.8 %collective-permute-start.19 = (bf16[1024,384]{1,0:T(8,128)(2,1)}, bf16[1024,384]{1,0:T(8,128)(2,1)S(1)}, u32[]{:S(2)}, u32[]{:S(2)}) collective-permute-start(bf16[1024,384]{1,0:T(8,128)(2,1)} %collective-permute-done.18), channel_id=1, source_target_pairs={{0,4},{4,0},{8,12},{12,8},{16,20},{20,16},{24,28},{28,24},{1,5},{5... | collective-permute-start | bytes 2359304 | tf_op jit(solution)/shard_map/ppermute | solution.py:152
  117.9 59.1 %collective-permute-start.32 = (bf16[2,256,256]{2,1,0:T(8,128)(2,1)S(1)}, bf16[2,256,256]{2,1,0:T(8,128)(2,1)}, u32[]{:S(2)}, u32[]{:S(2)}) collective-permute-start(bf16[2,256,256]{2,1,0:T(8,128)(2,1)S(1)} %copy-done.93), channel_id=1, source_target_pairs={{0,2},{1,3},{2,0},{3,1},{4,6},{5,7},{6,4},{7,5},{8,10},{9,11},{10,... | collective-permute-start | bytes 786440 | tf_op jit(solution)/shard_map/ppermute | solution.py:56
  127.8 46.0 %collective-permute-start.31 = (bf16[2,256,256]{2,1,0:T(8,128)(2,1)}, bf16[2,256,256]{2,1,0:T(8,128)(2,1)}, u32[]{:S(2)}, u32[]{:S(2)}) collective-permute-start(bf16[2,256,256]{2,1,0:T(8,128)(2,1)} %get-tuple-element.304), channel_id=1, source_target_pairs={{0,1},{1,0},{2,3},{3,2},{4,5},{5,4},{6,7},{7,6},{8,9},{9,8},{10,11... | collective-permute-start | bytes 786440 | tf_op jit(solution)/shard_map/ppermute | solution.py:56
  143.8 27.3 %collective-permute-start.29 = (bf16[512,256]{1,0:T(8,128)(2,1)}, bf16[512,256]{1,0:T(8,128)(2,1)}, u32[]{:S(2)}, u32[]{:S(2)}) collective-permute-start(bf16[512,256]{1,0:T(8,128)(2,1)} %collective-permute-done.28), channel_id=1, source_target_pairs={{0,4},{4,0},{8,12},{12,8},{16,20},{20,16},{24,28},{28,24},{1,5},{5... | collective-permute-start | bytes 786440 | tf_op jit(solution)/shard_map/ppermute | solution.py:152
  173.8 35.6 %collective-permute-start.30 = (bf16[256,2048]{1,0:T(8,128)(2,1)S(1)}, bf16[256,2048]{1,0:T(8,128)(2,1)S(1)}, u32[]{:S(2)}, u32[]{:S(2)}) collective-permute-start(bf16[256,2048]{1,0:T(8,128)(2,1)S(1)} %get-tuple-element.276), channel_id=1, source_target_pairs={{0,1},{1,0},{2,3},{3,2},{4,5},{5,4},{6,7},{7,6},{8,9},{9,8},{10,11... | collective-permute-start | bytes 3145736 | tf_op jit(solution)/shard_map/ppermute | solution.py:56
  175.6 33.8 %collective-permute-start.42 = (bf16[256,2048]{1,0:T(8,128)(2,1)S(1)}, bf16[256,2048]{1,0:T(8,128)(2,1)S(1)}, u32[]{:S(2)}, u32[]{:S(2)}) collective-permute-start(bf16[256,2048]{1,0:T(8,128)(2,1)S(1)} %get-tuple-element.277), channel_id=1, source_target_pairs={{0,2},{1,3},{2,0},{3,1},{4,6},{5,7},{6,4},{7,5},{8,10},{9,11},{10,... | collective-permute-start | bytes 3145736 | tf_op jit(solution)/shard_map/ppermute | solution.py:56
  179.2 15.2 %collective-permute-start.39 = (bf16[256,256]{1,0:T(8,128)(2,1)S(1)}, bf16[256,256]{1,0:T(8,128)(2,1)S(1)}, u32[]{:S(2)}, u32[]{:S(2)}) collective-permute-start(bf16[256,256]{1,0:T(8,128)(2,1)S(1)} %get-tuple-element.295), channel_id=1, source_target_pairs={{0,24},{4,28},{8,16},{12,20},{16,8},{20,12},{24,0},{28,4},{1,25},{... | collective-permute-start | bytes 393224 | tf_op jit(solution)/shard_map/ppermute | solution.py:197
  180.9 18.1 %collective-permute-start.38 = (bf16[256,256]{1,0:T(8,128)(2,1)S(1)}, bf16[256,256]{1,0:T(8,128)(2,1)S(1)}, u32[]{:S(2)}, u32[]{:S(2)}) collective-permute-start(bf16[256,256]{1,0:T(8,128)(2,1)S(1)} %get-tuple-element.296), channel_id=1, source_target_pairs={{0,20},{4,16},{8,28},{12,24},{16,4},{20,0},{24,12},{28,8},{1,21},{... | collective-permute-start | bytes 393224 | tf_op jit(solution)/shard_map/ppermute | solution.py:197
  186.2 16.2 %collective-permute-start.37 = (bf16[256,256]{1,0:T(8,128)(2,1)S(1)}, bf16[256,256]{1,0:T(8,128)(2,1)S(1)}, u32[]{:S(2)}, u32[]{:S(2)}) collective-permute-start(bf16[256,256]{1,0:T(8,128)(2,1)S(1)} %get-tuple-element.297), channel_id=1, source_target_pairs={{0,16},{4,20},{8,24},{12,28},{16,0},{20,4},{24,8},{28,12},{1,17},{... | collective-permute-start | bytes 393224 | tf_op jit(solution)/shard_map/ppermute | solution.py:197
  233.0 344.2 %reduce-scatter.4.cloned.1.call-start = ((), (), s32[]{:S(2)}) async-start(), calls=%async_computation.5 | async-start | bytes 5242880 | tf_op jit(solution)/shard_map/reduce_scatter | solution.py:656
  233.1 25.4 %collective-permute-start.44 = (bf16[256,2048]{1,0:T(8,128)(2,1)S(1)}, bf16[256,2048]{1,0:T(8,128)(2,1)S(1)}, u32[]{:S(2)}, u32[]{:S(2)}) collective-permute-start(bf16[256,2048]{1,0:T(8,128)(2,1)S(1)} %get-tuple-element.251), channel_id=1, source_target_pairs={{0,8},{4,12},{8,16},{12,20},{16,24},{20,28},{24,0},{28,4},{1,9},{5... | collective-permute-start | bytes 3145736 | tf_op jit(solution)/shard_map/ppermute | solution.py:148
  258.4 24.6 %collective-permute-start.46 = (bf16[256,2048]{1,0:T(8,128)(2,1)S(1)}, bf16[256,2048]{1,0:T(8,128)(2,1)S(1)}, u32[]{:S(2)}, u32[]{:S(2)}) collective-permute-start(bf16[256,2048]{1,0:T(8,128)(2,1)S(1)} %collective-permute-done.44), channel_id=1, source_target_pairs={{0,8},{4,12},{8,16},{12,20},{16,24},{20,28},{24,0},{28,4},{1,9},{5... | collective-permute-start | bytes 3145736 | tf_op jit(solution)/shard_map/ppermute | solution.py:148
  258.6 24.4 %collective-permute-start.45 = (bf16[256,2048]{1,0:T(8,128)(2,1)S(1)}, bf16[256,2048]{1,0:T(8,128)(2,1)}, u32[]{:S(2)}, u32[]{:S(2)}) collective-permute-start(bf16[256,2048]{1,0:T(8,128)(2,1)S(1)} %collective-permute-done.44), channel_id=1, source_target_pairs={{0,4},{4,0},{8,12},{12,8},{16,20},{20,16},{24,28},{28,24},{1,5},{5... | collective-permute-start | bytes 3145736 | tf_op jit(solution)/shard_map/ppermute | solution.py:152
  283.0 23.5 %collective-permute-start.50 = (bf16[256,2048]{1,0:T(8,128)(2,1)S(1)}, bf16[256,2048]{1,0:T(8,128)(2,1)S(1)}, u32[]{:S(2)}, u32[]{:S(2)}) collective-permute-start(bf16[256,2048]{1,0:T(8,128)(2,1)S(1)} %collective-permute-done.46), channel_id=1, source_target_pairs={{0,8},{4,12},{8,16},{12,20},{16,24},{20,28},{24,0},{28,4},{1,9},{5... | collective-permute-start | bytes 3145736 | tf_op jit(solution)/shard_map/ppermute | solution.py:148
  283.1 23.5 %collective-permute-start.49 = (bf16[256,2048]{1,0:T(8,128)(2,1)S(1)}, bf16[256,2048]{1,0:T(8,128)(2,1)S(1)}, u32[]{:S(2)}, u32[]{:S(2)}) collective-permute-start(bf16[256,2048]{1,0:T(8,128)(2,1)S(1)} %collective-permute-done.46), channel_id=1, source_target_pairs={{0,4},{4,0},{8,12},{12,8},{16,20},{20,16},{24,28},{28,24},{1,5},{5... | collective-permute-start | bytes 3145736 | tf_op jit(solution)/shard_map/ppermute | solution.py:152
  300.3 19.6 %collective-permute-start.56 = (bf16[256,2048]{1,0:T(8,128)(2,1)S(1)}, bf16[256,2048]{1,0:T(8,128)(2,1)S(1)}, u32[]{:S(2)}, u32[]{:S(2)}) collective-permute-start(bf16[256,2048]{1,0:T(8,128)(2,1)S(1)} %copy-done.85), channel_id=1, source_target_pairs={{0,4},{4,0},{8,12},{12,8},{16,20},{20,16},{24,28},{28,24},{1,5},{5... | collective-permute-start | bytes 3145736 | tf_op jit(solution)/shard_map/ppermute | solution.py:152
  307.9 26.7 %collective-permute-start.48 = (bf16[256,2048]{1,0:T(8,128)(2,1)S(1)}, bf16[256,2048]{1,0:T(8,128)(2,1)S(1)}, u32[]{:S(2)}, u32[]{:S(2)}) collective-permute-start(bf16[256,2048]{1,0:T(8,128)(2,1)S(1)} %fusion.50), channel_id=1, source_target_pairs={{0,8},{4,12},{8,16},{12,20},{16,24},{20,28},{24,0},{28,4},{1,9},{5... | collective-permute-start | bytes 3145736 | tf_op jit(solution)/shard_map/ppermute | solution.py:148
  335.1 26.2 %collective-permute-start.52 = (bf16[256,2048]{1,0:T(8,128)(2,1)S(1)}, bf16[256,2048]{1,0:T(8,128)(2,1)S(1)}, u32[]{:S(2)}, u32[]{:S(2)}) collective-permute-start(bf16[256,2048]{1,0:T(8,128)(2,1)S(1)} %fusion.49), channel_id=1, source_target_pairs={{0,8},{4,12},{8,16},{12,20},{16,24},{20,28},{24,0},{28,4},{1,9},{5... | collective-permute-start | bytes 3145736 | tf_op jit(solution)/shard_map/ppermute | solution.py:148
  344.8 16.6 %collective-permute-start.54 = (bf16[256,2048]{1,0:T(8,128)(2,1)S(1)}, bf16[256,2048]{1,0:T(8,128)(2,1)S(1)}, u32[]{:S(2)}, u32[]{:S(2)}) collective-permute-start(bf16[256,2048]{1,0:T(8,128)(2,1)S(1)} %slice.912), channel_id=1, source_target_pairs={{0,4},{4,0},{8,12},{12,8},{16,20},{20,16},{24,28},{28,24},{1,5},{5... | collective-permute-start | bytes 3145736 | tf_op jit(solution)/shard_map/ppermute | solution.py:152
  361.9 25.1 %collective-permute-start.55 = (bf16[256,2048]{1,0:T(8,128)(2,1)S(1)}, bf16[256,2048]{1,0:T(8,128)(2,1)S(1)}, u32[]{:S(2)}, u32[]{:S(2)}) collective-permute-start(bf16[256,2048]{1,0:T(8,128)(2,1)S(1)} %fusion.47), channel_id=1, source_target_pairs={{0,8},{4,12},{8,16},{12,20},{16,24},{20,28},{24,0},{28,4},{1,9},{5... | collective-permute-start | bytes 3145736 | tf_op jit(solution)/shard_map/ppermute | solution.py:148
  390.3 24.3 %collective-permute-start.58 = (bf16[256,2048]{1,0:T(8,128)(2,1)}, bf16[256,2048]{1,0:T(8,128)(2,1)}, u32[]{:S(2)}, u32[]{:S(2)}) collective-permute-start(bf16[256,2048]{1,0:T(8,128)(2,1)} %get-tuple-element.253), channel_id=1, source_target_pairs={{0,8},{4,12},{8,16},{12,20},{16,24},{20,28},{24,0},{28,4},{1,9},{5... | collective-permute-start | bytes 3145736 | tf_op jit(solution)/shard_map/ppermute | solution.py:148
  393.7 27.6 %collective-permute-start.63 = (bf16[256,2048]{1,0:T(8,128)(2,1)}, bf16[256,2048]{1,0:T(8,128)(2,1)S(1)}, u32[]{:S(2)}, u32[]{:S(2)}) collective-permute-start(bf16[256,2048]{1,0:T(8,128)(2,1)} %get-tuple-element.253), channel_id=1, source_target_pairs={{0,4},{4,0},{8,12},{12,8},{16,20},{20,16},{24,28},{28,24},{1,5},{5... | collective-permute-start | bytes 3145736 | tf_op jit(solution)/shard_map/ppermute | solution.py:152
  414.5 23.2 %collective-permute-start.60 = (bf16[256,2048]{1,0:T(8,128)(2,1)}, bf16[256,2048]{1,0:T(8,128)(2,1)S(1)}, u32[]{:S(2)}, u32[]{:S(2)}) collective-permute-start(bf16[256,2048]{1,0:T(8,128)(2,1)} %collective-permute-done.58), channel_id=1, source_target_pairs={{0,8},{4,12},{8,16},{12,20},{16,24},{20,28},{24,0},{28,4},{1,9},{5... | collective-permute-start | bytes 3145736 | tf_op jit(solution)/shard_map/ppermute | solution.py:148
  414.5 23.2 %collective-permute-start.59 = (bf16[256,2048]{1,0:T(8,128)(2,1)}, bf16[256,2048]{1,0:T(8,128)(2,1)S(1)}, u32[]{:S(2)}, u32[]{:S(2)}) collective-permute-start(bf16[256,2048]{1,0:T(8,128)(2,1)} %collective-permute-done.58), channel_id=1, source_target_pairs={{0,4},{4,0},{8,12},{12,8},{16,20},{20,16},{24,28},{28,24},{1,5},{5... | collective-permute-start | bytes 3145736 | tf_op jit(solution)/shard_map/ppermute | solution.py:152
  450.1 27.4 %collective-permute-start.61 = (bf16[256,2048]{1,0:T(8,128)(2,1)S(1)}, bf16[256,2048]{1,0:T(8,128)(2,1)S(1)}, u32[]{:S(2)}, u32[]{:S(2)}) collective-permute-start(bf16[256,2048]{1,0:T(8,128)(2,1)S(1)} %slice.910), channel_id=1, source_target_pairs={{0,4},{4,0},{8,12},{12,8},{16,20},{20,16},{24,28},{28,24},{1,5},{5... | collective-permute-start | bytes 3145736 | tf_op jit(solution)/shard_map/ppermute | solution.py:152
  450.1 27.4 %collective-permute-start.65 = (bf16[256,2048]{1,0:T(8,128)(2,1)S(1)}, bf16[256,2048]{1,0:T(8,128)(2,1)S(1)}, u32[]{:S(2)}, u32[]{:S(2)}) collective-permute-start(bf16[256,2048]{1,0:T(8,128)(2,1)S(1)} %collective-permute-done.60), channel_id=1, source_target_pairs={{0,8},{4,12},{8,16},{12,20},{16,24},{20,28},{24,0},{28,4},{1,9},{5... | collective-permute-start | bytes 3145736 | tf_op jit(solution)/shard_map/ppermute | solution.py:148
  450.2 27.3 %collective-permute-start.64 = (bf16[256,2048]{1,0:T(8,128)(2,1)S(1)}, bf16[256,2048]{1,0:T(8,128)(2,1)S(1)}, u32[]{:S(2)}, u32[]{:S(2)}) collective-permute-start(bf16[256,2048]{1,0:T(8,128)(2,1)S(1)} %collective-permute-done.60), channel_id=1, source_target_pairs={{0,4},{4,0},{8,12},{12,8},{16,20},{20,16},{24,28},{28,24},{1,5},{5... | collective-permute-start | bytes 3145736 | tf_op jit(solution)/shard_map/ppermute | solution.py:152
  478.8 31.6 %collective-permute-start.62 = (bf16[256,2048]{1,0:T(8,128)(2,1)}, bf16[256,2048]{1,0:T(8,128)(2,1)}, u32[]{:S(2)}, u32[]{:S(2)}) collective-permute-start(bf16[256,2048]{1,0:T(8,128)(2,1)} %fusion.44), channel_id=1, source_target_pairs={{0,8},{4,12},{8,16},{12,20},{16,24},{20,28},{24,0},{28,4},{1,9},{5... | collective-permute-start | bytes 3145736 | tf_op jit(solution)/shard_map/ppermute | solution.py:148
  479.2 17.9 %collective-permute-start.66 = (bf16[256,2048]{1,0:T(8,128)(2,1)S(1)}, bf16[256,2048]{1,0:T(8,128)(2,1)S(1)}, u32[]{:S(2)}, u32[]{:S(2)}) collective-permute-start(bf16[256,2048]{1,0:T(8,128)(2,1)S(1)} %collective-permute-done.65), channel_id=1, source_target_pairs={{0,4},{4,0},{8,12},{12,8},{16,20},{20,16},{24,28},{28,24},{1,5},{5... | collective-permute-start | bytes 3145736 | tf_op jit(solution)/shard_map/ppermute | solution.py:152
  510.3 303.9 %reduce-scatter.6.cloned.1.call-start = ((), (), s32[]{:S(2)}) async-start(), calls=%async_computation.6 | async-start | bytes 10485760 | tf_op jit(solution)/shard_map/reduce_scatter | solution.py:674
  513.2 27.8 %collective-permute-start.68 = (bf16[256,2048]{1,0:T(8,128)(2,1)S(1)}, bf16[256,2048]{1,0:T(8,128)(2,1)S(1)}, u32[]{:S(2)}, u32[]{:S(2)}) collective-permute-start(bf16[256,2048]{1,0:T(8,128)(2,1)S(1)} %fusion.43), channel_id=1, source_target_pairs={{0,8},{4,12},{8,16},{12,20},{16,24},{20,28},{24,0},{28,4},{1,9},{5... | collective-permute-start | bytes 3145736 | tf_op jit(solution)/shard_map/ppermute | solution.py:148
  536.1 49.1 %collective-permute-start.71 = (bf16[256,2048]{1,0:T(8,128)(2,1)}, bf16[256,2048]{1,0:T(8,128)(2,1)}, u32[]{:S(2)}, u32[]{:S(2)}) collective-permute-start(bf16[256,2048]{1,0:T(8,128)(2,1)} %slice.907), channel_id=1, source_target_pairs={{0,4},{4,0},{8,12},{12,8},{16,20},{20,16},{24,28},{28,24},{1,5},{5... | collective-permute-start | bytes 3145736 | tf_op jit(solution)/shard_map/ppermute | solution.py:152
  542.5 40.1 %collective-permute-start.70 = (bf16[256,2048]{1,0:T(8,128)(2,1)}, bf16[256,2048]{1,0:T(8,128)(2,1)}, u32[]{:S(2)}, u32[]{:S(2)}) collective-permute-start(bf16[256,2048]{1,0:T(8,128)(2,1)} %fusion.41), channel_id=1, source_target_pairs={{0,8},{4,12},{8,16},{12,20},{16,24},{20,28},{24,0},{28,4},{1,9},{5... | collective-permute-start | bytes 3145736 | tf_op jit(solution)/shard_map/ppermute | solution.py:148
  578.6 31.9 %collective-permute-start.81 = (bf16[256,256]{1,0:T(8,128)(2,1)S(1)}, bf16[256,256]{1,0:T(8,128)(2,1)S(1)}, u32[]{:S(2)}, u32[]{:S(2)}) collective-permute-start(bf16[256,256]{1,0:T(8,128)(2,1)S(1)} %get-tuple-element.284), channel_id=1, source_target_pairs={{0,28},{4,24},{8,20},{12,16},{16,12},{20,8},{24,4},{28,0},{1,29},{... | collective-permute-start | bytes 393224 | tf_op jit(solution)/shard_map/ppermute | solution.py:197
  581.5 29.0 %collective-permute-start.80 = (bf16[256,256]{1,0:T(8,128)(2,1)S(1)}, bf16[256,256]{1,0:T(8,128)(2,1)S(1)}, u32[]{:S(2)}, u32[]{:S(2)}) collective-permute-start(bf16[256,256]{1,0:T(8,128)(2,1)S(1)} %get-tuple-element.285), channel_id=1, source_target_pairs={{0,24},{4,28},{8,16},{12,20},{16,8},{20,12},{24,0},{28,4},{1,25},{... | collective-permute-start | bytes 393224 | tf_op jit(solution)/shard_map/ppermute | solution.py:197
  582.6 28.0 %collective-permute-start.79 = (bf16[256,256]{1,0:T(8,128)(2,1)S(1)}, bf16[256,256]{1,0:T(8,128)(2,1)S(1)}, u32[]{:S(2)}, u32[]{:S(2)}) collective-permute-start(bf16[256,256]{1,0:T(8,128)(2,1)S(1)} %get-tuple-element.286), channel_id=1, source_target_pairs={{0,20},{4,16},{8,28},{12,24},{16,4},{20,0},{24,12},{28,8},{1,21},{... | collective-permute-start | bytes 393224 | tf_op jit(solution)/shard_map/ppermute | solution.py:197
  582.6 27.0 %collective-permute-start.78 = (bf16[256,256]{1,0:T(8,128)(2,1)S(1)}, bf16[256,256]{1,0:T(8,128)(2,1)S(1)}, u32[]{:S(2)}, u32[]{:S(2)}) collective-permute-start(bf16[256,256]{1,0:T(8,128)(2,1)S(1)} %get-tuple-element.287), channel_id=1, source_target_pairs={{0,16},{4,20},{8,24},{12,28},{16,0},{20,4},{24,8},{28,12},{1,17},{... | collective-permute-start | bytes 393224 | tf_op jit(solution)/shard_map/ppermute | solution.py:197
  609.5 20.6 %collective-permute-start.76 = (bf16[128,2048]{1,0:T(8,128)(2,1)S(1)}, bf16[128,2048]{1,0:T(8,128)(2,1)S(1)}, u32[]{:S(2)}, u32[]{:S(2)}) collective-permute-start(bf16[128,2048]{1,0:T(8,128)(2,1)S(1)} %get-tuple-element.291), channel_id=1, source_target_pairs={{0,1},{1,0},{2,3},{3,2},{4,5},{5,4},{6,7},{7,6},{8,9},{9,8},{10,11... | collective-permute-start | bytes 1572872 | tf_op jit(solution)/shard_map/ppermute | solution.py:56
  609.6 20.5 %collective-permute-start.72 = (bf16[128,2048]{1,0:T(8,128)(2,1)S(1)}, bf16[128,2048]{1,0:T(8,128)(2,1)S(1)}, u32[]{:S(2)}, u32[]{:S(2)}) collective-permute-start(bf16[128,2048]{1,0:T(8,128)(2,1)S(1)} %get-tuple-element.293), channel_id=1, source_target_pairs={{0,2},{1,3},{2,0},{3,1},{4,6},{5,7},{6,4},{7,5},{8,10},{9,11},{10,... | collective-permute-start | bytes 1572872 | tf_op jit(solution)/shard_map/ppermute | solution.py:56
  611.4 122.8 %collective-permute-start.90 = (bf16[2,256,256]{2,1,0:T(8,128)(2,1)S(1)}, bf16[2,256,256]{2,1,0:T(8,128)(2,1)S(1)}, u32[]{:S(2)}, u32[]{:S(2)}) collective-permute-start(bf16[2,256,256]{2,1,0:T(8,128)(2,1)S(1)} %get-tuple-element.281), channel_id=1, source_target_pairs={{0,3},{1,2},{2,1},{3,0},{4,7},{5,6},{6,5},{7,4},{8,11},{9,10},{10,... | collective-permute-start | bytes 786440 | tf_op jit(solution)/shard_map/ppermute | solution.py:56
  614.0 87.5 %collective-permute-start.89 = (bf16[2,256,256]{2,1,0:T(8,128)(2,1)}, bf16[2,256,256]{2,1,0:T(8,128)(2,1)S(1)}, u32[]{:S(2)}, u32[]{:S(2)}) collective-permute-start(bf16[2,256,256]{2,1,0:T(8,128)(2,1)} %get-tuple-element.282), channel_id=1, source_target_pairs={{0,2},{1,3},{2,0},{3,1},{4,6},{5,7},{6,4},{7,5},{8,10},{9,11},{10,... | collective-permute-start | bytes 786440 | tf_op jit(solution)/shard_map/ppermute | solution.py:56
  614.0 21.6 %collective-permute-start.88 = (bf16[2,256,256]{2,1,0:T(8,128)(2,1)S(1)}, bf16[2,256,256]{2,1,0:T(8,128)(2,1)S(1)}, u32[]{:S(2)}, u32[]{:S(2)}) collective-permute-start(bf16[2,256,256]{2,1,0:T(8,128)(2,1)S(1)} %get-tuple-element.283), channel_id=1, source_target_pairs={{0,1},{1,0},{2,3},{3,2},{4,5},{5,4},{6,7},{7,6},{8,9},{9,8},{10,11... | collective-permute-start | bytes 786440 | tf_op jit(solution)/shard_map/ppermute | solution.py:56
  630.2 26.8 %collective-permute-start.77 = (bf16[256,2048]{1,0:T(8,128)(2,1)S(1)}, bf16[256,2048]{1,0:T(8,128)(2,1)S(1)}, u32[]{:S(2)}, u32[]{:S(2)}) collective-permute-start(bf16[256,2048]{1,0:T(8,128)(2,1)S(1)} %pad_maximum_fusion.11), channel_id=1, source_target_pairs={{0,1},{1,0},{2,3},{3,2},{4,5},{5,4},{6,7},{7,6},{8,9},{9,8},{10,11... | collective-permute-start | bytes 3145736 | tf_op jit(solution)/shard_map/ppermute | solution.py:56
  632.4 24.6 %collective-permute-start.82 = (bf16[256,2048]{1,0:T(8,128)(2,1)S(1)}, bf16[256,2048]{1,0:T(8,128)(2,1)S(1)}, u32[]{:S(2)}, u32[]{:S(2)}) collective-permute-start(bf16[256,2048]{1,0:T(8,128)(2,1)S(1)} %pad_maximum_fusion.12), channel_id=1, source_target_pairs={{0,2},{1,3},{2,0},{3,1},{4,6},{5,7},{6,4},{7,5},{8,10},{9,11},{10,... | collective-permute-start | bytes 3145736 | tf_op jit(solution)/shard_map/ppermute | solution.py:56
  662.5 187.7 %reduce-scatter.8.cloned.1.call-start = ((), (), s32[]{:S(2)}) async-start(), calls=%async_computation.7 | async-start | bytes 2359296 | tf_op jit(solution)/shard_map/reduce_scatter | solution.py:708
  743.4 20.2 %collective-permute-start.87 = (bf16[1024,384]{1,0:T(8,128)(2,1)S(1)}, bf16[1024,384]{1,0:T(8,128)(2,1)S(1)}, u32[]{:S(2)}, u32[]{:S(2)}) collective-permute-start(bf16[1024,384]{1,0:T(8,128)(2,1)S(1)} %fusion.90), channel_id=1, source_target_pairs={{0,8},{4,12},{8,16},{12,20},{16,24},{20,28},{24,0},{28,4},{1,9},{5... | collective-permute-start | bytes 2359304 | tf_op jit(solution)/shard_map/ppermute | solution.py:148
  748.8 14.8 %collective-permute-start.91 = (bf16[1024,384]{1,0:T(8,128)(2,1)S(1)}, bf16[1024,384]{1,0:T(8,128)(2,1)S(1)}, u32[]{:S(2)}, u32[]{:S(2)}) collective-permute-start(bf16[1024,384]{1,0:T(8,128)(2,1)S(1)} %slice.917), channel_id=1, source_target_pairs={{0,4},{4,0},{8,12},{12,8},{16,20},{20,16},{24,28},{28,24},{1,5},{5... | collective-permute-start | bytes 2359304 | tf_op jit(solution)/shard_map/ppermute | solution.py:152
  758.0 31.4 %collective-permute-start.92 = (bf16[256,2048]{1,0:T(8,128)(2,1)S(1)}, bf16[256,2048]{1,0:T(8,128)(2,1)S(1)}, u32[]{:S(2)}, u32[]{:S(2)}) collective-permute-start(bf16[256,2048]{1,0:T(8,128)(2,1)S(1)} %get-tuple-element.274), channel_id=1, source_target_pairs={{0,1},{1,0},{2,3},{3,2},{4,5},{5,4},{6,7},{7,6},{8,9},{9,8},{10,11... | collective-permute-start | bytes 3145736 | tf_op jit(solution)/shard_map/ppermute | solution.py:56
  758.3 32.5 %collective-permute-start.108 = (bf16[256,2048]{1,0:T(8,128)(2,1)S(1)}, bf16[256,2048]{1,0:T(8,128)(2,1)S(1)}, u32[]{:S(2)}, u32[]{:S(2)}) collective-permute-start(bf16[256,2048]{1,0:T(8,128)(2,1)S(1)} %get-tuple-element.275), channel_id=1, source_target_pairs={{0,2},{1,3},{2,0},{3,1},{4,6},{5,7},{6,4},{7,5},{8,10},{9,11},{10,... | collective-permute-start | bytes 3145736 | tf_op jit(solution)/shard_map/ppermute | solution.py:56
  763.9 19.0 %collective-permute-start.94 = (bf16[1024,384]{1,0:T(8,128)(2,1)S(1)}, bf16[1024,384]{1,0:T(8,128)(2,1)S(1)}, u32[]{:S(2)}, u32[]{:S(2)}) collective-permute-start(bf16[1024,384]{1,0:T(8,128)(2,1)S(1)} %fusion.89), channel_id=1, source_target_pairs={{0,8},{4,12},{8,16},{12,20},{16,24},{20,28},{24,0},{28,4},{1,9},{5... | collective-permute-start | bytes 2359304 | tf_op jit(solution)/shard_map/ppermute | solution.py:148
  784.0 18.4 %collective-permute-start.106 = (bf16[1024,384]{1,0:T(8,128)(2,1)}, bf16[1024,384]{1,0:T(8,128)(2,1)}, u32[]{:S(2)}, u32[]{:S(2)}) collective-permute-start(bf16[1024,384]{1,0:T(8,128)(2,1)} %fusion.87), channel_id=1, source_target_pairs={{0,8},{4,12},{8,16},{12,20},{16,24},{20,28},{24,0},{28,4},{1,9},{5... | collective-permute-start | bytes 2359304 | tf_op jit(solution)/shard_map/ppermute | solution.py:148
  (195 other events, 1726.3 us)
Sparse Core Ops, SparseCore 0:
  95.5 102.9 all-gather.2
  233.1 52.8 all-gather.4
  510.4 51.9 reduce-scatter.3
  662.6 88.3 reduce-scatter.5
  814.3 35.8 reduce-scatter.7

commit v3 on v2

v3 whole, which is shorter than its diff:
```python
import jax
import jax.numpy as jnp
from jax import lax
from jax.experimental import pallas as pl
from jax.experimental.pallas import tpu as pltpu
from jax.sharding import PartitionSpec as P

HEADS = 16
HEAD_DIM = 128
PIECE = 256
SCALE = HEAD_DIM ** (-0.5)

LOG2_E = 1.4426950408889634
VMEM = 24 << 20
WIDE_VMEM = 56 << 20

epsilon = 1e-06
rope_base = 500000.0

F32 = jnp.float32
BF16 = jnp.bfloat16

SQUARE = ((0, 0), (0, 2), (1, 0), (1, 1), (0, 1), (0, 3), (1, 2), (1, 3))


def token_order(count):
    return SQUARE if count == 4 else tuple((0, j) for j in range(count))


def to_low(tensor):
    return tensor.astype(BF16)


def dot(left, right, contract):
    return lax.dot_general(left, right, ((contract[0], contract[1]), ((), ())), preferred_element_type=F32)


def mm(left, right):
    return dot(left, right, ((1,), (0,)))


def mm_first(left, right):
    return dot(left, right, ((0,), (0,)))


def mm_last(left, right):
    return dot(left, right, ((1,), (1,)))


def after(value, *others):
    return lax.optimization_barrier((value,) + others)[0]


def send_shard(value, k):
    count = lax.axis_size("shard")
    return lax.ppermute(value, "shard", [(s, s ^ k) for s in range(count)])


def gather_tokens(own, first_hold=(), last_hold=()):
    count = lax.axis_size("shard")
    if count != 4:
        others = [send_shard(own, k) for k in range(1, count)]
        return jnp.concatenate([own] + others), others[0]
    half = own.shape[0] // 2
    a0, b0 = own[:half], own[half:]
    a2 = send_shard(a0, 2)
    b1 = send_shard(b0, 1)
    if first_hold:
        a2, b1 = after(a2, *first_hold), after(b1, *first_hold)
    a02 = jnp.concatenate([a0, a2])
    b01 = jnp.concatenate([b0, b1])
    a13 = send_shard(a02, 1)
    b23 = send_shard(b01, 2)
    last = a13
    if last_hold:
        a13, b23 = after(a13, *last_hold), after(b23, *last_hold)
    return jnp.concatenate([a02, b01, a13, b23]), last


def scatter_tokens(keep, send, first_hold=(), last_hold=()):
    count = lax.axis_size("shard")
    if count != 4:
        parts = jnp.split(jnp.concatenate([keep, send]), count)
        return parts[0] + sum(send_shard(to_low(parts[k]), k).astype(F32) for k in range(1, count))
    q = keep.shape[0] // 2
    send_low = to_low(send)
    a_in = send_shard(send_low[:q], 1)
    b_in = send_shard(send_low[q:], 2)
    if first_hold:
        a_in, b_in = after(a_in, *first_hold), after(b_in, *first_hold)
    a02 = keep[:q] + a_in.astype(F32)
    b01 = keep[q:] + b_in.astype(F32)
    h = q // 2
    a_last = send_shard(to_low(a02[h:]), 2)
    b_last = send_shard(to_low(b01[h:]), 1)
    if last_hold:
        a_last, b_last = after(a_last, *last_hold), after(b_last, *last_hold)
    return jnp.concatenate([a02[:h] + a_last.astype(F32), b01[:h] + b_last.astype(F32)])


def swap_blocks(rows, k):
    order = token_order(lax.axis_size("shard"))
    step = rows.shape[-1] // len(order)
    index = [order.index((h, j ^ k)) for h, j in order]
    return jnp.concatenate([rows[..., i * step : (i + 1) * step] for i in index], axis=-1)


def sum_rows(rows):
    return rows + sum(swap_blocks(send_shard(rows, k), k) for k in range(1, lax.axis_size("shard")))


def unrelative(blocks, s):
    shape = blocks.shape
    bits = shape[0].bit_length() - 1
    cube = blocks.reshape((2,) * bits + shape[1:])
    for bit in range(bits):
        cube = jnp.where((s >> bit) % 2 == 1, jnp.flip(cube, bits - 1 - bit), cube)
    return cube.reshape(shape)


def exchange(blocks, axis):
    return lax.all_to_all(blocks, axis, 0, 0, tiled=True)


def rows_perm(count, heads, k):
    c = count // heads
    return [(s, heads * (s % c) + (s // c + k) % heads) for s in range(count)]


def spread_heads(blocks, s):
    heads, count = blocks.shape[0], lax.axis_size("shard")
    if heads == count:
        return exchange(blocks, "shard")
    q = s // (count // heads)
    got = [lax.ppermute(pick(blocks, (q + k) % heads), "shard", rows_perm(count, heads, k)) for k in range(heads)]
    return reverse_pick(jnp.stack(got), s % heads)


def collect_heads(blocks, s):
    heads, count = blocks.shape[0], lax.axis_size("shard")
    if heads == count:
        return exchange(blocks, "shard")
    q = s // (count // heads)
    got = [
        lax.ppermute(pick(blocks, (s - k) % heads), "shard", flip(rows_perm(count, heads, k))) for k in range(heads)
    ]
    return roll_pick(jnp.stack(got), -q)


def ring(value, count):
    return lax.ppermute(value, "rep", [(r, (r + 2) % count) for r in range(count)])


def sibling(value, count):
    return lax.ppermute(value, "rep", [(r, r ^ 1) for r in range(count)])


def gather_pairs(own, count):
    blocks = [own]
    for _ in range(count // 2 - 1):
        blocks.append(ring(blocks[-1], count))
    pairs = []
    for i, block in enumerate(blocks):
        other = sibling(block, count)
        pairs.append((block, after(other, blocks[i + 1]) if i + 1 < len(blocks) else other))
    return pairs


def scatter_pairs(part_of, count, beside=lambda i, low: ()):
    total = low = None
    for i, step in enumerate(list(range(1, count // 2)) + [0]):
        part = part_of(step, low)
        half = part.shape[0] // 2
        mine = part[:half].astype(F32) + sibling(to_low(part[half:]), count).astype(F32)
        if total is None:
            total = mine
        else:
            got = ring(low, count)
            hold = beside(i - 1, low)
            if hold:
                got = after(got, *hold)
            total = got.astype(F32) + mine
        low = to_low(total)
    return total


def round_the_ring(own, compute, count, early, late):
    chips = count // 2

    def mine(part):
        middle = part.shape[0] // 2
        return part[:middle] + sibling(to_low(part[middle:]), count).astype(F32)

    block, parts, total = own, [], None
    for t in range(chips):
        following = ring(block, count) if t + 1 < chips else None
        parts.append(compute(t, jnp.concatenate([block, sibling(block, count)])))
        if t == 1:
            total = mine(parts[1])
        if following is not None:
            hold = early(t) + ((to_low(total),) if t == chips - 2 else ())
            block = after(following, *hold) if hold else following
    for step, t in enumerate(list(range(2, chips)) + [0]):
        low = to_low(total)
        got = ring(low, count)
        hold = late(step, low)
        if hold:
            got = after(got, *hold)
        total = got.astype(F32) + mine(parts[t])
    return total


def heads_perm(shard_count, rep_count, per, k):
    group = shard_count // per
    pairs = []
    for r in range(rep_count):
        for s in range(shard_count):
            j = (s % per + k) % per
            target = (r // group * group + s // per, per * (r % group) + j)
            pairs.append((r * shard_count + s, target[0] * shard_count + target[1]))
    return pairs


def flip_rep(value, d):
    count = lax.axis_size("rep")
    return lax.ppermute(value, "rep", [(i, i ^ d) for i in range(count)])


def sum_rep(value):
    d = 1
    while d < lax.axis_size("rep"):
        value = value + flip_rep(value, d)
        d *= 2
    return value


def spread_down(rows):
    S, R = lax.axis_size("shard"), lax.axis_size("rep")
    share, columns = rows.shape[0] // R, rows.shape[1]
    units = rows.reshape(R // S, S, share, columns).transpose(1, 0, 2, 3)
    return exchange(units, "shard").reshape(R, share, columns)


def join_down(pieces):
    R, share, columns = pieces.shape
    return pieces.transpose(1, 0, 2).reshape(share, R * columns)


def part_down(rows):
    share, R = rows.shape[0], lax.axis_size("rep")
    return rows.reshape(share, R, -1).transpose(1, 0, 2)


def collect_down(pieces):
    R, share, columns = pieces.shape
    S = lax.axis_size("shard")
    units = exchange(pieces.reshape(S, R // S, share, columns), "shard")
    return units.transpose(1, 0, 2, 3).reshape(R * share, columns)


def flip(pairs):
    return [(b, a) for a, b in pairs]


def permute(value, pairs):
    return lax.ppermute(value, ("rep", "shard"), pairs)


def pick(values, index):
    return lax.dynamic_index_in_dim(values, index, 0, keepdims=False)


def roll_pick(values, shift):
    n = values.shape[0]
    if n == 1:
        return values
    return lax.dynamic_slice_in_dim(jnp.concatenate([values, values]), shift % n, n, 0)


def reverse_pick(values, base):
    n = values.shape[0]
    if n == 1:
        return values
    return roll_pick(values[::-1], n - 1 - base)


def frequencies():
    return jnp.power(jnp.float32(rope_base), -2.0 * jnp.arange(HEAD_DIM // 2, dtype=F32) / HEAD_DIM)


def bias_of(piece_first, row, col):
    row_in = (row >= piece_first) & (row < piece_first + PIECE)
    col_in = (col >= piece_first) & (col < piece_first + PIECE)
    return jnp.where((col <= row) | (row_in & col_in), 0.0, -1e30).astype(F32)


def attend_kernel(where_ref, q_ref, k_ref, v_ref, row_ref, col_ref, o_ref, bias_ref):
    @pl.when(pl.program_id(1) == 0)
    def _():
        bias_ref[...] = bias_of(where_ref[where_ref.shape[0] - 1], row_ref[...], col_ref[...])

    scores = mm_last(q_ref[0], k_ref[0]) * (SCALE * LOG2_E) + bias_ref[...]
    powers = jnp.exp2(scores - jnp.max(scores, axis=-1, keepdims=True))
    weights = powers * (1.0 / jnp.sum(powers, axis=-1, keepdims=True))
    o_ref[...] = to_low(mm(to_low(weights), v_ref[0]))


def attend(q, k, v, place, where, block=256):
    heads, n, hd = q.shape
    whole = pl.BlockSpec((1, n, hd), lambda b, t, w: (t, 0, 0))
    return pl.pallas_call(
        attend_kernel,
        out_shape=jax.ShapeDtypeStruct((n, heads * hd), BF16),
        grid_spec=pltpu.PrefetchScalarGridSpec(
            num_scalar_prefetch=1,
            grid=(n // block, heads),
            in_specs=[
                pl.BlockSpec((1, block, hd), lambda b, t, w: (t, b, 0)),
                whole,
                whole,
                pl.BlockSpec((block, 1), lambda b, t, w: (b, 0)),
                pl.BlockSpec((1, n), lambda b, t, w: (0, 0)),
            ],
            out_specs=pl.BlockSpec((block, hd), lambda b, t, w: (b, w[t])),
            scratch_shapes=[pltpu.VMEM((block, n), F32)],
        ),
        compiler_params=pltpu.CompilerParams(vmem_limit_bytes=VMEM),
        cost_estimate=pl.CostEstimate(
            flops=4 * heads * n * n * hd, bytes_accessed=8 * heads * n * hd, transcendentals=heads * n * n
        ),
        name="attend",
    )(where, q, k, v, place[:, None], place[None, :])


def attend_back_kernel(where_ref, q_ref, k_ref, v_ref, do_ref, row_ref, col_ref, dq_ref, dk_ref, dv_ref, products_ref, bias_ref):
    t, b = pl.program_id(0), pl.program_id(1)

    @pl.when(pl.program_id(0) == 0)
    def _():
        bias_ref[b] = bias_of(where_ref[where_ref.shape[0] - 1], row_ref[...], col_ref[...])

    q, k, v, do = q_ref[0], k_ref[0], v_ref[0], do_ref[...]
    scores = mm_last(k, q) * (SCALE * LOG2_E) + bias_ref[b]
    powers = jnp.exp2(scores - jnp.max(scores, axis=0, keepdims=True))
    probs = powers * (1.0 / jnp.sum(powers, axis=0, keepdims=True))
    grad_probs = mm_last(v, do)
    delta = jnp.sum(probs * grad_probs, axis=0, keepdims=True)
    grad_scores = to_low(probs * (grad_probs - delta))
    dq = mm_first(grad_scores, k) * SCALE
    dq_ref[0] = dq
    dk = mm(grad_scores, q) * SCALE
    dv = mm(to_low(probs), do)

    @pl.when((t == 0) & (b == 0))
    def _():
        products_ref[...] = jnp.zeros_like(products_ref)

    own = pl.ds(pl.multiple_of(b * q.shape[0], q.shape[0]), q.shape[0])
    products_ref[0:1, own] += jnp.sum((dq * q.astype(F32)).T, axis=0, keepdims=True)

    @pl.when(b == 0)
    def _():
        dk_ref[0] = dk
        dv_ref[0] = dv

    @pl.when(b > 0)
    def _():
        dk_ref[0] += dk
        dv_ref[0] += dv

    @pl.when(b == pl.num_programs(1) - 1)
    def _():
        products_ref[1:2, :] += jnp.sum((dk_ref[0] * k.astype(F32)).T, axis=0, keepdims=True)


def attend_back(q, k, v, do, place, where, block=512):
    heads, n, hd = q.shape
    one = pl.BlockSpec((1, block, hd), lambda t, b, w: (t, b, 0))
    whole = pl.BlockSpec((1, n, hd), lambda t, b, w: (t, 0, 0))
    return pl.pallas_call(
        attend_back_kernel,
        out_shape=[jax.ShapeDtypeStruct((heads, n, hd), F32)] * 3 + [jax.ShapeDtypeStruct((2, n), F32)],
        grid_spec=pltpu.PrefetchScalarGridSpec(
            num_scalar_prefetch=1,
            grid=(heads, n // block),
            in_specs=[
                one,
                whole,
                whole,
                pl.BlockSpec((block, hd), lambda t, b, w: (b, w[t])),
                pl.BlockSpec((1, block), lambda t, b, w: (0, b)),
                pl.BlockSpec((n, 1), lambda t, b, w: (0, 0)),
            ],
            out_specs=[one, whole, whole, pl.BlockSpec((2, n), lambda t, b, w: (0, 0))],
            scratch_shapes=[pltpu.VMEM((n // block, n, block), F32)],
        ),
        compiler_params=pltpu.CompilerParams(vmem_limit_bytes=32 << 20),
        cost_estimate=pl.CostEstimate(
            flops=10 * heads * n * n * hd, bytes_accessed=20 * heads * n * hd, transcendentals=heads * n * n
        ),
        name="attend_back",
    )(where, q, k, v, do, place[None, :], place[:, None])


def columns_of(t, i):
    return slice((3 * t + i) * HEAD_DIM, (3 * t + i + 1) * HEAD_DIM)


def squares_kernel(heads, raw_ref, out_ref):
    for i in (0, 1):
        total = sum(jnp.square(raw_ref[:, columns_of(t, i)]) for t in range(heads))
        out_ref[i : i + 1, :] = jnp.sum(total.T, axis=0, keepdims=True)


def squares(raw, heads, block=256):
    n, width = raw.shape
    return pl.pallas_call(
        lambda *refs: squares_kernel(heads, *refs),
        out_shape=jax.ShapeDtypeStruct((2, n), F32),
        grid=(n // block,),
        in_specs=[pl.BlockSpec((block, width), lambda b: (b, 0))],
        out_specs=pl.BlockSpec((2, block), lambda b: (0, b)),
        compiler_params=pltpu.CompilerParams(vmem_limit_bytes=VMEM),
        cost_estimate=pl.CostEstimate(flops=heads * n * 512, bytes_accessed=heads * n * 1536, transcendentals=0),
        name="squares",
    )(raw)


def turn_half(tensor):
    return pltpu.roll(tensor, HEAD_DIM // 2, 1)


def rope_kernel(heads, raw_ref, inv_ref, gain_ref, turn_ref, q_ref, k_ref, v_ref):
    cosines, sines = turn_ref[:, :HEAD_DIM], turn_ref[:, HEAD_DIM:]
    for t in range(heads):
        for i, out in enumerate((q_ref, k_ref)):
            value = raw_ref[:, columns_of(t, i)] * inv_ref[:, i : i + 1] * gain_ref[t, i : i + 1, :]
            out[t] = to_low(value * cosines + turn_half(value) * sines)
        v_ref[t] = to_low(raw_ref[:, columns_of(t, 2)])


def rope(raw, inv, gain, turn, block=256):
    heads, n = gain.shape[0], raw.shape[0]
    rows = lambda width: pl.BlockSpec((block, width), lambda b: (b, 0))
    out = pl.BlockSpec((heads, block, HEAD_DIM), lambda b: (0, b, 0))
    return pl.pallas_call(
        lambda *refs: rope_kernel(heads, *refs),
        out_shape=[jax.ShapeDtypeStruct((heads, n, HEAD_DIM), BF16)] * 3,
        grid=(n // block,),
        in_specs=[
            rows(raw.shape[1]),
            rows(2),
            pl.BlockSpec((heads, 2, HEAD_DIM), lambda b: (0, 0, 0)),
            rows(2 * HEAD_DIM),
        ],
        out_specs=[out] * 3,
        compiler_params=pltpu.CompilerParams(vmem_limit_bytes=VMEM),
        cost_estimate=pl.CostEstimate(flops=heads * n * 2000, bytes_accessed=heads * n * 2304, transcendentals=0),
        name="rope",
    )(raw, inv, gain, turn)


def rope_back_kernel(
    heads, raw_ref, dq_ref, dk_ref, dv_ref, inv_ref, mean_ref, gain_ref, turn_ref, out_ref, grad_ref
):
    @pl.when(pl.program_id(0) == 0)
    def _():
        grad_ref[...] = jnp.zeros_like(grad_ref)

    cosines, sines = turn_ref[:, :HEAD_DIM], turn_ref[:, HEAD_DIM:]
    for t in range(heads):
        for i, grad in enumerate((dq_ref, dk_ref)):
            inv = inv_ref[:, i : i + 1]
            hat = raw_ref[:, columns_of(t, i)] * inv
            back = grad[t] * cosines - turn_half(grad[t]) * sines
            grad_ref[t, i : i + 1, :] += jnp.sum(back * hat, axis=0, keepdims=True)
            row = inv * (back * gain_ref[t, i : i + 1, :] - hat * mean_ref[:, i : i + 1])
            out_ref[:, columns_of(t, i)] = to_low(row)
        out_ref[:, columns_of(t, 2)] = to_low(dv_ref[t])


def rope_back(raw, dq, dk, dv, inv, mean, gain, turn, block=256):
    heads, (n, width) = gain.shape[0], raw.shape
    rows = lambda width: pl.BlockSpec((block, width), lambda b: (b, 0))
    grad = pl.BlockSpec((heads, block, HEAD_DIM), lambda b: (0, b, 0))
    gains = pl.BlockSpec((heads, 2, HEAD_DIM), lambda b: (0, 0, 0))
    return pl.pallas_call(
        lambda *refs: rope_back_kernel(heads, *refs),
        out_shape=[jax.ShapeDtypeStruct((n, width), BF16), jax.ShapeDtypeStruct((heads, 2, HEAD_DIM), F32)],
        grid=(n // block,),
        in_specs=[rows(width)] + [grad] * 3 + [rows(2), rows(2), gains, rows(2 * HEAD_DIM)],
        out_specs=[rows(width), gains],
        compiler_params=pltpu.CompilerParams(vmem_limit_bytes=WIDE_VMEM),
        cost_estimate=pl.CostEstimate(flops=heads * n * 4000, bytes_accessed=heads * n * 3840, transcendentals=0),
        name="rope_back",
    )(raw, dq, dk, dv, inv, mean, gain, turn)


def body(
    tokens,
    piece_start,
    positions,
    w_query,
    w_key,
    w_value,
    w_out,
    query_gain,
    key_gain,
    attn_gain,
    w_gate,
    w_up,
    w_down,
    mlp_gain,
    cotangent,
):
    S = lax.axis_size("shard")
    R = lax.axis_size("rep")
    s = lax.axis_index("shard")
    r = lax.axis_index("rep")
    _, span, width = tokens.shape
    heads = HEADS // S
    per = HEADS // R
    own_width = width // S
    x_own = tokens.reshape(span, width)

    by_ring = per * 2 == S
    chip, core = r // 2, r % 2

    def head_columns(j):
        start = j * HEAD_DIM
        return jnp.concatenate(
            [to_low(lax.dynamic_slice_in_dim(w, start, HEAD_DIM, 1)) for w in (w_query, w_key, w_value)], axis=1
        )

    def by_core(value):
        if not by_ring:
            return value
        middle = value.shape[1] // 2
        return jnp.where(core == 1, jnp.concatenate([value[:, middle:], value[:, :middle]], axis=1), value)

    own_columns = [head_columns((s + k) % per) for k in range(per)]
    got = [permute(value, heads_perm(S, R, per, k)) for k, value in enumerate(own_columns)]
    gains_own = jnp.stack([to_low(g).astype(F32) for g in (query_gain, key_gain, attn_gain, mlp_gain)])
    small = jnp.concatenate([positions.reshape(span).astype(F32), gains_own.reshape(-1)])
    small_all = [small] + [send_shard(small, k) for k in range(1, S)]
    own_out = spread_heads(after(to_low(w_out), *own_columns).reshape(heads, HEAD_DIM, -1), s)
    got, small_all, own_out = lax.optimization_barrier((got, small_all, own_out))

    got = reverse_pick(jnp.stack(got), s % per).reshape(per * own_width, 3 * HEAD_DIM)
    if by_ring:
        qkv_pairs = gather_pairs(got, R)
        qkv_w = jnp.zeros((width, heads * 3 * HEAD_DIM), BF16)
        for t, pair in enumerate(qkv_pairs):
            for i, block in enumerate(pair):
                qkv_w = lax.dynamic_update_slice(qkv_w, block, (i * block.shape[0], t * block.shape[1]))
        head_order = (chip - jnp.arange(heads)) % heads
        ring_start, ring_late, ring_end = qkv_pairs[1][0], qkv_pairs[-2][0], qkv_pairs[-1][0]
    else:
        qkv_w = lax.all_gather(got, "rep", axis=0, tiled=True).reshape(heads, width, 3 * HEAD_DIM)
        qkv_w = jnp.concatenate(list(qkv_w), axis=1)
        head_order = jnp.arange(heads)
        ring_start = ring_late = ring_end = qkv_w
    where = jnp.concatenate([head_order, piece_start]).astype(jnp.int32)
    x_all, x_last = gather_tokens(by_core(after(x_own, got)), (ring_start,), (ring_late,))
    gate_up = after(jnp.concatenate([to_low(w_gate), to_low(w_up)], axis=1), x_last)
    gate_up_w = lax.all_gather(gate_up, "shard", axis=0, tiled=True)

    own_out = own_out.reshape(own_width, -1)
    columns = own_out.shape[1]

    gains = unrelative(jnp.stack([v[span:].reshape(4, own_width) for v in small_all]), s)
    gains = gains.transpose(1, 0, 2).reshape(4, width)
    head_gains = gains[:2].reshape(2, heads, S, HEAD_DIM)
    head_gains = lax.dynamic_index_in_dim(head_gains, s, 2, keepdims=False)
    head_gains = head_gains.transpose(1, 0, 2)
    if by_ring:
        head_gains = reverse_pick(head_gains, chip)
    again, mgain = gains[2], gains[3]
    order = token_order(S)
    step = S * span // len(order)
    place_pos = jnp.concatenate([small_all[j][h * step : (h + 1) * step] for h, j in order])
    place = jnp.concatenate([(s ^ j) * span + h * step + lax.iota(jnp.int32, step) for h, j in order])
    angles = place_pos[:, None] * frequencies()
    cosines, sines = jnp.cos(angles), jnp.sin(angles)
    turn = jnp.concatenate([cosines, cosines, -sines, sines], axis=1)

    raw = mm(x_all, qkv_w)
    pieces = spread_down(after(to_low(w_down), raw))
    raw_squares = squares(raw, heads)
    inv = lax.rsqrt(sum_rows(raw_squares) / width + epsilon).T
    q, k, v = rope(raw, inv, head_gains, turn)
    o = attend(q, k, v, place, where)

    out_w = jnp.zeros((own_width, width), BF16)
    block = after(own_out, ring_end)
    for t in range(R // 2):
        if t:
            block = after(ring(block, R), (raw_squares, q, o)[min(t - 1, 2)])
        for i, value in enumerate((block, sibling(block, R))):
            start = ((chip - t) % (R // 2) * 2 + (core ^ i)) * columns
            out_w = lax.dynamic_update_slice_in_dim(out_w, value, start, 1)
    rows = S * span // 2
    a_send = mm(o[rows:], out_w)
    a_keep = mm(o[:rows], out_w)
    down_blocks = exchange(after(pieces, a_send), "rep")
    a = scatter_tokens(a_keep, a_send, (down_blocks,))
    ainv = lax.rsqrt(jnp.mean(a * a, axis=-1, keepdims=True) + epsilon)
    ahat = a * ainv
    h = x_own.astype(F32) + ahat * again
    hb = to_low(h)

    down_w = lax.all_gather(join_down(after(down_blocks, hb)), "shard", axis=0, tiled=True)
    chips, ff = R // 2, w_gate.shape[1]
    kept = {}

    def forward(t, pair):
        gu = mm(pair, gate_up_w)
        g, u = gu[:, :ff], gu[:, ff:]
        inner = to_low(g * jax.nn.sigmoid(g) * u)
        kept[t] = (g, u, inner, pair)
        return mm(inner, down_w)

    z = round_the_ring(hb, forward, R, lambda t: (), lambda step, low: ())
    zinv = lax.rsqrt(jnp.mean(z * z, axis=-1, keepdims=True) + epsilon)
    zhat = z * zinv
    output = to_low(h + zhat * mgain).reshape(tokens.shape)

    dy = cotangent.reshape(span, width).astype(F32)
    grad_mgain = jnp.sum(dy * zhat, axis=0)
    scaled = dy * mgain
    dz = to_low(zinv * (scaled - zhat * jnp.mean(scaled * zhat, axis=-1, keepdims=True)))
    dgs, dus, dz_pairs, dh_parts, weight_grads = {}, {}, {}, {}, {}

    def backward(t, pair):
        g, u = kept[t][:2]
        dm = mm_last(pair, down_w)
        sig = jax.nn.sigmoid(g)
        dz_pairs[t] = pair
        dgs[t] = to_low(dm * u * sig * (1.0 + g * (1.0 - sig)))
        dus[t] = to_low(dm * g * sig)
        dh_parts[t] = mm_last(jnp.concatenate([dgs[t], dus[t]], axis=1), gate_up_w)
        return dh_parts[t]

    def all_tokens(values):
        return jnp.concatenate([values[t] for t in range(chips)])

    def weight_grad(step, low):
        hold = (dh_parts[chips - 1],) if step == 0 else ()
        if step == chips - 3:
            inner_all = after(jnp.concatenate([kept[t][2] for t in range(chips)]), low)
            down_grad = to_low(mm_first(inner_all, all_tokens(dz_pairs)))
            weight_grads["down"] = down_grad
            weight_grads["down_share"] = lax.psum_scatter(down_grad, "shard", scatter_dimension=0, tiled=True)
            hold += (down_grad,)
        if step == chips - 2:
            hb_all = after(jnp.concatenate([kept[t][3] for t in range(chips)]), low)
            weight_grads["gate"] = to_low(mm_first(hb_all, all_tokens(dgs)))
            weight_grads["up"] = to_low(mm_first(hb_all, all_tokens(dus)))
            hold += (weight_grads["gate"],)
        return hold

    dh = dy + round_the_ring(dz, backward, R, lambda t: (dh_parts[t],), weight_grad)

    grad_again = jnp.sum(dh * ahat, axis=0)
    scaled = dh * again
    da = to_low(ainv * (scaled - ahat * jnp.mean(scaled * ahat, axis=-1, keepdims=True)))
    gate_up_grad = jnp.concatenate([weight_grads["gate"], after(weight_grads["up"], da)], axis=1)
    da_all, _ = gather_tokens(da, (), (gate_up_grad, weight_grads["down_share"]))
    do = to_low(mm_last(da_all, out_w))
    gate_up_share = lax.psum_scatter(after(gate_up_grad, da_all), "shard", scatter_dimension=0, tiled=True)
    dq, dk, dv, products = attend_back(q, k, v, do, place, where)
    down_back = after(exchange(part_down(after(weight_grads["down_share"], da_all)), "rep"), dv)
    products = after(products, down_back)
    out_grad = to_low(mm_first(o, after(da_all, products)))
    out_share = lax.psum_scatter(out_grad, "rep", scatter_dimension=1, tiled=True)
    means = (sum_rows(products) / width).T
    dqkv, head_grads = rope_back(raw, dq, dk, dv, inv, means, head_gains, turn)
    if by_ring:
        head_grads = reverse_pick(head_grads, chip)
    grad_down = collect_down(down_back)
    dqkv = after(dqkv, grad_down)
    grad_down = grad_down.astype(F32)
    late = {}
    qkv_grad = to_low(mm_first(x_all, dqkv))

    def qkv_part(t, hold):
        return qkv_grad[:, t * 3 * HEAD_DIM : (t + 1) * 3 * HEAD_DIM]

    def input_grad(i, hold=None):
        if i == 0:
            dx_all = mm_last(after(dqkv, hold), qkv_w)
            late["keep"], late["send"] = dx_all[:rows], to_low(dx_all[rows:])
            late["gains"] = gain_shares(head_grads, s)
            return (late["keep"], late["send"], late["gains"], gate_up_share, out_grad)
        if i == 2:
            late["hold"] = (hold,)
        return ()

    def gain_shares(head_grads, s):
        wide = jnp.stack([grad_again, grad_mgain]).reshape(2, S, own_width).transpose(1, 0, 2)
        if heads != S:
            head_grads = collect_heads(head_grads, s)
            wide = jnp.sum(exchange(wide, "shard"), axis=0)
        else:
            got = exchange(jnp.concatenate([head_grads, wide], axis=2), "shard")
            head_grads, wide = got[..., :HEAD_DIM], jnp.sum(got[..., HEAD_DIM:], axis=0)
        return jnp.concatenate([head_grads.transpose(1, 0, 2).reshape(2, own_width), wide])

    if by_ring:
        qkv_share = to_low(scatter_pairs(qkv_part, R, input_grad))
    else:
        parts = jnp.concatenate([qkv_part(t, None) for t in range(heads)])
        qkv_share = lax.psum_scatter(parts, "rep", scatter_dimension=0, tiled=True)
        input_grad(0, dqkv)
    dx = dh + by_core(scatter_tokens(late["keep"], late["send"], late.get("hold", ()), (qkv_share,)))

    grad_out = collect_heads(after(out_share, qkv_share).reshape(heads, HEAD_DIM, -1), s)
    grad_out = grad_out.reshape(w_out.shape).astype(F32)
    slots = qkv_share.reshape(per, own_width, 3 * HEAD_DIM)
    back = jnp.stack([permute(pick(slots, (s - k) % per), flip(heads_perm(S, R, per, k))) for k in range(per)])
    back = roll_pick(back, -(s % per)).reshape(per, own_width, 3, HEAD_DIM)
    back = back.transpose(2, 1, 0, 3).reshape(3, own_width, per * HEAD_DIM).astype(F32)

    gain_grads = sum_rep(after(late["gains"], qkv_share))
    gate_up_share = gate_up_share.astype(F32)

    return (
        output,
        dx.reshape(tokens.shape),
        back[0],
        back[1],
        back[2],
        grad_out,
        gain_grads[0],
        gain_grads[1],
        gain_grads[2],
        gate_up_share[:, :ff],
        gate_up_share[:, ff:],
        grad_down,
        gain_grads[3],
    )


def solution(mesh):
    grid = P("shard", "rep")
    rows = P("rep", "shard", None)
    gain = P("shard")
    in_specs = (rows, P("rep"), P("rep", "shard"), grid, grid, grid, grid, gain, gain, gain, grid, grid, grid, gain, rows)
    out_specs = (rows, rows, grid, grid, grid, grid, gain, gain, gain, grid, grid, grid, gain)
    return jax.shard_map(body, mesh=mesh, in_specs=in_specs, out_specs=out_specs, check_vma=False)
```

time: 880 us -> 851 us (0.967)
  waiting for transfers between devices: 341 us -> 316 us
  other arithmetic: 53.8 us -> 73.3 us
  matrix products: 195 us -> 178 us
  local copies, waits for them, and re-layouts: 113 us -> 122 us
    all_to_all x0 -> x7, starting transfers between devices: none -> 31.7 us  [exchange(): return lax.all_to_all(blocks, axis, 0, 0, tiled=True)]
    ppermute x21 -> x3, waiting for transfers between devices: 34.8 us -> 6.02 us  [flip_rep(): return lax.ppermute(value, 'rep', [(i, i ^ d) for i in range(count)])]
    ppermute x21 -> x3, starting transfers between devices: 26.7 us -> 0.14 us  [flip_rep(): return lax.ppermute(value, 'rep', [(i, i ^ d) for i in range(count)])]
    ppermute x21, waiting for transfers between devices: 214 us -> 236 us  [ring(): lax.ppermute(value, 'rep', [(r, (r + 2) % count) for r in range(count)])]
    dot_general x38 -> x26, matrix products: 195 us -> 178 us  [dot(): lax.dot_general(left, right, ((contract[0], contract[1]), ((), ())), pref...]
    dynamic_update_slice x28 -> x16, local copies, waits for them, and re-layouts: 3.62 us -> 18.4 us  [the longest x8 15.3 us: body(): lax.dynamic_update_slice(qkv_w, block, (i * block.shape[0], t * block.sha...]
    reduce_scatter x1, waiting for transfers between devices: 11.2 us -> 0.02 us  [body(): lax.psum_scatter(out_grad, 'rep', scatter_dimension=1, tiled=True)]
    unnamed x356 -> x258, local copies, waits for them, and re-layouts: 74 us -> 63.2 us
  transfers between devices with their start and end apart: 125 -> 93, of which waited for: 48 -> 35; matrix products, arithmetic and copies ran while one was open for 34% -> 39% of each run, Pallas kernels for 7% -> 6%
where the time goes in v3:
time: 851 us; the launch traced here: 841 us
  waiting for transfers between devices  316 us (37%)
  matrix products  178 us (21%)
  local copies, waits for them, and re-layouts  122 us (14%)
  starting transfers between devices  81.2 us (10%)
  other arithmetic  73.3 us (9%)
  Pallas kernels  54.3 us (6%)
  between operations  17.1 us (2%)
    ppermute x21, waiting for transfers between devices, ring(): lax.ppermute(value, 'rep', [(r, (r + 2) % count) for r in range(count)])  236 us
    dot_general x26, matrix products, dot(): lax.dot_general(left, right, ((contract[0], contract[1]), ((), ())), pref...  178 us
    ppermute x25, waiting for transfers between devices, send_shard(): return lax.ppermute(value, 'shard', [(s, s ^ k) for s in range(count)])  67.6 us
    unnamed x258, local copies, waits for them, and re-layouts  63.2 us
    all_to_all x7, starting transfers between devices, exchange(): return lax.all_to_all(blocks, axis, 0, 0, tiled=True)  31.7 us
    ppermute x25, starting transfers between devices, send_shard(): return lax.ppermute(value, 'shard', [(s, s ^ k) for s in range(count)])  27.2 us
    pallas_call x1, Pallas kernels, attend_back(): pl.pallas_call(attend_back_kernel, out_shape=[jax.ShapeDtypeStruct((heads...  26.2 us
    convert_element_type x23, other arithmetic, to_low(): return tensor.astype(BF16)  24.7 us
  transfers between devices with their start and end apart: 93, of which 35 were waited for; matrix products, arithmetic and copies ran while one was open for 39% of the time, Pallas kernels for 6%

profile of v3, /device:TPU:4, one launch (start us, length us, event | category | flops | bytes accessed | tf_op | source)
XLA Modules:
  0.0 841.2 jit_solution(14131295658941927855)
XLA Ops:
  22.9 3.4 all-to-all-start
  43.9 3.2 multiply_cosine_fusion
  49.2 9.4 %collective-permute-done.6 = bf16[1024,384]{1,0:T(8,128)(2,1)} collective-permute-done((bf16[1024,384]{1,0:T(8,128)(2,1)S(1)}, bf16[1024,384]{1,0:T(8,128)(2,1)}, u32[]{:S(2)}, u32[]{:S(2)}) %collective-permute-start.6) | collective-permute-done | bytes 786464 | tf_op jit(solution)/shard_map/ppermute | solution.py:151
  58.6 3.0 dynamic_update_slice.48
  69.4 10.4 %collective-permute-done.9 = bf16[1024,384]{1,0:T(8,128)(2,1)} collective-permute-done((bf16[1024,384]{1,0:T(8,128)(2,1)}, bf16[1024,384]{1,0:T(8,128)(2,1)}, u32[]{:S(2)}, u32[]{:S(2)}) %collective-permute-start.9) | collective-permute-done | bytes 786464 | tf_op jit(solution)/shard_map/ppermute | solution.py:151
  90.8 9.3 %collective-permute-done.14 = bf16[1024,384]{1,0:T(8,128)(2,1)} collective-permute-done((bf16[1024,384]{1,0:T(8,128)(2,1)}, bf16[1024,384]{1,0:T(8,128)(2,1)}, u32[]{:S(2)}, u32[]{:S(2)}) %collective-permute-start.14) | collective-permute-done | bytes 786464 | tf_op jit(solution)/shard_map/ppermute | solution.py:151
  112.0 8.7 %fusion.135.refs_0_ = f32[1024,1536]{1,0:T(8,128)S(1)} fusion(bf16[1024,2048]{1,0:T(8,128)(2,1)S(1)} %copy-done.71, bf16[2048,1536]{1,0:T(8,128)(2,1)} %constant_dynamic-update-slice_fusion.96), kind=kOutput, calls=%fused_computation.356 | convolution fusion | flops 6442450944 | bytes 16777216 | tf_op jit(solution)/shard_map/dot_general | solution.py:35
  128.0 5.2 all-to-all-start.1
  135.5 3.0 copy-done.1
  138.4 3.8 rope.1
  142.8 15.1 %attend.1 = bf16[1024,512]{1,0:T(8,128)(2,1)S(1)} custom-call(s32[5]{0:T(128)S(1)} %pad_add_fusion.where_ref, bf16[4,1024,128]{2,1,0:T(8,128)(2,1)S(1)} %get-tuple-element.89.q_ref, bf16[4,1024,128]{2,1,0:T(8,128)(2,1)S(1)} %get-tuple-element.90.k_ref, bf16[4,1024,128]{2,1,0:T(8,128)(2,1)S(1)} %get-tuple-element.91.v_ref, ...), custom_call_target="tpu_custom_call" | custom-call | flops 2147483648 | bytes 4194304 | tf_op jit(solution)/shard_map/attend/pallas_call | solution.py:311
  164.7 5.5 all-to-all-start.2
  175.2 3.2 fusion.102
  178.4 33.6 %collective-permute-done.28 = bf16[256,2048]{1,0:T(8,128)(2,1)} collective-permute-done((bf16[256,2048]{1,0:T(8,128)(2,1)S(1)}, bf16[256,2048]{1,0:T(8,128)(2,1)}, u32[]{:S(2)}, u32[]{:S(2)}) %collective-permute-start.28) | collective-permute-done | bytes 1048608 | tf_op jit(solution)/shard_map/ppermute | solution.py:56
  213.1 3.4 slice_add_fusion.11
  218.8 11.6 %collective-permute-done.27 = bf16[128,2048]{1,0:T(8,128)(2,1)S(1)} collective-permute-done((bf16[128,2048]{1,0:T(8,128)(2,1)S(1)}, bf16[128,2048]{1,0:T(8,128)(2,1)S(1)}, u32[]{:S(2)}, u32[]{:S(2)}) %collective-permute-start.27) | collective-permute-done | bytes 524320 | tf_op jit(solution)/shard_map/ppermute | solution.py:56
  237.2 24.4 %collective-permute-done.30 = bf16[256,2048]{1,0:T(8,128)(2,1)S(1)} collective-permute-done((bf16[256,2048]{1,0:T(8,128)(2,1)S(1)}, bf16[256,2048]{1,0:T(8,128)(2,1)S(1)}, u32[]{:S(2)}, u32[]{:S(2)}) %collective-permute-start.30) | collective-permute-done | bytes 1048608 | tf_op jit(solution)/shard_map/ppermute | solution.py:151
  261.7 25.1 %collective-permute-done.34 = bf16[256,2048]{1,0:T(8,128)(2,1)} collective-permute-done((bf16[256,2048]{1,0:T(8,128)(2,1)S(1)}, bf16[256,2048]{1,0:T(8,128)(2,1)}, u32[]{:S(2)}, u32[]{:S(2)}) %collective-permute-start.34) | collective-permute-done | bytes 1048608 | tf_op jit(solution)/shard_map/ppermute | solution.py:151
  287.2 7.2 fusion.43
  297.0 4.6 fusion.136
  302.3 7.6 fusion.47
  310.6 4.9 fusion.137
  318.3 25.1 %collective-permute-done.33 = bf16[256,2048]{1,0:T(8,128)(2,1)S(1)} collective-permute-done((bf16[256,2048]{1,0:T(8,128)(2,1)S(1)}, bf16[256,2048]{1,0:T(8,128)(2,1)S(1)}, u32[]{:S(2)}, u32[]{:S(2)}) %collective-permute-start.33) | collective-permute-done | bytes 1048608 | tf_op jit(solution)/shard_map/ppermute | solution.py:151
  344.2 6.2 fusion.51
  355.2 7.3 fusion.55
  366.3 4.4 collective-permute-done.37
  371.5 25.6 %collective-permute-done.41 = bf16[256,2048]{1,0:T(8,128)(2,1)S(1)} collective-permute-done((bf16[256,2048]{1,0:T(8,128)(2,1)S(1)}, bf16[256,2048]{1,0:T(8,128)(2,1)S(1)}, u32[]{:S(2)}, u32[]{:S(2)}) %collective-permute-start.41) | collective-permute-done | bytes 1048608 | tf_op jit(solution)/shard_map/ppermute | solution.py:151
  403.3 4.3 multiply_convert_fusion.8
  407.6 10.6 %fusion.63 = f32[512,2048]{1,0:T(8,128)} fusion(bf16[2048,2048]{1,0:T(8,128)(2,1)} %all-gather.3.cloned.1.call-done, bf16[512,1024]{1,0:T(8,128)(2,1)} %get-tuple-element.237, bf16[512,1024]{1,0:T(8,128)(2,1)} %get-tuple-element.236), kind=kOutput, calls=%fused_computation.94 | convolution fusion | flops 4299161600 | bytes 14680064 | tf_op jit(solution)/shard_map/dot_general | solution.py:35
  418.2 9.9 %collective-permute-done.44 = bf16[256,2048]{1,0:T(8,128)(2,1)} collective-permute-done((bf16[256,2048]{1,0:T(8,128)(2,1)S(1)}, bf16[256,2048]{1,0:T(8,128)(2,1)}, u32[]{:S(2)}, u32[]{:S(2)}) %collective-permute-start.44) | collective-permute-done | bytes 1048608 | tf_op jit(solution)/shard_map/ppermute | solution.py:151
  430.3 2.9 constant_dynamic-update-slice_fusion.40
  436.0 6.8 multiply_convert_fusion.6
  442.8 7.6 fusion.71
  455.9 7.6 collective-permute-done.49
  467.6 3.0 multiply_convert_fusion.4
  470.6 7.7 fusion.79
  478.3 14.2 %collective-permute-done.50 = bf16[256,2048]{1,0:T(8,128)(2,1)S(1)} collective-permute-done((bf16[256,2048]{1,0:T(8,128)(2,1)S(1)}, bf16[256,2048]{1,0:T(8,128)(2,1)S(1)}, u32[]{:S(2)}, u32[]{:S(2)}) %collective-permute-start.50) | collective-permute-done | bytes 1048608 | tf_op jit(solution)/shard_map/ppermute | solution.py:151
  500.0 4.3 multiply_convert_fusion.2
  504.2 7.6 fusion.87
  513.1 11.5 %collective-permute-done.48 = bf16[256,2048]{1,0:T(8,128)(2,1)S(1)} collective-permute-done((bf16[256,2048]{1,0:T(8,128)(2,1)}, bf16[256,2048]{1,0:T(8,128)(2,1)S(1)}, u32[]{:S(2)}, u32[]{:S(2)}) %collective-permute-start.48) | collective-permute-done | bytes 1048608 | tf_op jit(solution)/shard_map/ppermute | solution.py:151
  527.2 13.0 %convolution_convert_fusion.1 = bf16[1024,2048]{1,0:T(8,128)(2,1)} fusion(bf16[2048,1024]{1,0:T(8,128)(2,1)S(1)} %pad_maximum_fusion.1, bf16[2048,2048]{1,0:T(8,128)(2,1)} %constant_dynamic-update-slice_fusion.28), kind=kOutput, calls=%fused_computation.21 | convolution fusion | flops 8592031744 | bytes 16777216 | tf_op jit(solution)/shard_map/dot_general | solution.py:35
  545.0 8.0 collective-permute-done.54
  556.0 13.3 %fusion.19 = bf16[2048,1024]{0,1:T(8,128)(2,1)} fusion(bf16[2048,2048]{1,0:T(8,128)(2,1)} %constant_dynamic-update-slice_fusion.36, bf16[512,1024]{1,0:T(8,128)(2,1)S(1)} %copy-done.89, bf16[512,1024]{1,0:T(8,128)(2,1)S(1)} %copy-done.88, bf16[512,1024]{1,0:T(8,128)(2,1)S(1)} %copy-done.83, bf16[512,1024]{1,0:T(8,128)(2,1)S(1)} %copy-done.82), kind=kOutput, calls=%fused_computation.20 | convolution fusion | flops 8608808960 | bytes 16777216 | tf_op jit(solution)/shard_map/dot_general | solution.py:35
  569.3 12.1 %collective-permute-done.56 = bf16[256,2048]{1,0:T(8,128)(2,1)S(1)} collective-permute-done((bf16[256,2048]{1,0:T(8,128)(2,1)S(1)}, bf16[256,2048]{1,0:T(8,128)(2,1)S(1)}, u32[]{:S(2)}, u32[]{:S(2)}) %collective-permute-start.56) | collective-permute-done | bytes 1048608 | tf_op jit(solution)/shard_map/ppermute | solution.py:151
  588.0 11.6 %fusion.16 = bf16[2048,1024]{0,1:T(8,128)(2,1)} fusion(bf16[2048,2048]{1,0:T(8,128)(2,1)S(1)} %bitcast.161, bf16[512,1024]{1,0:T(8,128)(2,1)S(1)} %copy-done.86, bf16[512,1024]{1,0:T(8,128)(2,1)S(1)} %copy-done.85, bf16[512,1024]{1,0:T(8,128)(2,1)S(1)} %copy-done.81, bf16[512,1024]{1,0:T(8,128)(2,1)S(1)} %copy-done.79), kind=kOutput, calls=%fused_computation.19 | convolution fusion | flops 8608808960 | bytes 16777216 | tf_op jit(solution)/shard_map/dot_general | solution.py:35
  599.6 4.1 collective-permute-done.59
  606.6 8.5 %pad_maximum_fusion = bf16[2048,2048]{0,1:T(8,128)(2,1)} fusion(bf16[2048,1024]{0,1:T(8,128)(2,1)} %fusion.16, bf16[2048,1024]{0,1:T(8,128)(2,1)} %fusion.19), kind=kLoop, calls=%fused_computation | loop fusion | flops 16777216 | bytes 16777216 | tf_op jit(solution)/shard_map/concatenate | solution.py:667
  617.6 11.4 %collective-permute-done.61 = bf16[256,2048]{1,0:T(8,128)(2,1)} collective-permute-done((bf16[256,2048]{1,0:T(8,128)(2,1)}, bf16[256,2048]{1,0:T(8,128)(2,1)}, u32[]{:S(2)}, u32[]{:S(2)}) %collective-permute-start.61) | collective-permute-done | bytes 1048608 | tf_op jit(solution)/shard_map/ppermute | solution.py:56
  637.5 4.5 all-to-all-start.3
  642.1 4.8 convolution_convert_fusion.3.do_ref
  646.9 26.2 %attend_back.1 = (f32[4,1024,128]{2,1,0:T(8,128)S(1)}, f32[4,1024,128]{2,1,0:T(8,128)S(1)}, f32[4,1024,128]{2,1,0:T(8,128)S(1)}, f32[2,1024]{1,0:T(2,128)S(1)}) custom-call(s32[5]{0:T(128)S(1)} %pad_add_fusion.where_ref, bf16[4,1024,128]{2,1,0:T(8,128)(2,1)S(1)} %copy-done.11, bf16[4,1024,128]{2,1,0:T(8,128)(2,1)S(1)} %copy-done.13, ...), custom_call_target="tpu_custom_call" | custom-call | flops 5368709120 | bytes 10485760 | tf_op jit(solution)/shard_map/attend_back/pallas_call | solution.py:380
  685.0 8.6 %rope_back.1 = (bf16[1024,1536]{1,0:T(8,128)(2,1)}, f32[4,2,128]{2,1,0:T(2,128)}) custom-call(f32[1024,1536]{1,0:T(8,128)} %copy-done, f32[4,1024,128]{2,1,0:T(8,128)} %copy-done.4, f32[4,1024,128]{2,1,0:T(8,128)} %copy-done.5, f32[4,1024,128]{2,1,0:T(8,128)} %copy-done.6, f32[1024,2]{1,0:T(8,128)} %bitcast.132, f32[1024,2]{1,0:T(8,128)} %bitcast.146, ...), custom_call_target="tpu_custom_call" | custom-call | flops 16384000 | bytes 15728640 | tf_op jit(solution)/shard_map/rope_back/pallas_call | solution.py:487
  694.9 4.4 all-to-all-start.5
  699.4 9.9 %convolution_convert_fusion = bf16[2048,1536]{1,0:T(8,128)(2,1)S(1)} fusion(bf16[1024,2048]{1,0:T(8,128)(2,1)} %constant_dynamic-update-slice_fusion, bf16[1024,1536]{1,0:T(8,128)(2,1)} %get-tuple-element.124), kind=kOutput, calls=%fused_computation.1 | convolution fusion | flops 6445596672 | bytes 13631488 | tf_op jit(solution)/shard_map/dot_general | solution.py:35
  714.7 3.8 convolution_convert_fusion.2
  719.1 4.3 all-to-all-start.4
  726.9 12.4 %fusion.134 = (bf16[1024,2048]{1,0:T(8,128)(2,1)}, f32[1024,2048]{1,0:T(8,128)}) fusion(bf16[1024,1536]{1,0:T(8,128)(2,1)} %get-tuple-element.124, bf16[2048,1536]{1,0:T(8,128)(2,1)} %constant_dynamic-update-slice_fusion.96), kind=kOutput, calls=%fused_computation.355 | convolution fusion | flops 6444548096 | bytes 22020096 | tf_op jit(solution)/shard_map/dot_general | solution.py:35
  739.3 19.6 %collective-permute-done.67 = bf16[1024,384]{1,0:T(8,128)(2,1)S(1)} collective-permute-done((bf16[1024,384]{1,0:T(8,128)(2,1)S(1)}, bf16[1024,384]{1,0:T(8,128)(2,1)S(1)}, u32[]{:S(2)}, u32[]{:S(2)}) %collective-permute-start.67) | collective-permute-done | bytes 786464 | tf_op jit(solution)/shard_map/ppermute | solution.py:151
  761.2 3.1 fusion.126
  768.0 14.8 %collective-permute-done.69 = bf16[1024,384]{1,0:T(8,128)(2,1)} collective-permute-done((bf16[1024,384]{1,0:T(8,128)(2,1)}, bf16[1024,384]{1,0:T(8,128)(2,1)}, u32[]{:S(2)}, u32[]{:S(2)}) %collective-permute-start.69) | collective-permute-done | bytes 786464 | tf_op jit(solution)/shard_map/ppermute | solution.py:151
  792.3 3.1 copy.168
  800.8 4.5 collective-permute-done.72
  807.3 4.4 all-to-all-start.6
  820.0 3.4 collective-permute-done.79
  (587 shorter events, 238.3 us)
Async XLA Ops:
  10.7 21.3 %collective-permute-start.2 = (f32[2304]{0:T(1024)S(1)}, f32[2304]{0:T(1024)S(1)}, u32[]{:S(2)}, u32[]{:S(2)}) collective-permute-start(f32[2304]{0:T(1024)S(1)} %pad_maximum_fusion.15), channel_id=1, source_target_pairs={{0,1},{1,0},{2,3},{3,2},{4,5},{5,4},{6,7},{7,6},{8,9},{9,8},{10,11... | collective-permute-start | bytes 27656 | tf_op jit(solution)/shard_map/ppermute | solution.py:56
  12.2 19.8 %collective-permute-start.3 = (f32[2304]{0:T(1024)S(1)}, f32[2304]{0:T(1024)S(1)}, u32[]{:S(2)}, u32[]{:S(2)}) collective-permute-start(f32[2304]{0:T(1024)S(1)} %pad_maximum_fusion.15), channel_id=1, source_target_pairs={{0,2},{1,3},{2,0},{3,1},{4,6},{5,7},{6,4},{7,5},{8,10},{9,11},{10,... | collective-permute-start | bytes 27656 | tf_op jit(solution)/shard_map/ppermute | solution.py:56
  12.7 19.3 %collective-permute-start.4 = (f32[2304]{0:T(1024)S(1)}, f32[2304]{0:T(1024)S(1)}, u32[]{:S(2)}, u32[]{:S(2)}) collective-permute-start(f32[2304]{0:T(1024)S(1)} %pad_maximum_fusion.15), channel_id=1, source_target_pairs={{0,3},{1,2},{2,1},{3,0},{4,7},{5,6},{6,5},{7,4},{8,11},{9,10},{10,... | collective-permute-start | bytes 27656 | tf_op jit(solution)/shard_map/ppermute | solution.py:56
  16.8 16.1 %collective-permute-start = (bf16[512,384]{1,0:T(8,128)(2,1)S(1)}, bf16[512,384]{1,0:T(8,128)(2,1)}, u32[]{:S(2)}, u32[]{:S(2)}) collective-permute-start(bf16[512,384]{1,0:T(8,128)(2,1)S(1)} %pad_maximum_fusion.11), channel_id=1, source_target_pairs={{0,0},{1,1},{2,4},{3,5},{4,2},{5,3},{6,6},{7,7},{8,8},{9,9},{10,12... | collective-permute-start | bytes 1179656 | tf_op jit(solution)/shard_map/ppermute | solution.py:266
  26.3 260.8 %all-gather.3.cloned.1.call-start = ((), (), s32[]{:S(2)}) async-start(), calls=%async_computation.10 | async-start | bytes 10485760 | tf_op jit(solution)/shard_map/all_gather | solution.py:566
  36.7 44.0 %collective-permute-start.11 = (bf16[1024,384]{1,0:T(8,128)(2,1)S(1)}, bf16[1024,384]{1,0:T(8,128)(2,1)}, u32[]{:S(2)}, u32[]{:S(2)}) collective-permute-start(bf16[1024,384]{1,0:T(8,128)(2,1)S(1)} %bitcast.141), channel_id=1, source_target_pairs={{0,4},{4,0},{8,12},{12,8},{16,20},{20,16},{24,28},{28,24},{1,5},{5... | collective-permute-start | bytes 2359304 | tf_op jit(solution)/shard_map/ppermute | solution.py:155
  36.8 21.8 %collective-permute-start.6 = (bf16[1024,384]{1,0:T(8,128)(2,1)S(1)}, bf16[1024,384]{1,0:T(8,128)(2,1)}, u32[]{:S(2)}, u32[]{:S(2)}) collective-permute-start(bf16[1024,384]{1,0:T(8,128)(2,1)S(1)} %bitcast.142), channel_id=1, source_target_pairs={{0,8},{4,12},{8,16},{12,20},{16,24},{20,28},{24,0},{28,4},{1,9},{5... | collective-permute-start | bytes 2359304 | tf_op jit(solution)/shard_map/ppermute | solution.py:151
  41.3 20.4 %collective-permute-start.7 = (bf16[128,2048]{1,0:T(8,128)(2,1)}, bf16[128,2048]{1,0:T(8,128)(2,1)}, u32[]{:S(2)}, u32[]{:S(2)}) collective-permute-start(bf16[128,2048]{1,0:T(8,128)(2,1)} %get-tuple-element.256), channel_id=1, source_target_pairs={{0,1},{1,0},{2,3},{3,2},{4,5},{5,4},{6,7},{7,6},{8,9},{9,8},{10,11... | collective-permute-start | bytes 1572872 | tf_op jit(solution)/shard_map/ppermute | solution.py:56
  43.5 21.5 %collective-permute-start.5 = (bf16[128,2048]{1,0:T(8,128)(2,1)}, bf16[128,2048]{1,0:T(8,128)(2,1)}, u32[]{:S(2)}, u32[]{:S(2)}) collective-permute-start(bf16[128,2048]{1,0:T(8,128)(2,1)} %get-tuple-element.258), channel_id=1, source_target_pairs={{0,2},{1,3},{2,0},{3,1},{4,6},{5,7},{6,4},{7,5},{8,10},{9,11},{10,... | collective-permute-start | bytes 1572872 | tf_op jit(solution)/shard_map/ppermute | solution.py:56
  58.6 21.2 %collective-permute-start.9 = (bf16[1024,384]{1,0:T(8,128)(2,1)}, bf16[1024,384]{1,0:T(8,128)(2,1)}, u32[]{:S(2)}, u32[]{:S(2)}) collective-permute-start(bf16[1024,384]{1,0:T(8,128)(2,1)} %collective-permute-done.6), channel_id=1, source_target_pairs={{0,8},{4,12},{8,16},{12,20},{16,24},{20,28},{24,0},{28,4},{1,9},{5... | collective-permute-start | bytes 2359304 | tf_op jit(solution)/shard_map/ppermute | solution.py:151
  63.9 38.6 %collective-permute-start.10 = (bf16[256,2048]{1,0:T(8,128)(2,1)}, bf16[256,2048]{1,0:T(8,128)(2,1)}, u32[]{:S(2)}, u32[]{:S(2)}) collective-permute-start(bf16[256,2048]{1,0:T(8,128)(2,1)} %pad_maximum_fusion.6), channel_id=1, source_target_pairs={{0,2},{1,3},{2,0},{3,1},{4,6},{5,7},{6,4},{7,5},{8,10},{9,11},{10,... | collective-permute-start | bytes 3145736 | tf_op jit(solution)/shard_map/ppermute | solution.py:56
  66.3 24.5 %collective-permute-start.8 = (bf16[256,2048]{1,0:T(8,128)(2,1)S(1)}, bf16[256,2048]{1,0:T(8,128)(2,1)}, u32[]{:S(2)}, u32[]{:S(2)}) collective-permute-start(bf16[256,2048]{1,0:T(8,128)(2,1)S(1)} %pad_maximum_fusion.5), channel_id=1, source_target_pairs={{0,1},{1,0},{2,3},{3,2},{4,5},{5,4},{6,7},{7,6},{8,9},{9,8},{10,11... | collective-permute-start | bytes 3145736 | tf_op jit(solution)/shard_map/ppermute | solution.py:56
  67.5 19.3 %collective-permute-start.12 = (bf16[1024,384]{1,0:T(8,128)(2,1)}, bf16[1024,384]{1,0:T(8,128)(2,1)S(1)}, u32[]{:S(2)}, u32[]{:S(2)}) collective-permute-start(bf16[1024,384]{1,0:T(8,128)(2,1)} %collective-permute-done.6), channel_id=1, source_target_pairs={{0,4},{4,0},{8,12},{12,8},{16,20},{20,16},{24,28},{28,24},{1,5},{5... | collective-permute-start | bytes 2359304 | tf_op jit(solution)/shard_map/ppermute | solution.py:155
  79.8 20.3 %collective-permute-start.14 = (bf16[1024,384]{1,0:T(8,128)(2,1)}, bf16[1024,384]{1,0:T(8,128)(2,1)}, u32[]{:S(2)}, u32[]{:S(2)}) collective-permute-start(bf16[1024,384]{1,0:T(8,128)(2,1)} %collective-permute-done.9), channel_id=1, source_target_pairs={{0,8},{4,12},{8,16},{12,20},{16,24},{20,28},{24,0},{28,4},{1,9},{5... | collective-permute-start | bytes 2359304 | tf_op jit(solution)/shard_map/ppermute | solution.py:151
  84.7 20.9 %collective-permute-start.13 = (bf16[1024,384]{1,0:T(8,128)(2,1)}, bf16[1024,384]{1,0:T(8,128)(2,1)S(1)}, u32[]{:S(2)}, u32[]{:S(2)}) collective-permute-start(bf16[1024,384]{1,0:T(8,128)(2,1)} %collective-permute-done.9), channel_id=1, source_target_pairs={{0,4},{4,0},{8,12},{12,8},{16,20},{20,16},{24,28},{28,24},{1,5},{5... | collective-permute-start | bytes 2359304 | tf_op jit(solution)/shard_map/ppermute | solution.py:155
  105.1 21.8 %collective-permute-start.20 = (bf16[512,256]{1,0:T(8,128)(2,1)S(1)}, bf16[512,256]{1,0:T(8,128)(2,1)}, u32[]{:S(2)}, u32[]{:S(2)}) collective-permute-start(bf16[512,256]{1,0:T(8,128)(2,1)S(1)} %bitcast.150), channel_id=1, source_target_pairs={{0,8},{4,12},{8,16},{12,20},{16,24},{20,28},{24,0},{28,4},{1,9},{5... | collective-permute-start | bytes 786440 | tf_op jit(solution)/shard_map/ppermute | solution.py:151
  126.9 31.0 %collective-permute-start.21 = (bf16[512,256]{1,0:T(8,128)(2,1)}, bf16[512,256]{1,0:T(8,128)(2,1)}, u32[]{:S(2)}, u32[]{:S(2)}) collective-permute-start(bf16[512,256]{1,0:T(8,128)(2,1)} %collective-permute-done.20), channel_id=1, source_target_pairs={{0,4},{4,0},{8,12},{12,8},{16,20},{20,16},{24,28},{28,24},{1,5},{5... | collective-permute-start | bytes 786440 | tf_op jit(solution)/shard_map/ppermute | solution.py:155
  128.0 36.8 %all-to-all-start.1 = ((bf16[4,2,256,256]{3,2,1,0:T(8,128)(2,1)}), bf16[4,2,256,256]{3,2,1,0:T(8,128)(2,1)}, u32[]{:S(2)}, u32[]{:S(2)}) async-start(bf16[4,2,256,256]{3,2,1,0:T(8,128)(2,1)} %copy.156), calls=%async_computation.1 | async-start | bytes 2097152 | tf_op jit(solution)/shard_map/all_to_all | solution.py:122
  142.3 16.8 %collective-permute-start.24 = (bf16[512,256]{1,0:T(8,128)(2,1)S(1)}, bf16[512,256]{1,0:T(8,128)(2,1)S(1)}, u32[]{:S(2)}, u32[]{:S(2)}) collective-permute-start(bf16[512,256]{1,0:T(8,128)(2,1)S(1)} %collective-permute-done.22), channel_id=1, source_target_pairs={{0,8},{4,12},{8,16},{12,20},{16,24},{20,28},{24,0},{28,4},{1,9},{5... | collective-permute-start | bytes 786440 | tf_op jit(solution)/shard_map/ppermute | solution.py:151
  142.8 16.9 %collective-permute-start.23 = (bf16[512,256]{1,0:T(8,128)(2,1)S(1)}, bf16[512,256]{1,0:T(8,128)(2,1)S(1)}, u32[]{:S(2)}, u32[]{:S(2)}) collective-permute-start(bf16[512,256]{1,0:T(8,128)(2,1)S(1)} %collective-permute-done.22), channel_id=1, source_target_pairs={{0,4},{4,0},{8,12},{12,8},{16,20},{20,16},{24,28},{28,24},{1,5},{5... | collective-permute-start | bytes 786440 | tf_op jit(solution)/shard_map/ppermute | solution.py:155
  164.7 47.2 %all-to-all-start.2 = ((bf16[8,256,256]{2,1,0:T(8,128)(2,1)}), bf16[8,256,256]{2,1,0:T(8,128)(2,1)}, u32[]{:S(2)}, u32[]{:S(2)}) async-start(bf16[8,256,256]{2,1,0:T(8,128)(2,1)} %bitcast.19), calls=%async_computation.2 | async-start | bytes 2097152 | tf_op jit(solution)/shard_map/all_to_all | solution.py:122
  170.2 126.8 %all-gather.5.cloned.1.call-start = ((), (), s32[]{:S(2)}) async-start(), calls=%async_computation.11 | async-start | bytes 5242880 | tf_op jit(solution)/shard_map/all_gather | solution.py:612
  173.1 38.8 %collective-permute-start.28 = (bf16[256,2048]{1,0:T(8,128)(2,1)S(1)}, bf16[256,2048]{1,0:T(8,128)(2,1)}, u32[]{:S(2)}, u32[]{:S(2)}) collective-permute-start(bf16[256,2048]{1,0:T(8,128)(2,1)S(1)} %get-tuple-element.249), channel_id=1, source_target_pairs={{0,2},{1,3},{2,0},{3,1},{4,6},{5,7},{6,4},{7,5},{8,10},{9,11},{10,... | collective-permute-start | bytes 3145736 | tf_op jit(solution)/shard_map/ppermute | solution.py:56
  173.3 39.8 %collective-permute-start.26 = (bf16[256,2048]{1,0:T(8,128)(2,1)}, bf16[256,2048]{1,0:T(8,128)(2,1)}, u32[]{:S(2)}, u32[]{:S(2)}) collective-permute-start(bf16[256,2048]{1,0:T(8,128)(2,1)} %get-tuple-element.248), channel_id=1, source_target_pairs={{0,1},{1,0},{2,3},{3,2},{4,5},{5,4},{6,7},{7,6},{8,9},{9,8},{10,11... | collective-permute-start | bytes 3145736 | tf_op jit(solution)/shard_map/ppermute | solution.py:56
  235.7 393.4 %reduce-scatter.4.cloned.1.call-start = ((), (), s32[]{:S(2)}) async-start(), calls=%async_computation.12 | async-start | bytes 5242880 | tf_op jit(solution)/shard_map/reduce_scatter | solution.py:653
  235.7 25.9 %collective-permute-start.30 = (bf16[256,2048]{1,0:T(8,128)(2,1)S(1)}, bf16[256,2048]{1,0:T(8,128)(2,1)S(1)}, u32[]{:S(2)}, u32[]{:S(2)}) collective-permute-start(bf16[256,2048]{1,0:T(8,128)(2,1)S(1)} %copy-done.66), channel_id=1, source_target_pairs={{0,8},{4,12},{8,16},{12,20},{16,24},{20,28},{24,0},{28,4},{1,9},{5... | collective-permute-start | bytes 3145736 | tf_op jit(solution)/shard_map/ppermute | solution.py:151
  261.7 25.1 %collective-permute-start.34 = (bf16[256,2048]{1,0:T(8,128)(2,1)S(1)}, bf16[256,2048]{1,0:T(8,128)(2,1)}, u32[]{:S(2)}, u32[]{:S(2)}) collective-permute-start(bf16[256,2048]{1,0:T(8,128)(2,1)S(1)} %collective-permute-done.30), channel_id=1, source_target_pairs={{0,8},{4,12},{8,16},{12,20},{16,24},{20,28},{24,0},{28,4},{1,9},{5... | collective-permute-start | bytes 3145736 | tf_op jit(solution)/shard_map/ppermute | solution.py:151
  261.7 25.5 %collective-permute-start.31 = (bf16[256,2048]{1,0:T(8,128)(2,1)S(1)}, bf16[256,2048]{1,0:T(8,128)(2,1)}, u32[]{:S(2)}, u32[]{:S(2)}) collective-permute-start(bf16[256,2048]{1,0:T(8,128)(2,1)S(1)} %collective-permute-done.30), channel_id=1, source_target_pairs={{0,4},{4,0},{8,12},{12,8},{16,20},{20,16},{24,28},{28,24},{1,5},{5... | collective-permute-start | bytes 3145736 | tf_op jit(solution)/shard_map/ppermute | solution.py:155
  286.7 29.4 %collective-permute-start.38 = (bf16[256,2048]{1,0:T(8,128)(2,1)}, bf16[256,2048]{1,0:T(8,128)(2,1)}, u32[]{:S(2)}, u32[]{:S(2)}) collective-permute-start(bf16[256,2048]{1,0:T(8,128)(2,1)} %collective-permute-done.34), channel_id=1, source_target_pairs={{0,8},{4,12},{8,16},{12,20},{16,24},{20,28},{24,0},{28,4},{1,9},{5... | collective-permute-start | bytes 3145736 | tf_op jit(solution)/shard_map/ppermute | solution.py:151
  316.0 27.4 %collective-permute-start.33 = (bf16[256,2048]{1,0:T(8,128)(2,1)S(1)}, bf16[256,2048]{1,0:T(8,128)(2,1)S(1)}, u32[]{:S(2)}, u32[]{:S(2)}) collective-permute-start(bf16[256,2048]{1,0:T(8,128)(2,1)S(1)} %fusion.42), channel_id=1, source_target_pairs={{0,8},{4,12},{8,16},{12,20},{16,24},{20,28},{24,0},{28,4},{1,9},{5... | collective-permute-start | bytes 3145736 | tf_op jit(solution)/shard_map/ppermute | solution.py:151
  316.1 28.1 %collective-permute-start.39 = (bf16[256,2048]{1,0:T(8,128)(2,1)}, bf16[256,2048]{1,0:T(8,128)(2,1)S(1)}, u32[]{:S(2)}, u32[]{:S(2)}) collective-permute-start(bf16[256,2048]{1,0:T(8,128)(2,1)} %collective-permute-done.38), channel_id=1, source_target_pairs={{0,4},{4,0},{8,12},{12,8},{16,20},{20,16},{24,28},{28,24},{1,5},{5... | collective-permute-start | bytes 3145736 | tf_op jit(solution)/shard_map/ppermute | solution.py:155
  316.8 38.4 %collective-permute-start.42 = (bf16[256,2048]{1,0:T(8,128)(2,1)S(1)}, bf16[256,2048]{1,0:T(8,128)(2,1)S(1)}, u32[]{:S(2)}, u32[]{:S(2)}) collective-permute-start(bf16[256,2048]{1,0:T(8,128)(2,1)S(1)} %copy-done.67), channel_id=1, source_target_pairs={{0,4},{4,0},{8,12},{12,8},{16,20},{20,16},{24,28},{28,24},{1,5},{5... | collective-permute-start | bytes 3145736 | tf_op jit(solution)/shard_map/ppermute | solution.py:155
  343.9 26.8 %collective-permute-start.37 = (bf16[256,2048]{1,0:T(8,128)(2,1)S(1)}, bf16[256,2048]{1,0:T(8,128)(2,1)S(1)}, u32[]{:S(2)}, u32[]{:S(2)}) collective-permute-start(bf16[256,2048]{1,0:T(8,128)(2,1)S(1)} %fusion.41), channel_id=1, source_target_pairs={{0,8},{4,12},{8,16},{12,20},{16,24},{20,28},{24,0},{28,4},{1,9},{5... | collective-permute-start | bytes 3145736 | tf_op jit(solution)/shard_map/ppermute | solution.py:151
  371.2 25.9 %collective-permute-start.41 = (bf16[256,2048]{1,0:T(8,128)(2,1)S(1)}, bf16[256,2048]{1,0:T(8,128)(2,1)S(1)}, u32[]{:S(2)}, u32[]{:S(2)}) collective-permute-start(bf16[256,2048]{1,0:T(8,128)(2,1)S(1)} %fusion.39), channel_id=1, source_target_pairs={{0,8},{4,12},{8,16},{12,20},{16,24},{20,28},{24,0},{28,4},{1,9},{5... | collective-permute-start | bytes 3145736 | tf_op jit(solution)/shard_map/ppermute | solution.py:151
  400.7 27.5 %collective-permute-start.44 = (bf16[256,2048]{1,0:T(8,128)(2,1)S(1)}, bf16[256,2048]{1,0:T(8,128)(2,1)}, u32[]{:S(2)}, u32[]{:S(2)}) collective-permute-start(bf16[256,2048]{1,0:T(8,128)(2,1)S(1)} %get-tuple-element.221), channel_id=1, source_target_pairs={{0,8},{4,12},{8,16},{12,20},{16,24},{20,28},{24,0},{28,4},{1,9},{5... | collective-permute-start | bytes 3145736 | tf_op jit(solution)/shard_map/ppermute | solution.py:151
  435.5 28.0 %collective-permute-start.49 = (bf16[256,2048]{1,0:T(8,128)(2,1)}, bf16[256,2048]{1,0:T(8,128)(2,1)S(1)}, u32[]{:S(2)}, u32[]{:S(2)}) collective-permute-start(bf16[256,2048]{1,0:T(8,128)(2,1)} %collective-permute-done.44), channel_id=1, source_target_pairs={{0,8},{4,12},{8,16},{12,20},{16,24},{20,28},{24,0},{28,4},{1,9},{5... | collective-permute-start | bytes 3145736 | tf_op jit(solution)/shard_map/ppermute | solution.py:151
  465.2 27.3 %collective-permute-start.50 = (bf16[256,2048]{1,0:T(8,128)(2,1)S(1)}, bf16[256,2048]{1,0:T(8,128)(2,1)S(1)}, u32[]{:S(2)}, u32[]{:S(2)}) collective-permute-start(bf16[256,2048]{1,0:T(8,128)(2,1)S(1)} %collective-permute-done.49), channel_id=1, source_target_pairs={{0,8},{4,12},{8,16},{12,20},{16,24},{20,28},{24,0},{28,4},{1,9},{5... | collective-permute-start | bytes 3145736 | tf_op jit(solution)/shard_map/ppermute | solution.py:151
  496.9 27.7 %collective-permute-start.48 = (bf16[256,2048]{1,0:T(8,128)(2,1)}, bf16[256,2048]{1,0:T(8,128)(2,1)S(1)}, u32[]{:S(2)}, u32[]{:S(2)}) collective-permute-start(bf16[256,2048]{1,0:T(8,128)(2,1)} %fusion.36), channel_id=1, source_target_pairs={{0,8},{4,12},{8,16},{12,20},{16,24},{20,28},{24,0},{28,4},{1,9},{5... | collective-permute-start | bytes 3145736 | tf_op jit(solution)/shard_map/ppermute | solution.py:151
  497.2 27.4 %collective-permute-start.53 = (bf16[256,2048]{1,0:T(8,128)(2,1)S(1)}, bf16[256,2048]{1,0:T(8,128)(2,1)S(1)}, u32[]{:S(2)}, u32[]{:S(2)}) collective-permute-start(bf16[256,2048]{1,0:T(8,128)(2,1)S(1)} %slice.813), channel_id=1, source_target_pairs={{0,4},{4,0},{8,12},{12,8},{16,20},{20,16},{24,28},{28,24},{1,5},{5... | collective-permute-start | bytes 3145736 | tf_op jit(solution)/shard_map/ppermute | solution.py:155
  526.2 26.8 %collective-permute-start.54 = (bf16[256,2048]{1,0:T(8,128)(2,1)}, bf16[256,2048]{1,0:T(8,128)(2,1)S(1)}, u32[]{:S(2)}, u32[]{:S(2)}) collective-permute-start(bf16[256,2048]{1,0:T(8,128)(2,1)} %fusion.35), channel_id=1, source_target_pairs={{0,8},{4,12},{8,16},{12,20},{16,24},{20,28},{24,0},{28,4},{1,9},{5... | collective-permute-start | bytes 3145736 | tf_op jit(solution)/shard_map/ppermute | solution.py:151
  526.2 26.8 %collective-permute-start.55 = (bf16[256,2048]{1,0:T(8,128)(2,1)}, bf16[256,2048]{1,0:T(8,128)(2,1)}, u32[]{:S(2)}, u32[]{:S(2)}) collective-permute-start(bf16[256,2048]{1,0:T(8,128)(2,1)} %slice.812), channel_id=1, source_target_pairs={{0,4},{4,0},{8,12},{12,8},{16,20},{20,16},{24,28},{28,24},{1,5},{5... | collective-permute-start | bytes 3145736 | tf_op jit(solution)/shard_map/ppermute | solution.py:155
  540.3 218.6 %reduce-scatter.6.cloned.1.call-start = ((), (), s32[]{:S(2)}) async-start(), calls=%async_computation.13 | async-start | bytes 10485760 | tf_op jit(solution)/shard_map/reduce_scatter | solution.py:670
  544.4 36.9 %collective-permute-start.57 = (bf16[256,2048]{1,0:T(8,128)(2,1)S(1)}, bf16[256,2048]{1,0:T(8,128)(2,1)S(1)}, u32[]{:S(2)}, u32[]{:S(2)}) collective-permute-start(bf16[256,2048]{1,0:T(8,128)(2,1)S(1)} %slice.811), channel_id=1, source_target_pairs={{0,4},{4,0},{8,12},{12,8},{16,20},{20,16},{24,28},{28,24},{1,5},{5... | collective-permute-start | bytes 3145736 | tf_op jit(solution)/shard_map/ppermute | solution.py:155
  555.6 25.7 %collective-permute-start.56 = (bf16[256,2048]{1,0:T(8,128)(2,1)S(1)}, bf16[256,2048]{1,0:T(8,128)(2,1)S(1)}, u32[]{:S(2)}, u32[]{:S(2)}) collective-permute-start(bf16[256,2048]{1,0:T(8,128)(2,1)S(1)} %fusion.33), channel_id=1, source_target_pairs={{0,8},{4,12},{8,16},{12,20},{16,24},{20,28},{24,0},{28,4},{1,9},{5... | collective-permute-start | bytes 3145736 | tf_op jit(solution)/shard_map/ppermute | solution.py:151
  585.7 17.9 %collective-permute-start.59 = (bf16[128,2048]{1,0:T(8,128)(2,1)S(1)}, bf16[128,2048]{1,0:T(8,128)(2,1)S(1)}, u32[]{:S(2)}, u32[]{:S(2)}) collective-permute-start(bf16[128,2048]{1,0:T(8,128)(2,1)S(1)} %get-tuple-element.253), channel_id=1, source_target_pairs={{0,1},{1,0},{2,3},{3,2},{4,5},{5,4},{6,7},{7,6},{8,9},{9,8},{10,11... | collective-permute-start | bytes 1572872 | tf_op jit(solution)/shard_map/ppermute | solution.py:56
  586.5 18.8 %collective-permute-start.58 = (bf16[128,2048]{1,0:T(8,128)(2,1)S(1)}, bf16[128,2048]{1,0:T(8,128)(2,1)S(1)}, u32[]{:S(2)}, u32[]{:S(2)}) collective-permute-start(bf16[128,2048]{1,0:T(8,128)(2,1)S(1)} %get-tuple-element.255), channel_id=1, source_target_pairs={{0,2},{1,3},{2,0},{3,1},{4,6},{5,7},{6,4},{7,5},{8,10},{9,11},{10,... | collective-permute-start | bytes 1572872 | tf_op jit(solution)/shard_map/ppermute | solution.py:56
  604.7 24.4 %collective-permute-start.61 = (bf16[256,2048]{1,0:T(8,128)(2,1)}, bf16[256,2048]{1,0:T(8,128)(2,1)}, u32[]{:S(2)}, u32[]{:S(2)}) collective-permute-start(bf16[256,2048]{1,0:T(8,128)(2,1)} %pad_maximum_fusion.9), channel_id=1, source_target_pairs={{0,2},{1,3},{2,0},{3,1},{4,6},{5,7},{6,4},{7,5},{8,10},{9,11},{10,... | collective-permute-start | bytes 3145736 | tf_op jit(solution)/shard_map/ppermute | solution.py:56
  606.3 24.1 %collective-permute-start.60 = (bf16[256,2048]{1,0:T(8,128)(2,1)}, bf16[256,2048]{1,0:T(8,128)(2,1)}, u32[]{:S(2)}, u32[]{:S(2)}) collective-permute-start(bf16[256,2048]{1,0:T(8,128)(2,1)} %pad_maximum_fusion.8), channel_id=1, source_target_pairs={{0,1},{1,0},{2,3},{3,2},{4,5},{5,4},{6,7},{7,6},{8,9},{9,8},{10,11... | collective-permute-start | bytes 3145736 | tf_op jit(solution)/shard_map/ppermute | solution.py:56
  637.5 39.5 %all-to-all-start.3 = ((bf16[8,256,256]{2,1,0:T(8,128)(2,1)}), bf16[8,256,256]{2,1,0:T(8,128)(2,1)}, u32[]{:S(2)}, u32[]{:S(2)}) async-start(bf16[8,256,256]{2,1,0:T(8,128)(2,1)} %bitcast.140), calls=%async_computation.4 | async-start | bytes 2097152 | tf_op jit(solution)/shard_map/all_to_all | solution.py:122
  694.9 24.2 %all-to-all-start.5 = ((f32[4,2,640]{2,1,0:T(2,128)}), f32[4,2,640]{2,1,0:T(2,128)S(1)}, u32[]{:S(2)}, u32[]{:S(2)}) async-start(f32[4,2,640]{2,1,0:T(2,128)} %pad_maximum_fusion.14), calls=%async_computation.6 | async-start | bytes 40960 | tf_op jit(solution)/shard_map/all_to_all | solution.py:122
  699.4 107.9 %reduce-scatter.8.cloned.1.call-start = ((), (), s32[]{:S(2)}) async-start(), calls=%async_computation.14 | async-start | bytes 2359296 | tf_op jit(solution)/shard_map/reduce_scatter | solution.py:675
  718.5 40.4 %collective-permute-start.68 = (bf16[1024,384]{1,0:T(8,128)(2,1)S(1)}, bf16[1024,384]{1,0:T(8,128)(2,1)S(1)}, u32[]{:S(2)}, u32[]{:S(2)}) collective-permute-start(bf16[1024,384]{1,0:T(8,128)(2,1)S(1)} %get-tuple-element.228), channel_id=1, source_target_pairs={{0,4},{4,0},{8,12},{12,8},{16,20},{20,16},{24,28},{28,24},{1,5},{5... | collective-permute-start | bytes 2359304 | tf_op jit(solution)/shard_map/ppermute | solution.py:155
  718.6 49.4 %collective-permute-start.70 = (bf16[1024,384]{1,0:T(8,128)(2,1)}, bf16[1024,384]{1,0:T(8,128)(2,1)}, u32[]{:S(2)}, u32[]{:S(2)}) collective-permute-start(bf16[1024,384]{1,0:T(8,128)(2,1)} %get-tuple-element.227), channel_id=1, source_target_pairs={{0,4},{4,0},{8,12},{12,8},{16,20},{20,16},{24,28},{28,24},{1,5},{5... | collective-permute-start | bytes 2359304 | tf_op jit(solution)/shard_map/ppermute | solution.py:155
  719.1 47.3 %all-to-all-start.4 = ((bf16[4,2,256,256]{3,2,1,0:T(8,128)(2,1)}), bf16[4,2,256,256]{3,2,1,0:T(8,128)(2,1)S(1)}, u32[]{:S(2)}, u32[]{:S(2)}) async-start(bf16[4,2,256,256]{3,2,1,0:T(8,128)(2,1)} %bitcast.27), calls=%async_computation.5 | async-start | bytes 2097152 | tf_op jit(solution)/shard_map/all_to_all | solution.py:122
  725.0 33.9 %collective-permute-start.67 = (bf16[1024,384]{1,0:T(8,128)(2,1)S(1)}, bf16[1024,384]{1,0:T(8,128)(2,1)S(1)}, u32[]{:S(2)}, u32[]{:S(2)}) collective-permute-start(bf16[1024,384]{1,0:T(8,128)(2,1)S(1)} %add_convert_fusion.4), channel_id=1, source_target_pairs={{0,8},{4,12},{8,16},{12,20},{16,24},{20,28},{24,0},{28,4},{1,9},{5... | collective-permute-start | bytes 2359304 | tf_op jit(solution)/shard_map/ppermute | solution.py:151
  761.2 21.6 %collective-permute-start.69 = (bf16[1024,384]{1,0:T(8,128)(2,1)}, bf16[1024,384]{1,0:T(8,128)(2,1)}, u32[]{:S(2)}, u32[]{:S(2)}) collective-permute-start(bf16[1024,384]{1,0:T(8,128)(2,1)} %add_convert_fusion.3), channel_id=1, source_target_pairs={{0,8},{4,12},{8,16},{12,20},{16,24},{20,28},{24,0},{28,4},{1,9},{5... | collective-permute-start | bytes 2359304 | tf_op jit(solution)/shard_map/ppermute | solution.py:151
  764.4 21.4 %collective-permute-start.74 = (bf16[256,2048]{1,0:T(8,128)(2,1)}, bf16[256,2048]{1,0:T(8,128)(2,1)S(1)}, u32[]{:S(2)}, u32[]{:S(2)}) collective-permute-start(bf16[256,2048]{1,0:T(8,128)(2,1)} %get-tuple-element.239), channel_id=1, source_target_pairs={{0,2},{1,3},{2,0},{3,1},{4,6},{5,7},{6,4},{7,5},{8,10},{9,11},{10,... | collective-permute-start | bytes 3145736 | tf_op jit(solution)/shard_map/ppermute | solution.py:56
  764.4 21.6 %collective-permute-start.66 = (bf16[256,2048]{1,0:T(8,128)(2,1)}, bf16[256,2048]{1,0:T(8,128)(2,1)S(1)}, u32[]{:S(2)}, u32[]{:S(2)}) collective-permute-start(bf16[256,2048]{1,0:T(8,128)(2,1)} %get-tuple-element.238), channel_id=1, source_target_pairs={{0,1},{1,0},{2,3},{3,2},{4,5},{5,4},{6,7},{7,6},{8,9},{9,8},{10,11... | collective-permute-start | bytes 3145736 | tf_op jit(solution)/shard_map/ppermute | solution.py:56
  766.4 34.4 %collective-permute-start.73 = (bf16[1024,384]{1,0:T(8,128)(2,1)}, bf16[1024,384]{1,0:T(8,128)(2,1)}, u32[]{:S(2)}, u32[]{:S(2)}) collective-permute-start(bf16[1024,384]{1,0:T(8,128)(2,1)} %get-tuple-element.226), channel_id=1, source_target_pairs={{0,4},{4,0},{8,12},{12,8},{16,20},{20,16},{24,28},{28,24},{1,5},{5... | collective-permute-start | bytes 2359304 | tf_op jit(solution)/shard_map/ppermute | solution.py:155
  785.6 19.6 %collective-permute-start.72 = (bf16[1024,384]{1,0:T(8,128)(2,1)}, bf16[1024,384]{1,0:T(8,128)(2,1)}, u32[]{:S(2)}, u32[]{:S(2)}) collective-permute-start(bf16[1024,384]{1,0:T(8,128)(2,1)} %add_convert_fusion.2), channel_id=1, source_target_pairs={{0,8},{4,12},{8,16},{12,20},{16,24},{20,28},{24,0},{28,4},{1,9},{5... | collective-permute-start | bytes 2359304 | tf_op jit(solution)/shard_map/ppermute | solution.py:151
  789.0 27.9 %collective-permute-start.71 = (bf16[128,2048]{1,0:T(8,128)(2,1)}, bf16[128,2048]{1,0:T(8,128)(2,1)}, u32[]{:S(2)}, u32[]{:S(2)}) collective-permute-start(bf16[128,2048]{1,0:T(8,128)(2,1)} %slice.820), channel_id=1, source_target_pairs={{0,2},{1,3},{2,0},{3,1},{4,6},{5,7},{6,4},{7,5},{8,10},{9,11},{10,... | collective-permute-start | bytes 1572872 | tf_op jit(solution)/shard_map/ppermute | solution.py:56
  799.3 19.1 %collective-permute-start.75 = (bf16[128,2048]{1,0:T(8,128)(2,1)}, bf16[128,2048]{1,0:T(8,128)(2,1)}, u32[]{:S(2)}, u32[]{:S(2)}) collective-permute-start(bf16[128,2048]{1,0:T(8,128)(2,1)} %slice.819), channel_id=1, source_target_pairs={{0,1},{1,0},{2,3},{3,2},{4,5},{5,4},{6,7},{7,6},{8,9},{9,8},{10,11... | collective-permute-start | bytes 1572872 | tf_op jit(solution)/shard_map/ppermute | solution.py:56
  807.3 21.2 %all-to-all-start.6 = ((bf16[4,128,256]{2,1,0:T(8,128)(2,1)}), bf16[4,128,256]{2,1,0:T(8,128)(2,1)S(1)}, u32[]{:S(2)}, u32[]{:S(2)}) async-start(bf16[4,128,256]{2,1,0:T(8,128)(2,1)} %bitcast.157), calls=%async_computation.9 | async-start | bytes 524288 | tf_op jit(solution)/shard_map/all_to_all | solution.py:122
  812.0 17.4 %collective-permute-start.76 = (bf16[512,384]{0,1:T(8,128)(2,1)S(1)}, bf16[512,384]{0,1:T(8,128)(2,1)}, u32[]{:S(2)}, u32[]{:S(2)}) collective-permute-start(bf16[512,384]{0,1:T(8,128)(2,1)S(1)} %bitcast.154), channel_id=1, source_target_pairs={{0,0},{1,1},{4,2},{5,3},{2,4},{3,5},{6,6},{7,7},{8,8},{9,9},{12,10... | collective-permute-start | bytes 1179656 | tf_op jit(solution)/shard_map/ppermute | solution.py:266
  (123 other events, 1272.7 us)
Sparse Core Ops, SparseCore 0:
  90.9 114.0 all-gather.2
  235.8 53.1 all-gather.4
  540.4 58.9 reduce-scatter.3
  635.2 86.8 reduce-scatter.5
  724.3 45.9 reduce-scatter.7

commit v4 on v3

--- a/solution.py
+++ b/solution.py
@@ -184,7 +184,7 @@
     return total
 
 
-def round_the_ring(own, compute, count, early, late):
+def round_the_ring(own, compute, count, early, late, own_last=False):
     chips = count // 2
 
     def mine(part):
@@ -194,7 +194,10 @@
     block, parts, total = own, [], None
     for t in range(chips):
         following = ring(block, count) if t + 1 < chips else None
-        parts.append(compute(t, jnp.concatenate([block, sibling(block, count)])))
+        pair = jnp.concatenate([block, sibling(block, count)])
+        if t == 0 and own_last:
+            own_pair = pair
+        parts.append(compute(t, pair) if t or not own_last else None)
         if t == 1:
             total = mine(parts[1])
         if following is not None:
@@ -203,6 +206,8 @@
     for step, t in enumerate(list(range(2, chips)) + [0]):
         low = to_low(total)
         got = ring(low, count)
+        if parts[0] is None and step == 1:
+            parts[0] = compute(0, after(own_pair, low))
         hold = late(step, low)
         if hold:
             got = after(got, *hold)
@@ -585,10 +590,10 @@
     turn = jnp.concatenate([cosines, cosines, -sines, sines], axis=1)
 
     raw = mm(x_all, qkv_w)
-    pieces = spread_down(after(to_low(w_down), raw))
     raw_squares = squares(raw, heads)
     inv = lax.rsqrt(sum_rows(raw_squares) / width + epsilon).T
     q, k, v = rope(raw, inv, head_gains, turn)
+    pieces = spread_down(after(to_low(w_down), q))
     o = attend(q, k, v, place, where)
 
     out_w = jnp.zeros((own_width, width), BF16)
@@ -602,7 +607,7 @@
     rows = S * span // 2
     a_send = mm(o[rows:], out_w)
     a_keep = mm(o[:rows], out_w)
-    down_blocks = exchange(after(pieces, a_send), "rep")
+    down_blocks = exchange(after(pieces, a_keep), "rep")
     a = scatter_tokens(a_keep, a_send, (down_blocks,))
     ainv = lax.rsqrt(jnp.mean(a * a, axis=-1, keepdims=True) + epsilon)
     ahat = a * ainv
@@ -620,7 +625,7 @@
         kept[t] = (g, u, inner, pair)
         return mm(inner, down_w)
 
-    z = round_the_ring(hb, forward, R, lambda t: (), lambda step, low: ())
+    z = round_the_ring(hb, forward, R, lambda t: (), lambda step, low: (), True)
     zinv = lax.rsqrt(jnp.mean(z * z, axis=-1, keepdims=True) + epsilon)
     zhat = z * zinv
     output = to_low(h + zhat * mgain).reshape(tokens.shape)
@@ -641,21 +646,21 @@
         dh_parts[t] = mm_last(jnp.concatenate([dgs[t], dus[t]], axis=1), gate_up_w)
         return dh_parts[t]
 
-    def all_tokens(values):
-        return jnp.concatenate([values[t] for t in range(chips)])
+    def all_tokens(values, hold):
+        return jnp.concatenate([after(values[t], hold) for t in range(chips)])
 
     def weight_grad(step, low):
         hold = (dh_parts[chips - 1],) if step == 0 else ()
         if step == chips - 3:
-            inner_all = after(jnp.concatenate([kept[t][2] for t in range(chips)]), low)
-            down_grad = to_low(mm_first(inner_all, all_tokens(dz_pairs)))
+            inner_all = all_tokens({t: kept[t][2] for t in kept}, low)
+            down_grad = to_low(mm_first(inner_all, all_tokens(dz_pairs, low)))
             weight_grads["down"] = down_grad
             weight_grads["down_share"] = lax.psum_scatter(down_grad, "shard", scatter_dimension=0, tiled=True)
             hold += (down_grad,)
         if step == chips - 2:
-            hb_all = after(jnp.concatenate([kept[t][3] for t in range(chips)]), low)
-            weight_grads["gate"] = to_low(mm_first(hb_all, all_tokens(dgs)))
-            weight_grads["up"] = to_low(mm_first(hb_all, all_tokens(dus)))
+            hb_all = all_tokens({t: kept[t][3] for t in kept}, low)
+            weight_grads["gate"] = to_low(mm_first(hb_all, all_tokens(dgs, low)))
+            weight_grads["up"] = to_low(mm_first(hb_all, all_tokens(dus, low)))
             hold += (weight_grads["gate"],)
         return hold
 
@@ -671,8 +676,6 @@
     dq, dk, dv, products = attend_back(q, k, v, do, place, where)
     down_back = after(exchange(part_down(after(weight_grads["down_share"], da_all)), "rep"), dv)
     products = after(products, down_back)
-    out_grad = to_low(mm_first(o, after(da_all, products)))
-    out_share = lax.psum_scatter(out_grad, "rep", scatter_dimension=1, tiled=True)
     means = (sum_rows(products) / width).T
     dqkv, head_grads = rope_back(raw, dq, dk, dv, inv, means, head_gains, turn)
     if by_ring:
@@ -690,10 +693,14 @@
         if i == 0:
             dx_all = mm_last(after(dqkv, hold), qkv_w)
             late["keep"], late["send"] = dx_all[:rows], to_low(dx_all[rows:])
-            late["gains"] = gain_shares(head_grads, s)
+            out_grad = to_low(mm_first(o, after(da_all, hold)))
+            late["out"] = lax.psum_scatter(out_grad, "rep", scatter_dimension=1, tiled=True)
+            late["gains"] = gain_shares(after(head_grads, hold), s)
             return (late["keep"], late["send"], late["gains"], gate_up_share, out_grad)
         if i == 2:
             late["hold"] = (hold,)
+            late["out"] = collect_heads(after(late["out"], hold).reshape(heads, HEAD_DIM, -1), s)
+            return (late["out"],)
         return ()
 
     def gain_shares(head_grads, s):
@@ -714,8 +721,9 @@
         input_grad(0, dqkv)
     dx = dh + by_core(scatter_tokens(late["keep"], late["send"], late.get("hold", ()), (qkv_share,)))
 
-    grad_out = collect_heads(after(out_share, qkv_share).reshape(heads, HEAD_DIM, -1), s)
-    grad_out = grad_out.reshape(w_out.shape).astype(F32)
+    if not by_ring:
+        late["out"] = collect_heads(late["out"].reshape(heads, HEAD_DIM, -1), s)
+    grad_out = late["out"].reshape(w_out.shape).astype(F32)
     slots = qkv_share.reshape(per, own_width, 3 * HEAD_DIM)
     back = jnp.stack([permute(pick(slots, (s - k) % per), flip(heads_perm(S, R, per, k))) for k in range(per)])
     back = roll_pick(back, -(s % per)).reshape(per, own_width, 3, HEAD_DIM)

time: 851 us -> 838 us (0.985)
    convert_element_type x23 -> x25, other arithmetic: 24.7 us -> 27.1 us  [to_low(): return tensor.astype(BF16)]
    unnamed x258 -> x251, local copies, waits for them, and re-layouts: 63.2 us -> 64 us
  transfers between devices with their start and end apart: 93 -> 93, of which waited for: 35 -> 33; matrix products, arithmetic and copies ran while one was open for 39% -> 38% of each run, Pallas kernels for 6% -> 7%
where the time goes in v4:
time: 838 us; the launch traced here: 828 us
  waiting for transfers between devices  310 us (37%)
  matrix products  172 us (21%)
  local copies, waits for them, and re-layouts  116 us (14%)
  starting transfers between devices  82 us (10%)
  other arithmetic  75.9 us (9%)
  Pallas kernels  54.7 us (7%)
  between operations  17.1 us (2%)
    ppermute x21, waiting for transfers between devices, ring(): lax.ppermute(value, 'rep', [(r, (r + 2) % count) for r in range(count)])  231 us
    dot_general x26, matrix products, dot(): lax.dot_general(left, right, ((contract[0], contract[1]), ((), ())), pref...  172 us
    unnamed x251, local copies, waits for them, and re-layouts  64 us
    ppermute x25, waiting for transfers between devices, send_shard(): return lax.ppermute(value, 'shard', [(s, s ^ k) for s in range(count)])  63.2 us
    all_to_all x7, starting transfers between devices, exchange(): return lax.all_to_all(blocks, axis, 0, 0, tiled=True)  32 us
    convert_element_type x25, other arithmetic, to_low(): return tensor.astype(BF16)  27.1 us
    ppermute x25, starting transfers between devices, send_shard(): return lax.ppermute(value, 'shard', [(s, s ^ k) for s in range(count)])  26.3 us
    pallas_call x1, Pallas kernels, attend_back(): pl.pallas_call(attend_back_kernel, out_shape=[jax.ShapeDtypeStruct((heads...  26.2 us
  transfers between devices with their start and end apart: 93, of which 33 were waited for; matrix products, arithmetic and copies ran while one was open for 38% of the time, Pallas kernels for 7%

profile of v4, /device:TPU:4, one launch (start us, length us, event | category | flops | bytes accessed | tf_op | source)
XLA Modules:
  0.0 827.6 jit_solution(6303138942901786831)
XLA Ops:
  22.9 3.4 all-to-all-start
  43.9 3.0 multiply_cosine_fusion
  48.5 10.1 %collective-permute-done.6 = bf16[1024,384]{1,0:T(8,128)(2,1)} collective-permute-done((bf16[1024,384]{1,0:T(8,128)(2,1)S(1)}, bf16[1024,384]{1,0:T(8,128)(2,1)}, u32[]{:S(2)}, u32[]{:S(2)}) %collective-permute-start.6) | collective-permute-done | bytes 786464 | tf_op jit(solution)/shard_map/ppermute | solution.py:151
  58.6 3.1 dynamic_update_slice.48
  69.5 10.2 %collective-permute-done.9 = bf16[1024,384]{1,0:T(8,128)(2,1)} collective-permute-done((bf16[1024,384]{1,0:T(8,128)(2,1)}, bf16[1024,384]{1,0:T(8,128)(2,1)}, u32[]{:S(2)}, u32[]{:S(2)}) %collective-permute-start.9) | collective-permute-done | bytes 786464 | tf_op jit(solution)/shard_map/ppermute | solution.py:151
  90.9 9.0 %collective-permute-done.14 = bf16[1024,384]{1,0:T(8,128)(2,1)} collective-permute-done((bf16[1024,384]{1,0:T(8,128)(2,1)}, bf16[1024,384]{1,0:T(8,128)(2,1)}, u32[]{:S(2)}, u32[]{:S(2)}) %collective-permute-start.14) | collective-permute-done | bytes 786464 | tf_op jit(solution)/shard_map/ppermute | solution.py:151
  110.6 8.7 %fusion.114.refs_0_ = f32[1024,1536]{1,0:T(8,128)S(1)} fusion(bf16[1024,2048]{1,0:T(8,128)(2,1)S(1)} %copy-done.67, bf16[2048,1536]{1,0:T(8,128)(2,1)} %constant_dynamic-update-slice_fusion.96), kind=kOutput, calls=%fused_computation.334 | convolution fusion | flops 6442450944 | bytes 16777216 | tf_op jit(solution)/shard_map/dot_general | solution.py:35
  129.2 3.0 copy-done.1
  132.2 3.8 rope.1
  139.1 5.6 all-to-all-start.1
  147.1 15.1 %attend.1 = bf16[1024,512]{1,0:T(8,128)(2,1)S(1)} custom-call(s32[5]{0:T(128)S(1)} %pad_add_fusion.where_ref, bf16[4,1024,128]{2,1,0:T(8,128)(2,1)S(1)} %get-tuple-element.110.q_ref, bf16[4,1024,128]{2,1,0:T(8,128)(2,1)S(1)} %copy-done.11, bf16[4,1024,128]{2,1,0:T(8,128)(2,1)S(1)} %copy-done.14, s32[1024,1]{1,0:T(8,128)S(1)} %copy.155.row_ref.col_ref, ...), custom_call_target="tpu_custom_call" | custom-call | flops 2147483648 | bytes 4194304 | tf_op jit(solution)/shard_map/attend/pallas_call | solution.py:316
  166.5 3.2 fusion.89
  169.8 5.2 all-to-all-start.2
  175.1 2.8 convolution_convert_fusion.2
  181.2 30.9 %collective-permute-done.28 = bf16[256,2048]{1,0:T(8,128)(2,1)S(1)} collective-permute-done((bf16[256,2048]{1,0:T(8,128)(2,1)S(1)}, bf16[256,2048]{1,0:T(8,128)(2,1)S(1)}, u32[]{:S(2)}, u32[]{:S(2)}) %collective-permute-start.28) | collective-permute-done | bytes 1048608 | tf_op jit(solution)/shard_map/ppermute | solution.py:56
  213.3 3.1 slice_add_fusion.11
  218.6 11.6 %collective-permute-done.27 = bf16[128,2048]{1,0:T(8,128)(2,1)S(1)} collective-permute-done((bf16[128,2048]{1,0:T(8,128)(2,1)S(1)}, bf16[128,2048]{1,0:T(8,128)(2,1)S(1)}, u32[]{:S(2)}, u32[]{:S(2)}) %collective-permute-start.27) | collective-permute-done | bytes 524320 | tf_op jit(solution)/shard_map/ppermute | solution.py:56
  236.6 24.5 %collective-permute-done.30 = bf16[256,2048]{1,0:T(8,128)(2,1)S(1)} collective-permute-done((bf16[256,2048]{1,0:T(8,128)(2,1)S(1)}, bf16[256,2048]{1,0:T(8,128)(2,1)S(1)}, u32[]{:S(2)}, u32[]{:S(2)}) %collective-permute-start.30) | collective-permute-done | bytes 1048608 | tf_op jit(solution)/shard_map/ppermute | solution.py:151
  261.6 24.5 %collective-permute-done.34 = bf16[256,2048]{1,0:T(8,128)(2,1)} collective-permute-done((bf16[256,2048]{1,0:T(8,128)(2,1)S(1)}, bf16[256,2048]{1,0:T(8,128)(2,1)}, u32[]{:S(2)}, u32[]{:S(2)}) %collective-permute-start.34) | collective-permute-done | bytes 1048608 | tf_op jit(solution)/shard_map/ppermute | solution.py:151
  293.5 7.6 fusion.115
  303.7 4.9 fusion.116
  309.4 7.6 fusion.117
  324.1 4.5 fusion.119
  329.3 4.9 fusion.120
  334.9 15.1 %collective-permute-done.33 = bf16[256,2048]{1,0:T(8,128)(2,1)S(1)} collective-permute-done((bf16[256,2048]{1,0:T(8,128)(2,1)S(1)}, bf16[256,2048]{1,0:T(8,128)(2,1)S(1)}, u32[]{:S(2)}, u32[]{:S(2)}) %collective-permute-start.33) | collective-permute-done | bytes 1048608 | tf_op jit(solution)/shard_map/ppermute | solution.py:151
  350.7 4.5 fusion.121
  360.0 17.2 %collective-permute-done.37 = bf16[256,2048]{1,0:T(8,128)(2,1)S(1)} collective-permute-done((bf16[256,2048]{1,0:T(8,128)(2,1)S(1)}, bf16[256,2048]{1,0:T(8,128)(2,1)S(1)}, u32[]{:S(2)}, u32[]{:S(2)}) %collective-permute-start.37) | collective-permute-done | bytes 1048608 | tf_op jit(solution)/shard_map/ppermute | solution.py:151
  377.8 25.6 %collective-permute-done.41 = bf16[256,2048]{1,0:T(8,128)(2,1)S(1)} collective-permute-done((bf16[256,2048]{1,0:T(8,128)(2,1)S(1)}, bf16[256,2048]{1,0:T(8,128)(2,1)S(1)}, u32[]{:S(2)}, u32[]{:S(2)}) %collective-permute-start.41) | collective-permute-done | bytes 1048608 | tf_op jit(solution)/shard_map/ppermute | solution.py:151
  408.6 3.0 multiply_convert_fusion.8
  411.7 10.2 %fusion.63 = f32[512,2048]{1,0:T(8,128)} fusion(bf16[2048,2048]{1,0:T(8,128)(2,1)} %all-gather.3.cloned.1.call-done, bf16[512,1024]{1,0:T(8,128)(2,1)S(1)} %get-tuple-element.148, bf16[512,1024]{1,0:T(8,128)(2,1)S(1)} %get-tuple-element.143), kind=kOutput, calls=%fused_computation.91 | convolution fusion | flops 4299161600 | bytes 14680064 | tf_op jit(solution)/shard_map/dot_general | solution.py:35
  421.9 11.7 %collective-permute-done.44 = bf16[256,2048]{1,0:T(8,128)(2,1)S(1)} collective-permute-done((bf16[256,2048]{1,0:T(8,128)(2,1)S(1)}, bf16[256,2048]{1,0:T(8,128)(2,1)S(1)}, u32[]{:S(2)}, u32[]{:S(2)}) %collective-permute-start.44) | collective-permute-done | bytes 1048608 | tf_op jit(solution)/shard_map/ppermute | solution.py:151
  436.3 6.9 multiply_convert_fusion.6
  444.3 7.2 fusion.67
  451.9 9.0 %collective-permute-done.49 = bf16[256,2048]{1,0:T(8,128)(2,1)S(1)} collective-permute-done((bf16[256,2048]{1,0:T(8,128)(2,1)S(1)}, bf16[256,2048]{1,0:T(8,128)(2,1)S(1)}, u32[]{:S(2)}, u32[]{:S(2)}) %collective-permute-start.49) | collective-permute-done | bytes 1048608 | tf_op jit(solution)/shard_map/ppermute | solution.py:151
  464.1 2.9 multiply_convert_fusion.4
  467.1 7.7 fusion.71
  474.8 14.0 %collective-permute-done.50 = bf16[256,2048]{1,0:T(8,128)(2,1)} collective-permute-done((bf16[256,2048]{1,0:T(8,128)(2,1)S(1)}, bf16[256,2048]{1,0:T(8,128)(2,1)}, u32[]{:S(2)}, u32[]{:S(2)}) %collective-permute-start.50) | collective-permute-done | bytes 1048608 | tf_op jit(solution)/shard_map/ppermute | solution.py:151
  496.1 3.0 multiply_convert_fusion.2
  499.1 7.7 fusion.75
  506.9 13.8 %collective-permute-done.48 = bf16[256,2048]{1,0:T(8,128)(2,1)S(1)} collective-permute-done((bf16[256,2048]{1,0:T(8,128)(2,1)S(1)}, bf16[256,2048]{1,0:T(8,128)(2,1)S(1)}, u32[]{:S(2)}, u32[]{:S(2)}) %collective-permute-start.48) | collective-permute-done | bytes 1048608 | tf_op jit(solution)/shard_map/ppermute | solution.py:151
  524.1 13.5 %fusion.37 = bf16[1024,2048]{1,0:T(8,128)(2,1)} fusion(bf16[512,2048]{1,0:T(8,128)(2,1)} %copy-done.63, bf16[512,2048]{1,0:T(8,128)(2,1)} %copy-done.62, bf16[512,2048]{1,0:T(8,128)(2,1)} %copy-done.64, bf16[512,2048]{1,0:T(8,128)(2,1)S(1)} %copy-done.48, bf16[512,1024]{1,0:T(8,128)(2,1)} %copy-done.53, bf16[512,1024]{1,0:T(8,128)(2,1)} %copy-done.52, ...), kind=kOutput, calls=%fused_computation.35 | convolution fusion | flops 8642363392 | bytes 16777216 | tf_op jit(solution)/shard_map/dot_general | solution.py:35
  537.7 11.0 %collective-permute-done.54 = bf16[256,2048]{1,0:T(8,128)(2,1)} collective-permute-done((bf16[256,2048]{1,0:T(8,128)(2,1)}, bf16[256,2048]{1,0:T(8,128)(2,1)}, u32[]{:S(2)}, u32[]{:S(2)}) %collective-permute-start.54) | collective-permute-done | bytes 1048608 | tf_op jit(solution)/shard_map/ppermute | solution.py:151
  557.5 12.8 %fusion.34 = bf16[2048,1024]{0,1:T(8,128)(2,1)} fusion(bf16[2048,2048]{1,0:T(8,128)(2,1)S(1)} %constant_dynamic-update-slice_fusion.40, bf16[512,1024]{1,0:T(8,128)(2,1)} %copy-done.86, bf16[512,1024]{1,0:T(8,128)(2,1)S(1)} %copy-done.85, bf16[512,1024]{1,0:T(8,128)(2,1)S(1)} %copy-done.81, bf16[512,1024]{1,0:T(8,128)(2,1)} %copy-done.89), kind=kOutput, calls=%fused_computation.34 | convolution fusion | flops 8608808960 | bytes 16777216 | tf_op jit(solution)/shard_map/dot_general | solution.py:35
  570.3 6.4 collective-permute-done.56
  584.2 11.4 %fusion.31 = bf16[2048,1024]{0,1:T(8,128)(2,1)} fusion(bf16[2048,2048]{1,0:T(8,128)(2,1)S(1)} %constant_dynamic-update-slice_fusion.40, bf16[512,1024]{1,0:T(8,128)(2,1)S(1)} %copy-done.83, bf16[512,1024]{1,0:T(8,128)(2,1)S(1)} %copy-done.80, bf16[512,1024]{1,0:T(8,128)(2,1)S(1)} %copy-done.78, bf16[512,1024]{1,0:T(8,128)(2,1)S(1)} %copy-done.88), kind=kOutput, calls=%fused_computation.33 | convolution fusion | flops 8608808960 | bytes 16777216 | tf_op jit(solution)/shard_map/dot_general | solution.py:35
  595.6 4.6 collective-permute-done.59
  603.2 8.4 %pad_maximum_fusion = bf16[2048,2048]{0,1:T(8,128)(2,1)} fusion(bf16[2048,1024]{0,1:T(8,128)(2,1)} %fusion.31, bf16[2048,1024]{0,1:T(8,128)(2,1)} %fusion.34), kind=kLoop, calls=%fused_computation.8 | loop fusion | flops 16777216 | bytes 16777216 | tf_op jit(solution)/shard_map/concatenate | solution.py:672
  615.2 10.3 %collective-permute-done.61 = bf16[256,2048]{1,0:T(8,128)(2,1)} collective-permute-done((bf16[256,2048]{1,0:T(8,128)(2,1)}, bf16[256,2048]{1,0:T(8,128)(2,1)}, u32[]{:S(2)}, u32[]{:S(2)}) %collective-permute-start.61) | collective-permute-done | bytes 1048608 | tf_op jit(solution)/shard_map/ppermute | solution.py:56
  633.9 4.7 all-to-all-start.3
  638.6 5.5 convolution_convert_fusion.3.do_ref
  644.1 26.2 %attend_back.1 = (f32[4,1024,128]{2,1,0:T(8,128)S(1)}, f32[4,1024,128]{2,1,0:T(8,128)S(1)}, f32[4,1024,128]{2,1,0:T(8,128)S(1)}, f32[2,1024]{1,0:T(2,128)S(1)}) custom-call(s32[5]{0:T(128)S(1)} %pad_add_fusion.where_ref, bf16[4,1024,128]{2,1,0:T(8,128)(2,1)S(1)} %get-tuple-element.110.q_ref, bf16[4,1024,128]{2,1,0:T(8,128)(2,1)S(1)} %copy-done.12, ...), custom_call_target="tpu_custom_call" | custom-call | flops 5368709120 | bytes 10485760 | tf_op jit(solution)/shard_map/attend_back/pallas_call | solution.py:385
  677.8 5.0 all-to-all-start.4
  684.1 8.9 %rope_back.1 = (bf16[1024,1536]{1,0:T(8,128)(2,1)}, f32[4,2,128]{2,1,0:T(2,128)}) custom-call(f32[1024,1536]{1,0:T(8,128)} %copy-done, f32[4,1024,128]{2,1,0:T(8,128)} %copy-done.4, f32[4,1024,128]{2,1,0:T(8,128)} %copy-done.5, f32[4,1024,128]{2,1,0:T(8,128)} %copy-done.6, f32[1024,2]{1,0:T(8,128)} %bitcast.135, f32[1024,2]{1,0:T(8,128)} %bitcast.148, ...), custom_call_target="tpu_custom_call" | custom-call | flops 16384000 | bytes 15728640 | tf_op jit(solution)/shard_map/rope_back/pallas_call | solution.py:492
  693.0 8.9 %convolution_convert_fusion = bf16[2048,1536]{1,0:T(8,128)(2,1)S(1)} fusion(bf16[1024,2048]{1,0:T(8,128)(2,1)S(1)} %copy-done.68, bf16[1024,1536]{1,0:T(8,128)(2,1)} %get-tuple-element.164), kind=kOutput, calls=%fused_computation.9 | convolution fusion | flops 6445596672 | bytes 13631488 | tf_op jit(solution)/shard_map/dot_general | solution.py:35
  713.4 4.0 all-to-all-start.5
  717.4 5.9 convolution_convert_fusion.1
  723.3 11.8 %fusion.113 = (bf16[1024,2048]{1,0:T(8,128)(2,1)S(1)}, f32[1024,2048]{1,0:T(8,128)}) fusion(bf16[1024,1536]{1,0:T(8,128)(2,1)} %get-tuple-element.164, bf16[2048,1536]{1,0:T(8,128)(2,1)} %constant_dynamic-update-slice_fusion.96), kind=kOutput, calls=%fused_computation.333 | convolution fusion | flops 6444548096 | bytes 22020096 | tf_op jit(solution)/shard_map/dot_general | solution.py:35
  738.8 2.8 add_convert_fusion.3
  746.6 3.3 copy.168
  751.8 21.8 %collective-permute-done.69 = bf16[1024,384]{1,0:T(8,128)(2,1)} collective-permute-done((bf16[1024,384]{1,0:T(8,128)(2,1)}, bf16[1024,384]{1,0:T(8,128)(2,1)}, u32[]{:S(2)}, u32[]{:S(2)}) %collective-permute-start.69) | collective-permute-done | bytes 786464 | tf_op jit(solution)/shard_map/ppermute | solution.py:151
  776.3 4.1 all-to-all-start.6
  780.5 3.0 slice_add_fusion.1
  789.5 7.6 collective-permute-done.72
  807.3 3.4 collective-permute-done.79
  (585 shorter events, 235.4 us)
Async XLA Ops:
  10.7 21.3 %collective-permute-start.2 = (f32[2304]{0:T(1024)S(1)}, f32[2304]{0:T(1024)S(1)}, u32[]{:S(2)}, u32[]{:S(2)}) collective-permute-start(f32[2304]{0:T(1024)S(1)} %pad_maximum_fusion.16), channel_id=1, source_target_pairs={{0,1},{1,0},{2,3},{3,2},{4,5},{5,4},{6,7},{7,6},{8,9},{9,8},{10,11... | collective-permute-start | bytes 27656 | tf_op jit(solution)/shard_map/ppermute | solution.py:56
  12.2 19.8 %collective-permute-start.3 = (f32[2304]{0:T(1024)S(1)}, f32[2304]{0:T(1024)S(1)}, u32[]{:S(2)}, u32[]{:S(2)}) collective-permute-start(f32[2304]{0:T(1024)S(1)} %pad_maximum_fusion.16), channel_id=1, source_target_pairs={{0,2},{1,3},{2,0},{3,1},{4,6},{5,7},{6,4},{7,5},{8,10},{9,11},{10,... | collective-permute-start | bytes 27656 | tf_op jit(solution)/shard_map/ppermute | solution.py:56
  12.7 19.3 %collective-permute-start.4 = (f32[2304]{0:T(1024)S(1)}, f32[2304]{0:T(1024)S(1)}, u32[]{:S(2)}, u32[]{:S(2)}) collective-permute-start(f32[2304]{0:T(1024)S(1)} %pad_maximum_fusion.16), channel_id=1, source_target_pairs={{0,3},{1,2},{2,1},{3,0},{4,7},{5,6},{6,5},{7,4},{8,11},{9,10},{10,... | collective-permute-start | bytes 27656 | tf_op jit(solution)/shard_map/ppermute | solution.py:56
  26.3 267.2 %all-gather.3.cloned.1.call-start = ((), (), s32[]{:S(2)}) async-start(), calls=%async_computation.10 | async-start | bytes 10485760 | tf_op jit(solution)/shard_map/all_gather | solution.py:571
  36.6 43.9 %collective-permute-start.11 = (bf16[1024,384]{1,0:T(8,128)(2,1)S(1)}, bf16[1024,384]{1,0:T(8,128)(2,1)}, u32[]{:S(2)}, u32[]{:S(2)}) collective-permute-start(bf16[1024,384]{1,0:T(8,128)(2,1)S(1)} %bitcast.143), channel_id=1, source_target_pairs={{0,4},{4,0},{8,12},{12,8},{16,20},{20,16},{24,28},{28,24},{1,5},{5... | collective-permute-start | bytes 2359304 | tf_op jit(solution)/shard_map/ppermute | solution.py:155
  36.8 21.7 %collective-permute-start.6 = (bf16[1024,384]{1,0:T(8,128)(2,1)S(1)}, bf16[1024,384]{1,0:T(8,128)(2,1)}, u32[]{:S(2)}, u32[]{:S(2)}) collective-permute-start(bf16[1024,384]{1,0:T(8,128)(2,1)S(1)} %bitcast.144), channel_id=1, source_target_pairs={{0,8},{4,12},{8,16},{12,20},{16,24},{20,28},{24,0},{28,4},{1,9},{5... | collective-permute-start | bytes 2359304 | tf_op jit(solution)/shard_map/ppermute | solution.py:151
  41.3 20.4 %collective-permute-start.7 = (bf16[128,2048]{1,0:T(8,128)(2,1)}, bf16[128,2048]{1,0:T(8,128)(2,1)}, u32[]{:S(2)}, u32[]{:S(2)}) collective-permute-start(bf16[128,2048]{1,0:T(8,128)(2,1)} %get-tuple-element.294), channel_id=1, source_target_pairs={{0,1},{1,0},{2,3},{3,2},{4,5},{5,4},{6,7},{7,6},{8,9},{9,8},{10,11... | collective-permute-start | bytes 1572872 | tf_op jit(solution)/shard_map/ppermute | solution.py:56
  43.5 21.6 %collective-permute-start.5 = (bf16[128,2048]{1,0:T(8,128)(2,1)}, bf16[128,2048]{1,0:T(8,128)(2,1)}, u32[]{:S(2)}, u32[]{:S(2)}) collective-permute-start(bf16[128,2048]{1,0:T(8,128)(2,1)} %get-tuple-element.296), channel_id=1, source_target_pairs={{0,2},{1,3},{2,0},{3,1},{4,6},{5,7},{6,4},{7,5},{8,10},{9,11},{10,... | collective-permute-start | bytes 1572872 | tf_op jit(solution)/shard_map/ppermute | solution.py:56
  58.6 21.1 %collective-permute-start.9 = (bf16[1024,384]{1,0:T(8,128)(2,1)}, bf16[1024,384]{1,0:T(8,128)(2,1)}, u32[]{:S(2)}, u32[]{:S(2)}) collective-permute-start(bf16[1024,384]{1,0:T(8,128)(2,1)} %collective-permute-done.6), channel_id=1, source_target_pairs={{0,8},{4,12},{8,16},{12,20},{16,24},{20,28},{24,0},{28,4},{1,9},{5... | collective-permute-start | bytes 2359304 | tf_op jit(solution)/shard_map/ppermute | solution.py:151
  64.0 38.4 %collective-permute-start.10 = (bf16[256,2048]{1,0:T(8,128)(2,1)}, bf16[256,2048]{1,0:T(8,128)(2,1)}, u32[]{:S(2)}, u32[]{:S(2)}) collective-permute-start(bf16[256,2048]{1,0:T(8,128)(2,1)} %pad_maximum_fusion.7), channel_id=1, source_target_pairs={{0,2},{1,3},{2,0},{3,1},{4,6},{5,7},{6,4},{7,5},{8,10},{9,11},{10,... | collective-permute-start | bytes 3145736 | tf_op jit(solution)/shard_map/ppermute | solution.py:56
  66.4 24.5 %collective-permute-start.8 = (bf16[256,2048]{1,0:T(8,128)(2,1)S(1)}, bf16[256,2048]{1,0:T(8,128)(2,1)}, u32[]{:S(2)}, u32[]{:S(2)}) collective-permute-start(bf16[256,2048]{1,0:T(8,128)(2,1)S(1)} %pad_maximum_fusion.6), channel_id=1, source_target_pairs={{0,1},{1,0},{2,3},{3,2},{4,5},{5,4},{6,7},{7,6},{8,9},{9,8},{10,11... | collective-permute-start | bytes 3145736 | tf_op jit(solution)/shard_map/ppermute | solution.py:56
  67.6 19.2 %collective-permute-start.12 = (bf16[1024,384]{1,0:T(8,128)(2,1)}, bf16[1024,384]{1,0:T(8,128)(2,1)S(1)}, u32[]{:S(2)}, u32[]{:S(2)}) collective-permute-start(bf16[1024,384]{1,0:T(8,128)(2,1)} %collective-permute-done.6), channel_id=1, source_target_pairs={{0,4},{4,0},{8,12},{12,8},{16,20},{20,16},{24,28},{28,24},{1,5},{5... | collective-permute-start | bytes 2359304 | tf_op jit(solution)/shard_map/ppermute | solution.py:155
  79.7 20.2 %collective-permute-start.14 = (bf16[1024,384]{1,0:T(8,128)(2,1)}, bf16[1024,384]{1,0:T(8,128)(2,1)}, u32[]{:S(2)}, u32[]{:S(2)}) collective-permute-start(bf16[1024,384]{1,0:T(8,128)(2,1)} %collective-permute-done.9), channel_id=1, source_target_pairs={{0,8},{4,12},{8,16},{12,20},{16,24},{20,28},{24,0},{28,4},{1,9},{5... | collective-permute-start | bytes 2359304 | tf_op jit(solution)/shard_map/ppermute | solution.py:151
  84.6 20.9 %collective-permute-start.13 = (bf16[1024,384]{1,0:T(8,128)(2,1)}, bf16[1024,384]{1,0:T(8,128)(2,1)S(1)}, u32[]{:S(2)}, u32[]{:S(2)}) collective-permute-start(bf16[1024,384]{1,0:T(8,128)(2,1)} %collective-permute-done.9), channel_id=1, source_target_pairs={{0,4},{4,0},{8,12},{12,8},{16,20},{20,16},{24,28},{28,24},{1,5},{5... | collective-permute-start | bytes 2359304 | tf_op jit(solution)/shard_map/ppermute | solution.py:155
  105.1 20.4 %collective-permute-start.20 = (bf16[512,256]{1,0:T(8,128)(2,1)S(1)}, bf16[512,256]{1,0:T(8,128)(2,1)}, u32[]{:S(2)}, u32[]{:S(2)}) collective-permute-start(bf16[512,256]{1,0:T(8,128)(2,1)S(1)} %bitcast.152), channel_id=1, source_target_pairs={{0,8},{4,12},{8,16},{12,20},{16,24},{20,28},{24,0},{28,4},{1,9},{5... | collective-permute-start | bytes 786440 | tf_op jit(solution)/shard_map/ppermute | solution.py:151
  125.5 19.1 %collective-permute-start.22 = (bf16[512,256]{1,0:T(8,128)(2,1)}, bf16[512,256]{1,0:T(8,128)(2,1)S(1)}, u32[]{:S(2)}, u32[]{:S(2)}) collective-permute-start(bf16[512,256]{1,0:T(8,128)(2,1)} %collective-permute-done.20), channel_id=1, source_target_pairs={{0,8},{4,12},{8,16},{12,20},{16,24},{20,28},{24,0},{28,4},{1,9},{5... | collective-permute-start | bytes 786440 | tf_op jit(solution)/shard_map/ppermute | solution.py:151
  125.8 36.5 %collective-permute-start.21 = (bf16[512,256]{1,0:T(8,128)(2,1)}, bf16[512,256]{1,0:T(8,128)(2,1)}, u32[]{:S(2)}, u32[]{:S(2)}) collective-permute-start(bf16[512,256]{1,0:T(8,128)(2,1)} %collective-permute-done.20), channel_id=1, source_target_pairs={{0,4},{4,0},{8,12},{12,8},{16,20},{20,16},{24,28},{28,24},{1,5},{5... | collective-permute-start | bytes 786440 | tf_op jit(solution)/shard_map/ppermute | solution.py:155
  139.1 30.8 %all-to-all-start.1 = ((bf16[4,2,256,256]{3,2,1,0:T(8,128)(2,1)}), bf16[4,2,256,256]{3,2,1,0:T(8,128)(2,1)}, u32[]{:S(2)}, u32[]{:S(2)}) async-start(bf16[4,2,256,256]{3,2,1,0:T(8,128)(2,1)} %copy.156), calls=%async_computation.1 | async-start | bytes 2097152 | tf_op jit(solution)/shard_map/all_to_all | solution.py:122
  144.6 18.8 %collective-permute-start.24 = (bf16[512,256]{1,0:T(8,128)(2,1)S(1)}, bf16[512,256]{1,0:T(8,128)(2,1)S(1)}, u32[]{:S(2)}, u32[]{:S(2)}) collective-permute-start(bf16[512,256]{1,0:T(8,128)(2,1)S(1)} %collective-permute-done.22), channel_id=1, source_target_pairs={{0,8},{4,12},{8,16},{12,20},{16,24},{20,28},{24,0},{28,4},{1,9},{5... | collective-permute-start | bytes 786440 | tf_op jit(solution)/shard_map/ppermute | solution.py:151
  144.6 19.4 %collective-permute-start.23 = (bf16[512,256]{1,0:T(8,128)(2,1)S(1)}, bf16[512,256]{1,0:T(8,128)(2,1)S(1)}, u32[]{:S(2)}, u32[]{:S(2)}) collective-permute-start(bf16[512,256]{1,0:T(8,128)(2,1)S(1)} %collective-permute-done.22), channel_id=1, source_target_pairs={{0,4},{4,0},{8,12},{12,8},{16,20},{20,16},{24,28},{28,24},{1,5},{5... | collective-permute-start | bytes 786440 | tf_op jit(solution)/shard_map/ppermute | solution.py:155
  169.8 42.2 %all-to-all-start.2 = ((bf16[8,256,256]{2,1,0:T(8,128)(2,1)}), bf16[8,256,256]{2,1,0:T(8,128)(2,1)}, u32[]{:S(2)}, u32[]{:S(2)}) async-start(bf16[8,256,256]{2,1,0:T(8,128)(2,1)} %bitcast.19), calls=%async_computation.2 | async-start | bytes 2097152 | tf_op jit(solution)/shard_map/all_to_all | solution.py:122
  175.1 128.7 %all-gather.5.cloned.1.call-start = ((), (), s32[]{:S(2)}) async-start(), calls=%async_computation.11 | async-start | bytes 5242880 | tf_op jit(solution)/shard_map/all_gather | solution.py:617
  179.1 32.9 %collective-permute-start.28 = (bf16[256,2048]{1,0:T(8,128)(2,1)S(1)}, bf16[256,2048]{1,0:T(8,128)(2,1)S(1)}, u32[]{:S(2)}, u32[]{:S(2)}) collective-permute-start(bf16[256,2048]{1,0:T(8,128)(2,1)S(1)} %get-tuple-element.287), channel_id=1, source_target_pairs={{0,2},{1,3},{2,0},{3,1},{4,6},{5,7},{6,4},{7,5},{8,10},{9,11},{10,... | collective-permute-start | bytes 3145736 | tf_op jit(solution)/shard_map/ppermute | solution.py:56
  179.4 33.9 %collective-permute-start.26 = (bf16[256,2048]{1,0:T(8,128)(2,1)}, bf16[256,2048]{1,0:T(8,128)(2,1)}, u32[]{:S(2)}, u32[]{:S(2)}) collective-permute-start(bf16[256,2048]{1,0:T(8,128)(2,1)} %get-tuple-element.286), channel_id=1, source_target_pairs={{0,1},{1,0},{2,3},{3,2},{4,5},{5,4},{6,7},{7,6},{8,9},{9,8},{10,11... | collective-permute-start | bytes 3145736 | tf_op jit(solution)/shard_map/ppermute | solution.py:56
  235.1 390.4 %reduce-scatter.4.cloned.1.call-start = ((), (), s32[]{:S(2)}) async-start(), calls=%async_computation.12 | async-start | bytes 5242880 | tf_op jit(solution)/shard_map/reduce_scatter | solution.py:658
  235.1 25.9 %collective-permute-start.30 = (bf16[256,2048]{1,0:T(8,128)(2,1)S(1)}, bf16[256,2048]{1,0:T(8,128)(2,1)S(1)}, u32[]{:S(2)}, u32[]{:S(2)}) collective-permute-start(bf16[256,2048]{1,0:T(8,128)(2,1)S(1)} %fusion.80), channel_id=1, source_target_pairs={{0,8},{4,12},{8,16},{12,20},{16,24},{20,28},{24,0},{28,4},{1,9},{5... | collective-permute-start | bytes 3145736 | tf_op jit(solution)/shard_map/ppermute | solution.py:151
  261.0 25.0 %collective-permute-start.34 = (bf16[256,2048]{1,0:T(8,128)(2,1)S(1)}, bf16[256,2048]{1,0:T(8,128)(2,1)}, u32[]{:S(2)}, u32[]{:S(2)}) collective-permute-start(bf16[256,2048]{1,0:T(8,128)(2,1)S(1)} %collective-permute-done.30), channel_id=1, source_target_pairs={{0,8},{4,12},{8,16},{12,20},{16,24},{20,28},{24,0},{28,4},{1,9},{5... | collective-permute-start | bytes 3145736 | tf_op jit(solution)/shard_map/ppermute | solution.py:151
  261.0 26.2 %collective-permute-start.42 = (bf16[256,2048]{1,0:T(8,128)(2,1)S(1)}, bf16[256,2048]{1,0:T(8,128)(2,1)S(1)}, u32[]{:S(2)}, u32[]{:S(2)}) collective-permute-start(bf16[256,2048]{1,0:T(8,128)(2,1)S(1)} %fusion.80), channel_id=1, source_target_pairs={{0,4},{4,0},{8,12},{12,8},{16,20},{20,16},{24,28},{28,24},{1,5},{5... | collective-permute-start | bytes 3145736 | tf_op jit(solution)/shard_map/ppermute | solution.py:155
  261.0 30.3 %collective-permute-start.31 = (bf16[256,2048]{1,0:T(8,128)(2,1)S(1)}, bf16[256,2048]{1,0:T(8,128)(2,1)S(1)}, u32[]{:S(2)}, u32[]{:S(2)}) collective-permute-start(bf16[256,2048]{1,0:T(8,128)(2,1)S(1)} %collective-permute-done.30), channel_id=1, source_target_pairs={{0,4},{4,0},{8,12},{12,8},{16,20},{20,16},{24,28},{28,24},{1,5},{5... | collective-permute-start | bytes 3145736 | tf_op jit(solution)/shard_map/ppermute | solution.py:155
  288.7 28.6 %collective-permute-start.38 = (bf16[256,2048]{1,0:T(8,128)(2,1)}, bf16[256,2048]{1,0:T(8,128)(2,1)}, u32[]{:S(2)}, u32[]{:S(2)}) collective-permute-start(bf16[256,2048]{1,0:T(8,128)(2,1)} %collective-permute-done.34), channel_id=1, source_target_pairs={{0,8},{4,12},{8,16},{12,20},{16,24},{20,28},{24,0},{28,4},{1,9},{5... | collective-permute-start | bytes 3145736 | tf_op jit(solution)/shard_map/ppermute | solution.py:151
  322.1 27.9 %collective-permute-start.33 = (bf16[256,2048]{1,0:T(8,128)(2,1)S(1)}, bf16[256,2048]{1,0:T(8,128)(2,1)S(1)}, u32[]{:S(2)}, u32[]{:S(2)}) collective-permute-start(bf16[256,2048]{1,0:T(8,128)(2,1)S(1)} %fusion.62), channel_id=1, source_target_pairs={{0,8},{4,12},{8,16},{12,20},{16,24},{20,28},{24,0},{28,4},{1,9},{5... | collective-permute-start | bytes 3145736 | tf_op jit(solution)/shard_map/ppermute | solution.py:151
  334.4 25.6 %collective-permute-start.40 = (bf16[256,2048]{1,0:T(8,128)(2,1)S(1)}, bf16[256,2048]{1,0:T(8,128)(2,1)S(1)}, u32[]{:S(2)}, u32[]{:S(2)}) collective-permute-start(bf16[256,2048]{1,0:T(8,128)(2,1)S(1)} %slice.816), channel_id=1, source_target_pairs={{0,4},{4,0},{8,12},{12,8},{16,20},{20,16},{24,28},{28,24},{1,5},{5... | collective-permute-start | bytes 3145736 | tf_op jit(solution)/shard_map/ppermute | solution.py:155
  350.5 26.7 %collective-permute-start.37 = (bf16[256,2048]{1,0:T(8,128)(2,1)S(1)}, bf16[256,2048]{1,0:T(8,128)(2,1)S(1)}, u32[]{:S(2)}, u32[]{:S(2)}) collective-permute-start(bf16[256,2048]{1,0:T(8,128)(2,1)S(1)} %fusion.61), channel_id=1, source_target_pairs={{0,8},{4,12},{8,16},{12,20},{16,24},{20,28},{24,0},{28,4},{1,9},{5... | collective-permute-start | bytes 3145736 | tf_op jit(solution)/shard_map/ppermute | solution.py:151
  359.9 17.9 %collective-permute-start.43 = (bf16[256,2048]{1,0:T(8,128)(2,1)S(1)}, bf16[256,2048]{1,0:T(8,128)(2,1)S(1)}, u32[]{:S(2)}, u32[]{:S(2)}) collective-permute-start(bf16[256,2048]{1,0:T(8,128)(2,1)S(1)} %slice.815), channel_id=1, source_target_pairs={{0,4},{4,0},{8,12},{12,8},{16,20},{20,16},{24,28},{28,24},{1,5},{5... | collective-permute-start | bytes 3145736 | tf_op jit(solution)/shard_map/ppermute | solution.py:155
  377.7 25.7 %collective-permute-start.41 = (bf16[256,2048]{1,0:T(8,128)(2,1)S(1)}, bf16[256,2048]{1,0:T(8,128)(2,1)S(1)}, u32[]{:S(2)}, u32[]{:S(2)}) collective-permute-start(bf16[256,2048]{1,0:T(8,128)(2,1)S(1)} %fusion.59), channel_id=1, source_target_pairs={{0,8},{4,12},{8,16},{12,20},{16,24},{20,28},{24,0},{28,4},{1,9},{5... | collective-permute-start | bytes 3145736 | tf_op jit(solution)/shard_map/ppermute | solution.py:151
  406.0 27.6 %collective-permute-start.44 = (bf16[256,2048]{1,0:T(8,128)(2,1)S(1)}, bf16[256,2048]{1,0:T(8,128)(2,1)S(1)}, u32[]{:S(2)}, u32[]{:S(2)}) collective-permute-start(bf16[256,2048]{1,0:T(8,128)(2,1)S(1)} %fusion.46), channel_id=1, source_target_pairs={{0,8},{4,12},{8,16},{12,20},{16,24},{20,28},{24,0},{28,4},{1,9},{5... | collective-permute-start | bytes 3145736 | tf_op jit(solution)/shard_map/ppermute | solution.py:151
  433.6 27.4 %collective-permute-start.49 = (bf16[256,2048]{1,0:T(8,128)(2,1)S(1)}, bf16[256,2048]{1,0:T(8,128)(2,1)S(1)}, u32[]{:S(2)}, u32[]{:S(2)}) collective-permute-start(bf16[256,2048]{1,0:T(8,128)(2,1)S(1)} %collective-permute-done.44), channel_id=1, source_target_pairs={{0,8},{4,12},{8,16},{12,20},{16,24},{20,28},{24,0},{28,4},{1,9},{5... | collective-permute-start | bytes 3145736 | tf_op jit(solution)/shard_map/ppermute | solution.py:151
  460.9 27.9 %collective-permute-start.50 = (bf16[256,2048]{1,0:T(8,128)(2,1)S(1)}, bf16[256,2048]{1,0:T(8,128)(2,1)}, u32[]{:S(2)}, u32[]{:S(2)}) collective-permute-start(bf16[256,2048]{1,0:T(8,128)(2,1)S(1)} %collective-permute-done.49), channel_id=1, source_target_pairs={{0,8},{4,12},{8,16},{12,20},{16,24},{20,28},{24,0},{28,4},{1,9},{5... | collective-permute-start | bytes 3145736 | tf_op jit(solution)/shard_map/ppermute | solution.py:151
  491.6 85.0 %collective-permute-start.57 = (bf16[256,2048]{1,0:T(8,128)(2,1)}, bf16[256,2048]{1,0:T(8,128)(2,1)}, u32[]{:S(2)}, u32[]{:S(2)}) collective-permute-start(bf16[256,2048]{1,0:T(8,128)(2,1)} %slice.811), channel_id=1, source_target_pairs={{0,4},{4,0},{8,12},{12,8},{16,20},{20,16},{24,28},{28,24},{1,5},{5... | collective-permute-start | bytes 3145736 | tf_op jit(solution)/shard_map/ppermute | solution.py:155
  493.6 27.0 %collective-permute-start.48 = (bf16[256,2048]{1,0:T(8,128)(2,1)S(1)}, bf16[256,2048]{1,0:T(8,128)(2,1)S(1)}, u32[]{:S(2)}, u32[]{:S(2)}) collective-permute-start(bf16[256,2048]{1,0:T(8,128)(2,1)S(1)} %copy-done.60), channel_id=1, source_target_pairs={{0,8},{4,12},{8,16},{12,20},{16,24},{20,28},{24,0},{28,4},{1,9},{5... | collective-permute-start | bytes 3145736 | tf_op jit(solution)/shard_map/ppermute | solution.py:151
  493.7 26.9 %collective-permute-start.53 = (bf16[256,2048]{1,0:T(8,128)(2,1)S(1)}, bf16[256,2048]{1,0:T(8,128)(2,1)S(1)}, u32[]{:S(2)}, u32[]{:S(2)}) collective-permute-start(bf16[256,2048]{1,0:T(8,128)(2,1)S(1)} %slice.813), channel_id=1, source_target_pairs={{0,4},{4,0},{8,12},{12,8},{16,20},{20,16},{24,28},{28,24},{1,5},{5... | collective-permute-start | bytes 3145736 | tf_op jit(solution)/shard_map/ppermute | solution.py:155
  522.2 26.5 %collective-permute-start.54 = (bf16[256,2048]{1,0:T(8,128)(2,1)}, bf16[256,2048]{1,0:T(8,128)(2,1)}, u32[]{:S(2)}, u32[]{:S(2)}) collective-permute-start(bf16[256,2048]{1,0:T(8,128)(2,1)} %fusion.55), channel_id=1, source_target_pairs={{0,8},{4,12},{8,16},{12,20},{16,24},{20,28},{24,0},{28,4},{1,9},{5... | collective-permute-start | bytes 3145736 | tf_op jit(solution)/shard_map/ppermute | solution.py:151
  523.3 25.4 %collective-permute-start.55 = (bf16[256,2048]{1,0:T(8,128)(2,1)}, bf16[256,2048]{1,0:T(8,128)(2,1)}, u32[]{:S(2)}, u32[]{:S(2)}) collective-permute-start(bf16[256,2048]{1,0:T(8,128)(2,1)} %slice.812), channel_id=1, source_target_pairs={{0,4},{4,0},{8,12},{12,8},{16,20},{20,16},{24,28},{28,24},{1,5},{5... | collective-permute-start | bytes 3145736 | tf_op jit(solution)/shard_map/ppermute | solution.py:155
  537.6 201.2 %reduce-scatter.6.cloned.1.call-start = ((), (), s32[]{:S(2)}) async-start(), calls=%async_computation.13 | async-start | bytes 10485760 | tf_op jit(solution)/shard_map/reduce_scatter | solution.py:675
  551.4 25.3 %collective-permute-start.56 = (bf16[256,2048]{1,0:T(8,128)(2,1)S(1)}, bf16[256,2048]{1,0:T(8,128)(2,1)S(1)}, u32[]{:S(2)}, u32[]{:S(2)}) collective-permute-start(bf16[256,2048]{1,0:T(8,128)(2,1)S(1)} %fusion.53), channel_id=1, source_target_pairs={{0,8},{4,12},{8,16},{12,20},{16,24},{20,28},{24,0},{28,4},{1,9},{5... | collective-permute-start | bytes 3145736 | tf_op jit(solution)/shard_map/ppermute | solution.py:151
  582.0 18.2 %collective-permute-start.59 = (bf16[128,2048]{1,0:T(8,128)(2,1)S(1)}, bf16[128,2048]{1,0:T(8,128)(2,1)S(1)}, u32[]{:S(2)}, u32[]{:S(2)}) collective-permute-start(bf16[128,2048]{1,0:T(8,128)(2,1)S(1)} %get-tuple-element.291), channel_id=1, source_target_pairs={{0,1},{1,0},{2,3},{3,2},{4,5},{5,4},{6,7},{7,6},{8,9},{9,8},{10,11... | collective-permute-start | bytes 1572872 | tf_op jit(solution)/shard_map/ppermute | solution.py:56
  582.5 19.2 %collective-permute-start.58 = (bf16[128,2048]{1,0:T(8,128)(2,1)S(1)}, bf16[128,2048]{1,0:T(8,128)(2,1)S(1)}, u32[]{:S(2)}, u32[]{:S(2)}) collective-permute-start(bf16[128,2048]{1,0:T(8,128)(2,1)S(1)} %get-tuple-element.293), channel_id=1, source_target_pairs={{0,2},{1,3},{2,0},{3,1},{4,6},{5,7},{6,4},{7,5},{8,10},{9,11},{10,... | collective-permute-start | bytes 1572872 | tf_op jit(solution)/shard_map/ppermute | solution.py:56
  601.2 24.3 %collective-permute-start.61 = (bf16[256,2048]{1,0:T(8,128)(2,1)}, bf16[256,2048]{1,0:T(8,128)(2,1)}, u32[]{:S(2)}, u32[]{:S(2)}) collective-permute-start(bf16[256,2048]{1,0:T(8,128)(2,1)} %pad_maximum_fusion.10), channel_id=1, source_target_pairs={{0,2},{1,3},{2,0},{3,1},{4,6},{5,7},{6,4},{7,5},{8,10},{9,11},{10,... | collective-permute-start | bytes 3145736 | tf_op jit(solution)/shard_map/ppermute | solution.py:56
  602.9 24.1 %collective-permute-start.60 = (bf16[256,2048]{1,0:T(8,128)(2,1)}, bf16[256,2048]{1,0:T(8,128)(2,1)}, u32[]{:S(2)}, u32[]{:S(2)}) collective-permute-start(bf16[256,2048]{1,0:T(8,128)(2,1)} %pad_maximum_fusion.9), channel_id=1, source_target_pairs={{0,1},{1,0},{2,3},{3,2},{4,5},{5,4},{6,7},{7,6},{8,9},{9,8},{10,11... | collective-permute-start | bytes 3145736 | tf_op jit(solution)/shard_map/ppermute | solution.py:56
  633.9 40.3 %all-to-all-start.3 = ((bf16[8,256,256]{2,1,0:T(8,128)(2,1)}), bf16[8,256,256]{2,1,0:T(8,128)(2,1)}, u32[]{:S(2)}, u32[]{:S(2)}) async-start(bf16[8,256,256]{2,1,0:T(8,128)(2,1)} %bitcast.132), calls=%async_computation.4 | async-start | bytes 2097152 | tf_op jit(solution)/shard_map/all_to_all | solution.py:122
  677.8 28.9 %all-to-all-start.4 = ((bf16[4,2,256,256]{3,2,1,0:T(8,128)(2,1)}), bf16[4,2,256,256]{3,2,1,0:T(8,128)(2,1)S(1)}, u32[]{:S(2)}, u32[]{:S(2)}) async-start(bf16[4,2,256,256]{3,2,1,0:T(8,128)(2,1)} %bitcast.27), calls=%async_computation.5 | async-start | bytes 2097152 | tf_op jit(solution)/shard_map/all_to_all | solution.py:122
  705.5 33.3 %collective-permute-start.68 = (bf16[1024,384]{1,0:T(8,128)(2,1)}, bf16[1024,384]{1,0:T(8,128)(2,1)}, u32[]{:S(2)}, u32[]{:S(2)}) collective-permute-start(bf16[1024,384]{1,0:T(8,128)(2,1)} %get-tuple-element.266), channel_id=1, source_target_pairs={{0,4},{4,0},{8,12},{12,8},{16,20},{20,16},{24,28},{28,24},{1,5},{5... | collective-permute-start | bytes 2359304 | tf_op jit(solution)/shard_map/ppermute | solution.py:155
  706.1 45.6 %collective-permute-start.70 = (bf16[1024,384]{1,0:T(8,128)(2,1)}, bf16[1024,384]{1,0:T(8,128)(2,1)}, u32[]{:S(2)}, u32[]{:S(2)}) collective-permute-start(bf16[1024,384]{1,0:T(8,128)(2,1)} %get-tuple-element.265), channel_id=1, source_target_pairs={{0,4},{4,0},{8,12},{12,8},{16,20},{20,16},{24,28},{28,24},{1,5},{5... | collective-permute-start | bytes 2359304 | tf_op jit(solution)/shard_map/ppermute | solution.py:155
  706.2 90.9 %collective-permute-start.73 = (bf16[1024,384]{1,0:T(8,128)(2,1)}, bf16[1024,384]{1,0:T(8,128)(2,1)}, u32[]{:S(2)}, u32[]{:S(2)}) collective-permute-start(bf16[1024,384]{1,0:T(8,128)(2,1)} %get-tuple-element.264), channel_id=1, source_target_pairs={{0,4},{4,0},{8,12},{12,8},{16,20},{20,16},{24,28},{28,24},{1,5},{5... | collective-permute-start | bytes 2359304 | tf_op jit(solution)/shard_map/ppermute | solution.py:155
  710.6 26.3 %collective-permute-start.67 = (bf16[1024,384]{1,0:T(8,128)(2,1)}, bf16[1024,384]{1,0:T(8,128)(2,1)}, u32[]{:S(2)}, u32[]{:S(2)}) collective-permute-start(bf16[1024,384]{1,0:T(8,128)(2,1)} %add_convert_fusion.4), channel_id=1, source_target_pairs={{0,8},{4,12},{8,16},{12,20},{16,24},{20,28},{24,0},{28,4},{1,9},{5... | collective-permute-start | bytes 2359304 | tf_op jit(solution)/shard_map/ppermute | solution.py:151
  713.4 23.4 %all-to-all-start.5 = ((f32[4,2,640]{2,1,0:T(2,128)}), f32[4,2,640]{2,1,0:T(2,128)S(1)}, u32[]{:S(2)}, u32[]{:S(2)}) async-start(f32[4,2,640]{2,1,0:T(2,128)} %pad_maximum_fusion.15), calls=%async_computation.6 | async-start | bytes 40960 | tf_op jit(solution)/shard_map/all_to_all | solution.py:122
  717.4 59.0 %reduce-scatter.8.cloned.1.call-start = ((), (), s32[]{:S(2)}) async-start(), calls=%async_computation.14 | async-start | bytes 2359296 | tf_op jit(solution)/shard_map/reduce_scatter | solution.py:697
  736.7 43.8 %collective-permute-start.74 = (bf16[256,2048]{1,0:T(8,128)(2,1)}, bf16[256,2048]{1,0:T(8,128)(2,1)S(1)}, u32[]{:S(2)}, u32[]{:S(2)}) collective-permute-start(bf16[256,2048]{1,0:T(8,128)(2,1)} %get-tuple-element.277), channel_id=1, source_target_pairs={{0,2},{1,3},{2,0},{3,1},{4,6},{5,7},{6,4},{7,5},{8,10},{9,11},{10,... | collective-permute-start | bytes 3145736 | tf_op jit(solution)/shard_map/ppermute | solution.py:56
  736.9 43.6 %collective-permute-start.66 = (bf16[256,2048]{1,0:T(8,128)(2,1)}, bf16[256,2048]{1,0:T(8,128)(2,1)}, u32[]{:S(2)}, u32[]{:S(2)}) collective-permute-start(bf16[256,2048]{1,0:T(8,128)(2,1)} %get-tuple-element.276), channel_id=1, source_target_pairs={{0,1},{1,0},{2,3},{3,2},{4,5},{5,4},{6,7},{7,6},{8,9},{9,8},{10,11... | collective-permute-start | bytes 3145736 | tf_op jit(solution)/shard_map/ppermute | solution.py:56
  741.7 31.9 %collective-permute-start.69 = (bf16[1024,384]{1,0:T(8,128)(2,1)}, bf16[1024,384]{1,0:T(8,128)(2,1)}, u32[]{:S(2)}, u32[]{:S(2)}) collective-permute-start(bf16[1024,384]{1,0:T(8,128)(2,1)} %add_convert_fusion.3), channel_id=1, source_target_pairs={{0,8},{4,12},{8,16},{12,20},{16,24},{20,28},{24,0},{28,4},{1,9},{5... | collective-permute-start | bytes 2359304 | tf_op jit(solution)/shard_map/ppermute | solution.py:151
  776.3 20.8 %collective-permute-start.72 = (bf16[1024,384]{1,0:T(8,128)(2,1)}, bf16[1024,384]{1,0:T(8,128)(2,1)}, u32[]{:S(2)}, u32[]{:S(2)}) collective-permute-start(bf16[1024,384]{1,0:T(8,128)(2,1)} %add_convert_fusion.2), channel_id=1, source_target_pairs={{0,8},{4,12},{8,16},{12,20},{16,24},{20,28},{24,0},{28,4},{1,9},{5... | collective-permute-start | bytes 2359304 | tf_op jit(solution)/shard_map/ppermute | solution.py:151
  785.8 18.6 %collective-permute-start.71 = (bf16[128,2048]{1,0:T(8,128)(2,1)}, bf16[128,2048]{1,0:T(8,128)(2,1)}, u32[]{:S(2)}, u32[]{:S(2)}) collective-permute-start(bf16[128,2048]{1,0:T(8,128)(2,1)} %slice.820), channel_id=1, source_target_pairs={{0,2},{1,3},{2,0},{3,1},{4,6},{5,7},{6,4},{7,5},{8,10},{9,11},{10,... | collective-permute-start | bytes 1572872 | tf_op jit(solution)/shard_map/ppermute | solution.py:56
  786.7 19.1 %collective-permute-start.75 = (bf16[128,2048]{1,0:T(8,128)(2,1)}, bf16[128,2048]{1,0:T(8,128)(2,1)}, u32[]{:S(2)}, u32[]{:S(2)}) collective-permute-start(bf16[128,2048]{1,0:T(8,128)(2,1)} %slice.819), channel_id=1, source_target_pairs={{0,1},{1,0},{2,3},{3,2},{4,5},{5,4},{6,7},{7,6},{8,9},{9,8},{10,11... | collective-permute-start | bytes 1572872 | tf_op jit(solution)/shard_map/ppermute | solution.py:56
  799.4 16.5 %collective-permute-start.76 = (bf16[512,384]{0,1:T(8,128)(2,1)S(1)}, bf16[512,384]{0,1:T(8,128)(2,1)}, u32[]{:S(2)}, u32[]{:S(2)}) collective-permute-start(bf16[512,384]{0,1:T(8,128)(2,1)S(1)} %bitcast.156), channel_id=1, source_target_pairs={{0,0},{1,1},{4,2},{5,3},{2,4},{3,5},{6,6},{7,7},{8,8},{9,9},{12,10... | collective-permute-start | bytes 1179656 | tf_op jit(solution)/shard_map/ppermute | solution.py:271
  (121 other events, 945.1 us)
Sparse Core Ops, SparseCore 0:
  91.0 108.3 all-gather.2
  235.2 52.4 all-gather.4
  537.7 58.5 reduce-scatter.3
  631.8 91.8 reduce-scatter.5
  725.8 43.1 reduce-scatter.7

commit v5 on v4

--- a/solution.py
+++ b/solution.py
@@ -606,7 +606,7 @@
             out_w = lax.dynamic_update_slice_in_dim(out_w, value, start, 1)
     rows = S * span // 2
     a_send = mm(o[rows:], out_w)
-    a_keep = mm(o[:rows], out_w)
+    a_keep = mm(after(o[:rows], to_low(a_send)), out_w)
     down_blocks = exchange(after(pieces, a_keep), "rep")
     a = scatter_tokens(a_keep, a_send, (down_blocks,))
     ainv = lax.rsqrt(jnp.mean(a * a, axis=-1, keepdims=True) + epsilon)

time: 838 us -> 841 us (level)
    all_to_all x7, waiting for transfers between devices: 0.9 us -> 11.4 us  [exchange(): return lax.all_to_all(blocks, axis, 0, 0, tiled=True)]
    unnamed x251, local copies, waits for them, and re-layouts: 64 us -> 54.9 us
  transfers between devices with their start and end apart: 93 -> 93, of which waited for: 33 -> 32; matrix products, arithmetic and copies ran while one was open for 38% -> 38% of each run, Pallas kernels for 7% -> 7%
where the time goes in v5:
time: 841 us; the launch traced here: 830 us
  waiting for transfers between devices  311 us (37%)
  matrix products  171 us (20%)
  local copies, waits for them, and re-layouts  114 us (14%)
  starting transfers between devices  83.4 us (10%)
  other arithmetic  77.3 us (9%)
  Pallas kernels  55.4 us (7%)
  between operations  17.1 us (2%)
    ppermute x21, waiting for transfers between devices, ring(): lax.ppermute(value, 'rep', [(r, (r + 2) % count) for r in range(count)])  229 us
    dot_general x26, matrix products, dot(): lax.dot_general(left, right, ((contract[0], contract[1]), ((), ())), pref...  171 us
    ppermute x25, waiting for transfers between devices, send_shard(): return lax.ppermute(value, 'shard', [(s, s ^ k) for s in range(count)])  57.3 us
    unnamed x251, local copies, waits for them, and re-layouts  54.9 us
    all_to_all x7, starting transfers between devices, exchange(): return lax.all_to_all(blocks, axis, 0, 0, tiled=True)  34.9 us
    convert_element_type x25, other arithmetic, to_low(): return tensor.astype(BF16)  29.1 us
    pallas_call x1, Pallas kernels, attend_back(): pl.pallas_call(attend_back_kernel, out_shape=[jax.ShapeDtypeStruct((heads...  26.9 us
    ppermute x25, starting transfers between devices, send_shard(): return lax.ppermute(value, 'shard', [(s, s ^ k) for s in range(count)])  25.5 us
  transfers between devices with their start and end apart: 93, of which 32 were waited for; matrix products, arithmetic and copies ran while one was open for 38% of the time, Pallas kernels for 7%

profile of v5, /device:TPU:4, one launch (start us, length us, event | category | flops | bytes accessed | tf_op | source)
XLA Modules:
  0.0 830.1 jit_solution(9345385426828267235)
XLA Ops:
  17.7 4.5 collective-permute-start
  23.0 5.2 all-to-all-start
  44.7 3.2 multiply_cosine_fusion
  49.9 9.8 %collective-permute-done.6 = bf16[1024,384]{1,0:T(8,128)(2,1)} collective-permute-done((bf16[1024,384]{1,0:T(8,128)(2,1)S(1)}, bf16[1024,384]{1,0:T(8,128)(2,1)}, u32[]{:S(2)}, u32[]{:S(2)}) %collective-permute-start.6) | collective-permute-done | bytes 786464 | tf_op jit(solution)/shard_map/ppermute | solution.py:151
  59.7 3.1 dynamic_update_slice.48
  70.4 10.5 %collective-permute-done.9 = bf16[1024,384]{1,0:T(8,128)(2,1)} collective-permute-done((bf16[1024,384]{1,0:T(8,128)(2,1)}, bf16[1024,384]{1,0:T(8,128)(2,1)}, u32[]{:S(2)}, u32[]{:S(2)}) %collective-permute-start.9) | collective-permute-done | bytes 786464 | tf_op jit(solution)/shard_map/ppermute | solution.py:151
  92.1 9.2 %collective-permute-done.14 = bf16[1024,384]{1,0:T(8,128)(2,1)} collective-permute-done((bf16[1024,384]{1,0:T(8,128)(2,1)}, bf16[1024,384]{1,0:T(8,128)(2,1)}, u32[]{:S(2)}, u32[]{:S(2)}) %collective-permute-start.14) | collective-permute-done | bytes 786464 | tf_op jit(solution)/shard_map/ppermute | solution.py:151
  112.0 8.8 %fusion.112.refs_0_ = f32[1024,1536]{1,0:T(8,128)S(1)} fusion(bf16[1024,2048]{1,0:T(8,128)(2,1)S(1)} %copy-done.66, bf16[2048,1536]{1,0:T(8,128)(2,1)} %constant_dynamic-update-slice_fusion.96), kind=kOutput, calls=%fused_computation.332 | convolution fusion | flops 6442450944 | bytes 16777216 | tf_op jit(solution)/shard_map/dot_general | solution.py:35
  133.4 3.8 rope.1
  137.6 15.2 %attend.1 = bf16[1024,512]{1,0:T(8,128)(2,1)S(1)} custom-call(s32[5]{0:T(128)S(1)} %pad_add_fusion.where_ref, bf16[4,1024,128]{2,1,0:T(8,128)(2,1)S(1)} %get-tuple-element.111.q_ref, bf16[4,1024,128]{2,1,0:T(8,128)(2,1)S(1)} %get-tuple-element.112.k_ref, bf16[4,1024,128]{2,1,0:T(8,128)(2,1)S(1)} %get-tuple-element.113.v_ref, ...), custom_call_target="tpu_custom_call" | custom-call | flops 2147483648 | bytes 4194304 | tf_op jit(solution)/shard_map/attend/pallas_call | solution.py:316
  154.1 6.3 all-to-all-start.1
  167.0 4.3 convolution_convert_fusion.2
  171.4 3.2 fusion.113
  174.6 11.4 %all-to-all-done.1 = bf16[4,2,256,256]{3,2,1,0:T(8,128)(2,1)} async-done(((bf16[4,2,256,256]{3,2,1,0:T(8,128)(2,1)}), bf16[4,2,256,256]{3,2,1,0:T(8,128)(2,1)}, u32[]{:S(2)}, u32[]{:S(2)}) %all-to-all-start.1) | async-done | bytes 1048608 | tf_op jit(solution)/shard_map/all_to_all | solution.py:122
  186.0 5.1 all-to-all-start.2
  195.8 23.6 %collective-permute-done.28 = bf16[256,2048]{1,0:T(8,128)(2,1)} collective-permute-done((bf16[256,2048]{1,0:T(8,128)(2,1)S(1)}, bf16[256,2048]{1,0:T(8,128)(2,1)}, u32[]{:S(2)}, u32[]{:S(2)}) %collective-permute-start.28) | collective-permute-done | bytes 1048608 | tf_op jit(solution)/shard_map/ppermute | solution.py:56
  219.9 3.4 slice_add_fusion.11
  225.4 11.3 %collective-permute-done.27 = bf16[128,2048]{1,0:T(8,128)(2,1)S(1)} collective-permute-done((bf16[128,2048]{1,0:T(8,128)(2,1)S(1)}, bf16[128,2048]{1,0:T(8,128)(2,1)S(1)}, u32[]{:S(2)}, u32[]{:S(2)}) %collective-permute-start.27) | collective-permute-done | bytes 524320 | tf_op jit(solution)/shard_map/ppermute | solution.py:56
  242.5 23.7 %collective-permute-done.30 = bf16[256,2048]{1,0:T(8,128)(2,1)S(1)} collective-permute-done((bf16[256,2048]{1,0:T(8,128)(2,1)S(1)}, bf16[256,2048]{1,0:T(8,128)(2,1)S(1)}, u32[]{:S(2)}, u32[]{:S(2)}) %collective-permute-start.30) | collective-permute-done | bytes 1048608 | tf_op jit(solution)/shard_map/ppermute | solution.py:151
  266.8 23.7 %collective-permute-done.34 = bf16[256,2048]{1,0:T(8,128)(2,1)} collective-permute-done((bf16[256,2048]{1,0:T(8,128)(2,1)S(1)}, bf16[256,2048]{1,0:T(8,128)(2,1)}, u32[]{:S(2)}, u32[]{:S(2)}) %collective-permute-start.34) | collective-permute-done | bytes 1048608 | tf_op jit(solution)/shard_map/ppermute | solution.py:151
  296.9 7.6 fusion.114
  308.1 4.9 fusion.115
  313.7 7.6 fusion.116
  328.4 4.6 fusion.118
  333.6 4.9 fusion.119
  339.2 15.0 %collective-permute-done.33 = bf16[256,2048]{1,0:T(8,128)(2,1)S(1)} collective-permute-done((bf16[256,2048]{1,0:T(8,128)(2,1)S(1)}, bf16[256,2048]{1,0:T(8,128)(2,1)S(1)}, u32[]{:S(2)}, u32[]{:S(2)}) %collective-permute-start.33) | collective-permute-done | bytes 1048608 | tf_op jit(solution)/shard_map/ppermute | solution.py:151
  355.0 4.6 fusion.120
  364.4 17.1 %collective-permute-done.37 = bf16[256,2048]{1,0:T(8,128)(2,1)S(1)} collective-permute-done((bf16[256,2048]{1,0:T(8,128)(2,1)S(1)}, bf16[256,2048]{1,0:T(8,128)(2,1)S(1)}, u32[]{:S(2)}, u32[]{:S(2)}) %collective-permute-start.37) | collective-permute-done | bytes 1048608 | tf_op jit(solution)/shard_map/ppermute | solution.py:151
  382.1 25.6 %collective-permute-done.41 = bf16[256,2048]{1,0:T(8,128)(2,1)S(1)} collective-permute-done((bf16[256,2048]{1,0:T(8,128)(2,1)S(1)}, bf16[256,2048]{1,0:T(8,128)(2,1)S(1)}, u32[]{:S(2)}, u32[]{:S(2)}) %collective-permute-start.41) | collective-permute-done | bytes 1048608 | tf_op jit(solution)/shard_map/ppermute | solution.py:151
  412.9 3.0 multiply_convert_fusion.8
  416.0 10.2 %fusion.63 = f32[512,2048]{1,0:T(8,128)} fusion(bf16[2048,2048]{1,0:T(8,128)(2,1)} %all-gather.3.cloned.1.call-done, bf16[512,1024]{1,0:T(8,128)(2,1)S(1)} %get-tuple-element.150, bf16[512,1024]{1,0:T(8,128)(2,1)S(1)} %get-tuple-element.145), kind=kOutput, calls=%fused_computation.91 | convolution fusion | flops 4299161600 | bytes 14680064 | tf_op jit(solution)/shard_map/dot_general | solution.py:35
  426.2 11.6 %collective-permute-done.44 = bf16[256,2048]{1,0:T(8,128)(2,1)S(1)} collective-permute-done((bf16[256,2048]{1,0:T(8,128)(2,1)S(1)}, bf16[256,2048]{1,0:T(8,128)(2,1)S(1)}, u32[]{:S(2)}, u32[]{:S(2)}) %collective-permute-start.44) | collective-permute-done | bytes 1048608 | tf_op jit(solution)/shard_map/ppermute | solution.py:151
  440.7 5.9 multiply_convert_fusion.6
  447.6 7.0 fusion.67
  454.9 10.3 %collective-permute-done.49 = bf16[256,2048]{1,0:T(8,128)(2,1)S(1)} collective-permute-done((bf16[256,2048]{1,0:T(8,128)(2,1)S(1)}, bf16[256,2048]{1,0:T(8,128)(2,1)S(1)}, u32[]{:S(2)}, u32[]{:S(2)}) %collective-permute-start.49) | collective-permute-done | bytes 1048608 | tf_op jit(solution)/shard_map/ppermute | solution.py:151
  468.4 3.0 multiply_convert_fusion.4
  471.4 7.7 fusion.71
  479.1 13.9 %collective-permute-done.50 = bf16[256,2048]{1,0:T(8,128)(2,1)S(1)} collective-permute-done((bf16[256,2048]{1,0:T(8,128)(2,1)S(1)}, bf16[256,2048]{1,0:T(8,128)(2,1)S(1)}, u32[]{:S(2)}, u32[]{:S(2)}) %collective-permute-start.50) | collective-permute-done | bytes 1048608 | tf_op jit(solution)/shard_map/ppermute | solution.py:151
  500.0 3.0 multiply_convert_fusion.2
  503.0 7.7 fusion.75
  510.7 14.1 %collective-permute-done.48 = bf16[256,2048]{1,0:T(8,128)(2,1)S(1)} collective-permute-done((bf16[256,2048]{1,0:T(8,128)(2,1)S(1)}, bf16[256,2048]{1,0:T(8,128)(2,1)S(1)}, u32[]{:S(2)}, u32[]{:S(2)}) %collective-permute-start.48) | collective-permute-done | bytes 1048608 | tf_op jit(solution)/shard_map/ppermute | solution.py:151
  528.3 13.2 %fusion.37 = bf16[1024,2048]{1,0:T(8,128)(2,1)} fusion(bf16[512,2048]{1,0:T(8,128)(2,1)} %copy-done.62, bf16[512,2048]{1,0:T(8,128)(2,1)} %copy-done.61, bf16[512,2048]{1,0:T(8,128)(2,1)} %copy-done.63, bf16[512,2048]{1,0:T(8,128)(2,1)S(1)} %copy-done.49, bf16[512,1024]{1,0:T(8,128)(2,1)} %copy-done.53, bf16[512,1024]{1,0:T(8,128)(2,1)S(1)} %copy-done.52, ...), kind=kOutput, calls=%fused_computation.35 | convolution fusion | flops 8642363392 | bytes 16777216 | tf_op jit(solution)/shard_map/dot_general | solution.py:35
  541.6 11.2 %collective-permute-done.54 = bf16[256,2048]{1,0:T(8,128)(2,1)} collective-permute-done((bf16[256,2048]{1,0:T(8,128)(2,1)}, bf16[256,2048]{1,0:T(8,128)(2,1)}, u32[]{:S(2)}, u32[]{:S(2)}) %collective-permute-start.54) | collective-permute-done | bytes 1048608 | tf_op jit(solution)/shard_map/ppermute | solution.py:151
  561.7 12.7 %fusion.34 = bf16[2048,1024]{0,1:T(8,128)(2,1)} fusion(bf16[2048,2048]{1,0:T(8,128)(2,1)S(1)} %constant_dynamic-update-slice_fusion.40, bf16[512,1024]{1,0:T(8,128)(2,1)} %copy-done.86, bf16[512,1024]{1,0:T(8,128)(2,1)S(1)} %copy-done.85, bf16[512,1024]{1,0:T(8,128)(2,1)S(1)} %copy-done.81, bf16[512,1024]{1,0:T(8,128)(2,1)} %copy-done.89), kind=kOutput, calls=%fused_computation.34 | convolution fusion | flops 8608808960 | bytes 16777216 | tf_op jit(solution)/shard_map/dot_general | solution.py:35
  574.4 6.3 collective-permute-done.56
  588.1 11.4 %fusion.31 = bf16[2048,1024]{0,1:T(8,128)(2,1)} fusion(bf16[2048,2048]{1,0:T(8,128)(2,1)S(1)} %constant_dynamic-update-slice_fusion.40, bf16[512,1024]{1,0:T(8,128)(2,1)S(1)} %copy-done.83, bf16[512,1024]{1,0:T(8,128)(2,1)S(1)} %copy-done.79, bf16[512,1024]{1,0:T(8,128)(2,1)S(1)} %copy-done.77, bf16[512,1024]{1,0:T(8,128)(2,1)S(1)} %copy-done.88), kind=kOutput, calls=%fused_computation.33 | convolution fusion | flops 8608808960 | bytes 16777216 | tf_op jit(solution)/shard_map/dot_general | solution.py:35
  599.5 5.2 collective-permute-done.59
  607.7 8.4 %pad_maximum_fusion = bf16[2048,2048]{0,1:T(8,128)(2,1)} fusion(bf16[2048,1024]{0,1:T(8,128)(2,1)} %fusion.31, bf16[2048,1024]{0,1:T(8,128)(2,1)} %fusion.34), kind=kLoop, calls=%fused_computation.8 | loop fusion | flops 16777216 | bytes 16777216 | tf_op jit(solution)/shard_map/concatenate | solution.py:672
  618.5 11.6 %collective-permute-done.61 = bf16[256,2048]{1,0:T(8,128)(2,1)} collective-permute-done((bf16[256,2048]{1,0:T(8,128)(2,1)}, bf16[256,2048]{1,0:T(8,128)(2,1)}, u32[]{:S(2)}, u32[]{:S(2)}) %collective-permute-start.61) | collective-permute-done | bytes 1048608 | tf_op jit(solution)/shard_map/ppermute | solution.py:56
  638.4 4.5 all-to-all-start.3
  642.9 4.8 convolution_convert_fusion.3.do_ref
  647.8 26.9 %attend_back.1 = (f32[4,1024,128]{2,1,0:T(8,128)S(1)}, f32[4,1024,128]{2,1,0:T(8,128)S(1)}, f32[4,1024,128]{2,1,0:T(8,128)S(1)}, f32[2,1024]{1,0:T(2,128)S(1)}) custom-call(s32[5]{0:T(128)S(1)} %pad_add_fusion.where_ref, bf16[4,1024,128]{2,1,0:T(8,128)(2,1)S(1)} %copy-done.11, bf16[4,1024,128]{2,1,0:T(8,128)(2,1)S(1)} %copy-done.13, ...), custom_call_target="tpu_custom_call" | custom-call | flops 5368709120 | bytes 10485760 | tf_op jit(solution)/shard_map/attend_back/pallas_call | solution.py:385
  682.1 5.3 all-to-all-start.4
  688.7 8.9 %rope_back.1 = (bf16[1024,1536]{1,0:T(8,128)(2,1)}, f32[4,2,128]{2,1,0:T(2,128)}) custom-call(f32[1024,1536]{1,0:T(8,128)} %copy-done, f32[4,1024,128]{2,1,0:T(8,128)} %copy-done.4, f32[4,1024,128]{2,1,0:T(8,128)} %copy-done.5, f32[4,1024,128]{2,1,0:T(8,128)} %copy-done.6, f32[1024,2]{1,0:T(8,128)} %bitcast.136, f32[1024,2]{1,0:T(8,128)} %bitcast.151, ...), custom_call_target="tpu_custom_call" | custom-call | flops 16384000 | bytes 15728640 | tf_op jit(solution)/shard_map/rope_back/pallas_call | solution.py:492
  697.6 9.1 %convolution_convert_fusion = bf16[2048,1536]{1,0:T(8,128)(2,1)S(1)} fusion(bf16[1024,2048]{1,0:T(8,128)(2,1)S(1)} %copy-done.67, bf16[1024,1536]{1,0:T(8,128)(2,1)} %get-tuple-element.166), kind=kOutput, calls=%fused_computation.9 | convolution fusion | flops 6445596672 | bytes 13631488 | tf_op jit(solution)/shard_map/dot_general | solution.py:35
  718.0 4.1 all-to-all-start.5
  722.0 5.9 convolution_convert_fusion.1
  727.9 11.7 %fusion.111 = (bf16[1024,2048]{1,0:T(8,128)(2,1)S(1)}, f32[1024,2048]{1,0:T(8,128)}) fusion(bf16[1024,1536]{1,0:T(8,128)(2,1)} %get-tuple-element.166, bf16[2048,1536]{1,0:T(8,128)(2,1)} %constant_dynamic-update-slice_fusion.96), kind=kOutput, calls=%fused_computation.331 | convolution fusion | flops 6444548096 | bytes 22020096 | tf_op jit(solution)/shard_map/dot_general | solution.py:35
  751.1 3.3 copy.168
  756.3 19.8 %collective-permute-done.69 = bf16[1024,384]{1,0:T(8,128)(2,1)} collective-permute-done((bf16[1024,384]{1,0:T(8,128)(2,1)}, bf16[1024,384]{1,0:T(8,128)(2,1)}, u32[]{:S(2)}, u32[]{:S(2)}) %collective-permute-start.69) | collective-permute-done | bytes 786464 | tf_op jit(solution)/shard_map/ppermute | solution.py:151
  778.9 4.4 all-to-all-start.6
  783.3 3.1 slice_add_fusion.1
  792.3 7.4 collective-permute-done.72
  809.7 3.4 collective-permute-done.79
  (586 shorter events, 232.0 us)
Async XLA Ops:
  10.7 23.2 %collective-permute-start.2 = (f32[2304]{0:T(1024)S(1)}, f32[2304]{0:T(1024)S(1)}, u32[]{:S(2)}, u32[]{:S(2)}) collective-permute-start(f32[2304]{0:T(1024)S(1)} %pad_maximum_fusion.16), channel_id=1, source_target_pairs={{0,1},{1,0},{2,3},{3,2},{4,5},{5,4},{6,7},{7,6},{8,9},{9,8},{10,11... | collective-permute-start | bytes 27656 | tf_op jit(solution)/shard_map/ppermute | solution.py:56
  12.2 21.7 %collective-permute-start.3 = (f32[2304]{0:T(1024)S(1)}, f32[2304]{0:T(1024)S(1)}, u32[]{:S(2)}, u32[]{:S(2)}) collective-permute-start(f32[2304]{0:T(1024)S(1)} %pad_maximum_fusion.16), channel_id=1, source_target_pairs={{0,2},{1,3},{2,0},{3,1},{4,6},{5,7},{6,4},{7,5},{8,10},{9,11},{10,... | collective-permute-start | bytes 27656 | tf_op jit(solution)/shard_map/ppermute | solution.py:56
  12.7 21.2 %collective-permute-start.4 = (f32[2304]{0:T(1024)S(1)}, f32[2304]{0:T(1024)S(1)}, u32[]{:S(2)}, u32[]{:S(2)}) collective-permute-start(f32[2304]{0:T(1024)S(1)} %pad_maximum_fusion.16), channel_id=1, source_target_pairs={{0,3},{1,2},{2,1},{3,0},{4,7},{5,6},{6,5},{7,4},{8,11},{9,10},{10,... | collective-permute-start | bytes 27656 | tf_op jit(solution)/shard_map/ppermute | solution.py:56
  16.8 17.1 %collective-permute-start.1 = (bf16[512,384]{1,0:T(8,128)(2,1)S(1)}, bf16[512,384]{1,0:T(8,128)(2,1)}, u32[]{:S(2)}, u32[]{:S(2)}) collective-permute-start(bf16[512,384]{1,0:T(8,128)(2,1)S(1)} %pad_maximum_fusion.13), channel_id=1, source_target_pairs={{0,1},{1,0},{2,5},{3,4},{4,3},{5,2},{6,7},{7,6},{8,9},{9,8},{10,13... | collective-permute-start | bytes 1179656 | tf_op jit(solution)/shard_map/ppermute | solution.py:271
  28.2 268.7 %all-gather.3.cloned.1.call-start = ((), (), s32[]{:S(2)}) async-start(), calls=%async_computation.10 | async-start | bytes 10485760 | tf_op jit(solution)/shard_map/all_gather | solution.py:571
  37.7 44.1 %collective-permute-start.11 = (bf16[1024,384]{1,0:T(8,128)(2,1)S(1)}, bf16[1024,384]{1,0:T(8,128)(2,1)}, u32[]{:S(2)}, u32[]{:S(2)}) collective-permute-start(bf16[1024,384]{1,0:T(8,128)(2,1)S(1)} %bitcast.146), channel_id=1, source_target_pairs={{0,4},{4,0},{8,12},{12,8},{16,20},{20,16},{24,28},{28,24},{1,5},{5... | collective-permute-start | bytes 2359304 | tf_op jit(solution)/shard_map/ppermute | solution.py:155
  37.8 21.9 %collective-permute-start.6 = (bf16[1024,384]{1,0:T(8,128)(2,1)S(1)}, bf16[1024,384]{1,0:T(8,128)(2,1)}, u32[]{:S(2)}, u32[]{:S(2)}) collective-permute-start(bf16[1024,384]{1,0:T(8,128)(2,1)S(1)} %bitcast.147), channel_id=1, source_target_pairs={{0,8},{4,12},{8,16},{12,20},{16,24},{20,28},{24,0},{28,4},{1,9},{5... | collective-permute-start | bytes 2359304 | tf_op jit(solution)/shard_map/ppermute | solution.py:151
  42.1 20.7 %collective-permute-start.7 = (bf16[128,2048]{1,0:T(8,128)(2,1)}, bf16[128,2048]{1,0:T(8,128)(2,1)}, u32[]{:S(2)}, u32[]{:S(2)}) collective-permute-start(bf16[128,2048]{1,0:T(8,128)(2,1)} %get-tuple-element.296), channel_id=1, source_target_pairs={{0,1},{1,0},{2,3},{3,2},{4,5},{5,4},{6,7},{7,6},{8,9},{9,8},{10,11... | collective-permute-start | bytes 1572872 | tf_op jit(solution)/shard_map/ppermute | solution.py:56
  43.6 22.5 %collective-permute-start.5 = (bf16[128,2048]{1,0:T(8,128)(2,1)}, bf16[128,2048]{1,0:T(8,128)(2,1)}, u32[]{:S(2)}, u32[]{:S(2)}) collective-permute-start(bf16[128,2048]{1,0:T(8,128)(2,1)} %get-tuple-element.298), channel_id=1, source_target_pairs={{0,2},{1,3},{2,0},{3,1},{4,6},{5,7},{6,4},{7,5},{8,10},{9,11},{10,... | collective-permute-start | bytes 1572872 | tf_op jit(solution)/shard_map/ppermute | solution.py:56
  59.7 21.3 %collective-permute-start.9 = (bf16[1024,384]{1,0:T(8,128)(2,1)}, bf16[1024,384]{1,0:T(8,128)(2,1)}, u32[]{:S(2)}, u32[]{:S(2)}) collective-permute-start(bf16[1024,384]{1,0:T(8,128)(2,1)} %collective-permute-done.6), channel_id=1, source_target_pairs={{0,8},{4,12},{8,16},{12,20},{16,24},{20,28},{24,0},{28,4},{1,9},{5... | collective-permute-start | bytes 2359304 | tf_op jit(solution)/shard_map/ppermute | solution.py:151
  65.1 38.8 %collective-permute-start.10 = (bf16[256,2048]{1,0:T(8,128)(2,1)}, bf16[256,2048]{1,0:T(8,128)(2,1)}, u32[]{:S(2)}, u32[]{:S(2)}) collective-permute-start(bf16[256,2048]{1,0:T(8,128)(2,1)} %pad_maximum_fusion.7), channel_id=1, source_target_pairs={{0,2},{1,3},{2,0},{3,1},{4,6},{5,7},{6,4},{7,5},{8,10},{9,11},{10,... | collective-permute-start | bytes 3145736 | tf_op jit(solution)/shard_map/ppermute | solution.py:56
  67.4 24.7 %collective-permute-start.8 = (bf16[256,2048]{1,0:T(8,128)(2,1)S(1)}, bf16[256,2048]{1,0:T(8,128)(2,1)}, u32[]{:S(2)}, u32[]{:S(2)}) collective-permute-start(bf16[256,2048]{1,0:T(8,128)(2,1)S(1)} %pad_maximum_fusion.6), channel_id=1, source_target_pairs={{0,1},{1,0},{2,3},{3,2},{4,5},{5,4},{6,7},{7,6},{8,9},{9,8},{10,11... | collective-permute-start | bytes 3145736 | tf_op jit(solution)/shard_map/ppermute | solution.py:56
  68.5 19.6 %collective-permute-start.12 = (bf16[1024,384]{1,0:T(8,128)(2,1)}, bf16[1024,384]{1,0:T(8,128)(2,1)S(1)}, u32[]{:S(2)}, u32[]{:S(2)}) collective-permute-start(bf16[1024,384]{1,0:T(8,128)(2,1)} %collective-permute-done.6), channel_id=1, source_target_pairs={{0,4},{4,0},{8,12},{12,8},{16,20},{20,16},{24,28},{28,24},{1,5},{5... | collective-permute-start | bytes 2359304 | tf_op jit(solution)/shard_map/ppermute | solution.py:155
  80.9 20.4 %collective-permute-start.14 = (bf16[1024,384]{1,0:T(8,128)(2,1)}, bf16[1024,384]{1,0:T(8,128)(2,1)}, u32[]{:S(2)}, u32[]{:S(2)}) collective-permute-start(bf16[1024,384]{1,0:T(8,128)(2,1)} %collective-permute-done.9), channel_id=1, source_target_pairs={{0,8},{4,12},{8,16},{12,20},{16,24},{20,28},{24,0},{28,4},{1,9},{5... | collective-permute-start | bytes 2359304 | tf_op jit(solution)/shard_map/ppermute | solution.py:151
  85.9 21.0 %collective-permute-start.13 = (bf16[1024,384]{1,0:T(8,128)(2,1)}, bf16[1024,384]{1,0:T(8,128)(2,1)S(1)}, u32[]{:S(2)}, u32[]{:S(2)}) collective-permute-start(bf16[1024,384]{1,0:T(8,128)(2,1)} %collective-permute-done.9), channel_id=1, source_target_pairs={{0,4},{4,0},{8,12},{12,8},{16,20},{20,16},{24,28},{28,24},{1,5},{5... | collective-permute-start | bytes 2359304 | tf_op jit(solution)/shard_map/ppermute | solution.py:155
  106.5 20.4 %collective-permute-start.20 = (bf16[512,256]{1,0:T(8,128)(2,1)S(1)}, bf16[512,256]{1,0:T(8,128)(2,1)}, u32[]{:S(2)}, u32[]{:S(2)}) collective-permute-start(bf16[512,256]{1,0:T(8,128)(2,1)S(1)} %bitcast.155), channel_id=1, source_target_pairs={{0,8},{4,12},{8,16},{12,20},{16,24},{20,28},{24,0},{28,4},{1,9},{5... | collective-permute-start | bytes 786440 | tf_op jit(solution)/shard_map/ppermute | solution.py:151
  126.9 33.5 %collective-permute-start.21 = (bf16[512,256]{1,0:T(8,128)(2,1)}, bf16[512,256]{1,0:T(8,128)(2,1)}, u32[]{:S(2)}, u32[]{:S(2)}) collective-permute-start(bf16[512,256]{1,0:T(8,128)(2,1)} %collective-permute-done.20), channel_id=1, source_target_pairs={{0,4},{4,0},{8,12},{12,8},{16,20},{20,16},{24,28},{28,24},{1,5},{5... | collective-permute-start | bytes 786440 | tf_op jit(solution)/shard_map/ppermute | solution.py:155
  137.2 24.8 %collective-permute-start.24 = (bf16[512,256]{1,0:T(8,128)(2,1)S(1)}, bf16[512,256]{1,0:T(8,128)(2,1)}, u32[]{:S(2)}, u32[]{:S(2)}) collective-permute-start(bf16[512,256]{1,0:T(8,128)(2,1)S(1)} %collective-permute-done.22), channel_id=1, source_target_pairs={{0,8},{4,12},{8,16},{12,20},{16,24},{20,28},{24,0},{28,4},{1,9},{5... | collective-permute-start | bytes 786440 | tf_op jit(solution)/shard_map/ppermute | solution.py:151
  137.5 25.4 %collective-permute-start.23 = (bf16[512,256]{1,0:T(8,128)(2,1)S(1)}, bf16[512,256]{1,0:T(8,128)(2,1)}, u32[]{:S(2)}, u32[]{:S(2)}) collective-permute-start(bf16[512,256]{1,0:T(8,128)(2,1)S(1)} %collective-permute-done.22), channel_id=1, source_target_pairs={{0,4},{4,0},{8,12},{12,8},{16,20},{20,16},{24,28},{28,24},{1,5},{5... | collective-permute-start | bytes 786440 | tf_op jit(solution)/shard_map/ppermute | solution.py:155
  154.1 31.9 %all-to-all-start.1 = ((bf16[4,2,256,256]{3,2,1,0:T(8,128)(2,1)}), bf16[4,2,256,256]{3,2,1,0:T(8,128)(2,1)}, u32[]{:S(2)}, u32[]{:S(2)}) async-start(bf16[4,2,256,256]{3,2,1,0:T(8,128)(2,1)} %copy.156), calls=%async_computation.1 | async-start | bytes 2097152 | tf_op jit(solution)/shard_map/all_to_all | solution.py:122
  186.0 33.5 %all-to-all-start.2 = ((bf16[8,256,256]{2,1,0:T(8,128)(2,1)}), bf16[8,256,256]{2,1,0:T(8,128)(2,1)S(1)}, u32[]{:S(2)}, u32[]{:S(2)}) async-start(bf16[8,256,256]{2,1,0:T(8,128)(2,1)} %bitcast.19), calls=%async_computation.2 | async-start | bytes 2097152 | tf_op jit(solution)/shard_map/all_to_all | solution.py:122
  191.1 117.0 %all-gather.5.cloned.1.call-start = ((), (), s32[]{:S(2)}) async-start(), calls=%async_computation.11 | async-start | bytes 5242880 | tf_op jit(solution)/shard_map/all_gather | solution.py:617
  193.8 25.6 %collective-permute-start.28 = (bf16[256,2048]{1,0:T(8,128)(2,1)S(1)}, bf16[256,2048]{1,0:T(8,128)(2,1)}, u32[]{:S(2)}, u32[]{:S(2)}) collective-permute-start(bf16[256,2048]{1,0:T(8,128)(2,1)S(1)} %get-tuple-element.289), channel_id=1, source_target_pairs={{0,2},{1,3},{2,0},{3,1},{4,6},{5,7},{6,4},{7,5},{8,10},{9,11},{10,... | collective-permute-start | bytes 3145736 | tf_op jit(solution)/shard_map/ppermute | solution.py:56
  194.4 25.6 %collective-permute-start.26 = (bf16[256,2048]{1,0:T(8,128)(2,1)}, bf16[256,2048]{1,0:T(8,128)(2,1)}, u32[]{:S(2)}, u32[]{:S(2)}) collective-permute-start(bf16[256,2048]{1,0:T(8,128)(2,1)} %get-tuple-element.288), channel_id=1, source_target_pairs={{0,1},{1,0},{2,3},{3,2},{4,5},{5,4},{6,7},{7,6},{8,9},{9,8},{10,11... | collective-permute-start | bytes 3145736 | tf_op jit(solution)/shard_map/ppermute | solution.py:56
  241.1 389.0 %reduce-scatter.4.cloned.1.call-start = ((), (), s32[]{:S(2)}) async-start(), calls=%async_computation.12 | async-start | bytes 5242880 | tf_op jit(solution)/shard_map/reduce_scatter | solution.py:658
  241.2 25.1 %collective-permute-start.30 = (bf16[256,2048]{1,0:T(8,128)(2,1)S(1)}, bf16[256,2048]{1,0:T(8,128)(2,1)S(1)}, u32[]{:S(2)}, u32[]{:S(2)}) collective-permute-start(bf16[256,2048]{1,0:T(8,128)(2,1)S(1)} %copy-done.42), channel_id=1, source_target_pairs={{0,8},{4,12},{8,16},{12,20},{16,24},{20,28},{24,0},{28,4},{1,9},{5... | collective-permute-start | bytes 3145736 | tf_op jit(solution)/shard_map/ppermute | solution.py:151
  266.2 24.2 %collective-permute-start.34 = (bf16[256,2048]{1,0:T(8,128)(2,1)S(1)}, bf16[256,2048]{1,0:T(8,128)(2,1)}, u32[]{:S(2)}, u32[]{:S(2)}) collective-permute-start(bf16[256,2048]{1,0:T(8,128)(2,1)S(1)} %collective-permute-done.30), channel_id=1, source_target_pairs={{0,8},{4,12},{8,16},{12,20},{16,24},{20,28},{24,0},{28,4},{1,9},{5... | collective-permute-start | bytes 3145736 | tf_op jit(solution)/shard_map/ppermute | solution.py:151
  266.3 25.3 %collective-permute-start.42 = (bf16[256,2048]{1,0:T(8,128)(2,1)S(1)}, bf16[256,2048]{1,0:T(8,128)(2,1)S(1)}, u32[]{:S(2)}, u32[]{:S(2)}) collective-permute-start(bf16[256,2048]{1,0:T(8,128)(2,1)S(1)} %copy-done.42), channel_id=1, source_target_pairs={{0,4},{4,0},{8,12},{12,8},{16,20},{20,16},{24,28},{28,24},{1,5},{5... | collective-permute-start | bytes 3145736 | tf_op jit(solution)/shard_map/ppermute | solution.py:155
  266.3 28.5 %collective-permute-start.31 = (bf16[256,2048]{1,0:T(8,128)(2,1)S(1)}, bf16[256,2048]{1,0:T(8,128)(2,1)S(1)}, u32[]{:S(2)}, u32[]{:S(2)}) collective-permute-start(bf16[256,2048]{1,0:T(8,128)(2,1)S(1)} %collective-permute-done.30), channel_id=1, source_target_pairs={{0,4},{4,0},{8,12},{12,8},{16,20},{20,16},{24,28},{28,24},{1,5},{5... | collective-permute-start | bytes 3145736 | tf_op jit(solution)/shard_map/ppermute | solution.py:155
  291.7 29.9 %collective-permute-start.38 = (bf16[256,2048]{1,0:T(8,128)(2,1)}, bf16[256,2048]{1,0:T(8,128)(2,1)}, u32[]{:S(2)}, u32[]{:S(2)}) collective-permute-start(bf16[256,2048]{1,0:T(8,128)(2,1)} %collective-permute-done.34), channel_id=1, source_target_pairs={{0,8},{4,12},{8,16},{12,20},{16,24},{20,28},{24,0},{28,4},{1,9},{5... | collective-permute-start | bytes 3145736 | tf_op jit(solution)/shard_map/ppermute | solution.py:151
  326.4 27.9 %collective-permute-start.33 = (bf16[256,2048]{1,0:T(8,128)(2,1)S(1)}, bf16[256,2048]{1,0:T(8,128)(2,1)S(1)}, u32[]{:S(2)}, u32[]{:S(2)}) collective-permute-start(bf16[256,2048]{1,0:T(8,128)(2,1)S(1)} %fusion.62), channel_id=1, source_target_pairs={{0,8},{4,12},{8,16},{12,20},{16,24},{20,28},{24,0},{28,4},{1,9},{5... | collective-permute-start | bytes 3145736 | tf_op jit(solution)/shard_map/ppermute | solution.py:151
  338.7 25.6 %collective-permute-start.40 = (bf16[256,2048]{1,0:T(8,128)(2,1)S(1)}, bf16[256,2048]{1,0:T(8,128)(2,1)S(1)}, u32[]{:S(2)}, u32[]{:S(2)}) collective-permute-start(bf16[256,2048]{1,0:T(8,128)(2,1)S(1)} %slice.814), channel_id=1, source_target_pairs={{0,4},{4,0},{8,12},{12,8},{16,20},{20,16},{24,28},{28,24},{1,5},{5... | collective-permute-start | bytes 3145736 | tf_op jit(solution)/shard_map/ppermute | solution.py:155
  354.8 26.7 %collective-permute-start.37 = (bf16[256,2048]{1,0:T(8,128)(2,1)S(1)}, bf16[256,2048]{1,0:T(8,128)(2,1)S(1)}, u32[]{:S(2)}, u32[]{:S(2)}) collective-permute-start(bf16[256,2048]{1,0:T(8,128)(2,1)S(1)} %fusion.61), channel_id=1, source_target_pairs={{0,8},{4,12},{8,16},{12,20},{16,24},{20,28},{24,0},{28,4},{1,9},{5... | collective-permute-start | bytes 3145736 | tf_op jit(solution)/shard_map/ppermute | solution.py:151
  364.3 17.8 %collective-permute-start.43 = (bf16[256,2048]{1,0:T(8,128)(2,1)S(1)}, bf16[256,2048]{1,0:T(8,128)(2,1)S(1)}, u32[]{:S(2)}, u32[]{:S(2)}) collective-permute-start(bf16[256,2048]{1,0:T(8,128)(2,1)S(1)} %slice.813), channel_id=1, source_target_pairs={{0,4},{4,0},{8,12},{12,8},{16,20},{20,16},{24,28},{28,24},{1,5},{5... | collective-permute-start | bytes 3145736 | tf_op jit(solution)/shard_map/ppermute | solution.py:155
  382.0 25.7 %collective-permute-start.41 = (bf16[256,2048]{1,0:T(8,128)(2,1)S(1)}, bf16[256,2048]{1,0:T(8,128)(2,1)S(1)}, u32[]{:S(2)}, u32[]{:S(2)}) collective-permute-start(bf16[256,2048]{1,0:T(8,128)(2,1)S(1)} %fusion.59), channel_id=1, source_target_pairs={{0,8},{4,12},{8,16},{12,20},{16,24},{20,28},{24,0},{28,4},{1,9},{5... | collective-permute-start | bytes 3145736 | tf_op jit(solution)/shard_map/ppermute | solution.py:151
  410.3 27.6 %collective-permute-start.44 = (bf16[256,2048]{1,0:T(8,128)(2,1)S(1)}, bf16[256,2048]{1,0:T(8,128)(2,1)S(1)}, u32[]{:S(2)}, u32[]{:S(2)}) collective-permute-start(bf16[256,2048]{1,0:T(8,128)(2,1)S(1)} %fusion.46), channel_id=1, source_target_pairs={{0,8},{4,12},{8,16},{12,20},{16,24},{20,28},{24,0},{28,4},{1,9},{5... | collective-permute-start | bytes 3145736 | tf_op jit(solution)/shard_map/ppermute | solution.py:151
  437.9 27.4 %collective-permute-start.49 = (bf16[256,2048]{1,0:T(8,128)(2,1)S(1)}, bf16[256,2048]{1,0:T(8,128)(2,1)S(1)}, u32[]{:S(2)}, u32[]{:S(2)}) collective-permute-start(bf16[256,2048]{1,0:T(8,128)(2,1)S(1)} %collective-permute-done.44), channel_id=1, source_target_pairs={{0,8},{4,12},{8,16},{12,20},{16,24},{20,28},{24,0},{28,4},{1,9},{5... | collective-permute-start | bytes 3145736 | tf_op jit(solution)/shard_map/ppermute | solution.py:151
  465.2 27.8 %collective-permute-start.50 = (bf16[256,2048]{1,0:T(8,128)(2,1)S(1)}, bf16[256,2048]{1,0:T(8,128)(2,1)S(1)}, u32[]{:S(2)}, u32[]{:S(2)}) collective-permute-start(bf16[256,2048]{1,0:T(8,128)(2,1)S(1)} %collective-permute-done.49), channel_id=1, source_target_pairs={{0,8},{4,12},{8,16},{12,20},{16,24},{20,28},{24,0},{28,4},{1,9},{5... | collective-permute-start | bytes 3145736 | tf_op jit(solution)/shard_map/ppermute | solution.py:151
  495.8 84.9 %collective-permute-start.57 = (bf16[256,2048]{1,0:T(8,128)(2,1)}, bf16[256,2048]{1,0:T(8,128)(2,1)}, u32[]{:S(2)}, u32[]{:S(2)}) collective-permute-start(bf16[256,2048]{1,0:T(8,128)(2,1)} %slice.809), channel_id=1, source_target_pairs={{0,4},{4,0},{8,12},{12,8},{16,20},{20,16},{24,28},{28,24},{1,5},{5... | collective-permute-start | bytes 3145736 | tf_op jit(solution)/shard_map/ppermute | solution.py:155
  497.8 27.0 %collective-permute-start.48 = (bf16[256,2048]{1,0:T(8,128)(2,1)S(1)}, bf16[256,2048]{1,0:T(8,128)(2,1)S(1)}, u32[]{:S(2)}, u32[]{:S(2)}) collective-permute-start(bf16[256,2048]{1,0:T(8,128)(2,1)S(1)} %copy-done.59), channel_id=1, source_target_pairs={{0,8},{4,12},{8,16},{12,20},{16,24},{20,28},{24,0},{28,4},{1,9},{5... | collective-permute-start | bytes 3145736 | tf_op jit(solution)/shard_map/ppermute | solution.py:151
  497.9 26.9 %collective-permute-start.53 = (bf16[256,2048]{1,0:T(8,128)(2,1)S(1)}, bf16[256,2048]{1,0:T(8,128)(2,1)S(1)}, u32[]{:S(2)}, u32[]{:S(2)}) collective-permute-start(bf16[256,2048]{1,0:T(8,128)(2,1)S(1)} %slice.811), channel_id=1, source_target_pairs={{0,4},{4,0},{8,12},{12,8},{16,20},{20,16},{24,28},{28,24},{1,5},{5... | collective-permute-start | bytes 3145736 | tf_op jit(solution)/shard_map/ppermute | solution.py:155
  526.3 26.5 %collective-permute-start.54 = (bf16[256,2048]{1,0:T(8,128)(2,1)}, bf16[256,2048]{1,0:T(8,128)(2,1)}, u32[]{:S(2)}, u32[]{:S(2)}) collective-permute-start(bf16[256,2048]{1,0:T(8,128)(2,1)} %fusion.55), channel_id=1, source_target_pairs={{0,8},{4,12},{8,16},{12,20},{16,24},{20,28},{24,0},{28,4},{1,9},{5... | collective-permute-start | bytes 3145736 | tf_op jit(solution)/shard_map/ppermute | solution.py:151
  527.4 25.4 %collective-permute-start.55 = (bf16[256,2048]{1,0:T(8,128)(2,1)}, bf16[256,2048]{1,0:T(8,128)(2,1)}, u32[]{:S(2)}, u32[]{:S(2)}) collective-permute-start(bf16[256,2048]{1,0:T(8,128)(2,1)} %slice.810), channel_id=1, source_target_pairs={{0,4},{4,0},{8,12},{12,8},{16,20},{20,16},{24,28},{28,24},{1,5},{5... | collective-permute-start | bytes 3145736 | tf_op jit(solution)/shard_map/ppermute | solution.py:155
  541.5 201.9 %reduce-scatter.6.cloned.1.call-start = ((), (), s32[]{:S(2)}) async-start(), calls=%async_computation.13 | async-start | bytes 10485760 | tf_op jit(solution)/shard_map/reduce_scatter | solution.py:675
  555.4 25.3 %collective-permute-start.56 = (bf16[256,2048]{1,0:T(8,128)(2,1)S(1)}, bf16[256,2048]{1,0:T(8,128)(2,1)S(1)}, u32[]{:S(2)}, u32[]{:S(2)}) collective-permute-start(bf16[256,2048]{1,0:T(8,128)(2,1)S(1)} %fusion.53), channel_id=1, source_target_pairs={{0,8},{4,12},{8,16},{12,20},{16,24},{20,28},{24,0},{28,4},{1,9},{5... | collective-permute-start | bytes 3145736 | tf_op jit(solution)/shard_map/ppermute | solution.py:151
  586.1 18.6 %collective-permute-start.59 = (bf16[128,2048]{1,0:T(8,128)(2,1)S(1)}, bf16[128,2048]{1,0:T(8,128)(2,1)S(1)}, u32[]{:S(2)}, u32[]{:S(2)}) collective-permute-start(bf16[128,2048]{1,0:T(8,128)(2,1)S(1)} %get-tuple-element.293), channel_id=1, source_target_pairs={{0,1},{1,0},{2,3},{3,2},{4,5},{5,4},{6,7},{7,6},{8,9},{9,8},{10,11... | collective-permute-start | bytes 1572872 | tf_op jit(solution)/shard_map/ppermute | solution.py:56
  587.5 18.8 %collective-permute-start.58 = (bf16[128,2048]{1,0:T(8,128)(2,1)S(1)}, bf16[128,2048]{1,0:T(8,128)(2,1)S(1)}, u32[]{:S(2)}, u32[]{:S(2)}) collective-permute-start(bf16[128,2048]{1,0:T(8,128)(2,1)S(1)} %get-tuple-element.295), channel_id=1, source_target_pairs={{0,2},{1,3},{2,0},{3,1},{4,6},{5,7},{6,4},{7,5},{8,10},{9,11},{10,... | collective-permute-start | bytes 1572872 | tf_op jit(solution)/shard_map/ppermute | solution.py:56
  605.7 24.3 %collective-permute-start.61 = (bf16[256,2048]{1,0:T(8,128)(2,1)}, bf16[256,2048]{1,0:T(8,128)(2,1)}, u32[]{:S(2)}, u32[]{:S(2)}) collective-permute-start(bf16[256,2048]{1,0:T(8,128)(2,1)} %pad_maximum_fusion.10), channel_id=1, source_target_pairs={{0,2},{1,3},{2,0},{3,1},{4,6},{5,7},{6,4},{7,5},{8,10},{9,11},{10,... | collective-permute-start | bytes 3145736 | tf_op jit(solution)/shard_map/ppermute | solution.py:56
  607.3 24.0 %collective-permute-start.60 = (bf16[256,2048]{1,0:T(8,128)(2,1)}, bf16[256,2048]{1,0:T(8,128)(2,1)}, u32[]{:S(2)}, u32[]{:S(2)}) collective-permute-start(bf16[256,2048]{1,0:T(8,128)(2,1)} %pad_maximum_fusion.9), channel_id=1, source_target_pairs={{0,1},{1,0},{2,3},{3,2},{4,5},{5,4},{6,7},{7,6},{8,9},{9,8},{10,11... | collective-permute-start | bytes 3145736 | tf_op jit(solution)/shard_map/ppermute | solution.py:56
  638.4 40.2 %all-to-all-start.3 = ((bf16[8,256,256]{2,1,0:T(8,128)(2,1)}), bf16[8,256,256]{2,1,0:T(8,128)(2,1)}, u32[]{:S(2)}, u32[]{:S(2)}) async-start(bf16[8,256,256]{2,1,0:T(8,128)(2,1)} %bitcast.145), calls=%async_computation.4 | async-start | bytes 2097152 | tf_op jit(solution)/shard_map/all_to_all | solution.py:122
  682.1 29.3 %all-to-all-start.4 = ((bf16[4,2,256,256]{3,2,1,0:T(8,128)(2,1)}), bf16[4,2,256,256]{3,2,1,0:T(8,128)(2,1)S(1)}, u32[]{:S(2)}, u32[]{:S(2)}) async-start(bf16[4,2,256,256]{3,2,1,0:T(8,128)(2,1)} %bitcast.27), calls=%async_computation.5 | async-start | bytes 2097152 | tf_op jit(solution)/shard_map/all_to_all | solution.py:122
  710.3 33.1 %collective-permute-start.68 = (bf16[1024,384]{1,0:T(8,128)(2,1)}, bf16[1024,384]{1,0:T(8,128)(2,1)}, u32[]{:S(2)}, u32[]{:S(2)}) collective-permute-start(bf16[1024,384]{1,0:T(8,128)(2,1)} %get-tuple-element.268), channel_id=1, source_target_pairs={{0,4},{4,0},{8,12},{12,8},{16,20},{20,16},{24,28},{28,24},{1,5},{5... | collective-permute-start | bytes 2359304 | tf_op jit(solution)/shard_map/ppermute | solution.py:155
  710.8 45.4 %collective-permute-start.70 = (bf16[1024,384]{1,0:T(8,128)(2,1)}, bf16[1024,384]{1,0:T(8,128)(2,1)}, u32[]{:S(2)}, u32[]{:S(2)}) collective-permute-start(bf16[1024,384]{1,0:T(8,128)(2,1)} %get-tuple-element.267), channel_id=1, source_target_pairs={{0,4},{4,0},{8,12},{12,8},{16,20},{20,16},{24,28},{28,24},{1,5},{5... | collective-permute-start | bytes 2359304 | tf_op jit(solution)/shard_map/ppermute | solution.py:155
  710.9 88.8 %collective-permute-start.73 = (bf16[1024,384]{1,0:T(8,128)(2,1)}, bf16[1024,384]{1,0:T(8,128)(2,1)}, u32[]{:S(2)}, u32[]{:S(2)}) collective-permute-start(bf16[1024,384]{1,0:T(8,128)(2,1)} %get-tuple-element.266), channel_id=1, source_target_pairs={{0,4},{4,0},{8,12},{12,8},{16,20},{20,16},{24,28},{28,24},{1,5},{5... | collective-permute-start | bytes 2359304 | tf_op jit(solution)/shard_map/ppermute | solution.py:155
  715.4 26.0 %collective-permute-start.67 = (bf16[1024,384]{1,0:T(8,128)(2,1)}, bf16[1024,384]{1,0:T(8,128)(2,1)}, u32[]{:S(2)}, u32[]{:S(2)}) collective-permute-start(bf16[1024,384]{1,0:T(8,128)(2,1)} %add_convert_fusion.4), channel_id=1, source_target_pairs={{0,8},{4,12},{8,16},{12,20},{16,24},{20,28},{24,0},{28,4},{1,9},{5... | collective-permute-start | bytes 2359304 | tf_op jit(solution)/shard_map/ppermute | solution.py:151
  718.0 23.4 %all-to-all-start.5 = ((f32[4,2,640]{2,1,0:T(2,128)}), f32[4,2,640]{2,1,0:T(2,128)S(1)}, u32[]{:S(2)}, u32[]{:S(2)}) async-start(f32[4,2,640]{2,1,0:T(2,128)} %pad_maximum_fusion.15), calls=%async_computation.6 | async-start | bytes 40960 | tf_op jit(solution)/shard_map/all_to_all | solution.py:122
  722.0 56.8 %reduce-scatter.8.cloned.1.call-start = ((), (), s32[]{:S(2)}) async-start(), calls=%async_computation.14 | async-start | bytes 2359296 | tf_op jit(solution)/shard_map/reduce_scatter | solution.py:697
  741.2 42.0 %collective-permute-start.74 = (bf16[256,2048]{1,0:T(8,128)(2,1)}, bf16[256,2048]{1,0:T(8,128)(2,1)S(1)}, u32[]{:S(2)}, u32[]{:S(2)}) collective-permute-start(bf16[256,2048]{1,0:T(8,128)(2,1)} %get-tuple-element.279), channel_id=1, source_target_pairs={{0,2},{1,3},{2,0},{3,1},{4,6},{5,7},{6,4},{7,5},{8,10},{9,11},{10,... | collective-permute-start | bytes 3145736 | tf_op jit(solution)/shard_map/ppermute | solution.py:56
  741.4 41.9 %collective-permute-start.66 = (bf16[256,2048]{1,0:T(8,128)(2,1)}, bf16[256,2048]{1,0:T(8,128)(2,1)}, u32[]{:S(2)}, u32[]{:S(2)}) collective-permute-start(bf16[256,2048]{1,0:T(8,128)(2,1)} %get-tuple-element.278), channel_id=1, source_target_pairs={{0,1},{1,0},{2,3},{3,2},{4,5},{5,4},{6,7},{7,6},{8,9},{9,8},{10,11... | collective-permute-start | bytes 3145736 | tf_op jit(solution)/shard_map/ppermute | solution.py:56
  746.2 29.8 %collective-permute-start.69 = (bf16[1024,384]{1,0:T(8,128)(2,1)}, bf16[1024,384]{1,0:T(8,128)(2,1)}, u32[]{:S(2)}, u32[]{:S(2)}) collective-permute-start(bf16[1024,384]{1,0:T(8,128)(2,1)} %add_convert_fusion.3), channel_id=1, source_target_pairs={{0,8},{4,12},{8,16},{12,20},{16,24},{20,28},{24,0},{28,4},{1,9},{5... | collective-permute-start | bytes 2359304 | tf_op jit(solution)/shard_map/ppermute | solution.py:151
  778.8 20.9 %collective-permute-start.72 = (bf16[1024,384]{1,0:T(8,128)(2,1)}, bf16[1024,384]{1,0:T(8,128)(2,1)}, u32[]{:S(2)}, u32[]{:S(2)}) collective-permute-start(bf16[1024,384]{1,0:T(8,128)(2,1)} %add_convert_fusion.2), channel_id=1, source_target_pairs={{0,8},{4,12},{8,16},{12,20},{16,24},{20,28},{24,0},{28,4},{1,9},{5... | collective-permute-start | bytes 2359304 | tf_op jit(solution)/shard_map/ppermute | solution.py:151
  788.6 18.1 %collective-permute-start.71 = (bf16[128,2048]{1,0:T(8,128)(2,1)}, bf16[128,2048]{1,0:T(8,128)(2,1)}, u32[]{:S(2)}, u32[]{:S(2)}) collective-permute-start(bf16[128,2048]{1,0:T(8,128)(2,1)} %slice.818), channel_id=1, source_target_pairs={{0,2},{1,3},{2,0},{3,1},{4,6},{5,7},{6,4},{7,5},{8,10},{9,11},{10,... | collective-permute-start | bytes 1572872 | tf_op jit(solution)/shard_map/ppermute | solution.py:56
  789.5 18.7 %collective-permute-start.75 = (bf16[128,2048]{1,0:T(8,128)(2,1)}, bf16[128,2048]{1,0:T(8,128)(2,1)}, u32[]{:S(2)}, u32[]{:S(2)}) collective-permute-start(bf16[128,2048]{1,0:T(8,128)(2,1)} %slice.817), channel_id=1, source_target_pairs={{0,1},{1,0},{2,3},{3,2},{4,5},{5,4},{6,7},{7,6},{8,9},{9,8},{10,11... | collective-permute-start | bytes 1572872 | tf_op jit(solution)/shard_map/ppermute | solution.py:56
  802.0 16.3 %collective-permute-start.76 = (bf16[512,384]{0,1:T(8,128)(2,1)S(1)}, bf16[512,384]{0,1:T(8,128)(2,1)}, u32[]{:S(2)}, u32[]{:S(2)}) collective-permute-start(bf16[512,384]{0,1:T(8,128)(2,1)S(1)} %bitcast.159), channel_id=1, source_target_pairs={{0,0},{1,1},{4,2},{5,3},{2,4},{3,5},{6,6},{7,7},{8,8},{9,9},{12,10... | collective-permute-start | bytes 1179656 | tf_op jit(solution)/shard_map/ppermute | solution.py:271
  (121 other events, 1095.9 us)
Sparse Core Ops, SparseCore 0:
  92.2 99.7 all-gather.2
  241.2 52.6 all-gather.4
  541.7 59.6 reduce-scatter.3
  636.1 89.0 reduce-scatter.5
  728.1 42.0 reduce-scatter.7
